TPU v7x, 128 devices: a whole 4x4x4 slice. The times are simulated.
128 devices in a mesh: gx: 16 (over y, x), gy: 8 (over z, core).
Axes of the slice: x: 4, y: 4, z: 4, core: 2. Of those that a mesh axis runs over, the one named last changes fastest.
Arguments:
- inputs: bfloat16 [8192, 6144], P('gy', 'gx'), may hold values from -24 to 24, as said below
- preact: bfloat16 [8192, 24576], P('gy', 'gx'), may hold values from -6 to 6
- upstream: bfloat16 [8192, 24576], P('gy', 'gx'), as said below
- weight: float32 [6144, 24576], P('gy', 'gx'), may hold values from -72 to 72, as said below
- row_factor: float32 [6144], P('gy'), may hold values from 0.2 to 20, as said below
- column_factor: float32 [24576], P('gx'), may hold values from 0.5 to 5
Outputs:
- update: float32 [6144, 24576], P('gy', 'gx')
- new_row_factor: float32 [6144], P('gy')
- new_column_factor: float32 [24576], P('gx')
Inputs may be any that keep to these rules, and one draw needn't show every extreme that they name: `inputs`: entries lie within 24 in magnitude. `upstream`: entries lie within 36 / sqrt(8192) in magnitude. `weight`: entries lie within 72 in magnitude. `row_factor`: positive entries.
All inputs are finite; a program needn't handle non-finite values.
Results may differ from a plain program's by a relative error of at most 0.015.
Values may be sent and summed in bfloat16 or wider, within the bound.
No kernel may reach another device: no remote copies, remote signals or barrier semaphores. Data moves between devices by JAX's collectives and lax.ppermute only.
A program may use at most 192 MiB of HBM per device.

v0:
```python
import jax
import jax.numpy as jnp
from jax import lax
from jax.experimental import pallas as pl
from jax.experimental.pallas import tpu as pltpu
from jax.sharding import PartitionSpec as P

D = 6144
FF = 24576
TOK = 1024
FEAT = 384
HALF = 768
NCH = 2

second_decay = 0.8
clip_ratio = 1.0
unit_eps = 1e-06
factor_eps = 1e-30

BOTH = ("gx", "gy")
FLIP = (0, 2, 1, 3)


def moves(dx, dy, dz, other_core):
    pairs = []
    for y in range(4):
        for x in range(4):
            for z in range(4):
                for core in range(2):
                    s = 1 - 2 * core
                    tx, ty, tz = (x + s * dx) % 4, (y + s * dy) % 4, (z + s * dz) % 4
                    tc = 1 - core if other_core else core
                    pairs.append(((y * 4 + x) * 8 + z * 2 + core, (ty * 4 + tx) * 8 + tz * 2 + tc))
    return pairs


ALONG_X = moves(1, 0, 0, False)
ALONG_Y = moves(0, 1, 0, False)
ALONG_Z = moves(0, 0, 1, False)
ALONG_Z2 = moves(0, 0, 2, False)
ALONG_Z3 = moves(0, 0, 3, False)
SWAP = moves(0, 0, 0, True)


STEPS = (0, -1, 1, 2)
CHEAP = pl.CostEstimate(flops=1024, bytes_accessed=1024, transcendentals=0)


def coordinates():
    gx, gy = lax.axis_index("gx"), lax.axis_index("gy")
    return gx >> 2, gx & 3, gy >> 1, gy & 1


def send(value, pairs):
    return lax.ppermute(value, BOTH, pairs)


def slope_half(preact, upstream, other, waits=()):
    count = 4
    rows = TOK // count

    def kernel(pre_ref, up_ref, *refs):
        out, pre, up, sems = refs[len(waits) :]
        core = coordinates()[3]
        half = 1 - core if other else core
        columns = pl.ds(pl.multiple_of(half * HALF, HALF), HALF)
        for k in range(count):
            at = pl.ds(k * rows, rows)
            pltpu.make_async_copy(pre_ref.at[at, columns], pre.at[at], sems.at[0, k]).start()
            pltpu.make_async_copy(up_ref.at[at, columns], up.at[at], sems.at[1, k]).start()
        for k in range(count):
            at = pl.ds(k * rows, rows)
            pltpu.make_async_copy(pre.at[at], pre.at[at], sems.at[0, k]).wait()
            pltpu.make_async_copy(up.at[at], up.at[at], sems.at[1, k]).wait()

            @pl.loop(0, rows // 16)
            def _(j):
                tile = pl.ds(pl.multiple_of(k * rows + j * 16, 16), 16)
                value = pre[tile].astype(jnp.float32)
                normal_cdf = 0.5 * (1.0 + lax.erf(value * 0.7071067811865476))
                density = jnp.exp(-0.5 * value * value) * 0.3989422804014327
                slope = up[tile].astype(jnp.float32) * (normal_cdf + value * density)
                out[tile] = slope.astype(jnp.bfloat16)

    anywhere = pl.BlockSpec(memory_space=pl.ANY)
    half_block = pltpu.VMEM((TOK, HALF), jnp.bfloat16)
    return pl.pallas_call(
        kernel,
        out_shape=jax.ShapeDtypeStruct((TOK, HALF), jnp.bfloat16),
        in_specs=[anywhere] * (2 + len(waits)),
        out_specs=pl.BlockSpec(memory_space=pltpu.VMEM),
        scratch_shapes=[half_block, half_block, pltpu.SemaphoreType.DMA((2, count))],
        compiler_params=pltpu.CompilerParams(vmem_limit_bytes=24 << 20),
        cost_estimate=CHEAP,
    )(preact, upstream, *waits)


def unit_partials(slope_own, slope_other, entries, low, high, waits=()):
    arrays = []
    position = {}
    plan = []
    rows = 0
    for places in entries:
        count = places[0][0][0].shape[-2]
        for i, halves in enumerate(places):
            for h, (array, index) in enumerate(halves):
                if id(array) not in position:
                    position[id(array)] = len(arrays)
                    arrays.append(array)
                plan.append((i, h, rows, count, position[id(array)], index))
        rows += count
    many = high - low

    def kernel(own_ref, other_ref, *refs):
        feature_refs = refs[: len(arrays)]
        outs = refs[len(arrays) + len(waits) : len(arrays) + len(waits) + many]
        held, slopes, feature_sem, slope_sem = refs[len(arrays) + len(waits) + many :]
        pltpu.make_async_copy(own_ref, slopes.at[pl.ds(0, TOK)], slope_sem).start()
        pltpu.make_async_copy(other_ref, slopes.at[pl.ds(TOK, TOK)], slope_sem).start()
        y, _, z, core = coordinates()
        for i in range(4):
            place = ((1 - 2 * core) * (z - y) - STEPS[i] + 3) & 3

            @pl.when((place >= low) & (place < high))
            def _():
                base = pl.multiple_of((place - low) * rows, rows)
                for at, h, start, count, which, index in plan:
                    if at == i:
                        source = feature_refs[which]
                        source = source.at[index] if index is not None else source
                        pltpu.make_async_copy(
                            source,
                            held.at[pl.ds(base + start, count), pl.ds(h * TOK, TOK)],
                            feature_sem,
                        ).start()

        pltpu.make_async_copy(slopes, slopes, slope_sem).wait()
        pltpu.make_async_copy(held, held, feature_sem).wait()

        @pl.loop(0, HALF // 256)
        def _(j):
            columns = pl.ds(pl.multiple_of(j * 256, 256), 256)
            total = jnp.dot(held[...], slopes[:, columns], preferred_element_type=jnp.float32)
            for k, out in enumerate(outs):
                out[:, columns] = total[k * rows : (k + 1) * rows].astype(out.dtype)

    vmem = pl.BlockSpec(memory_space=pltpu.VMEM)
    anywhere = pl.BlockSpec(memory_space=pl.ANY)
    return pl.pallas_call(
        kernel,
        out_shape=tuple(
            jax.ShapeDtypeStruct((rows, HALF), jnp.float32 if k == 3 else jnp.bfloat16)
            for k in range(low, high)
        ),
        in_specs=[anywhere] * (2 + len(arrays) + len(waits)),
        out_specs=(vmem,) * many,
        scratch_shapes=[
            pltpu.VMEM((many * rows, 2 * TOK), jnp.bfloat16),
            pltpu.VMEM((2 * TOK, HALF), jnp.bfloat16),
            pltpu.SemaphoreType.DMA,
            pltpu.SemaphoreType.DMA,
        ],
        compiler_params=pltpu.CompilerParams(vmem_limit_bytes=44 << 20),
        cost_estimate=CHEAP,
    )(slope_own, slope_other, *arrays, *waits)


def add_narrow(a, b):
    return (a.astype(jnp.float32) + b.astype(jnp.float32)).astype(jnp.bfloat16)


def after(value, *before):
    return lax.optimization_barrier((value,) + before)[0]


def stack_places(values):
    size = values[0].shape[0] // NCH

    def kernel(*refs):
        sources, outs, sems = refs[:4], refs[4 : 4 + NCH], refs[4 + NCH]
        for k in range(NCH):
            for i, source in enumerate(sources):
                pltpu.make_async_copy(
                    source.at[pl.ds(k * size, size)], outs[k].at[i], sems.at[k]
                ).start()
        for k in range(NCH):
            pltpu.make_async_copy(outs[k], outs[k], sems.at[k]).wait()

    anywhere = pl.BlockSpec(memory_space=pl.ANY)
    return pl.pallas_call(
        kernel,
        out_shape=(jax.ShapeDtypeStruct((4, size, TOK), jnp.bfloat16),) * NCH,
        in_specs=[anywhere] * 4,
        out_specs=(anywhere,) * NCH,
        scratch_shapes=[pltpu.SemaphoreType.DMA((NCH,))],
        cost_estimate=CHEAP,
    )(*values)


def place_rows(last, got, pieces, before):
    rows = last.shape[0]

    def kernel(last_ref, got_ref, *refs):
        kept, sent, sums, value, sem = refs[len(before) :]
        total = last_ref[...] + got_ref[...].astype(jnp.float32)
        value[...] = total
        _, x, _, core = coordinates()
        for g, low, start, count in pieces:
            column = (x + (1 - 2 * core) * STEPS[g]) & 3
            row = pl.multiple_of((column & 1) * FEAT + low, 32)
            source = value.at[pl.ds(start, count)]

            @pl.when((column >> 1) == core)
            def _():
                pltpu.make_async_copy(source, kept.at[pl.ds(row, count)], sem).start()

            @pl.when((column >> 1) != core)
            def _():
                pltpu.make_async_copy(source, sent.at[pl.ds(row, count)], sem).start()

        squares = jnp.sum(total * total, axis=0, keepdims=True)
        sums[...] = squares + refs[2][...] if before else squares
        pltpu.make_async_copy(value, value, sem).wait()

    anywhere = pl.BlockSpec(memory_space=pl.ANY)
    vmem = pl.BlockSpec(memory_space=pltpu.VMEM)
    block = jax.ShapeDtypeStruct((HALF, HALF), jnp.float32)
    return pl.pallas_call(
        kernel,
        out_shape=(block, block, jax.ShapeDtypeStruct((1, HALF), jnp.float32)),
        in_specs=[vmem, vmem]
        + ([anywhere, anywhere, vmem] if before else []),
        out_specs=(anywhere, anywhere, vmem),
        scratch_shapes=[pltpu.VMEM((rows, HALF), jnp.float32), pltpu.SemaphoreType.DMA],
        input_output_aliases={2: 0, 3: 1} if before else {},
        compiler_params=pltpu.CompilerParams(vmem_limit_bytes=24 << 20),
        cost_estimate=CHEAP,
    )(last, got, *before)


def everyone(vector, axis, count):
    return lax.all_to_all(
        jnp.broadcast_to(vector[None, :], (count,) + vector.shape), axis, 0, 0, tiled=True
    )


def per_device(inputs, preact, upstream, weight, row_factor, column_factor):
    core = coordinates()[3]

    mine = inputs.T
    p, q = lax.optimization_barrier((mine[: FEAT // 2], mine[FEAT // 2 :]))
    size = FEAT // 2 // NCH

    p_swap, q_swap = send(p, SWAP), send(q, SWAP)
    ya, xa = send(p, ALONG_Y), send(q, ALONG_X)
    yb, xb = send(p_swap, ALONG_Y), send(q_swap, ALONG_X)

    slope_yours = slope_half(preact, upstream, True, (p_swap, q_swap))
    slope_other = send(slope_yours, SWAP)
    slope_mine = slope_half(preact, upstream, False, (p_swap, q_swap))
    ya, xa, yb, xb = lax.optimization_barrier((ya, xa, yb, xb, slope_other, slope_mine))[:4]
    y2, x2 = send(ya, ALONG_Y), send(xa, ALONG_X)
    weight = after(weight, slope_mine)
    weight_local = jnp.sum(weight * weight, axis=0)
    row_local = jnp.broadcast_to(jnp.sum(row_factor)[None], (128,))
    weight_mine = lax.dynamic_slice_in_dim(weight_local, core * HALF, HALF)
    weight_yours = lax.dynamic_slice_in_dim(weight_local, (1 - core) * HALF, HALF)

    ya_swap, yb_swap = send(ya, SWAP), send(yb, SWAP)
    xa_swap = send(after(xa, ya_swap, yb_swap), SWAP)
    xb_swap = send(after(xb, ya_swap, yb_swap), SWAP)
    early_swap = send(after(jnp.concatenate([weight_yours, row_local]), ya_swap, yb_swap), SWAP)
    early = jnp.concatenate([weight_mine, row_local]) + early_swap
    y2_swap = send(after(y2, xa_swap, xb_swap, early_swap), SWAP)
    x2_swap = send(after(x2, xa_swap, xb_swap, early_swap), SWAP)
    p_own = stack_places((p, ya, yb_swap, y2))
    q_own = stack_places((q, xa, xb_swap, x2))
    p_other = stack_places((p_swap, yb, ya_swap, y2_swap))
    q_other = stack_places((q_swap, xb, xa_swap, x2_swap))

    def units(entries, low=0, high=4, waits=()):
        return unit_partials(slope_mine, slope_other, entries, low, high, waits)

    def hop(value):
        return send(value, ALONG_Z)

    own_entries = [((p, None), (p_swap, None)), ((ya, None), (yb, None))]
    own_entries += [((yb_swap, None), (ya_swap, None)), ((y2, None), (y2_swap, None))]
    own = units([own_entries], waits=(early, p_other[0], q_other[0]))

    def gather(chunk, gate_a, gate_b, gate_2):
        xa, ya = send(after(p_own[chunk], *gate_a), ALONG_X), send(after(q_own[chunk], *gate_a), ALONG_Y)
        xb, yb = send(after(p_other[chunk], *gate_b), ALONG_X), send(after(q_other[chunk], *gate_b), ALONG_Y)
        x2, y2 = send(after(xa, *gate_2), ALONG_X), send(after(ya, *gate_2), ALONG_Y)
        return xa, ya, xb, yb, x2, y2

    def swap_near(xa, ya, xb, yb, *gate):
        xa, ya, xb, yb = lax.optimization_barrier((xa, ya, xb, yb, *gate))[:4]
        xa_swap, xb_swap = send(xa, SWAP), send(xb, SWAP)
        ya_swap = send(after(ya, xa_swap, xb_swap), SWAP)
        yb_swap = send(after(yb, xa_swap, xb_swap), SWAP)
        return xa_swap, ya_swap, xb_swap, yb_swap

    def swap_far(x2, y2, *gate):
        x2, y2 = lax.optimization_barrier((x2, y2, *gate))[:2]
        return send(x2, SWAP), send(y2, SWAP)

    def near_entries(xa, xb, xa_swap, xb_swap):
        return [
            [((xa, i), (xb, i)) for i in range(4)],
            [((xb_swap, FLIP[i]), (xa_swap, FLIP[i])) for i in range(4)],
        ]

    def far_entries(chunk, ya, yb, ya_swap, yb_swap, x2, x2_swap, y2, y2_swap):
        entries = [[((x2, i), (x2_swap, FLIP[i])) for i in range(4)]]
        for g in range(4):
            entries.append(
                [
                    ((q_own[chunk], g), (q_other[chunk], g)),
                    ((ya, g), (yb, g)),
                    ((yb_swap, FLIP[g]), (ya_swap, FLIP[g])),
                    ((y2, g), (y2_swap, FLIP[g])),
                ]
            )
        return entries

    xa, ya, xb, yb, x2, y2 = gather(0, (), (), (own[0],))
    own_got = hop(own[0])
    own_2 = add_narrow(own[1], own_got)
    xa_swap, ya_swap, xb_swap, yb_swap = swap_near(xa, ya, xb, yb, own_2)
    own_got = hop(own_2)
    near0 = units(near_entries(xa, xb, xa_swap, xb_swap))
    near0_got = hop(near0[0])
    own_3 = add_narrow(own[2], own_got)
    x2_swap, y2_swap = swap_far(x2, y2, near0[0], ya_swap, yb_swap)
    own_got = hop(own_3)
    far0_entries = far_entries(0, ya, yb, ya_swap, yb_swap, x2, x2_swap, y2, y2_swap)
    xa, ya, xb, yb, x2, y2 = gather(1, (ya_swap, yb_swap, near0[0]), (x2_swap, y2_swap), ())
    far0 = units(far0_entries, 0, 2, waits=(xa, ya, own_3))
    far0_got = hop(far0[0])

    near0_2 = add_narrow(near0[1], near0_got)
    near0_got = hop(near0_2)
    far0 += units(far0_entries, 2, 4, waits=(near0_2,))
    xa_swap, ya_swap, xb_swap, yb_swap = swap_near(xa, ya, xb, yb, far0[2])
    far0_2 = add_narrow(far0[1], far0_got)
    near1 = units(near_entries(xa, xb, xa_swap, xb_swap), waits=(far0_2,))
    far0_got = hop(far0_2)
    near1_got = hop(near1[0])
    near0_3 = add_narrow(near0[2], near0_got)
    x2_swap, y2_swap = swap_far(x2, y2, near1[0], ya_swap, yb_swap)
    near0_got = hop(near0_3)
    far1_entries = far_entries(1, ya, yb, ya_swap, yb_swap, x2, x2_swap, y2, y2_swap)
    far1 = units(far1_entries, 0, 2, waits=(near0_3,))
    far1_got = hop(far1[0])
    near1_2 = add_narrow(near1[1], near1_got)
    near1_got = hop(near1_2)
    far0_3 = add_narrow(far0[2], far0_got)
    far1 += units(far1_entries, 2, 4, waits=(near1_2, far0_3))
    far0_got = hop(far0_3)

    placed = place_rows(own[3], own_got, [(0, 0, 0, FEAT // 2)], ())
    near_pieces = lambda chunk: [(1, chunk * size, 0, size), (2, chunk * size, size, size)]
    far_pieces = lambda chunk: [(3, chunk * size, 0, size)] + [
        (g, FEAT // 2 + chunk * size, (g + 1) * size, size) for g in range(4)
    ]
    placed = place_rows(near0[3], near0_got, near_pieces(0), placed)
    far1_got = hop(after(add_narrow(far1[1], far1_got), placed[2]))
    near1_got = hop(add_narrow(near1[2], near1_got))
    placed = place_rows(far0[3], far0_got, far_pieces(0), placed)
    far1_got = hop(after(add_narrow(far1[2], far1_got), placed[2]))
    placed = place_rows(near1[3], near1_got, near_pieces(1), placed)
    placed = place_rows(far1[3], far1_got, far_pieces(1), placed)
    kept, sent, grad_local = placed
    got = send(sent, SWAP)
    grad_local = grad_local[0]
    column_stats = jnp.concatenate([grad_local, early])
    for pairs in (ALONG_Z, ALONG_Z2, ALONG_Z3):
        column_stats = column_stats + send(jnp.concatenate([grad_local, early]), pairs)
    mine_stats = column_stats[: 2 * HALF]
    yours_stats = send(mine_stats, SWAP)

    def all_columns(start):
        a, b = mine_stats[start : start + HALF], yours_stats[start : start + HALF]
        return jnp.concatenate([jnp.where(core == 0, a, b), jnp.where(core == 0, b, a)])

    grad_sq = all_columns(0)
    weight_col_sq = all_columns(HALF)
    row_total = column_stats[2 * HALF]

    clip_factor = jnp.minimum(
        1.0, clip_ratio * jnp.sqrt(weight_col_sq) / (jnp.sqrt(grad_sq) + unit_eps)
    )
    column_sums = clip_factor * clip_factor * grad_sq
    new_column = second_decay * column_factor + (1.0 - second_decay) * (
        column_sums / D + factor_eps
    )
    grad = jnp.concatenate(
        [jnp.where(core == 0, kept, got), jnp.where(core == 0, got, kept)], axis=1
    )
    clipped = grad * clip_factor[None, :]
    row_part = jnp.sum(clipped * clipped, axis=1)
    totals = jnp.concatenate(
        [
            jnp.broadcast_to(jnp.sum(column_sums)[None], (128,)),
            jnp.broadcast_to(jnp.sum(weight_col_sq)[None], (128,)),
        ]
    )
    summed = jnp.sum(everyone(jnp.concatenate([row_part, totals]), "gx", 16), axis=0)
    row_sums, clipped_total, weight_total = summed[:768], summed[768], summed[896]
    new_row = second_decay * row_factor + (1.0 - second_decay) * (row_sums / FF + factor_eps)
    row_mean = (
        second_decay * row_total + (1.0 - second_decay) * (clipped_total / FF + D * factor_eps)
    ) / D
    weight_rms = jnp.sqrt(weight_total / (D * FF))
    update = (
        -weight_rms
        * clipped
        * lax.rsqrt(new_row)[:, None]
        * (jnp.sqrt(row_mean) * lax.rsqrt(new_column))[None, :]
    )
    return (update, new_row, new_column)


def solution(mesh):
    in_specs = (P("gy", "gx"), P("gy", "gx"), P("gy", "gx"), P("gy", "gx"), P("gy"), P("gx"))
    out_specs = (P("gy", "gx"), P("gy"), P("gx"))
    return jax.shard_map(
        per_device, mesh=mesh, in_specs=in_specs, out_specs=out_specs, check_vma=False
    )
```

profile of v0, /device:TPU:0, one launch (start us, length us, event | category | flops | bytes accessed | tf_op | source)
XLA Modules:
  0.0 451.5 jit_solution(13238996169573044114)
XLA Ops:
  0.6 2.4 copy.19
  6.7 1.9 copy-done.6
  8.5 2.5 shard_map.86
  11.3 1.6 collective-permute-start.4
  12.9 1.6 collective-permute-start.3
  14.4 1.5 collective-permute-start.6
  15.9 1.6 collective-permute-start.5
  17.5 2.5 shard_map.85.own_ref
  20.3 1.6 collective-permute-done.3.refs_1_.refs_2_
  21.9 2.6 collective-permute-done.6.refs_1_
  24.5 1.7 collective-permute-done.5.refs_1_.refs_3_
  29.2 1.7 collective-permute-start.11
  31.0 2.7 multiply_reduce_fusion.1
  35.0 2.4 collective-permute-done.12.refs_3_
  38.4 48.8 %shard_map.87 = (bf16[4,96,1024]{2,1,0:T(8,128)(2,1)}, bf16[4,96,1024]{2,1,0:T(8,128)(2,1)}) custom-call(bf16[192,1024]{1,0:T(8,128)(2,1)} %copy-done.14, bf16[192,1024]{1,0:T(8,128)(2,1)} %copy-done.21, bf16[192,1024]{1,0:T(8,128)(2,1)} %collective-permute-done.7.refs_2_.refs_4_, bf16[192,1024]{1,0:T(8,128)(2,1)} %collective-permute-done.8.refs_3_.refs_6_), custom_call_target="tpu_custom_call" | custom-call | flops 1024 | bytes 1024 | tf_op jit(solution)/shard_map/pallas_call | solution.py:190
  87.6 48.8 %shard_map.88 = (bf16[4,96,1024]{2,1,0:T(8,128)(2,1)}, bf16[4,96,1024]{2,1,0:T(8,128)(2,1)}) custom-call(bf16[192,1024]{1,0:T(8,128)(2,1)} %copy-done.35, bf16[192,1024]{1,0:T(8,128)(2,1)} %copy-done.37, bf16[192,1024]{1,0:T(8,128)(2,1)} %copy-done.39, bf16[192,1024]{1,0:T(8,128)(2,1)} %collective-permute-done.12.refs_3_), custom_call_target="tpu_custom_call" | custom-call | flops 1024 | bytes 1024 | tf_op jit(solution)/shard_map/pallas_call | solution.py:190
  136.3 1.3 collective-permute-start.13
  137.6 48.8 %shard_map.90 = (bf16[4,96,1024]{2,1,0:T(8,128)(2,1)}, bf16[4,96,1024]{2,1,0:T(8,128)(2,1)}) custom-call(bf16[192,1024]{1,0:T(8,128)(2,1)} %copy-done.13, bf16[192,1024]{1,0:T(8,128)(2,1)} %copy-done.36, bf16[192,1024]{1,0:T(8,128)(2,1)} %copy-done.38, bf16[192,1024]{1,0:T(8,128)(2,1)} %collective-permute-done.18.refs_3_), custom_call_target="tpu_custom_call" | custom-call | flops 1024 | bytes 1024 | tf_op jit(solution)/shard_map/pallas_call | solution.py:190
  186.4 2.1 collective-permute-start.19
  188.5 48.8 %shard_map.89 = (bf16[4,96,1024]{2,1,0:T(8,128)(2,1)}, bf16[4,96,1024]{2,1,0:T(8,128)(2,1)}) custom-call(bf16[192,1024]{1,0:T(8,128)(2,1)} %copy-done.11, bf16[192,1024]{1,0:T(8,128)(2,1)} %collective-permute-done.5.refs_1_.refs_3_, bf16[192,1024]{1,0:T(8,128)(2,1)} %collective-permute-done.10.refs_2_.refs_5_, ...), custom_call_target="tpu_custom_call" | custom-call | flops 1024 | bytes 1024 | tf_op jit(solution)/shard_map/pallas_call | solution.py:190
  242.7 4.8 %shard_map.91 = (bf16[192,768]{1,0:T(8,128)(2,1)S(1)}, bf16[192,768]{1,0:T(8,128)(2,1)S(1)}, bf16[192,768]{1,0:T(8,128)(2,1)S(1)}, f32[192,768]{1,0:T(8,128)S(1)}) custom-call(bf16[1024,768]{1,0:T(8,128)(2,1)S(1)} %shard_map.85.own_ref, bf16[1024,768]{1,0:T(8,128)(2,1)S(1)} %collective-permute-done.2.other_ref, bf16[192,1024]{1,0:T(8,128)(2,1)S(1)} %copy-done.15, ...), custom_call_target="tpu_custom_call" | custom-call | flops 1024 | bytes 1024 | tf_op jit(solution)/shard_map/pallas_call | solution.py:149
  248.3 1.9 collective-permute-start.20
  250.2 6.8 %collective-permute-done.20 = bf16[192,768]{1,0:T(8,128)(2,1)S(1)} collective-permute-done((bf16[192,768]{1,0:T(8,128)(2,1)S(1)}, bf16[192,768]{1,0:T(8,128)(2,1)S(1)}, u32[]{:S(2)}, u32[]{:S(2)}) %collective-permute-start.20) | collective-permute-done | bytes 294944 | tf_op jit(solution)/shard_map/ppermute | solution.py:55
  258.4 1.3 collective-permute-start.30
  261.6 4.5 shard_map.92
  267.0 4.2 collective-permute-done.29.refs_0_
  272.4 3.6 collective-permute-start.25
  276.0 2.9 collective-permute-start.33
  278.9 7.9 %collective-permute-done.35 = bf16[192,768]{1,0:T(8,128)(2,1)S(1)} collective-permute-done((bf16[192,768]{1,0:T(8,128)(2,1)S(1)}, bf16[192,768]{1,0:T(8,128)(2,1)S(1)}, u32[]{:S(2)}, u32[]{:S(2)}) %collective-permute-start.35) | collective-permute-done | bytes 294944 | tf_op jit(solution)/shard_map/ppermute | solution.py:55
  286.9 5.5 %shard_map.93 = (bf16[480,768]{1,0:T(8,128)(2,1)S(1)}, f32[480,768]{1,0:T(8,128)S(1)}) custom-call(bf16[1024,768]{1,0:T(8,128)(2,1)} %copy-done, bf16[1024,768]{1,0:T(8,128)(2,1)} %copy-done.2, bf16[4,96,1024]{2,1,0:T(8,128)(2,1)S(1)} %collective-permute-done.29.refs_0_, bf16[4,96,1024]{2,1,0:T(8,128)(2,1)S(1)} %collective-permute-done.31.refs_1_, ...), custom_call_target="tpu_custom_call" | custom-call | flops 1024 | bytes 1024 | tf_op jit(solution)/shard_map/pallas_call | solution.py:149
  294.0 3.6 collective-permute-done.34.refs_5_
  298.2 7.9 %collective-permute-done.38 = bf16[192,768]{1,0:T(8,128)(2,1)S(1)} collective-permute-done((bf16[192,768]{1,0:T(8,128)(2,1)S(1)}, bf16[192,768]{1,0:T(8,128)(2,1)S(1)}, u32[]{:S(2)}, u32[]{:S(2)}) %collective-permute-start.38) | collective-permute-done | bytes 294944 | tf_op jit(solution)/shard_map/ppermute | solution.py:55
  307.3 6.0 %shard_map.94 = (bf16[480,768]{1,0:T(8,128)(2,1)S(1)}, bf16[480,768]{1,0:T(8,128)(2,1)S(1)}) custom-call(bf16[1024,768]{1,0:T(8,128)(2,1)} %copy-done, bf16[1024,768]{1,0:T(8,128)(2,1)} %copy-done.2, bf16[4,96,1024]{2,1,0:T(8,128)(2,1)S(1)} %collective-permute-done.29.refs_0_, bf16[4,96,1024]{2,1,0:T(8,128)(2,1)S(1)} %collective-permute-done.31.refs_1_, ...), custom_call_target="tpu_custom_call" | custom-call | flops 1024 | bytes 1024 | tf_op jit(solution)/shard_map/pallas_call | solution.py:149
  314.5 11.6 %collective-permute-done.39 = bf16[480,768]{1,0:T(8,128)(2,1)S(1)} collective-permute-done((bf16[480,768]{1,0:T(8,128)(2,1)S(1)}, bf16[480,768]{1,0:T(8,128)(2,1)S(1)}, u32[]{:S(2)}, u32[]{:S(2)}) %collective-permute-start.39) | collective-permute-done | bytes 737312 | tf_op jit(solution)/shard_map/ppermute | solution.py:55
  326.3 3.7 shard_map.95
  331.4 7.9 %collective-permute-done.46 = bf16[192,768]{1,0:T(8,128)(2,1)S(1)} collective-permute-done((bf16[192,768]{1,0:T(8,128)(2,1)S(1)}, bf16[192,768]{1,0:T(8,128)(2,1)S(1)}, u32[]{:S(2)}, u32[]{:S(2)}) %collective-permute-start.46) | collective-permute-done | bytes 294944 | tf_op jit(solution)/shard_map/ppermute | solution.py:55
  339.5 5.6 %shard_map.97 = (bf16[480,768]{1,0:T(8,128)(2,1)S(1)}, bf16[480,768]{1,0:T(8,128)(2,1)S(1)}) custom-call(bf16[1024,768]{1,0:T(8,128)(2,1)} %copy-done, bf16[1024,768]{1,0:T(8,128)(2,1)} %copy-done.2, bf16[4,96,1024]{2,1,0:T(8,128)(2,1)S(1)} %collective-permute-done.26.refs_0_, bf16[4,96,1024]{2,1,0:T(8,128)(2,1)S(1)} %collective-permute-done.42.refs_1_, ...), custom_call_target="tpu_custom_call" | custom-call | flops 1024 | bytes 1024 | tf_op jit(solution)/shard_map/pallas_call | solution.py:149
  346.1 14.9 %collective-permute-done.49.got_ref = bf16[192,768]{1,0:T(8,128)(2,1)S(1)} collective-permute-done((bf16[192,768]{1,0:T(8,128)(2,1)S(1)}, bf16[192,768]{1,0:T(8,128)(2,1)S(1)}, u32[]{:S(2)}, u32[]{:S(2)}) %collective-permute-start.49) | collective-permute-done | bytes 294944 | tf_op jit(solution)/shard_map/ppermute | solution.py:55
  361.2 2.9 collective-permute-done.48.got_ref
  366.4 22.5 %collective-permute-done.44 = bf16[192,768]{1,0:T(8,128)(2,1)S(1)} collective-permute-done((bf16[192,768]{1,0:T(8,128)(2,1)S(1)}, bf16[192,768]{1,0:T(8,128)(2,1)S(1)}, u32[]{:S(2)}, u32[]{:S(2)}) %collective-permute-start.44) | collective-permute-done | bytes 294944 | tf_op jit(solution)/shard_map/ppermute | solution.py:55
  390.2 6.6 %shard_map.96 = (bf16[480,768]{1,0:T(8,128)(2,1)S(1)}, f32[480,768]{1,0:T(8,128)}) custom-call(bf16[1024,768]{1,0:T(8,128)(2,1)} %copy-done, bf16[1024,768]{1,0:T(8,128)(2,1)} %copy-done.2, bf16[4,96,1024]{2,1,0:T(8,128)(2,1)S(1)} %collective-permute-done.26.refs_0_, bf16[4,96,1024]{2,1,0:T(8,128)(2,1)S(1)} %collective-permute-done.42.refs_1_, ...), custom_call_target="tpu_custom_call" | custom-call | flops 1024 | bytes 1024 | tf_op jit(solution)/shard_map/pallas_call | solution.py:149
  398.2 14.8 %collective-permute-done.54.got_ref = bf16[192,768]{1,0:T(8,128)(2,1)S(1)} collective-permute-done((bf16[192,768]{1,0:T(8,128)(2,1)S(1)}, bf16[192,768]{1,0:T(8,128)(2,1)S(1)}, u32[]{:S(2)}, u32[]{:S(2)}) %collective-permute-start.54) | collective-permute-done | bytes 294944 | tf_op jit(solution)/shard_map/ppermute | solution.py:55
  418.8 2.2 collective-permute-done.57
  420.9 1.8 collective-permute-done.56
  426.5 2.0 broadcast_select_fusion.1
  431.9 3.5 all-to-all-start
  436.6 6.4 %all-to-all-done = f32[16,1,1024]{2,1,0:T(1,128)S(1)} async-done(((f32[16,1,1024]{2,1,0:T(1,128)}), f32[16,1,1024]{2,1,0:T(1,128)S(1)}, u32[]{:S(2)}, u32[]{:S(2)}) %all-to-all-start) | async-done | bytes 65568 | tf_op jit(solution)/shard_map/all_to_all | solution.py:242
  446.2 5.3 %multiply_multiply_fusion = f32[768,1536]{1,0:T(8,128)} fusion(f32[768,768]{1,0:T(8,128)} %copy-done.34, f32[768,768]{1,0:T(8,128)} %copy-done.33, f32[1536]{0:T(1024)S(1)} %get-tuple-element.163, f32[768]{0:T(1024)S(1)} %get-tuple-element.161, f32[]{:T(128)} %bitcast.1, f32[1536]{0:T(1024)S(1)} %get-tuple-element.166), kind=kLoop, calls=%fused_computation.1 | loop fusion | flops 5898240 | bytes 9452548 | tf_op jit(solution)/shard_map/mul | solution.py:417
  (212 shorter events, 47.4 us)
Async XLA Ops:
  11.1 15.1 %collective-permute-start.2 = (bf16[1024,768]{1,0:T(8,128)(2,1)S(1)}, bf16[1024,768]{1,0:T(8,128)(2,1)S(1)}, u32[]{:S(2)}, u32[]{:S(2)}) collective-permute-start(bf16[1024,768]{1,0:T(8,128)(2,1)S(1)} %shard_map.86), channel_id=1, source_target_pairs={{0,1},{1,0},{2,3},{3,2},{4,5},{5,4},{6,7},{7,6},{8,9},{9,8},{10,11... | collective-permute-start | bytes 4718600 | tf_op jit(solution)/shard_map/ppermute | solution.py:55
  11.3 9.0 %collective-permute-start.4 = (bf16[192,1024]{1,0:T(8,128)(2,1)S(1)}, bf16[192,1024]{1,0:T(8,128)(2,1)S(1)}, u32[]{:S(2)}, u32[]{:S(2)}) collective-permute-start(bf16[192,1024]{1,0:T(8,128)(2,1)S(1)} %get-tuple-element.83.refs_0_), channel_id=1, source_target_pairs={{0,8},{1,25},{2,10},{3,27},{4,12},{5,29},{6,14},{7,31},{8,16},{9,1... | collective-permute-start | bytes 1179656 | tf_op jit(solution)/shard_map/ppermute | solution.py:55
  12.9 9.0 %collective-permute-start.3 = (bf16[192,1024]{1,0:T(8,128)(2,1)S(1)}, bf16[192,1024]{1,0:T(8,128)(2,1)S(1)}, u32[]{:S(2)}, u32[]{:S(2)}) collective-permute-start(bf16[192,1024]{1,0:T(8,128)(2,1)S(1)} %get-tuple-element.82.refs_0_), channel_id=1, source_target_pairs={{0,32},{1,97},{2,34},{3,99},{4,36},{5,101},{6,38},{7,103},{8,40},{... | collective-permute-start | bytes 1179656 | tf_op jit(solution)/shard_map/ppermute | solution.py:55
  14.4 10.0 %collective-permute-start.6 = (bf16[192,1024]{1,0:T(8,128)(2,1)S(1)}, bf16[192,1024]{1,0:T(8,128)(2,1)S(1)}, u32[]{:S(2)}, u32[]{:S(2)}) collective-permute-start(bf16[192,1024]{1,0:T(8,128)(2,1)S(1)} %collective-permute-done.1.refs_1_.refs_0_), channel_id=1, source_target_pairs={{0,8},{1,25},{2,10},{3,27},{4,12},{5,29},{6,14},{7,31},{8,16},{9,1... | collective-permute-start | bytes 1179656 | tf_op jit(solution)/shard_map/ppermute | solution.py:55
  15.9 10.2 %collective-permute-start.5 = (bf16[192,1024]{1,0:T(8,128)(2,1)S(1)}, bf16[192,1024]{1,0:T(8,128)(2,1)}, u32[]{:S(2)}, u32[]{:S(2)}) collective-permute-start(bf16[192,1024]{1,0:T(8,128)(2,1)S(1)} %collective-permute-done.refs_0_.refs_1_), channel_id=1, source_target_pairs={{0,32},{1,97},{2,34},{3,99},{4,36},{5,101},{6,38},{7,103},{8,40},{... | collective-permute-start | bytes 1179656 | tf_op jit(solution)/shard_map/ppermute | solution.py:55
  27.4 10.2 %collective-permute-start.8 = (bf16[192,1024]{1,0:T(8,128)(2,1)S(1)}, bf16[192,1024]{1,0:T(8,128)(2,1)}, u32[]{:S(2)}, u32[]{:S(2)}) collective-permute-start(bf16[192,1024]{1,0:T(8,128)(2,1)S(1)} %collective-permute-done.3.refs_1_.refs_2_), channel_id=1, source_target_pairs={{0,32},{1,97},{2,34},{3,99},{4,36},{5,101},{6,38},{7,103},{8,40},{... | collective-permute-start | bytes 1179656 | tf_op jit(solution)/shard_map/ppermute | solution.py:55
  28.0 9.3 %collective-permute-start.12 = (bf16[192,1024]{1,0:T(8,128)(2,1)}, bf16[192,1024]{1,0:T(8,128)(2,1)}, u32[]{:S(2)}, u32[]{:S(2)}) collective-permute-start(bf16[192,1024]{1,0:T(8,128)(2,1)} %copy-done.37), channel_id=1, source_target_pairs={{0,8},{1,25},{2,10},{3,27},{4,12},{5,29},{6,14},{7,31},{8,16},{9,1... | collective-permute-start | bytes 1179656 | tf_op jit(solution)/shard_map/ppermute | solution.py:55
  29.2 8.1 %collective-permute-start.11 = (bf16[192,1024]{1,0:T(8,128)(2,1)}, bf16[192,1024]{1,0:T(8,128)(2,1)S(1)}, u32[]{:S(2)}, u32[]{:S(2)}) collective-permute-start(bf16[192,1024]{1,0:T(8,128)(2,1)} %copy-done.36), channel_id=1, source_target_pairs={{0,1},{1,0},{2,3},{3,2},{4,5},{5,4},{6,7},{7,6},{8,9},{9,8},{10,11... | collective-permute-start | bytes 1179656 | tf_op jit(solution)/shard_map/ppermute | solution.py:55
  30.9 6.4 %collective-permute-start.14 = (bf16[192,1024]{1,0:T(8,128)(2,1)}, bf16[192,1024]{1,0:T(8,128)(2,1)S(1)}, u32[]{:S(2)}, u32[]{:S(2)}) collective-permute-start(bf16[192,1024]{1,0:T(8,128)(2,1)} %copy-done.37), channel_id=1, source_target_pairs={{0,1},{1,0},{2,3},{3,2},{4,5},{5,4},{6,7},{7,6},{8,9},{9,8},{10,11... | collective-permute-start | bytes 1179656 | tf_op jit(solution)/shard_map/ppermute | solution.py:55
  37.4 100.2 %collective-permute-start.18 = (bf16[192,1024]{1,0:T(8,128)(2,1)}, bf16[192,1024]{1,0:T(8,128)(2,1)}, u32[]{:S(2)}, u32[]{:S(2)}) collective-permute-start(bf16[192,1024]{1,0:T(8,128)(2,1)} %collective-permute-done.12.refs_3_), channel_id=1, source_target_pairs={{0,1},{1,0},{2,3},{3,2},{4,5},{5,4},{6,7},{7,6},{8,9},{9,8},{10,11... | collective-permute-start | bytes 1179656 | tf_op jit(solution)/shard_map/ppermute | solution.py:55
  38.3 150.1 %collective-permute-start.16 = (bf16[192,1024]{1,0:T(8,128)(2,1)}, bf16[192,1024]{1,0:T(8,128)(2,1)}, u32[]{:S(2)}, u32[]{:S(2)}) collective-permute-start(bf16[192,1024]{1,0:T(8,128)(2,1)} %collective-permute-done.8.refs_3_.refs_6_), channel_id=1, source_target_pairs={{0,1},{1,0},{2,3},{3,2},{4,5},{5,4},{6,7},{7,6},{8,9},{9,8},{10,11... | collective-permute-start | bytes 1179656 | tf_op jit(solution)/shard_map/ppermute | solution.py:55
  87.2 169.9 %collective-permute-start.9 = (bf16[4,96,1024]{2,1,0:T(8,128)(2,1)}, bf16[4,96,1024]{2,1,0:T(8,128)(2,1)}, u32[]{:S(2)}, u32[]{:S(2)}) collective-permute-start(bf16[4,96,1024]{2,1,0:T(8,128)(2,1)} %get-tuple-element.87), channel_id=1, source_target_pairs={{0,8},{1,25},{2,10},{3,27},{4,12},{5,29},{6,14},{7,31},{8,16},{9,1... | collective-permute-start | bytes 2359304 | tf_op jit(solution)/shard_map/ppermute | solution.py:55
  136.3 120.8 %collective-permute-start.13 = (bf16[4,96,1024]{2,1,0:T(8,128)(2,1)}, bf16[4,96,1024]{2,1,0:T(8,128)(2,1)}, u32[]{:S(2)}, u32[]{:S(2)}) collective-permute-start(bf16[4,96,1024]{2,1,0:T(8,128)(2,1)} %get-tuple-element.91.refs_2_), channel_id=1, source_target_pairs={{0,32},{1,97},{2,34},{3,99},{4,36},{5,101},{6,38},{7,103},{8,40},{... | collective-permute-start | bytes 2359304 | tf_op jit(solution)/shard_map/ppermute | solution.py:55
  186.4 70.8 %collective-permute-start.19 = (bf16[4,96,1024]{2,1,0:T(8,128)(2,1)}, bf16[4,96,1024]{2,1,0:T(8,128)(2,1)}, u32[]{:S(2)}, u32[]{:S(2)}) collective-permute-start(bf16[4,96,1024]{2,1,0:T(8,128)(2,1)} %get-tuple-element.98.refs_10_.refs_3_), channel_id=1, source_target_pairs={{0,32},{1,97},{2,34},{3,99},{4,36},{5,101},{6,38},{7,103},{8,40},{... | collective-permute-start | bytes 2359304 | tf_op jit(solution)/shard_map/ppermute | solution.py:55
  237.2 20.0 %collective-permute-start.17 = (bf16[4,96,1024]{2,1,0:T(8,128)(2,1)}, bf16[4,96,1024]{2,1,0:T(8,128)(2,1)S(1)}, u32[]{:S(2)}, u32[]{:S(2)}) collective-permute-start(bf16[4,96,1024]{2,1,0:T(8,128)(2,1)} %get-tuple-element.96.refs_9_), channel_id=1, source_target_pairs={{0,8},{1,25},{2,10},{3,27},{4,12},{5,29},{6,14},{7,31},{8,16},{9,1... | collective-permute-start | bytes 2359304 | tf_op jit(solution)/shard_map/ppermute | solution.py:55
  248.3 8.7 %collective-permute-start.20 = (bf16[192,768]{1,0:T(8,128)(2,1)S(1)}, bf16[192,768]{1,0:T(8,128)(2,1)S(1)}, u32[]{:S(2)}, u32[]{:S(2)}) collective-permute-start(bf16[192,768]{1,0:T(8,128)(2,1)S(1)} %get-tuple-element.100), channel_id=1, source_target_pairs={{0,2},{1,7},{2,4},{3,1},{4,6},{5,3},{6,0},{7,5},{8,10},{9,15},{10,... | collective-permute-start | bytes 884744 | tf_op jit(solution)/shard_map/ppermute | solution.py:55
  257.8 13.4 %collective-permute-start.29 = (bf16[4,96,1024]{2,1,0:T(8,128)(2,1)}, bf16[4,96,1024]{2,1,0:T(8,128)(2,1)S(1)}, u32[]{:S(2)}, u32[]{:S(2)}) collective-permute-start(bf16[4,96,1024]{2,1,0:T(8,128)(2,1)} %collective-permute-done.9.refs_0_), channel_id=1, source_target_pairs={{0,8},{1,25},{2,10},{3,27},{4,12},{5,29},{6,14},{7,31},{8,16},{9,1... | collective-permute-start | bytes 2359304 | tf_op jit(solution)/shard_map/ppermute | solution.py:55
  258.4 13.4 %collective-permute-start.30 = (bf16[4,96,1024]{2,1,0:T(8,128)(2,1)}, bf16[4,96,1024]{2,1,0:T(8,128)(2,1)S(1)}, u32[]{:S(2)}, u32[]{:S(2)}) collective-permute-start(bf16[4,96,1024]{2,1,0:T(8,128)(2,1)} %collective-permute-done.13.refs_4_), channel_id=1, source_target_pairs={{0,32},{1,97},{2,34},{3,99},{4,36},{5,101},{6,38},{7,103},{8,40},{... | collective-permute-start | bytes 2359304 | tf_op jit(solution)/shard_map/ppermute | solution.py:55
  260.7 11.1 %collective-permute-start.23 = (bf16[4,96,1024]{2,1,0:T(8,128)(2,1)}, bf16[4,96,1024]{2,1,0:T(8,128)(2,1)S(1)}, u32[]{:S(2)}, u32[]{:S(2)}) collective-permute-start(bf16[4,96,1024]{2,1,0:T(8,128)(2,1)} %collective-permute-done.13.refs_4_), channel_id=1, source_target_pairs={{0,1},{1,0},{2,3},{3,2},{4,5},{5,4},{6,7},{7,6},{8,9},{9,8},{10,11... | collective-permute-start | bytes 2359304 | tf_op jit(solution)/shard_map/ppermute | solution.py:55
  261.3 10.4 %collective-permute-start.24 = (bf16[4,96,1024]{2,1,0:T(8,128)(2,1)}, bf16[4,96,1024]{2,1,0:T(8,128)(2,1)S(1)}, u32[]{:S(2)}, u32[]{:S(2)}) collective-permute-start(bf16[4,96,1024]{2,1,0:T(8,128)(2,1)} %collective-permute-done.19.refs_5_), channel_id=1, source_target_pairs={{0,1},{1,0},{2,3},{3,2},{4,5},{5,4},{6,7},{7,6},{8,9},{9,8},{10,11... | collective-permute-start | bytes 2359304 | tf_op jit(solution)/shard_map/ppermute | solution.py:55
  272.4 21.2 %collective-permute-start.25 = (bf16[4,96,1024]{2,1,0:T(8,128)(2,1)S(1)}, bf16[4,96,1024]{2,1,0:T(8,128)(2,1)S(1)}, u32[]{:S(2)}, u32[]{:S(2)}) collective-permute-start(bf16[4,96,1024]{2,1,0:T(8,128)(2,1)S(1)} %copy-done.42), channel_id=1, source_target_pairs={{0,8},{1,25},{2,10},{3,27},{4,12},{5,29},{6,14},{7,31},{8,16},{9,1... | collective-permute-start | bytes 2359304 | tf_op jit(solution)/shard_map/ppermute | solution.py:55
  276.0 17.6 %collective-permute-start.27 = (bf16[4,96,1024]{2,1,0:T(8,128)(2,1)S(1)}, bf16[4,96,1024]{2,1,0:T(8,128)(2,1)S(1)}, u32[]{:S(2)}, u32[]{:S(2)}) collective-permute-start(bf16[4,96,1024]{2,1,0:T(8,128)(2,1)S(1)} %copy-done.16), channel_id=1, source_target_pairs={{0,32},{1,97},{2,34},{3,99},{4,36},{5,101},{6,38},{7,103},{8,40},{... | collective-permute-start | bytes 2359304 | tf_op jit(solution)/shard_map/ppermute | solution.py:55
  276.0 18.0 %collective-permute-start.33 = (bf16[4,96,1024]{2,1,0:T(8,128)(2,1)}, bf16[4,96,1024]{2,1,0:T(8,128)(2,1)S(1)}, u32[]{:S(2)}, u32[]{:S(2)}) collective-permute-start(bf16[4,96,1024]{2,1,0:T(8,128)(2,1)} %get-tuple-element.116), channel_id=1, source_target_pairs={{0,8},{1,25},{2,10},{3,27},{4,12},{5,29},{6,14},{7,31},{8,16},{9,1... | collective-permute-start | bytes 2359304 | tf_op jit(solution)/shard_map/ppermute | solution.py:55
  278.9 18.7 %collective-permute-start.34 = (bf16[4,96,1024]{2,1,0:T(8,128)(2,1)S(1)}, bf16[4,96,1024]{2,1,0:T(8,128)(2,1)S(1)}, u32[]{:S(2)}, u32[]{:S(2)}) collective-permute-start(bf16[4,96,1024]{2,1,0:T(8,128)(2,1)S(1)} %copy-done.17), channel_id=1, source_target_pairs={{0,32},{1,97},{2,34},{3,99},{4,36},{5,101},{6,38},{7,103},{8,40},{... | collective-permute-start | bytes 2359304 | tf_op jit(solution)/shard_map/ppermute | solution.py:55
  278.9 7.9 %collective-permute-start.35 = (bf16[192,768]{1,0:T(8,128)(2,1)S(1)}, bf16[192,768]{1,0:T(8,128)(2,1)S(1)}, u32[]{:S(2)}, u32[]{:S(2)}) collective-permute-start(bf16[192,768]{1,0:T(8,128)(2,1)S(1)} %get-tuple-element.107), channel_id=1, source_target_pairs={{0,2},{1,7},{2,4},{3,1},{4,6},{5,3},{6,0},{7,5},{8,10},{9,15},{10,... | collective-permute-start | bytes 884744 | tf_op jit(solution)/shard_map/ppermute | solution.py:55
  297.6 15.9 %collective-permute-start.36 = (bf16[4,96,1024]{2,1,0:T(8,128)(2,1)S(1)}, bf16[4,96,1024]{2,1,0:T(8,128)(2,1)S(1)}, u32[]{:S(2)}, u32[]{:S(2)}) collective-permute-start(bf16[4,96,1024]{2,1,0:T(8,128)(2,1)S(1)} %collective-permute-done.33.refs_1_), channel_id=1, source_target_pairs={{0,1},{1,0},{2,3},{3,2},{4,5},{5,4},{6,7},{7,6},{8,9},{9,8},{10,11... | collective-permute-start | bytes 2359304 | tf_op jit(solution)/shard_map/ppermute | solution.py:55
  297.6 15.9 %collective-permute-start.37 = (bf16[4,96,1024]{2,1,0:T(8,128)(2,1)S(1)}, bf16[4,96,1024]{2,1,0:T(8,128)(2,1)S(1)}, u32[]{:S(2)}, u32[]{:S(2)}) collective-permute-start(bf16[4,96,1024]{2,1,0:T(8,128)(2,1)S(1)} %collective-permute-done.25.refs_10_.refs_0_), channel_id=1, source_target_pairs={{0,1},{1,0},{2,3},{3,2},{4,5},{5,4},{6,7},{7,6},{8,9},{9,8},{10,11... | collective-permute-start | bytes 2359304 | tf_op jit(solution)/shard_map/ppermute | solution.py:55
  298.1 7.9 %collective-permute-start.38 = (bf16[192,768]{1,0:T(8,128)(2,1)S(1)}, bf16[192,768]{1,0:T(8,128)(2,1)S(1)}, u32[]{:S(2)}, u32[]{:S(2)}) collective-permute-start(bf16[192,768]{1,0:T(8,128)(2,1)S(1)} %add_convert_fusion.9), channel_id=1, source_target_pairs={{0,2},{1,7},{2,4},{3,1},{4,6},{5,3},{6,0},{7,5},{8,10},{9,15},{10,... | collective-permute-start | bytes 884744 | tf_op jit(solution)/shard_map/ppermute | solution.py:55
  313.3 12.7 %collective-permute-start.39 = (bf16[480,768]{1,0:T(8,128)(2,1)S(1)}, bf16[480,768]{1,0:T(8,128)(2,1)S(1)}, u32[]{:S(2)}, u32[]{:S(2)}) collective-permute-start(bf16[480,768]{1,0:T(8,128)(2,1)S(1)} %get-tuple-element.125), channel_id=1, source_target_pairs={{0,2},{1,7},{2,4},{3,1},{4,6},{5,3},{6,0},{7,5},{8,10},{9,15},{10,... | collective-permute-start | bytes 2211848 | tf_op jit(solution)/shard_map/ppermute | solution.py:55
  313.4 17.4 %collective-permute-start.26 = (bf16[4,96,1024]{2,1,0:T(8,128)(2,1)S(1)}, bf16[4,96,1024]{2,1,0:T(8,128)(2,1)S(1)}, u32[]{:S(2)}, u32[]{:S(2)}) collective-permute-start(bf16[4,96,1024]{2,1,0:T(8,128)(2,1)S(1)} %collective-permute-done.25.refs_10_.refs_0_), channel_id=1, source_target_pairs={{0,8},{1,25},{2,10},{3,27},{4,12},{5,29},{6,14},{7,31},{8,16},{9,1... | collective-permute-start | bytes 2359304 | tf_op jit(solution)/shard_map/ppermute | solution.py:55
  313.6 17.3 %collective-permute-start.28 = (bf16[4,96,1024]{2,1,0:T(8,128)(2,1)}, bf16[4,96,1024]{2,1,0:T(8,128)(2,1)S(1)}, u32[]{:S(2)}, u32[]{:S(2)}) collective-permute-start(bf16[4,96,1024]{2,1,0:T(8,128)(2,1)} %copy-done.7), channel_id=1, source_target_pairs={{0,32},{1,97},{2,34},{3,99},{4,36},{5,101},{6,38},{7,103},{8,40},{... | collective-permute-start | bytes 2359304 | tf_op jit(solution)/shard_map/ppermute | solution.py:55
  313.6 17.2 %collective-permute-start.40 = (bf16[4,96,1024]{2,1,0:T(8,128)(2,1)}, bf16[4,96,1024]{2,1,0:T(8,128)(2,1)S(1)}, u32[]{:S(2)}, u32[]{:S(2)}) collective-permute-start(bf16[4,96,1024]{2,1,0:T(8,128)(2,1)} %copy-done.7), channel_id=1, source_target_pairs={{0,1},{1,0},{2,3},{3,2},{4,5},{5,4},{6,7},{7,6},{8,9},{9,8},{10,11... | collective-permute-start | bytes 2359304 | tf_op jit(solution)/shard_map/ppermute | solution.py:55
  314.4 16.4 %collective-permute-start.41 = (bf16[4,96,1024]{2,1,0:T(8,128)(2,1)S(1)}, bf16[4,96,1024]{2,1,0:T(8,128)(2,1)S(1)}, u32[]{:S(2)}, u32[]{:S(2)}) collective-permute-start(bf16[4,96,1024]{2,1,0:T(8,128)(2,1)S(1)} %collective-permute-done.34.refs_5_), channel_id=1, source_target_pairs={{0,1},{1,0},{2,3},{3,2},{4,5},{5,4},{6,7},{7,6},{8,9},{9,8},{10,11... | collective-permute-start | bytes 2359304 | tf_op jit(solution)/shard_map/ppermute | solution.py:55
  330.8 8.6 %collective-permute-start.42 = (bf16[4,96,1024]{2,1,0:T(8,128)(2,1)S(1)}, bf16[4,96,1024]{2,1,0:T(8,128)(2,1)S(1)}, u32[]{:S(2)}, u32[]{:S(2)}) collective-permute-start(bf16[4,96,1024]{2,1,0:T(8,128)(2,1)S(1)} %collective-permute-done.26.refs_0_), channel_id=1, source_target_pairs={{0,1},{1,0},{2,3},{3,2},{4,5},{5,4},{6,7},{7,6},{8,9},{9,8},{10,11... | collective-permute-start | bytes 2359304 | tf_op jit(solution)/shard_map/ppermute | solution.py:55
  330.9 8.5 %collective-permute-start.43 = (bf16[4,96,1024]{2,1,0:T(8,128)(2,1)S(1)}, bf16[4,96,1024]{2,1,0:T(8,128)(2,1)S(1)}, u32[]{:S(2)}, u32[]{:S(2)}) collective-permute-start(bf16[4,96,1024]{2,1,0:T(8,128)(2,1)S(1)} %collective-permute-done.28.refs_8_), channel_id=1, source_target_pairs={{0,1},{1,0},{2,3},{3,2},{4,5},{5,4},{6,7},{7,6},{8,9},{9,8},{10,11... | collective-permute-start | bytes 2359304 | tf_op jit(solution)/shard_map/ppermute | solution.py:55
  331.4 7.9 %collective-permute-start.46 = (bf16[192,768]{1,0:T(8,128)(2,1)S(1)}, bf16[192,768]{1,0:T(8,128)(2,1)S(1)}, u32[]{:S(2)}, u32[]{:S(2)}) collective-permute-start(bf16[192,768]{1,0:T(8,128)(2,1)S(1)} %add_convert_fusion.8.refs_10_), channel_id=1, source_target_pairs={{0,2},{1,7},{2,4},{3,1},{4,6},{5,3},{6,0},{7,5},{8,10},{9,15},{10,... | collective-permute-start | bytes 884744 | tf_op jit(solution)/shard_map/ppermute | solution.py:55
  331.4 33.5 %collective-permute-start.45 = (bf16[480,768]{1,0:T(8,128)(2,1)S(1)}, bf16[480,768]{1,0:T(8,128)(2,1)S(1)}, u32[]{:S(2)}, u32[]{:S(2)}) collective-permute-start(bf16[480,768]{1,0:T(8,128)(2,1)S(1)} %add_convert_fusion.3.refs_4_), channel_id=1, source_target_pairs={{0,2},{1,7},{2,4},{3,1},{4,6},{5,3},{6,0},{7,5},{8,10},{9,15},{10,... | collective-permute-start | bytes 2211848 | tf_op jit(solution)/shard_map/ppermute | solution.py:55
  345.1 20.2 %collective-permute-start.47 = (bf16[480,768]{1,0:T(8,128)(2,1)S(1)}, bf16[480,768]{1,0:T(8,128)(2,1)S(1)}, u32[]{:S(2)}, u32[]{:S(2)}) collective-permute-start(bf16[480,768]{1,0:T(8,128)(2,1)S(1)} %get-tuple-element.138), channel_id=1, source_target_pairs={{0,2},{1,7},{2,4},{3,1},{4,6},{5,3},{6,0},{7,5},{8,10},{9,15},{10,... | collective-permute-start | bytes 2211848 | tf_op jit(solution)/shard_map/ppermute | solution.py:55
  345.1 15.8 %collective-permute-start.49 = (bf16[192,768]{1,0:T(8,128)(2,1)S(1)}, bf16[192,768]{1,0:T(8,128)(2,1)S(1)}, u32[]{:S(2)}, u32[]{:S(2)}) collective-permute-start(bf16[192,768]{1,0:T(8,128)(2,1)S(1)} %add_convert_fusion.7.refs_12_), channel_id=1, source_target_pairs={{0,2},{1,7},{2,4},{3,1},{4,6},{5,3},{6,0},{7,5},{8,10},{9,15},{10,... | collective-permute-start | bytes 884744 | tf_op jit(solution)/shard_map/ppermute | solution.py:55
  345.2 18.9 %collective-permute-start.48 = (bf16[192,768]{1,0:T(8,128)(2,1)S(1)}, bf16[192,768]{1,0:T(8,128)(2,1)S(1)}, u32[]{:S(2)}, u32[]{:S(2)}) collective-permute-start(bf16[192,768]{1,0:T(8,128)(2,1)S(1)} %add_convert_fusion.5.refs_10_), channel_id=1, source_target_pairs={{0,2},{1,7},{2,4},{3,1},{4,6},{5,3},{6,0},{7,5},{8,10},{9,15},{10,... | collective-permute-start | bytes 884744 | tf_op jit(solution)/shard_map/ppermute | solution.py:55
  365.1 24.0 %collective-permute-start.51 = (bf16[480,768]{1,0:T(8,128)(2,1)S(1)}, bf16[480,768]{1,0:T(8,128)(2,1)S(1)}, u32[]{:S(2)}, u32[]{:S(2)}) collective-permute-start(bf16[480,768]{1,0:T(8,128)(2,1)S(1)} %add_convert_fusion.2.refs_11_), channel_id=1, source_target_pairs={{0,2},{1,7},{2,4},{3,1},{4,6},{5,3},{6,0},{7,5},{8,10},{9,15},{10,... | collective-permute-start | bytes 2211848 | tf_op jit(solution)/shard_map/ppermute | solution.py:55
  365.4 31.5 %collective-permute-start.50 = (bf16[480,768]{1,0:T(8,128)(2,1)S(1)}, bf16[480,768]{1,0:T(8,128)(2,1)S(1)}, u32[]{:S(2)}, u32[]{:S(2)}) collective-permute-start(bf16[480,768]{1,0:T(8,128)(2,1)S(1)} %add_convert_fusion.1), channel_id=1, source_target_pairs={{0,2},{1,7},{2,4},{3,1},{4,6},{5,3},{6,0},{7,5},{8,10},{9,15},{10,... | collective-permute-start | bytes 2211848 | tf_op jit(solution)/shard_map/ppermute | solution.py:55
  365.5 23.4 %collective-permute-start.44 = (bf16[192,768]{1,0:T(8,128)(2,1)S(1)}, bf16[192,768]{1,0:T(8,128)(2,1)S(1)}, u32[]{:S(2)}, u32[]{:S(2)}) collective-permute-start(bf16[192,768]{1,0:T(8,128)(2,1)S(1)} %get-tuple-element.126), channel_id=1, source_target_pairs={{0,2},{1,7},{2,4},{3,1},{4,6},{5,3},{6,0},{7,5},{8,10},{9,15},{10,... | collective-permute-start | bytes 884744 | tf_op jit(solution)/shard_map/ppermute | solution.py:55
  389.0 8.1 %collective-permute-start.53 = (bf16[192,768]{1,0:T(8,128)(2,1)S(1)}, bf16[192,768]{1,0:T(8,128)(2,1)S(1)}, u32[]{:S(2)}, u32[]{:S(2)}) collective-permute-start(bf16[192,768]{1,0:T(8,128)(2,1)S(1)} %add_convert_fusion.6.refs_10_), channel_id=1, source_target_pairs={{0,2},{1,7},{2,4},{3,1},{4,6},{5,3},{6,0},{7,5},{8,10},{9,15},{10,... | collective-permute-start | bytes 884744 | tf_op jit(solution)/shard_map/ppermute | solution.py:55
  397.0 16.7 %collective-permute-start.52 = (bf16[480,768]{1,0:T(8,128)(2,1)S(1)}, bf16[480,768]{1,0:T(8,128)(2,1)S(1)}, u32[]{:S(2)}, u32[]{:S(2)}) collective-permute-start(bf16[480,768]{1,0:T(8,128)(2,1)S(1)} %add_convert_fusion), channel_id=1, source_target_pairs={{0,2},{1,7},{2,4},{3,1},{4,6},{5,3},{6,0},{7,5},{8,10},{9,15},{10,... | collective-permute-start | bytes 2211848 | tf_op jit(solution)/shard_map/ppermute | solution.py:55
  397.2 15.7 %collective-permute-start.54 = (bf16[192,768]{1,0:T(8,128)(2,1)S(1)}, bf16[192,768]{1,0:T(8,128)(2,1)S(1)}, u32[]{:S(2)}, u32[]{:S(2)}) collective-permute-start(bf16[192,768]{1,0:T(8,128)(2,1)S(1)} %add_convert_fusion.4), channel_id=1, source_target_pairs={{0,2},{1,7},{2,4},{3,1},{4,6},{5,3},{6,0},{7,5},{8,10},{9,15},{10,... | collective-permute-start | bytes 884744 | tf_op jit(solution)/shard_map/ppermute | solution.py:55
  415.6 10.9 %collective-permute-start.55 = (f32[768,768]{1,0:T(8,128)}, f32[768,768]{1,0:T(8,128)}, u32[]{:S(2)}, u32[]{:S(2)}) collective-permute-start(f32[768,768]{1,0:T(8,128)} %get-tuple-element.159), channel_id=1, source_target_pairs={{0,1},{1,0},{2,3},{3,2},{4,5},{5,4},{6,7},{7,6},{8,9},{9,8},{10,11... | collective-permute-start | bytes 7077896 | tf_op jit(solution)/shard_map/ppermute | solution.py:55
  431.9 11.1 %all-to-all-start = ((f32[16,1,1024]{2,1,0:T(1,128)}), f32[16,1,1024]{2,1,0:T(1,128)S(1)}, u32[]{:S(2)}, u32[]{:S(2)}) async-start(f32[16,1,1024]{2,1,0:T(1,128)} %broadcast_in_dim.8), calls=%async_computation | async-start | bytes 131072 | tf_op jit(solution)/shard_map/all_to_all | solution.py:242
  (56 other events, 1077.1 us)
where the time goes:
time: 452 us; the launch traced here: 451 us
  Pallas kernels  241 us (53%)
  waiting for transfers between devices  129 us (29%)
  starting transfers between devices  40.8 us (9%)
  local copies, waits for them, and re-layouts  20.6 us (5%)
  other arithmetic  15.4 us (3%)
  between operations  4.88 us (1%)
    pallas_call x4, Pallas kernels, stack_places(): pl.pallas_call(kernel, out_shape=(jax.ShapeDtypeStruct((4, size, TOK), jn...  195 us
    ppermute x60, waiting for transfers between devices, send(): return lax.ppermute(value, BOTH, pairs)  123 us
    ppermute x60, starting transfers between devices, send(): return lax.ppermute(value, BOTH, pairs)  37.3 us
    pallas_call x7, Pallas kernels, unit_partials(): pl.pallas_call(kernel, out_shape=tuple((jax.ShapeDtypeStruct((rows, HALF)...  36.6 us
    unnamed x87, local copies, waits for them, and re-layouts  16.4 us
  transfers between devices with their start and end apart: 61, of which 26 were waited for; matrix products, arithmetic and copies ran while one was open for 2% of the time, Pallas kernels for 53%

commit v1 on v0

--- a/solution.py
+++ b/solution.py
@@ -173,28 +173,57 @@
     return lax.optimization_barrier((value,) + before)[0]
 
 
-def stack_places(values):
-    size = values[0].shape[0] // NCH
-
+def turn(inputs):
+    def kernel(ref, first, second):
+        turned = ref[...].T
+        first[...] = turned[: FEAT // 2]
+        second[...] = turned[FEAT // 2 :]
+
+    vmem = pl.BlockSpec(memory_space=pltpu.VMEM)
+    half = jax.ShapeDtypeStruct((FEAT // 2, TOK), jnp.bfloat16)
+    return pl.pallas_call(
+        kernel, out_shape=(half, half), in_specs=[vmem], out_specs=(vmem, vmem), cost_estimate=CHEAP
+    )(inputs)
+
+
+def join(*pairs):
     def kernel(*refs):
-        sources, outs, sems = refs[:4], refs[4 : 4 + NCH], refs[4 + NCH]
-        for k in range(NCH):
-            for i, source in enumerate(sources):
-                pltpu.make_async_copy(
-                    source.at[pl.ds(k * size, size)], outs[k].at[i], sems.at[k]
-                ).start()
-        for k in range(NCH):
-            pltpu.make_async_copy(outs[k], outs[k], sems.at[k]).wait()
-
-    anywhere = pl.BlockSpec(memory_space=pl.ANY)
+        for k, out in enumerate(refs[2 * len(pairs) :]):
+            out[0], out[1] = refs[2 * k][...], refs[2 * k + 1][...]
+
+    vmem = pl.BlockSpec(memory_space=pltpu.VMEM)
     return pl.pallas_call(
         kernel,
-        out_shape=(jax.ShapeDtypeStruct((4, size, TOK), jnp.bfloat16),) * NCH,
-        in_specs=[anywhere] * 4,
-        out_specs=(anywhere,) * NCH,
-        scratch_shapes=[pltpu.SemaphoreType.DMA((NCH,))],
+        out_shape=tuple(jax.ShapeDtypeStruct((2,) + a.shape, a.dtype) for a, _ in pairs),
+        in_specs=[vmem] * (2 * len(pairs)),
+        out_specs=(vmem,) * len(pairs),
         cost_estimate=CHEAP,
-    )(*values)
+    )(*[value for pair in pairs for value in pair])
+
+
+def stack_rows(sources, start, count):
+    arrays = []
+    which = []
+    for array, index in sources:
+        if not any(array is other for other in arrays):
+            arrays.append(array)
+        which.append(([array is other for other in arrays].index(True), index))
+
+    def kernel(*refs):
+        out = refs[-1]
+        for k, (at, index) in enumerate(which):
+            source = refs[at] if index is None else refs[at].at[index]
+            out[k // 4, k % 4] = source[pl.ds(start, count)]
+
+    vmem = pl.BlockSpec(memory_space=pltpu.VMEM)
+    return pl.pallas_call(
+        kernel,
+        out_shape=jax.ShapeDtypeStruct((2, 4, count, TOK), jnp.bfloat16),
+        in_specs=[vmem] * len(arrays),
+        out_specs=vmem,
+        compiler_params=pltpu.CompilerParams(vmem_limit_bytes=24 << 20),
+        cost_estimate=CHEAP,
+    )(*arrays)
 
 
 def place_rows(last, got, pieces, before):
@@ -247,36 +276,30 @@
 def per_device(inputs, preact, upstream, weight, row_factor, column_factor):
     core = coordinates()[3]
 
-    mine = inputs.T
-    p, q = lax.optimization_barrier((mine[: FEAT // 2], mine[FEAT // 2 :]))
+    p, q = turn(inputs)
     size = FEAT // 2 // NCH
 
-    p_swap, q_swap = send(p, SWAP), send(q, SWAP)
-    ya, xa = send(p, ALONG_Y), send(q, ALONG_X)
-    yb, xb = send(p_swap, ALONG_Y), send(q_swap, ALONG_X)
-
-    slope_yours = slope_half(preact, upstream, True, (p_swap, q_swap))
+    p_both, q_both = join((p, send(p, SWAP)), (q, send(q, SWAP)))
+    y1, x1 = send(p_both, ALONG_Y), send(q_both, ALONG_X)
+    slope_yours = slope_half(preact, upstream, True, (p_both, q_both))
     slope_other = send(slope_yours, SWAP)
-    slope_mine = slope_half(preact, upstream, False, (p_swap, q_swap))
-    ya, xa, yb, xb = lax.optimization_barrier((ya, xa, yb, xb, slope_other, slope_mine))[:4]
-    y2, x2 = send(ya, ALONG_Y), send(xa, ALONG_X)
+    slope_mine = slope_half(preact, upstream, False, (p_both, q_both))
     weight = after(weight, slope_mine)
     weight_local = jnp.sum(weight * weight, axis=0)
     row_local = jnp.broadcast_to(jnp.sum(row_factor)[None], (128,))
     weight_mine = lax.dynamic_slice_in_dim(weight_local, core * HALF, HALF)
     weight_yours = lax.dynamic_slice_in_dim(weight_local, (1 - core) * HALF, HALF)
-
-    ya_swap, yb_swap = send(ya, SWAP), send(yb, SWAP)
-    xa_swap = send(after(xa, ya_swap, yb_swap), SWAP)
-    xb_swap = send(after(xb, ya_swap, yb_swap), SWAP)
-    early_swap = send(after(jnp.concatenate([weight_yours, row_local]), ya_swap, yb_swap), SWAP)
-    early = jnp.concatenate([weight_mine, row_local]) + early_swap
-    y2_swap = send(after(y2, xa_swap, xb_swap, early_swap), SWAP)
-    x2_swap = send(after(x2, xa_swap, xb_swap, early_swap), SWAP)
-    p_own = stack_places((p, ya, yb_swap, y2))
-    q_own = stack_places((q, xa, xb_swap, x2))
-    p_other = stack_places((p_swap, yb, ya_swap, y2_swap))
-    q_other = stack_places((q_swap, xb, xa_swap, x2_swap))
+    early = jnp.concatenate([weight_mine, row_local])
+    early = early + send(jnp.concatenate([weight_yours, row_local]), SWAP)
+    y1, x1 = lax.optimization_barrier((y1, x1, slope_yours, slope_mine, early))[:2]
+    y2, x2 = send(y1[0], ALONG_Y), send(x1[0], ALONG_X)
+    y1_swap, x1_swap = send(y1, SWAP), send(x1, SWAP)
+    y2, x2 = lax.optimization_barrier((y2, x2, y1_swap, x1_swap))[:2]
+    y2_swap, x2_swap = send(y2, SWAP), send(x2, SWAP)
+    p_places = [(p_both, 0), (y1, 0), (y1_swap, 1), (y2, None)]
+    p_places += [(p_both, 1), (y1, 1), (y1_swap, 0), (y2_swap, None)]
+    q_places = [(q_both, 0), (x1, 0), (x1_swap, 1), (x2, None)]
+    q_places += [(q_both, 1), (x1, 1), (x1_swap, 0), (x2_swap, None)]
 
     def units(entries, low=0, high=4, waits=()):
         return unit_partials(slope_mine, slope_other, entries, low, high, waits)
@@ -284,88 +307,79 @@
     def hop(value):
         return send(value, ALONG_Z)
 
-    own_entries = [((p, None), (p_swap, None)), ((ya, None), (yb, None))]
-    own_entries += [((yb_swap, None), (ya_swap, None)), ((y2, None), (y2_swap, None))]
-    own = units([own_entries], waits=(early, p_other[0], q_other[0]))
-
-    def gather(chunk, gate_a, gate_b, gate_2):
-        xa, ya = send(after(p_own[chunk], *gate_a), ALONG_X), send(after(q_own[chunk], *gate_a), ALONG_Y)
-        xb, yb = send(after(p_other[chunk], *gate_b), ALONG_X), send(after(q_other[chunk], *gate_b), ALONG_Y)
-        x2, y2 = send(after(xa, *gate_2), ALONG_X), send(after(ya, *gate_2), ALONG_Y)
-        return xa, ya, xb, yb, x2, y2
-
-    def swap_near(xa, ya, xb, yb, *gate):
-        xa, ya, xb, yb = lax.optimization_barrier((xa, ya, xb, yb, *gate))[:4]
-        xa_swap, xb_swap = send(xa, SWAP), send(xb, SWAP)
-        ya_swap = send(after(ya, xa_swap, xb_swap), SWAP)
-        yb_swap = send(after(yb, xa_swap, xb_swap), SWAP)
-        return xa_swap, ya_swap, xb_swap, yb_swap
-
-    def swap_far(x2, y2, *gate):
-        x2, y2 = lax.optimization_barrier((x2, y2, *gate))[:2]
-        return send(x2, SWAP), send(y2, SWAP)
-
-    def near_entries(xa, xb, xa_swap, xb_swap):
+    def near_entries(x1, x1_swap):
         return [
-            [((xa, i), (xb, i)) for i in range(4)],
-            [((xb_swap, FLIP[i]), (xa_swap, FLIP[i])) for i in range(4)],
+            [((x1, (0, i)), (x1, (1, i))) for i in range(4)],
+            [((x1_swap, (1, FLIP[i])), (x1_swap, (0, FLIP[i]))) for i in range(4)],
         ]
 
-    def far_entries(chunk, ya, yb, ya_swap, yb_swap, x2, x2_swap, y2, y2_swap):
+    def far_entries(q_here, y1, y1_swap, x2, x2_swap, y2, y2_swap):
         entries = [[((x2, i), (x2_swap, FLIP[i])) for i in range(4)]]
         for g in range(4):
             entries.append(
                 [
-                    ((q_own[chunk], g), (q_other[chunk], g)),
-                    ((ya, g), (yb, g)),
-                    ((yb_swap, FLIP[g]), (ya_swap, FLIP[g])),
+                    ((q_here, (0, g)), (q_here, (1, g))),
+                    ((y1, (0, g)), (y1, (1, g))),
+                    ((y1_swap, (1, FLIP[g])), (y1_swap, (0, FLIP[g]))),
                     ((y2, g), (y2_swap, FLIP[g])),
                 ]
             )
         return entries
 
-    xa, ya, xb, yb, x2, y2 = gather(0, (), (), (own[0],))
+    p_here = stack_rows(p_places, 0, size)
+    q_here = stack_rows(q_places, 0, size)
+    x1, y1 = send(p_here, ALONG_X), send(q_here, ALONG_Y)
+    own = units([[(p_places[i], p_places[4 + i]) for i in range(4)]], waits=(p_here, q_here))
     own_got = hop(own[0])
+    p_next = stack_rows(p_places, size, size)
+    q_next = stack_rows(q_places, size, size)
     own_2 = add_narrow(own[1], own_got)
-    xa_swap, ya_swap, xb_swap, yb_swap = swap_near(xa, ya, xb, yb, own_2)
     own_got = hop(own_2)
-    near0 = units(near_entries(xa, xb, xa_swap, xb_swap))
+    own_3 = add_narrow(own[2], own_got)
+    own_got = hop(own_3)
+    x1, y1 = lax.optimization_barrier((x1, y1, own_3, p_next, q_next))[:2]
+    x2, y2 = send(x1[0], ALONG_X), send(y1[0], ALONG_Y)
+    x1_swap, y1_swap = send(x1, SWAP), send(y1, SWAP)
+
+    p_next, q_next = lax.optimization_barrier((p_next, q_next, x1_swap, y1_swap))[:2]
+    x1_next, y1_next = send(p_next, ALONG_X), send(q_next, ALONG_Y)
+    near0 = units(near_entries(x1, x1_swap), waits=(y1_swap,))
     near0_got = hop(near0[0])
-    own_3 = add_narrow(own[2], own_got)
-    x2_swap, y2_swap = swap_far(x2, y2, near0[0], ya_swap, yb_swap)
-    own_got = hop(own_3)
-    far0_entries = far_entries(0, ya, yb, ya_swap, yb_swap, x2, x2_swap, y2, y2_swap)
-    xa, ya, xb, yb, x2, y2 = gather(1, (ya_swap, yb_swap, near0[0]), (x2_swap, y2_swap), ())
-    far0 = units(far0_entries, 0, 2, waits=(xa, ya, own_3))
+    x2, y2 = lax.optimization_barrier((x2, y2, near0[0]))[:2]
+    x2_swap, y2_swap = send(x2, SWAP), send(y2, SWAP)
+    placed = place_rows(own[3], own_got, [(0, 0, 0, FEAT // 2)], ())
+    far0_entries = far_entries(q_here, y1, y1_swap, x2, x2_swap, y2, y2_swap)
+    far0 = units(far0_entries, 0, 2, waits=(placed[2],))
     far0_got = hop(far0[0])
-
     near0_2 = add_narrow(near0[1], near0_got)
     near0_got = hop(near0_2)
-    far0 += units(far0_entries, 2, 4, waits=(near0_2,))
-    xa_swap, ya_swap, xb_swap, yb_swap = swap_near(xa, ya, xb, yb, far0[2])
+    far0 += units(far0_entries, 2, 4, waits=(near0_2, far0[0]))
+    x1, y1 = lax.optimization_barrier((x1_next, y1_next, far0[0]))[:2]
+    x2, y2 = send(x1[0], ALONG_X), send(y1[0], ALONG_Y)
+    x1, y1 = lax.optimization_barrier((x1, y1, far0[2]))[:2]
+    x1_swap, y1_swap = send(x1, SWAP), send(y1, SWAP)
     far0_2 = add_narrow(far0[1], far0_got)
-    near1 = units(near_entries(xa, xb, xa_swap, xb_swap), waits=(far0_2,))
     far0_got = hop(far0_2)
+    near1 = units(near_entries(x1, x1_swap), waits=(far0_2, y1_swap))
     near1_got = hop(near1[0])
     near0_3 = add_narrow(near0[2], near0_got)
-    x2_swap, y2_swap = swap_far(x2, y2, near1[0], ya_swap, yb_swap)
     near0_got = hop(near0_3)
-    far1_entries = far_entries(1, ya, yb, ya_swap, yb_swap, x2, x2_swap, y2, y2_swap)
-    far1 = units(far1_entries, 0, 2, waits=(near0_3,))
+    x2, y2 = lax.optimization_barrier((x2, y2, near1[0]))[:2]
+    x2_swap, y2_swap = send(x2, SWAP), send(y2, SWAP)
+    far0_3 = add_narrow(far0[2], far0_got)
+    far0_got = hop(far0_3)
+    far1_entries = far_entries(q_next, y1, y1_swap, x2, x2_swap, y2, y2_swap)
+    far1 = units(far1_entries, 0, 2, waits=(far0_3, near0_3))
     far1_got = hop(far1[0])
     near1_2 = add_narrow(near1[1], near1_got)
     near1_got = hop(near1_2)
-    far0_3 = add_narrow(far0[2], far0_got)
-    far1 += units(far1_entries, 2, 4, waits=(near1_2, far0_3))
-    far0_got = hop(far0_3)
-
-    placed = place_rows(own[3], own_got, [(0, 0, 0, FEAT // 2)], ())
     near_pieces = lambda chunk: [(1, chunk * size, 0, size), (2, chunk * size, size, size)]
     far_pieces = lambda chunk: [(3, chunk * size, 0, size)] + [
         (g, FEAT // 2 + chunk * size, (g + 1) * size, size) for g in range(4)
     ]
     placed = place_rows(near0[3], near0_got, near_pieces(0), placed)
-    far1_got = hop(after(add_narrow(far1[1], far1_got), placed[2]))
+    far1 += units(far1_entries, 2, 4, waits=(near1_2, placed[2], far1[0]))
+    far1_got = hop(add_narrow(far1[1], far1_got))
     near1_got = hop(add_narrow(near1[2], near1_got))
     placed = place_rows(far0[3], far0_got, far_pieces(0), placed)
     far1_got = hop(after(add_narrow(far1[2], far1_got), placed[2]))

time: 452 us -> 236 us (0.52)
  Pallas kernels: 241 us -> 48.9 us
  waiting for transfers between devices: 129 us -> 115 us
  starting transfers between devices: 40.8 us -> 34.6 us
  local copies, waits for them, and re-layouts: 20.6 us -> 15.2 us
    pallas_call x4 -> x6, Pallas kernels: 195 us -> 6.53 us  [the longest x1 2.57 us: join(): pl.pallas_call(kernel, out_shape=tuple((jax.ShapeDtypeStruct((2,) + a.sha...]
    ppermute x60 -> x48, waiting for transfers between devices: 123 us -> 108 us  [send(): return lax.ppermute(value, BOTH, pairs)]
    ppermute x60 -> x48, starting transfers between devices: 37.3 us -> 28.3 us  [send(): return lax.ppermute(value, BOTH, pairs)]
    unnamed x87 -> x46, local copies, waits for them, and re-layouts: 16.4 us -> 8.75 us
  transfers between devices with their start and end apart: 61 -> 49, of which waited for: 26 -> 26; matrix products, arithmetic and copies ran while one was open for 2% -> 5% of each run, Pallas kernels for 53% -> 16%
where the time goes in v1:
time: 236 us; the launch traced here: 235 us
  waiting for transfers between devices  115 us (49%)
  Pallas kernels  48.9 us (21%)
  starting transfers between devices  34.6 us (15%)
  other arithmetic  16.5 us (7%)
  local copies, waits for them, and re-layouts  15.2 us (6%)
  between operations  4.69 us (2%)
    ppermute x48, waiting for transfers between devices, send(): return lax.ppermute(value, BOTH, pairs)  108 us
    pallas_call x7, Pallas kernels, unit_partials(): pl.pallas_call(kernel, out_shape=tuple((jax.ShapeDtypeStruct((rows, HALF)...  33.2 us
    ppermute x48, starting transfers between devices, send(): return lax.ppermute(value, BOTH, pairs)  28.3 us
    unnamed x46, local copies, waits for them, and re-layouts  8.75 us
    all_to_all x1, waiting for transfers between devices, everyone(): lax.all_to_all(jnp.broadcast_to(vector[None, :], (count,) + vector.shape)...  6.5 us
    all_to_all x1, starting transfers between devices, everyone(): lax.all_to_all(jnp.broadcast_to(vector[None, :], (count,) + vector.shape)...  6.32 us
    mul x1, other arithmetic, per_device(): -weight_rms * clipped * lax.rsqrt(new_row)[:, None]  5.26 us
    pallas_call x2, Pallas kernels, slope_half(): pl.pallas_call(kernel, out_shape=jax.ShapeDtypeStruct((TOK, HALF), jnp.bf...  5.03 us
  transfers between devices with their start and end apart: 49, of which 26 were waited for; matrix products, arithmetic and copies ran while one was open for 5% of the time, Pallas kernels for 16%

profile of v1, /device:TPU:0, one launch (start us, length us, event | category | flops | bytes accessed | tf_op | source)
XLA Modules:
  0.0 234.8 jit_solution(11682034709626992272)
XLA Ops:
  0.6 2.3 shard_map.85
  3.4 1.4 collective-permute-done.refs_1_
  6.4 2.6 %shard_map.86 = (bf16[2,192,1024]{2,1,0:T(8,128)(2,1)}, bf16[2,192,1024]{2,1,0:T(8,128)(2,1)}) custom-call(bf16[192,1024]{1,0:T(8,128)(2,1)} %get-tuple-element.60.refs_0_, bf16[192,1024]{1,0:T(8,128)(2,1)} %copy-done.19, bf16[192,1024]{1,0:T(8,128)(2,1)} %get-tuple-element.61.refs_2_, bf16[192,1024]{1,0:T(8,128)(2,1)} %copy-done.20), custom_call_target="tpu_custom_call" | custom-call | flops 1024 | bytes 1024 | tf_op jit(solution)/shard_map/pallas_call | solution.py:195
  8.9 1.7 collective-permute-start.3
  10.6 1.5 collective-permute-start.4
  15.0 1.9 copy-done.9
  16.9 1.9 copy-done.10
  18.7 2.5 %shard_map.87.own_ref = bf16[1024,768]{1,0:T(8,128)(2,1)S(1)} custom-call(bf16[1024,1536]{1,0:T(8,128)(2,1)S(1)} %copy-done.9, bf16[1024,1536]{1,0:T(8,128)(2,1)S(1)} %copy-done.10, bf16[2,192,1024]{2,1,0:T(8,128)(2,1)S(1)} %copy-done.2, bf16[2,192,1024]{2,1,0:T(8,128)(2,1)S(1)} %copy-done.7), custom_call_target="tpu_custom_call" | custom-call | flops 1024 | bytes 1024 | tf_op jit(solution)/shard_map/pallas_call | solution.py:87
  21.3 2.7 %multiply_reduce_fusion.1 = f32[1536]{0:T(1024)S(1)} fusion(f32[768,1536]{1,0:T(8,128)} %param.9), kind=kLoop, calls=%fused_computation.3 | loop fusion | flops 2357760 | bytes 4724736 | tf_op jit(solution)/shard_map/reduce_sum | solution.py:288
  24.7 2.4 %collective-permute-start.5 = (f32[896]{0:T(1024)S(1)}, f32[896]{0:T(1024)S(1)}, u32[]{:S(2)}, u32[]{:S(2)}) collective-permute-start(f32[896]{0:T(1024)S(1)} %concatenate.33), channel_id=1, source_target_pairs={{0,1},{1,0},{2,3},{3,2},{4,5},{5,4},{6,7},{7,6},{8,9},{9,8},{10,11... | collective-permute-start | bytes 10760 | tf_op jit(solution)/shard_map/ppermute | solution.py:55
  27.1 2.5 %shard_map.88 = bf16[1024,768]{1,0:T(8,128)(2,1)S(1)} custom-call(bf16[1024,1536]{1,0:T(8,128)(2,1)S(1)} %copy-done.9, bf16[1024,1536]{1,0:T(8,128)(2,1)S(1)} %copy-done.10, bf16[2,192,1024]{2,1,0:T(8,128)(2,1)S(1)} %copy-done.2, bf16[2,192,1024]{2,1,0:T(8,128)(2,1)S(1)} %copy-done.7), custom_call_target="tpu_custom_call" | custom-call | flops 1024 | bytes 1024 | tf_op jit(solution)/shard_map/pallas_call | solution.py:87
  31.2 1.2 collective-permute-start.8
  32.4 7.8 %collective-permute-done.7.refs_3_ = bf16[192,1024]{1,0:T(8,128)(2,1)S(1)} collective-permute-done((bf16[192,1024]{1,0:T(8,128)(2,1)S(1)}, bf16[192,1024]{1,0:T(8,128)(2,1)S(1)}, u32[]{:S(2)}, u32[]{:S(2)}) %collective-permute-start.7) | collective-permute-done | bytes 393248 | tf_op jit(solution)/shard_map/ppermute | solution.py:55
  40.8 1.2 collective-permute-done.11.refs_4_
  43.6 3.5 %shard_map.93 = (bf16[192,768]{1,0:T(8,128)(2,1)S(1)}, bf16[192,768]{1,0:T(8,128)(2,1)S(1)}, bf16[192,768]{1,0:T(8,128)(2,1)S(1)}, f32[192,768]{1,0:T(8,128)S(1)}) custom-call(bf16[1024,768]{1,0:T(8,128)(2,1)S(1)} %shard_map.87.own_ref, bf16[1024,768]{1,0:T(8,128)(2,1)S(1)} %collective-permute-done.2.other_ref, bf16[2,192,1024]{2,1,0:T(8,128)(2,1)S(1)} %copy-done.3, ...), custom_call_target="tpu_custom_call" | custom-call | flops 1024 | bytes 1024 | tf_op jit(solution)/shard_map/pallas_call | solution.py:149
  47.1 2.0 collective-permute-start.14
  49.1 6.8 %collective-permute-done.14 = bf16[192,768]{1,0:T(8,128)(2,1)S(1)} collective-permute-done((bf16[192,768]{1,0:T(8,128)(2,1)S(1)}, bf16[192,768]{1,0:T(8,128)(2,1)S(1)}, u32[]{:S(2)}, u32[]{:S(2)}) %collective-permute-start.14) | collective-permute-done | bytes 294944 | tf_op jit(solution)/shard_map/ppermute | solution.py:55
  56.2 1.4 shard_map.89
  57.6 6.4 %collective-permute-done.15 = bf16[192,768]{1,0:T(8,128)(2,1)S(1)} collective-permute-done((bf16[192,768]{1,0:T(8,128)(2,1)S(1)}, bf16[192,768]{1,0:T(8,128)(2,1)S(1)}, u32[]{:S(2)}, u32[]{:S(2)}) %collective-permute-start.15) | collective-permute-done | bytes 294944 | tf_op jit(solution)/shard_map/ppermute | solution.py:55
  65.5 1.2 slice_bitcast_fusion.2
  68.1 2.5 %collective-permute-done.16.refs_1_ = bf16[2,4,96,1024]{3,2,1,0:T(8,128)(2,1)S(1)} collective-permute-done((bf16[2,4,96,1024]{3,2,1,0:T(8,128)(2,1)S(1)}, bf16[2,4,96,1024]{3,2,1,0:T(8,128)(2,1)S(1)}, u32[]{:S(2)}, u32[]{:S(2)}) %collective-permute-start.16) | collective-permute-done | bytes 1572896 | tf_op jit(solution)/shard_map/ppermute | solution.py:55
  72.1 1.7 collective-permute-start.24
  73.9 3.7 %shard_map.94 = (bf16[192,768]{1,0:T(8,128)(2,1)S(1)}, bf16[192,768]{1,0:T(8,128)(2,1)S(1)}, bf16[192,768]{1,0:T(8,128)(2,1)S(1)}, f32[192,768]{1,0:T(8,128)S(1)}) custom-call(bf16[1024,768]{1,0:T(8,128)(2,1)S(1)} %shard_map.87.own_ref, bf16[1024,768]{1,0:T(8,128)(2,1)S(1)} %collective-permute-done.2.other_ref, ...), custom_call_target="tpu_custom_call" | custom-call | flops 1024 | bytes 1024 | tf_op jit(solution)/shard_map/pallas_call | solution.py:149
  77.6 2.4 %collective-permute-done.20.refs_0_ = bf16[4,96,1024]{2,1,0:T(8,128)(2,1)S(1)} collective-permute-done((bf16[4,96,1024]{2,1,0:T(8,128)(2,1)S(1)}, bf16[4,96,1024]{2,1,0:T(8,128)(2,1)S(1)}, u32[]{:S(2)}, u32[]{:S(2)}) %collective-permute-start.20) | collective-permute-done | bytes 786464 | tf_op jit(solution)/shard_map/ppermute | solution.py:55
  82.8 6.6 %collective-permute-done.27 = bf16[192,768]{1,0:T(8,128)(2,1)S(1)} collective-permute-done((bf16[192,768]{1,0:T(8,128)(2,1)S(1)}, bf16[192,768]{1,0:T(8,128)(2,1)S(1)}, u32[]{:S(2)}, u32[]{:S(2)}) %collective-permute-start.27) | collective-permute-done | bytes 294944 | tf_op jit(solution)/shard_map/ppermute | solution.py:55
  89.5 5.3 %shard_map.96 = (bf16[480,768]{1,0:T(8,128)(2,1)S(1)}, bf16[480,768]{1,0:T(8,128)(2,1)S(1)}) custom-call(bf16[1024,768]{1,0:T(8,128)(2,1)S(1)} %shard_map.87.own_ref, bf16[1024,768]{1,0:T(8,128)(2,1)S(1)} %collective-permute-done.2.other_ref, bf16[4,96,1024]{2,1,0:T(8,128)(2,1)S(1)} %collective-permute-done.20.refs_0_, ...), custom_call_target="tpu_custom_call" | custom-call | flops 1024 | bytes 1024 | tf_op jit(solution)/shard_map/pallas_call | solution.py:149
  94.9 5.8 %shard_map.97 = (bf16[480,768]{1,0:T(8,128)(2,1)S(1)}, f32[480,768]{1,0:T(8,128)S(1)}) custom-call(bf16[1024,768]{1,0:T(8,128)(2,1)S(1)} %shard_map.87.own_ref, bf16[1024,768]{1,0:T(8,128)(2,1)S(1)} %collective-permute-done.2.other_ref, bf16[4,96,1024]{2,1,0:T(8,128)(2,1)S(1)} %collective-permute-done.20.refs_0_, ...), custom_call_target="tpu_custom_call" | custom-call | flops 1024 | bytes 1024 | tf_op jit(solution)/shard_map/pallas_call | solution.py:149
  102.3 1.2 slice_bitcast_fusion
  103.5 1.8 collective-permute-start.25
  105.3 8.7 %collective-permute-done.29 = bf16[480,768]{1,0:T(8,128)(2,1)S(1)} collective-permute-done((bf16[480,768]{1,0:T(8,128)(2,1)S(1)}, bf16[480,768]{1,0:T(8,128)(2,1)S(1)}, u32[]{:S(2)}, u32[]{:S(2)}) %collective-permute-start.29) | collective-permute-done | bytes 737312 | tf_op jit(solution)/shard_map/ppermute | solution.py:55
  114.6 3.7 %shard_map.98 = (bf16[192,768]{1,0:T(8,128)(2,1)S(1)}, bf16[192,768]{1,0:T(8,128)(2,1)S(1)}, bf16[192,768]{1,0:T(8,128)(2,1)S(1)}, f32[192,768]{1,0:T(8,128)S(1)}) custom-call(bf16[1024,768]{1,0:T(8,128)(2,1)S(1)} %shard_map.87.own_ref, bf16[1024,768]{1,0:T(8,128)(2,1)S(1)} %collective-permute-done.2.other_ref, ...), custom_call_target="tpu_custom_call" | custom-call | flops 1024 | bytes 1024 | tf_op jit(solution)/shard_map/pallas_call | solution.py:149
  119.7 10.3 %collective-permute-done.34 = bf16[192,768]{1,0:T(8,128)(2,1)S(1)} collective-permute-done((bf16[192,768]{1,0:T(8,128)(2,1)S(1)}, bf16[192,768]{1,0:T(8,128)(2,1)S(1)}, u32[]{:S(2)}, u32[]{:S(2)}) %collective-permute-start.34) | collective-permute-done | bytes 294944 | tf_op jit(solution)/shard_map/ppermute | solution.py:55
  130.2 1.3 add_convert_fusion.2.refs_7_
  131.5 5.3 %shard_map.100 = (bf16[480,768]{1,0:T(8,128)(2,1)S(1)}, bf16[480,768]{1,0:T(8,128)(2,1)S(1)}) custom-call(bf16[1024,768]{1,0:T(8,128)(2,1)S(1)} %shard_map.87.own_ref, bf16[1024,768]{1,0:T(8,128)(2,1)S(1)} %collective-permute-done.2.other_ref, bf16[4,96,1024]{2,1,0:T(8,128)(2,1)S(1)} %collective-permute-done.25.refs_0_, ...), custom_call_target="tpu_custom_call" | custom-call | flops 1024 | bytes 1024 | tf_op jit(solution)/shard_map/pallas_call | solution.py:149
  137.0 12.6 %collective-permute-done.37 = bf16[480,768]{1,0:T(8,128)(2,1)S(1)} collective-permute-done((bf16[480,768]{1,0:T(8,128)(2,1)S(1)}, bf16[480,768]{1,0:T(8,128)(2,1)S(1)}, u32[]{:S(2)}, u32[]{:S(2)}) %collective-permute-start.37) | collective-permute-done | bytes 737312 | tf_op jit(solution)/shard_map/ppermute | solution.py:55
  150.8 17.7 %collective-permute-done.35.got_ref = bf16[192,768]{1,0:T(8,128)(2,1)S(1)} collective-permute-done((bf16[192,768]{1,0:T(8,128)(2,1)S(1)}, bf16[192,768]{1,0:T(8,128)(2,1)S(1)}, u32[]{:S(2)}, u32[]{:S(2)}) %collective-permute-start.35) | collective-permute-done | bytes 294944 | tf_op jit(solution)/shard_map/ppermute | solution.py:55
  170.5 1.2 collective-permute-done.33
  171.9 5.8 %shard_map.101 = (bf16[480,768]{1,0:T(8,128)(2,1)S(1)}, f32[480,768]{1,0:T(8,128)S(1)}) custom-call(bf16[1024,768]{1,0:T(8,128)(2,1)S(1)} %shard_map.87.own_ref, bf16[1024,768]{1,0:T(8,128)(2,1)S(1)} %collective-permute-done.2.other_ref, bf16[4,96,1024]{2,1,0:T(8,128)(2,1)S(1)} %collective-permute-done.25.refs_0_, ...), custom_call_target="tpu_custom_call" | custom-call | flops 1024 | bytes 1024 | tf_op jit(solution)/shard_map/pallas_call | solution.py:149
  178.0 1.8 collective-permute-done.41
  180.0 13.9 %collective-permute-done.42.got_ref = bf16[192,768]{1,0:T(8,128)(2,1)S(1)} collective-permute-done((bf16[192,768]{1,0:T(8,128)(2,1)S(1)}, bf16[192,768]{1,0:T(8,128)(2,1)S(1)}, u32[]{:S(2)}, u32[]{:S(2)}) %collective-permute-start.42) | collective-permute-done | bytes 294944 | tf_op jit(solution)/shard_map/ppermute | solution.py:55
  196.0 3.4 %collective-permute-start.45 = (f32[1664]{0:T(1024)S(1)}, f32[1664]{0:T(1024)S(1)}, u32[]{:S(2)}, u32[]{:S(2)}) collective-permute-start(f32[1664]{0:T(1024)S(1)} %pad_maximum_fusion), channel_id=1, source_target_pairs={{0,4},{1,5},{2,6},{3,7},{4,0},{5,1},{6,2},{7,3},{8,12},{9,13},{10,... | collective-permute-start | bytes 19976 | tf_op jit(solution)/shard_map/ppermute | solution.py:55
  199.6 1.2 collective-permute-done.44
  201.2 1.9 collective-permute-done.46
  206.9 2.0 broadcast_select_fusion.1
  208.9 1.4 copy-done.17
  212.4 6.3 %all-to-all-start = ((f32[16,1,1024]{2,1,0:T(1,128)}), f32[16,1,1024]{2,1,0:T(1,128)S(1)}, u32[]{:S(2)}, u32[]{:S(2)}) async-start(f32[16,1,1024]{2,1,0:T(1,128)} %broadcast_in_dim.8), calls=%async_computation | async-start | bytes 131072 | tf_op jit(solution)/shard_map/all_to_all | solution.py:271
  219.9 6.5 %all-to-all-done = f32[16,1,1024]{2,1,0:T(1,128)S(1)} async-done(((f32[16,1,1024]{2,1,0:T(1,128)}), f32[16,1,1024]{2,1,0:T(1,128)S(1)}, u32[]{:S(2)}, u32[]{:S(2)}) %all-to-all-start) | async-done | bytes 65568 | tf_op jit(solution)/shard_map/all_to_all | solution.py:271
  229.5 5.3 %multiply_multiply_fusion = f32[768,1536]{1,0:T(8,128)} fusion(f32[768,768]{1,0:T(8,128)} %copy-done.18, f32[768,768]{1,0:T(8,128)} %copy-done.17, f32[1536]{0:T(1024)S(1)} %get-tuple-element.119, f32[768]{0:T(1024)S(1)} %get-tuple-element.117, f32[]{:T(128)} %bitcast.6, f32[1536]{0:T(1024)S(1)} %get-tuple-element.122), kind=kLoop, calls=%fused_computation.1 | loop fusion | flops 5898240 | bytes 9452548 | tf_op jit(solution)/shard_map/mul | solution.py:431
  (154 shorter events, 33.8 us)
Async XLA Ops:
  2.9 1.9 collective-permute-start
  2.9 2.5 %collective-permute-start.1 = (bf16[192,1024]{1,0:T(8,128)(2,1)}, bf16[192,1024]{1,0:T(8,128)(2,1)S(1)}, u32[]{:S(2)}, u32[]{:S(2)}) collective-permute-start(bf16[192,1024]{1,0:T(8,128)(2,1)} %get-tuple-element.61.refs_2_), channel_id=1, source_target_pairs={{0,1},{1,0},{2,3},{3,2},{4,5},{5,4},{6,7},{7,6},{8,9},{9,8},{10,11... | collective-permute-start | bytes 1179656 | tf_op jit(solution)/shard_map/ppermute | solution.py:55
  8.9 21.4 %collective-permute-start.3 = (bf16[2,192,1024]{2,1,0:T(8,128)(2,1)}, bf16[2,192,1024]{2,1,0:T(8,128)(2,1)S(1)}, u32[]{:S(2)}, u32[]{:S(2)}) collective-permute-start(bf16[2,192,1024]{2,1,0:T(8,128)(2,1)} %get-tuple-element.62.refs_0_), channel_id=1, source_target_pairs={{0,32},{1,97},{2,34},{3,99},{4,36},{5,101},{6,38},{7,103},{8,40},{... | collective-permute-start | bytes 2359304 | tf_op jit(solution)/shard_map/ppermute | solution.py:55
  10.6 19.8 %collective-permute-start.4 = (bf16[2,192,1024]{2,1,0:T(8,128)(2,1)}, bf16[2,192,1024]{2,1,0:T(8,128)(2,1)S(1)}, u32[]{:S(2)}, u32[]{:S(2)}) collective-permute-start(bf16[2,192,1024]{2,1,0:T(8,128)(2,1)} %get-tuple-element.63.refs_1_.refs_0_), channel_id=1, source_target_pairs={{0,8},{1,25},{2,10},{3,27},{4,12},{5,29},{6,14},{7,31},{8,16},{9,1... | collective-permute-start | bytes 2359304 | tf_op jit(solution)/shard_map/ppermute | solution.py:55
  24.7 5.0 %collective-permute-start.5 = (f32[896]{0:T(1024)S(1)}, f32[896]{0:T(1024)S(1)}, u32[]{:S(2)}, u32[]{:S(2)}) collective-permute-start(f32[896]{0:T(1024)S(1)} %concatenate.33), channel_id=1, source_target_pairs={{0,1},{1,0},{2,3},{3,2},{4,5},{5,4},{6,7},{7,6},{8,9},{9,8},{10,11... | collective-permute-start | bytes 10760 | tf_op jit(solution)/shard_map/ppermute | solution.py:55
  29.6 14.0 %collective-permute-start.2 = (bf16[1024,768]{1,0:T(8,128)(2,1)S(1)}, bf16[1024,768]{1,0:T(8,128)(2,1)S(1)}, u32[]{:S(2)}, u32[]{:S(2)}) collective-permute-start(bf16[1024,768]{1,0:T(8,128)(2,1)S(1)} %shard_map.88), channel_id=1, source_target_pairs={{0,1},{1,0},{2,3},{3,2},{4,5},{5,4},{6,7},{7,6},{8,9},{9,8},{10,11... | collective-permute-start | bytes 4718600 | tf_op jit(solution)/shard_map/ppermute | solution.py:55
  30.4 9.9 %collective-permute-start.6 = (bf16[2,192,1024]{2,1,0:T(8,128)(2,1)S(1)}, bf16[2,192,1024]{2,1,0:T(8,128)(2,1)S(1)}, u32[]{:S(2)}, u32[]{:S(2)}) collective-permute-start(bf16[2,192,1024]{2,1,0:T(8,128)(2,1)S(1)} %collective-permute-done.3.refs_1_), channel_id=1, source_target_pairs={{0,1},{1,0},{2,3},{3,2},{4,5},{5,4},{6,7},{7,6},{8,9},{9,8},{10,11... | collective-permute-start | bytes 2359304 | tf_op jit(solution)/shard_map/ppermute | solution.py:55
  31.0 9.3 %collective-permute-start.9 = (bf16[2,192,1024]{2,1,0:T(8,128)(2,1)S(1)}, bf16[2,192,1024]{2,1,0:T(8,128)(2,1)S(1)}, u32[]{:S(2)}, u32[]{:S(2)}) collective-permute-start(bf16[2,192,1024]{2,1,0:T(8,128)(2,1)S(1)} %collective-permute-done.4.refs_1_), channel_id=1, source_target_pairs={{0,1},{1,0},{2,3},{3,2},{4,5},{5,4},{6,7},{7,6},{8,9},{9,8},{10,11... | collective-permute-start | bytes 2359304 | tf_op jit(solution)/shard_map/ppermute | solution.py:55
  31.1 9.1 %collective-permute-start.7 = (bf16[192,1024]{1,0:T(8,128)(2,1)S(1)}, bf16[192,1024]{1,0:T(8,128)(2,1)S(1)}, u32[]{:S(2)}, u32[]{:S(2)}) collective-permute-start(bf16[192,1024]{1,0:T(8,128)(2,1)S(1)} %slice_bitcast_fusion.5), channel_id=1, source_target_pairs={{0,32},{1,97},{2,34},{3,99},{4,36},{5,101},{6,38},{7,103},{8,40},{... | collective-permute-start | bytes 1179656 | tf_op jit(solution)/shard_map/ppermute | solution.py:55
  31.2 9.1 %collective-permute-start.8 = (bf16[192,1024]{1,0:T(8,128)(2,1)S(1)}, bf16[192,1024]{1,0:T(8,128)(2,1)S(1)}, u32[]{:S(2)}, u32[]{:S(2)}) collective-permute-start(bf16[192,1024]{1,0:T(8,128)(2,1)S(1)} %slice_bitcast_fusion.4), channel_id=1, source_target_pairs={{0,8},{1,25},{2,10},{3,27},{4,12},{5,29},{6,14},{7,31},{8,16},{9,1... | collective-permute-start | bytes 1179656 | tf_op jit(solution)/shard_map/ppermute | solution.py:55
  40.3 1.8 collective-permute-start.11
  40.3 2.8 %collective-permute-start.10 = (bf16[192,1024]{1,0:T(8,128)(2,1)S(1)}, bf16[192,1024]{1,0:T(8,128)(2,1)S(1)}, u32[]{:S(2)}, u32[]{:S(2)}) collective-permute-start(bf16[192,1024]{1,0:T(8,128)(2,1)S(1)} %collective-permute-done.7.refs_3_), channel_id=1, source_target_pairs={{0,1},{1,0},{2,3},{3,2},{4,5},{5,4},{6,7},{7,6},{8,9},{9,8},{10,11... | collective-permute-start | bytes 1179656 | tf_op jit(solution)/shard_map/ppermute | solution.py:55
  42.2 21.9 %collective-permute-start.13 = (bf16[2,4,96,1024]{3,2,1,0:T(8,128)(2,1)S(1)}, bf16[2,4,96,1024]{3,2,1,0:T(8,128)(2,1)}, u32[]{:S(2)}, u32[]{:S(2)}) collective-permute-start(bf16[2,4,96,1024]{3,2,1,0:T(8,128)(2,1)S(1)} %shard_map.92.refs_6_.refs_2_), channel_id=1, source_target_pairs={{0,32},{1,97},{2,34},{3,99},{4,36},{5,101},{6,38},{7,103},{8,40},{... | collective-permute-start | bytes 4718600 | tf_op jit(solution)/shard_map/ppermute | solution.py:55
  43.3 21.6 %collective-permute-start.12 = (bf16[2,4,96,1024]{3,2,1,0:T(8,128)(2,1)S(1)}, bf16[2,4,96,1024]{3,2,1,0:T(8,128)(2,1)S(1)}, u32[]{:S(2)}, u32[]{:S(2)}) collective-permute-start(bf16[2,4,96,1024]{3,2,1,0:T(8,128)(2,1)S(1)} %shard_map.91.refs_5_), channel_id=1, source_target_pairs={{0,8},{1,25},{2,10},{3,27},{4,12},{5,29},{6,14},{7,31},{8,16},{9,1... | collective-permute-start | bytes 4718600 | tf_op jit(solution)/shard_map/ppermute | solution.py:55
  47.1 8.8 %collective-permute-start.14 = (bf16[192,768]{1,0:T(8,128)(2,1)S(1)}, bf16[192,768]{1,0:T(8,128)(2,1)S(1)}, u32[]{:S(2)}, u32[]{:S(2)}) collective-permute-start(bf16[192,768]{1,0:T(8,128)(2,1)S(1)} %get-tuple-element.71), channel_id=1, source_target_pairs={{0,2},{1,7},{2,4},{3,1},{4,6},{5,3},{6,0},{7,5},{8,10},{9,15},{10,... | collective-permute-start | bytes 884744 | tf_op jit(solution)/shard_map/ppermute | solution.py:55
  56.0 8.0 %collective-permute-start.15 = (bf16[192,768]{1,0:T(8,128)(2,1)S(1)}, bf16[192,768]{1,0:T(8,128)(2,1)S(1)}, u32[]{:S(2)}, u32[]{:S(2)}) collective-permute-start(bf16[192,768]{1,0:T(8,128)(2,1)S(1)} %add_convert_fusion.9), channel_id=1, source_target_pairs={{0,2},{1,7},{2,4},{3,1},{4,6},{5,3},{6,0},{7,5},{8,10},{9,15},{10,... | collective-permute-start | bytes 884744 | tf_op jit(solution)/shard_map/ppermute | solution.py:55
  65.0 5.6 %collective-permute-start.16 = (bf16[2,4,96,1024]{3,2,1,0:T(8,128)(2,1)S(1)}, bf16[2,4,96,1024]{3,2,1,0:T(8,128)(2,1)S(1)}, u32[]{:S(2)}, u32[]{:S(2)}) collective-permute-start(bf16[2,4,96,1024]{3,2,1,0:T(8,128)(2,1)S(1)} %collective-permute-done.12.refs_0_), channel_id=1, source_target_pairs={{0,1},{1,0},{2,3},{3,2},{4,5},{5,4},{6,7},{7,6},{8,9},{9,8},{10,11... | collective-permute-start | bytes 4718600 | tf_op jit(solution)/shard_map/ppermute | solution.py:55
  65.0 5.9 %collective-permute-start.17 = (bf16[2,4,96,1024]{3,2,1,0:T(8,128)(2,1)}, bf16[2,4,96,1024]{3,2,1,0:T(8,128)(2,1)S(1)}, u32[]{:S(2)}, u32[]{:S(2)}) collective-permute-start(bf16[2,4,96,1024]{3,2,1,0:T(8,128)(2,1)} %collective-permute-done.13.refs_3_), channel_id=1, source_target_pairs={{0,1},{1,0},{2,3},{3,2},{4,5},{5,4},{6,7},{7,6},{8,9},{9,8},{10,11... | collective-permute-start | bytes 4718600 | tf_op jit(solution)/shard_map/ppermute | solution.py:55
  66.7 13.3 %collective-permute-start.20 = (bf16[4,96,1024]{2,1,0:T(8,128)(2,1)S(1)}, bf16[4,96,1024]{2,1,0:T(8,128)(2,1)S(1)}, u32[]{:S(2)}, u32[]{:S(2)}) collective-permute-start(bf16[4,96,1024]{2,1,0:T(8,128)(2,1)S(1)} %slice_bitcast_fusion.3), channel_id=1, source_target_pairs={{0,8},{1,25},{2,10},{3,27},{4,12},{5,29},{6,14},{7,31},{8,16},{9,1... | collective-permute-start | bytes 2359304 | tf_op jit(solution)/shard_map/ppermute | solution.py:55
  67.2 13.2 %collective-permute-start.21 = (bf16[4,96,1024]{2,1,0:T(8,128)(2,1)S(1)}, bf16[4,96,1024]{2,1,0:T(8,128)(2,1)S(1)}, u32[]{:S(2)}, u32[]{:S(2)}) collective-permute-start(bf16[4,96,1024]{2,1,0:T(8,128)(2,1)S(1)} %slice_bitcast_fusion.2), channel_id=1, source_target_pairs={{0,32},{1,97},{2,34},{3,99},{4,36},{5,101},{6,38},{7,103},{8,40},{... | collective-permute-start | bytes 2359304 | tf_op jit(solution)/shard_map/ppermute | solution.py:55
  70.8 29.9 %collective-permute-start.18 = (bf16[2,4,96,1024]{3,2,1,0:T(8,128)(2,1)}, bf16[2,4,96,1024]{3,2,1,0:T(8,128)(2,1)S(1)}, u32[]{:S(2)}, u32[]{:S(2)}) collective-permute-start(bf16[2,4,96,1024]{3,2,1,0:T(8,128)(2,1)} %shard_map.89), channel_id=1, source_target_pairs={{0,8},{1,25},{2,10},{3,27},{4,12},{5,29},{6,14},{7,31},{8,16},{9,1... | collective-permute-start | bytes 4718600 | tf_op jit(solution)/shard_map/ppermute | solution.py:55
  71.2 29.5 %collective-permute-start.19 = (bf16[2,4,96,1024]{3,2,1,0:T(8,128)(2,1)S(1)}, bf16[2,4,96,1024]{3,2,1,0:T(8,128)(2,1)}, u32[]{:S(2)}, u32[]{:S(2)}) collective-permute-start(bf16[2,4,96,1024]{3,2,1,0:T(8,128)(2,1)S(1)} %shard_map.90.refs_2_), channel_id=1, source_target_pairs={{0,32},{1,97},{2,34},{3,99},{4,36},{5,101},{6,38},{7,103},{8,40},{... | collective-permute-start | bytes 4718600 | tf_op jit(solution)/shard_map/ppermute | solution.py:55
  72.1 9.3 %collective-permute-start.24 = (bf16[192,768]{1,0:T(8,128)(2,1)S(1)}, bf16[192,768]{1,0:T(8,128)(2,1)S(1)}, u32[]{:S(2)}, u32[]{:S(2)}) collective-permute-start(bf16[192,768]{1,0:T(8,128)(2,1)S(1)} %add_convert_fusion.8), channel_id=1, source_target_pairs={{0,2},{1,7},{2,4},{3,1},{4,6},{5,3},{6,0},{7,5},{8,10},{9,15},{10,... | collective-permute-start | bytes 884744 | tf_op jit(solution)/shard_map/ppermute | solution.py:55
  80.4 9.1 %collective-permute-start.22 = (bf16[4,96,1024]{2,1,0:T(8,128)(2,1)S(1)}, bf16[4,96,1024]{2,1,0:T(8,128)(2,1)S(1)}, u32[]{:S(2)}, u32[]{:S(2)}) collective-permute-start(bf16[4,96,1024]{2,1,0:T(8,128)(2,1)S(1)} %collective-permute-done.20.refs_0_), channel_id=1, source_target_pairs={{0,1},{1,0},{2,3},{3,2},{4,5},{5,4},{6,7},{7,6},{8,9},{9,8},{10,11... | collective-permute-start | bytes 2359304 | tf_op jit(solution)/shard_map/ppermute | solution.py:55
  81.4 8.1 %collective-permute-start.23 = (bf16[4,96,1024]{2,1,0:T(8,128)(2,1)S(1)}, bf16[4,96,1024]{2,1,0:T(8,128)(2,1)S(1)}, u32[]{:S(2)}, u32[]{:S(2)}) collective-permute-start(bf16[4,96,1024]{2,1,0:T(8,128)(2,1)S(1)} %collective-permute-done.21.refs_5_), channel_id=1, source_target_pairs={{0,1},{1,0},{2,3},{3,2},{4,5},{5,4},{6,7},{7,6},{8,9},{9,8},{10,11... | collective-permute-start | bytes 2359304 | tf_op jit(solution)/shard_map/ppermute | solution.py:55
  81.5 7.9 %collective-permute-start.27 = (bf16[192,768]{1,0:T(8,128)(2,1)S(1)}, bf16[192,768]{1,0:T(8,128)(2,1)S(1)}, u32[]{:S(2)}, u32[]{:S(2)}) collective-permute-start(bf16[192,768]{1,0:T(8,128)(2,1)S(1)} %get-tuple-element.76), channel_id=1, source_target_pairs={{0,2},{1,7},{2,4},{3,1},{4,6},{5,3},{6,0},{7,5},{8,10},{9,15},{10,... | collective-permute-start | bytes 884744 | tf_op jit(solution)/shard_map/ppermute | solution.py:55
  100.7 13.5 %collective-permute-start.28 = (bf16[2,4,96,1024]{3,2,1,0:T(8,128)(2,1)S(1)}, bf16[2,4,96,1024]{3,2,1,0:T(8,128)(2,1)S(1)}, u32[]{:S(2)}, u32[]{:S(2)}) collective-permute-start(bf16[2,4,96,1024]{3,2,1,0:T(8,128)(2,1)S(1)} %collective-permute-done.18.refs_0_), channel_id=1, source_target_pairs={{0,1},{1,0},{2,3},{3,2},{4,5},{5,4},{6,7},{7,6},{8,9},{9,8},{10,11... | collective-permute-start | bytes 4718600 | tf_op jit(solution)/shard_map/ppermute | solution.py:55
  100.8 13.8 %collective-permute-start.30 = (bf16[2,4,96,1024]{3,2,1,0:T(8,128)(2,1)}, bf16[2,4,96,1024]{3,2,1,0:T(8,128)(2,1)S(1)}, u32[]{:S(2)}, u32[]{:S(2)}) collective-permute-start(bf16[2,4,96,1024]{3,2,1,0:T(8,128)(2,1)} %collective-permute-done.19.refs_3_), channel_id=1, source_target_pairs={{0,1},{1,0},{2,3},{3,2},{4,5},{5,4},{6,7},{7,6},{8,9},{9,8},{10,11... | collective-permute-start | bytes 4718600 | tf_op jit(solution)/shard_map/ppermute | solution.py:55
  101.3 12.7 %collective-permute-start.29 = (bf16[480,768]{1,0:T(8,128)(2,1)S(1)}, bf16[480,768]{1,0:T(8,128)(2,1)S(1)}, u32[]{:S(2)}, u32[]{:S(2)}) collective-permute-start(bf16[480,768]{1,0:T(8,128)(2,1)S(1)} %get-tuple-element.81.refs_8_), channel_id=1, source_target_pairs={{0,2},{1,7},{2,4},{3,1},{4,6},{5,3},{6,0},{7,5},{8,10},{9,15},{10,... | collective-permute-start | bytes 2211848 | tf_op jit(solution)/shard_map/ppermute | solution.py:55
  103.5 14.9 %collective-permute-start.25 = (bf16[4,96,1024]{2,1,0:T(8,128)(2,1)}, bf16[4,96,1024]{2,1,0:T(8,128)(2,1)S(1)}, u32[]{:S(2)}, u32[]{:S(2)}) collective-permute-start(bf16[4,96,1024]{2,1,0:T(8,128)(2,1)} %slice_bitcast_fusion.1), channel_id=1, source_target_pairs={{0,8},{1,25},{2,10},{3,27},{4,12},{5,29},{6,14},{7,31},{8,16},{9,1... | collective-permute-start | bytes 2359304 | tf_op jit(solution)/shard_map/ppermute | solution.py:55
  105.3 13.2 %collective-permute-start.26 = (bf16[4,96,1024]{2,1,0:T(8,128)(2,1)S(1)}, bf16[4,96,1024]{2,1,0:T(8,128)(2,1)S(1)}, u32[]{:S(2)}, u32[]{:S(2)}) collective-permute-start(bf16[4,96,1024]{2,1,0:T(8,128)(2,1)S(1)} %slice_bitcast_fusion), channel_id=1, source_target_pairs={{0,32},{1,97},{2,34},{3,99},{4,36},{5,101},{6,38},{7,103},{8,40},{... | collective-permute-start | bytes 2359304 | tf_op jit(solution)/shard_map/ppermute | solution.py:55
  114.2 16.0 %collective-permute-start.36 = (bf16[480,768]{1,0:T(8,128)(2,1)S(1)}, bf16[480,768]{1,0:T(8,128)(2,1)}, u32[]{:S(2)}, u32[]{:S(2)}) collective-permute-start(bf16[480,768]{1,0:T(8,128)(2,1)S(1)} %add_convert_fusion.3.refs_2_), channel_id=1, source_target_pairs={{0,2},{1,7},{2,4},{3,1},{4,6},{5,3},{6,0},{7,5},{8,10},{9,15},{10,... | collective-permute-start | bytes 2211848 | tf_op jit(solution)/shard_map/ppermute | solution.py:55
  114.3 15.8 %collective-permute-start.34 = (bf16[192,768]{1,0:T(8,128)(2,1)S(1)}, bf16[192,768]{1,0:T(8,128)(2,1)S(1)}, u32[]{:S(2)}, u32[]{:S(2)}) collective-permute-start(bf16[192,768]{1,0:T(8,128)(2,1)S(1)} %add_convert_fusion.7.refs_7_), channel_id=1, source_target_pairs={{0,2},{1,7},{2,4},{3,1},{4,6},{5,3},{6,0},{7,5},{8,10},{9,15},{10,... | collective-permute-start | bytes 884744 | tf_op jit(solution)/shard_map/ppermute | solution.py:55
  118.5 13.0 %collective-permute-start.31 = (bf16[4,96,1024]{2,1,0:T(8,128)(2,1)S(1)}, bf16[4,96,1024]{2,1,0:T(8,128)(2,1)S(1)}, u32[]{:S(2)}, u32[]{:S(2)}) collective-permute-start(bf16[4,96,1024]{2,1,0:T(8,128)(2,1)S(1)} %collective-permute-done.25.refs_0_), channel_id=1, source_target_pairs={{0,1},{1,0},{2,3},{3,2},{4,5},{5,4},{6,7},{7,6},{8,9},{9,8},{10,11... | collective-permute-start | bytes 2359304 | tf_op jit(solution)/shard_map/ppermute | solution.py:55
  119.6 11.8 %collective-permute-start.32 = (bf16[4,96,1024]{2,1,0:T(8,128)(2,1)S(1)}, bf16[4,96,1024]{2,1,0:T(8,128)(2,1)S(1)}, u32[]{:S(2)}, u32[]{:S(2)}) collective-permute-start(bf16[4,96,1024]{2,1,0:T(8,128)(2,1)S(1)} %collective-permute-done.26.refs_5_), channel_id=1, source_target_pairs={{0,1},{1,0},{2,3},{3,2},{4,5},{5,4},{6,7},{7,6},{8,9},{9,8},{10,11... | collective-permute-start | bytes 2359304 | tf_op jit(solution)/shard_map/ppermute | solution.py:55
  136.9 12.7 %collective-permute-start.37 = (bf16[480,768]{1,0:T(8,128)(2,1)S(1)}, bf16[480,768]{1,0:T(8,128)(2,1)S(1)}, u32[]{:S(2)}, u32[]{:S(2)}) collective-permute-start(bf16[480,768]{1,0:T(8,128)(2,1)S(1)} %get-tuple-element.98.refs_9_), channel_id=1, source_target_pairs={{0,2},{1,7},{2,4},{3,1},{4,6},{5,3},{6,0},{7,5},{8,10},{9,15},{10,... | collective-permute-start | bytes 2211848 | tf_op jit(solution)/shard_map/ppermute | solution.py:55
  136.9 32.4 %collective-permute-start.39 = (bf16[480,768]{1,0:T(8,128)(2,1)S(1)}, bf16[480,768]{1,0:T(8,128)(2,1)S(1)}, u32[]{:S(2)}, u32[]{:S(2)}) collective-permute-start(bf16[480,768]{1,0:T(8,128)(2,1)S(1)} %add_convert_fusion.2.refs_7_), channel_id=1, source_target_pairs={{0,2},{1,7},{2,4},{3,1},{4,6},{5,3},{6,0},{7,5},{8,10},{9,15},{10,... | collective-permute-start | bytes 2211848 | tf_op jit(solution)/shard_map/ppermute | solution.py:55
  149.8 27.9 %collective-permute-start.38 = (bf16[480,768]{1,0:T(8,128)(2,1)S(1)}, bf16[480,768]{1,0:T(8,128)(2,1)S(1)}, u32[]{:S(2)}, u32[]{:S(2)}) collective-permute-start(bf16[480,768]{1,0:T(8,128)(2,1)S(1)} %add_convert_fusion.1), channel_id=1, source_target_pairs={{0,2},{1,7},{2,4},{3,1},{4,6},{5,3},{6,0},{7,5},{8,10},{9,15},{10,... | collective-permute-start | bytes 2211848 | tf_op jit(solution)/shard_map/ppermute | solution.py:55
  149.9 18.7 %collective-permute-start.35 = (bf16[192,768]{1,0:T(8,128)(2,1)S(1)}, bf16[192,768]{1,0:T(8,128)(2,1)S(1)}, u32[]{:S(2)}, u32[]{:S(2)}) collective-permute-start(bf16[192,768]{1,0:T(8,128)(2,1)S(1)} %add_convert_fusion.5.refs_8_), channel_id=1, source_target_pairs={{0,2},{1,7},{2,4},{3,1},{4,6},{5,3},{6,0},{7,5},{8,10},{9,15},{10,... | collective-permute-start | bytes 884744 | tf_op jit(solution)/shard_map/ppermute | solution.py:55
  150.0 21.8 %collective-permute-start.33 = (bf16[192,768]{1,0:T(8,128)(2,1)S(1)}, bf16[192,768]{1,0:T(8,128)(2,1)S(1)}, u32[]{:S(2)}, u32[]{:S(2)}) collective-permute-start(bf16[192,768]{1,0:T(8,128)(2,1)S(1)} %get-tuple-element.89), channel_id=1, source_target_pairs={{0,2},{1,7},{2,4},{3,1},{4,6},{5,3},{6,0},{7,5},{8,10},{9,15},{10,... | collective-permute-start | bytes 884744 | tf_op jit(solution)/shard_map/ppermute | solution.py:55
  171.8 8.0 %collective-permute-start.41 = (bf16[192,768]{1,0:T(8,128)(2,1)S(1)}, bf16[192,768]{1,0:T(8,128)(2,1)S(1)}, u32[]{:S(2)}, u32[]{:S(2)}) collective-permute-start(bf16[192,768]{1,0:T(8,128)(2,1)S(1)} %add_convert_fusion.6.refs_7_), channel_id=1, source_target_pairs={{0,2},{1,7},{2,4},{3,1},{4,6},{5,3},{6,0},{7,5},{8,10},{9,15},{10,... | collective-permute-start | bytes 884744 | tf_op jit(solution)/shard_map/ppermute | solution.py:55
  178.0 16.7 %collective-permute-start.40 = (bf16[480,768]{1,0:T(8,128)(2,1)S(1)}, bf16[480,768]{1,0:T(8,128)(2,1)S(1)}, u32[]{:S(2)}, u32[]{:S(2)}) collective-permute-start(bf16[480,768]{1,0:T(8,128)(2,1)S(1)} %add_convert_fusion), channel_id=1, source_target_pairs={{0,2},{1,7},{2,4},{3,1},{4,6},{5,3},{6,0},{7,5},{8,10},{9,15},{10,... | collective-permute-start | bytes 2211848 | tf_op jit(solution)/shard_map/ppermute | solution.py:55
  179.9 14.0 %collective-permute-start.42 = (bf16[192,768]{1,0:T(8,128)(2,1)S(1)}, bf16[192,768]{1,0:T(8,128)(2,1)S(1)}, u32[]{:S(2)}, u32[]{:S(2)}) collective-permute-start(bf16[192,768]{1,0:T(8,128)(2,1)S(1)} %add_convert_fusion.4), channel_id=1, source_target_pairs={{0,2},{1,7},{2,4},{3,1},{4,6},{5,3},{6,0},{7,5},{8,10},{9,15},{10,... | collective-permute-start | bytes 884744 | tf_op jit(solution)/shard_map/ppermute | solution.py:55
  195.8 11.1 %collective-permute-start.43 = (f32[768,768]{1,0:T(8,128)}, f32[768,768]{1,0:T(8,128)}, u32[]{:S(2)}, u32[]{:S(2)}) collective-permute-start(f32[768,768]{1,0:T(8,128)} %get-tuple-element.115), channel_id=1, source_target_pairs={{0,1},{1,0},{2,3},{3,2},{4,5},{5,4},{6,7},{7,6},{8,9},{9,8},{10,11... | collective-permute-start | bytes 7077896 | tf_op jit(solution)/shard_map/ppermute | solution.py:55
  195.9 4.9 %collective-permute-start.44 = (f32[1664]{0:T(1024)S(1)}, f32[1664]{0:T(1024)S(1)}, u32[]{:S(2)}, u32[]{:S(2)}) collective-permute-start(f32[1664]{0:T(1024)S(1)} %pad_maximum_fusion), channel_id=1, source_target_pairs={{0,2},{1,7},{2,4},{3,1},{4,6},{5,3},{6,0},{7,5},{8,10},{9,15},{10,... | collective-permute-start | bytes 19976 | tf_op jit(solution)/shard_map/ppermute | solution.py:55
  196.0 5.2 %collective-permute-start.45 = (f32[1664]{0:T(1024)S(1)}, f32[1664]{0:T(1024)S(1)}, u32[]{:S(2)}, u32[]{:S(2)}) collective-permute-start(f32[1664]{0:T(1024)S(1)} %pad_maximum_fusion), channel_id=1, source_target_pairs={{0,4},{1,5},{2,6},{3,7},{4,0},{5,1},{6,2},{7,3},{8,12},{9,13},{10,... | collective-permute-start | bytes 19976 | tf_op jit(solution)/shard_map/ppermute | solution.py:55
  199.4 3.7 %collective-permute-start.46 = (f32[1664]{0:T(1024)S(1)}, f32[1664]{0:T(1024)S(1)}, u32[]{:S(2)}, u32[]{:S(2)}) collective-permute-start(f32[1664]{0:T(1024)S(1)} %pad_maximum_fusion), channel_id=1, source_target_pairs={{0,6},{1,3},{2,0},{3,5},{4,2},{5,7},{6,4},{7,1},{8,14},{9,11},{10,... | collective-permute-start | bytes 19976 | tf_op jit(solution)/shard_map/ppermute | solution.py:55
  212.4 14.0 %all-to-all-start = ((f32[16,1,1024]{2,1,0:T(1,128)}), f32[16,1,1024]{2,1,0:T(1,128)S(1)}, u32[]{:S(2)}, u32[]{:S(2)}) async-start(f32[16,1,1024]{2,1,0:T(1,128)} %broadcast_in_dim.8), calls=%async_computation | async-start | bytes 131072 | tf_op jit(solution)/shard_map/all_to_all | solution.py:271
  (24 other events, 265.1 us)

commit v2 on v1

--- a/solution.py
+++ b/solution.py
@@ -87,7 +87,7 @@
     return pl.pallas_call(
         kernel,
         out_shape=jax.ShapeDtypeStruct((TOK, HALF), jnp.bfloat16),
-        in_specs=[anywhere] * (2 + len(waits)),
+        in_specs=[pl.BlockSpec(memory_space=pltpu.HBM)] * 2 + [anywhere] * len(waits),
         out_specs=pl.BlockSpec(memory_space=pltpu.VMEM),
         scratch_shapes=[half_block, half_block, pltpu.SemaphoreType.DMA((2, count))],
         compiler_params=pltpu.CompilerParams(vmem_limit_bytes=24 << 20),
@@ -186,21 +186,6 @@
     )(inputs)
 
 
-def join(*pairs):
-    def kernel(*refs):
-        for k, out in enumerate(refs[2 * len(pairs) :]):
-            out[0], out[1] = refs[2 * k][...], refs[2 * k + 1][...]
-
-    vmem = pl.BlockSpec(memory_space=pltpu.VMEM)
-    return pl.pallas_call(
-        kernel,
-        out_shape=tuple(jax.ShapeDtypeStruct((2,) + a.shape, a.dtype) for a, _ in pairs),
-        in_specs=[vmem] * (2 * len(pairs)),
-        out_specs=(vmem,) * len(pairs),
-        cost_estimate=CHEAP,
-    )(*[value for pair in pairs for value in pair])
-
-
 def stack_rows(sources, start, count):
     arrays = []
     which = []
@@ -267,10 +252,102 @@
     )(last, got, *before)
 
 
-def everyone(vector, axis, count):
-    return lax.all_to_all(
-        jnp.broadcast_to(vector[None, :], (count,) + vector.shape), axis, 0, 0, tiled=True
-    )
+def clip_rows(mine, yours, kept, got):
+    def kernel(mine_ref, yours_ref, kept_ref, got_ref, payload, clips, sums):
+        core = coordinates()[3]
+        total = weights = None
+        squares = None
+        both = []
+        for stats, grad in ((mine_ref, kept_ref), (yours_ref, got_ref)):
+            grad_sq, weight_sq = stats[:, :HALF], stats[:, HALF : 2 * HALF]
+            clip = jnp.minimum(
+                1.0, clip_ratio * jnp.sqrt(weight_sq) / (jnp.sqrt(grad_sq) + unit_eps)
+            )
+            column = clip * clip * grad_sq
+            both.append((clip, column))
+            clipped = grad[...] * clip
+            squares = clipped * clipped if squares is None else squares + clipped * clipped
+            column_total = jnp.sum(column, axis=1, keepdims=True)
+            weight_total = jnp.sum(weight_sq, axis=1, keepdims=True)
+            total = column_total if total is None else total + column_total
+            weights = weight_total if weights is None else weights + weight_total
+        for at in range(2):
+            columns = pl.ds(at * HALF, HALF)
+            here = core == at
+            clips[:, columns] = jnp.where(here, both[0][0], both[1][0])
+            sums[:, columns] = jnp.where(here, both[0][1], both[1][1])
+        payload[:, :HALF] = lax.dot_general(
+            jnp.ones((16, HALF), jnp.float32),
+            squares,
+            (((1,), (1,)), ((), ())),
+            precision=lax.Precision.HIGHEST,
+            preferred_element_type=jnp.float32,
+        )
+        payload[:, HALF : HALF + 128] = jnp.broadcast_to(total, (16, 128))
+        payload[:, HALF + 128 :] = jnp.broadcast_to(weights, (16, 128))
+
+    vmem = pl.BlockSpec(memory_space=pltpu.VMEM)
+    columns = jax.ShapeDtypeStruct((1, 2 * HALF), jnp.float32)
+    return pl.pallas_call(
+        kernel,
+        out_shape=(jax.ShapeDtypeStruct((16, HALF + 256), jnp.float32), columns, columns),
+        in_specs=[vmem] * 4,
+        out_specs=(vmem,) * 3,
+        compiler_params=pltpu.CompilerParams(vmem_limit_bytes=32 << 20),
+        cost_estimate=CHEAP,
+    )(mine, yours, kept, got)
+
+
+def finish(gathered, row_total, clips, sums, row_factor, column_factor, kept, got):
+    step = 128
+
+    def kernel(
+        gathered_ref, row_total_ref, clip_ref, sum_ref, row_ref, column_ref, kept_ref, got_ref,
+        update, new_row_ref, new_column_ref,
+    ):
+        core = coordinates()[3]
+        at = pl.ds(pl.multiple_of(pl.program_id(0) * step, step), step)
+        clipped_total = jnp.sum(gathered_ref[:, HALF : HALF + 1], axis=0, keepdims=True)
+        weight_total = jnp.sum(gathered_ref[:, HALF + 128 : HALF + 129], axis=0, keepdims=True)
+        row_mean = (
+            second_decay * row_total_ref[:, :1]
+            + (1.0 - second_decay) * (clipped_total / FF + D * factor_eps)
+        ) / D
+        weight_rms = jnp.sqrt(weight_total / (D * FF))
+        new_column = second_decay * column_ref[...] + (1.0 - second_decay) * (
+            sum_ref[...] / D + factor_eps
+        )
+        new_column_ref[...] = new_column
+        row_sums = jnp.sum(gathered_ref[:, at], axis=0, keepdims=True)
+        new_row = second_decay * row_ref[:, at] + (1.0 - second_decay) * (
+            row_sums / FF + factor_eps
+        )
+        new_row_ref[:, at] = new_row
+        down = jnp.broadcast_to(lax.rsqrt(new_row), (step, step)).T[:, :1]
+        across = -weight_rms * clip_ref[...] * (jnp.sqrt(row_mean) * lax.rsqrt(new_column))
+        first = jnp.where(core == 0, kept_ref[...], got_ref[...])
+        second = jnp.where(core == 0, got_ref[...], kept_ref[...])
+        update[:, :HALF] = first * across[:, :HALF] * down
+        update[:, HALF:] = second * across[:, HALF:] * down
+
+    whole = lambda *shape: pl.BlockSpec(shape, lambda i: (0, 0))
+    rows = lambda width: pl.BlockSpec((step, width), lambda i: (i, 0))
+    return pl.pallas_call(
+        kernel,
+        grid=(HALF // step,),
+        out_shape=(
+            jax.ShapeDtypeStruct((HALF, 2 * HALF), jnp.float32),
+            jax.ShapeDtypeStruct((1, HALF), jnp.float32),
+            jax.ShapeDtypeStruct((1, 2 * HALF), jnp.float32),
+        ),
+        in_specs=[
+            whole(16, HALF + 256), whole(1, 128), whole(1, 2 * HALF), whole(1, 2 * HALF),
+            whole(1, HALF), whole(1, 2 * HALF), rows(HALF), rows(HALF),
+        ],
+        out_specs=(rows(2 * HALF), whole(1, HALF), whole(1, 2 * HALF)),
+        compiler_params=pltpu.CompilerParams(vmem_limit_bytes=32 << 20),
+        cost_estimate=CHEAP,
+    )(gathered, row_total, clips, sums, row_factor, column_factor, kept, got)
 
 
 def per_device(inputs, preact, upstream, weight, row_factor, column_factor):
@@ -279,27 +356,23 @@
     p, q = turn(inputs)
     size = FEAT // 2 // NCH
 
-    p_both, q_both = join((p, send(p, SWAP)), (q, send(q, SWAP)))
-    y1, x1 = send(p_both, ALONG_Y), send(q_both, ALONG_X)
-    slope_yours = slope_half(preact, upstream, True, (p_both, q_both))
+    p_swap, q_swap = send(p, SWAP), send(q, SWAP)
+    ya, xa = send(p, ALONG_Y), send(q, ALONG_X)
+    yb, xb = send(p_swap, ALONG_Y), send(q_swap, ALONG_X)
+    slope_yours = slope_half(preact, upstream, True, (p_swap, q_swap))
     slope_other = send(slope_yours, SWAP)
-    slope_mine = slope_half(preact, upstream, False, (p_both, q_both))
-    weight = after(weight, slope_mine)
-    weight_local = jnp.sum(weight * weight, axis=0)
-    row_local = jnp.broadcast_to(jnp.sum(row_factor)[None], (128,))
-    weight_mine = lax.dynamic_slice_in_dim(weight_local, core * HALF, HALF)
-    weight_yours = lax.dynamic_slice_in_dim(weight_local, (1 - core) * HALF, HALF)
-    early = jnp.concatenate([weight_mine, row_local])
-    early = early + send(jnp.concatenate([weight_yours, row_local]), SWAP)
-    y1, x1 = lax.optimization_barrier((y1, x1, slope_yours, slope_mine, early))[:2]
-    y2, x2 = send(y1[0], ALONG_Y), send(x1[0], ALONG_X)
-    y1_swap, x1_swap = send(y1, SWAP), send(x1, SWAP)
-    y2, x2 = lax.optimization_barrier((y2, x2, y1_swap, x1_swap))[:2]
+    slope_mine = slope_half(preact, upstream, False, (p_swap, q_swap))
+    ya, xa = lax.optimization_barrier((ya, xa, slope_yours, slope_mine))[:2]
+    y2, x2 = send(ya, ALONG_Y), send(xa, ALONG_X)
+    ya_swap, xa_swap = send(ya, SWAP), send(xa, SWAP)
+    yb, xb = lax.optimization_barrier((yb, xb, ya_swap, xa_swap))[:2]
+    yb_swap, xb_swap = send(yb, SWAP), send(xb, SWAP)
+    y2, x2 = lax.optimization_barrier((y2, x2, yb_swap, xb_swap))[:2]
     y2_swap, x2_swap = send(y2, SWAP), send(x2, SWAP)
-    p_places = [(p_both, 0), (y1, 0), (y1_swap, 1), (y2, None)]
-    p_places += [(p_both, 1), (y1, 1), (y1_swap, 0), (y2_swap, None)]
-    q_places = [(q_both, 0), (x1, 0), (x1_swap, 1), (x2, None)]
-    q_places += [(q_both, 1), (x1, 1), (x1_swap, 0), (x2_swap, None)]
+    p_places = [(p, None), (ya, None), (yb_swap, None), (y2, None)]
+    p_places += [(p_swap, None), (yb, None), (ya_swap, None), (y2_swap, None)]
+    q_places = [(q, None), (xa, None), (xb_swap, None), (x2, None)]
+    q_places += [(q_swap, None), (xb, None), (xa_swap, None), (x2_swap, None)]
 
     def units(entries, low=0, high=4, waits=()):
         return unit_partials(slope_mine, slope_other, entries, low, high, waits)
@@ -331,13 +404,19 @@
     x1, y1 = send(p_here, ALONG_X), send(q_here, ALONG_Y)
     own = units([[(p_places[i], p_places[4 + i]) for i in range(4)]], waits=(p_here, q_here))
     own_got = hop(own[0])
+    weight = after(weight, own[0])
+    weight_local = jnp.sum(weight * weight, axis=0)
+    row_local = jnp.broadcast_to(jnp.sum(row_factor)[None], (128,))
+    weight_mine = lax.dynamic_slice_in_dim(weight_local, core * HALF, HALF)
+    weight_yours = lax.dynamic_slice_in_dim(weight_local, (1 - core) * HALF, HALF)
+    early = jnp.concatenate([weight_mine, row_local])
+    early = early + send(jnp.concatenate([weight_yours, row_local]), SWAP)
     p_next = stack_rows(p_places, size, size)
     q_next = stack_rows(q_places, size, size)
     own_2 = add_narrow(own[1], own_got)
     own_got = hop(own_2)
     own_3 = add_narrow(own[2], own_got)
-    own_got = hop(own_3)
-    x1, y1 = lax.optimization_barrier((x1, y1, own_3, p_next, q_next))[:2]
+    x1, y1 = lax.optimization_barrier((x1, y1, own_3, p_next, q_next, early))[:2]
     x2, y2 = send(x1[0], ALONG_X), send(y1[0], ALONG_Y)
     x1_swap, y1_swap = send(x1, SWAP), send(y1, SWAP)
 
@@ -347,93 +426,66 @@
     near0_got = hop(near0[0])
     x2, y2 = lax.optimization_barrier((x2, y2, near0[0]))[:2]
     x2_swap, y2_swap = send(x2, SWAP), send(y2, SWAP)
-    placed = place_rows(own[3], own_got, [(0, 0, 0, FEAT // 2)], ())
     far0_entries = far_entries(q_here, y1, y1_swap, x2, x2_swap, y2, y2_swap)
-    far0 = units(far0_entries, 0, 2, waits=(placed[2],))
-    far0_got = hop(far0[0])
     near0_2 = add_narrow(near0[1], near0_got)
     near0_got = hop(near0_2)
-    far0 += units(far0_entries, 2, 4, waits=(near0_2, far0[0]))
-    x1, y1 = lax.optimization_barrier((x1_next, y1_next, far0[0]))[:2]
+    far0 = units(far0_entries, 0, 2, waits=(near0_2,))
+    far0_got = hop(far0[0])
+    near0_3 = add_narrow(near0[2], after(near0_got, far0[0]))
+    x1, y1 = lax.optimization_barrier((x1_next, y1_next, far0[0], near0_3))[:2]
     x2, y2 = send(x1[0], ALONG_X), send(y1[0], ALONG_Y)
-    x1, y1 = lax.optimization_barrier((x1, y1, far0[2]))[:2]
     x1_swap, y1_swap = send(x1, SWAP), send(y1, SWAP)
-    far0_2 = add_narrow(far0[1], far0_got)
+    near0_got = hop(after(near0_3, x1_swap, y1_swap))
+    own_got = hop(after(own_3, x1_swap, y1_swap))
+    far0_2 = add_narrow(far0[1], after(far0_got, x1_swap))
     far0_got = hop(far0_2)
-    near1 = units(near_entries(x1, x1_swap), waits=(far0_2, y1_swap))
-    near1_got = hop(near1[0])
-    near0_3 = add_narrow(near0[2], near0_got)
-    near0_got = hop(near0_3)
-    x2, y2 = lax.optimization_barrier((x2, y2, near1[0]))[:2]
-    x2_swap, y2_swap = send(x2, SWAP), send(y2, SWAP)
-    far0_3 = add_narrow(far0[2], far0_got)
-    far0_got = hop(far0_3)
-    far1_entries = far_entries(q_next, y1, y1_swap, x2, x2_swap, y2, y2_swap)
-    far1 = units(far1_entries, 0, 2, waits=(far0_3, near0_3))
-    far1_got = hop(far1[0])
-    near1_2 = add_narrow(near1[1], near1_got)
-    near1_got = hop(near1_2)
+    far0 += units(far0_entries, 2, 4, waits=(far0_2,))
     near_pieces = lambda chunk: [(1, chunk * size, 0, size), (2, chunk * size, size, size)]
     far_pieces = lambda chunk: [(3, chunk * size, 0, size)] + [
         (g, FEAT // 2 + chunk * size, (g + 1) * size, size) for g in range(4)
     ]
-    placed = place_rows(near0[3], near0_got, near_pieces(0), placed)
-    far1 += units(far1_entries, 2, 4, waits=(near1_2, placed[2], far1[0]))
-    far1_got = hop(add_narrow(far1[1], far1_got))
-    near1_got = hop(add_narrow(near1[2], near1_got))
-    placed = place_rows(far0[3], far0_got, far_pieces(0), placed)
-    far1_got = hop(after(add_narrow(far1[2], far1_got), placed[2]))
-    placed = place_rows(near1[3], near1_got, near_pieces(1), placed)
-    placed = place_rows(far1[3], far1_got, far_pieces(1), placed)
+    placed = place_rows(own[3], after(own_got, far0[2]), [(0, 0, 0, FEAT // 2)], ())
+    placed = place_rows(near0[3], after(near0_got, far0[2]), near_pieces(0), placed)
+    near1 = units(near_entries(x1, x1_swap), waits=(far0[2], placed[2], y1_swap))
+    near1_got = hop(near1[0])
+    x2, y2 = lax.optimization_barrier((x2, y2, near1[0]))[:2]
+    x2_swap, y2_swap = send(x2, SWAP), send(y2, SWAP)
+    far1_entries = far_entries(q_next, y1, y1_swap, x2, x2_swap, y2, y2_swap)
+    far1 = units(far1_entries[:2])
+    far1_got = hop(far1[0])
+    near1_2 = add_narrow(near1[1], after(near1_got, far1[0]))
+    near1_got = hop(near1_2)
+    far0_3 = add_narrow(far0[2], after(far0_got, far1[0]))
+    far0_got = hop(far0_3)
+    last1 = units(far1_entries[2:], waits=(far0_3, near1_2))
+    last1_got = hop(last1[0])
+    near1_3 = add_narrow(near1[2], after(near1_got, last1[0]))
+    far1_2 = add_narrow(far1[1], after(far1_got, last1[0]))
+    far1_got = hop(far1_2)
+    near1_got = hop(near1_3)
+    placed = place_rows(far0[3], after(far0_got, far1_2), far_pieces(0), placed)
+    last1_2 = add_narrow(last1[1], after(last1_got, placed[2]))
+    last1_got = hop(last1_2)
+    placed = place_rows(near1[3], after(near1_got, last1_2), near_pieces(1), placed)
+    far1_got = hop(add_narrow(far1[2], after(far1_got, placed[2])))
+    last1_got = hop(add_narrow(last1[2], last1_got))
+    placed = place_rows(far1[3], far1_got, far_pieces(1)[:2], placed)
+    last_pieces = [(g, low, start - 2 * size, count) for g, low, start, count in far_pieces(1)[2:]]
+    placed = place_rows(last1[3], last1_got, last_pieces, placed)
     kept, sent, grad_local = placed
     got = send(sent, SWAP)
-    grad_local = grad_local[0]
-    column_stats = jnp.concatenate([grad_local, early])
+    local = jnp.concatenate([grad_local, early[None, :]], axis=1)
+    column_stats = local
     for pairs in (ALONG_Z, ALONG_Z2, ALONG_Z3):
-        column_stats = column_stats + send(jnp.concatenate([grad_local, early]), pairs)
-    mine_stats = column_stats[: 2 * HALF]
-    yours_stats = send(mine_stats, SWAP)
-
-    def all_columns(start):
-        a, b = mine_stats[start : start + HALF], yours_stats[start : start + HALF]
-        return jnp.concatenate([jnp.where(core == 0, a, b), jnp.where(core == 0, b, a)])
-
-    grad_sq = all_columns(0)
-    weight_col_sq = all_columns(HALF)
-    row_total = column_stats[2 * HALF]
-
-    clip_factor = jnp.minimum(
-        1.0, clip_ratio * jnp.sqrt(weight_col_sq) / (jnp.sqrt(grad_sq) + unit_eps)
+        column_stats = column_stats + send(local, pairs)
+    yours_stats = send(column_stats, SWAP)
+    payload, clips, sums = clip_rows(column_stats, yours_stats, kept, got)
+    gathered = lax.all_to_all(payload[:, None, :], "gx", 0, 0, tiled=True)[:, 0]
+    update, new_row, new_column = finish(
+        gathered, column_stats[:, 2 * HALF :], clips, sums, row_factor[None, :],
+        column_factor[None, :], kept, got,
     )
-    column_sums = clip_factor * clip_factor * grad_sq
-    new_column = second_decay * column_factor + (1.0 - second_decay) * (
-        column_sums / D + factor_eps
-    )
-    grad = jnp.concatenate(
-        [jnp.where(core == 0, kept, got), jnp.where(core == 0, got, kept)], axis=1
-    )
-    clipped = grad * clip_factor[None, :]
-    row_part = jnp.sum(clipped * clipped, axis=1)
-    totals = jnp.concatenate(
-        [
-            jnp.broadcast_to(jnp.sum(column_sums)[None], (128,)),
-            jnp.broadcast_to(jnp.sum(weight_col_sq)[None], (128,)),
-        ]
-    )
-    summed = jnp.sum(everyone(jnp.concatenate([row_part, totals]), "gx", 16), axis=0)
-    row_sums, clipped_total, weight_total = summed[:768], summed[768], summed[896]
-    new_row = second_decay * row_factor + (1.0 - second_decay) * (row_sums / FF + factor_eps)
-    row_mean = (
-        second_decay * row_total + (1.0 - second_decay) * (clipped_total / FF + D * factor_eps)
-    ) / D
-    weight_rms = jnp.sqrt(weight_total / (D * FF))
-    update = (
-        -weight_rms
-        * clipped
-        * lax.rsqrt(new_row)[:, None]
-        * (jnp.sqrt(row_mean) * lax.rsqrt(new_column))[None, :]
-    )
-    return (update, new_row, new_column)
+    return (update, new_row[0], new_column[0])
 
 
 def solution(mesh):

time: 236 us -> 226 us (0.958)
  waiting for transfers between devices: 115 us -> 98.9 us
  starting transfers between devices: 34.6 us -> 42.8 us
  other arithmetic: 16.5 us -> 8.36 us
  local copies, waits for them, and re-layouts: 15.2 us -> 20.5 us
  Pallas kernels: 48.9 us -> 52.9 us
  between operations: 4.69 us -> 1.61 us
    ppermute x48 -> x55, waiting for transfers between devices: 108 us -> 91.3 us  [send(): return lax.ppermute(value, BOTH, pairs)]
    ppermute x48 -> x55, starting transfers between devices: 28.3 us -> 36.9 us  [send(): return lax.ppermute(value, BOTH, pairs)]
    mul x2 -> x0, other arithmetic: 5.87 us -> none  [the longest x1 5.26 us: per_device(): -weight_rms * clipped * lax.rsqrt(new_row)[:, None]]
    unnamed x46 -> x118, local copies, waits for them, and re-layouts: 8.75 us -> 14.5 us
    pallas_call x1 -> x2, Pallas kernels: 2.57 us -> 5.56 us  [the longest x1 3.54 us: finish(): pl.pallas_call(kernel, grid=(HALF // step,), out_shape=(jax.ShapeDtypeStr...]
  transfers between devices with their start and end apart: 49 -> 56, of which waited for: 26 -> 29; matrix products, arithmetic and copies ran while one was open for 5% -> 5% of each run, Pallas kernels for 16% -> 20%
where the time goes in v2:
time: 226 us; the launch traced here: 225 us
  waiting for transfers between devices  98.9 us (44%)
  Pallas kernels  52.9 us (23%)
  starting transfers between devices  42.8 us (19%)
  local copies, waits for them, and re-layouts  20.5 us (9%)
  other arithmetic  8.36 us (4%)
    ppermute x55, waiting for transfers between devices, send(): return lax.ppermute(value, BOTH, pairs)  91.3 us
    ppermute x55, starting transfers between devices, send(): return lax.ppermute(value, BOTH, pairs)  36.9 us
    pallas_call x7, Pallas kernels, unit_partials(): pl.pallas_call(kernel, out_shape=tuple((jax.ShapeDtypeStruct((rows, HALF)...  34.9 us
    unnamed x118, local copies, waits for them, and re-layouts  14.5 us
    all_to_all x1, waiting for transfers between devices, per_device(): gathered = lax.all_to_all(payload[:, None, :], 'gx', 0, 0, tiled=True)[:, 0]  7.62 us
    all_to_all x1, starting transfers between devices, per_device(): gathered = lax.all_to_all(payload[:, None, :], 'gx', 0, 0, tiled=True)[:, 0]  5.9 us
    pallas_call x2, Pallas kernels, slope_half(): pl.pallas_call(kernel, out_shape=jax.ShapeDtypeStruct((TOK, HALF), jnp.bf...  5.05 us
  transfers between devices with their start and end apart: 56, of which 29 were waited for; matrix products, arithmetic and copies ran while one was open for 5% of the time, Pallas kernels for 20%

profile of v2, /device:TPU:0, one launch (start us, length us, event | category | flops | bytes accessed | tf_op | source)
XLA Modules:
  0.0 225.1 jit_solution(9264370056400305030)
XLA Ops:
  0.6 2.3 %shard_map.85 = (bf16[192,1024]{1,0:T(8,128)(2,1)}, bf16[192,1024]{1,0:T(8,128)(2,1)}) custom-call(bf16[1024,384]{1,0:T(8,128)(2,1)} %ref.1), custom_call_target="tpu_custom_call" | custom-call | flops 1024 | bytes 1024 | tf_op jit(solution)/shard_map/pallas_call | solution.py:184
  3.4 1.7 collective-permute-start.3
  5.1 1.5 collective-permute-start.4
  6.6 1.9 copy-done.6
  8.5 1.9 copy-done.7
  10.4 2.5 %shard_map.86.own_ref = bf16[1024,768]{1,0:T(8,128)(2,1)S(1)} custom-call(bf16[1024,1536]{1,0:T(8,128)(2,1)S(1)} %copy-done.6, bf16[1024,1536]{1,0:T(8,128)(2,1)S(1)} %copy-done.7, bf16[192,1024]{1,0:T(8,128)(2,1)S(1)} %collective-permute-done.refs_0_.refs_4_.refs_1_, bf16[192,1024]{1,0:T(8,128)(2,1)S(1)} %collective-permute-done.1.refs_1_.refs_4_), custom_call_target="tpu_custom_call" | custom-call | flops 1024 | bytes 1024 | tf_op jit(solution)/shard_map/pallas_call | solution.py:87
  12.9 2.5 %shard_map.87 = bf16[1024,768]{1,0:T(8,128)(2,1)S(1)} custom-call(bf16[1024,1536]{1,0:T(8,128)(2,1)S(1)} %copy-done.6, bf16[1024,1536]{1,0:T(8,128)(2,1)S(1)} %copy-done.7, bf16[192,1024]{1,0:T(8,128)(2,1)S(1)} %collective-permute-done.refs_0_.refs_4_.refs_1_, bf16[192,1024]{1,0:T(8,128)(2,1)S(1)} %collective-permute-done.1.refs_1_.refs_4_), custom_call_target="tpu_custom_call" | custom-call | flops 1024 | bytes 1024 | tf_op jit(solution)/shard_map/pallas_call | solution.py:87
  15.5 2.2 collective-permute-start.7
  17.8 1.3 collective-permute-start.6
  21.8 5.1 %collective-permute-done.5.refs_5_.refs_3_ = bf16[192,1024]{1,0:T(8,128)(2,1)S(1)} collective-permute-done((bf16[192,1024]{1,0:T(8,128)(2,1)S(1)}, bf16[192,1024]{1,0:T(8,128)(2,1)S(1)}, u32[]{:S(2)}, u32[]{:S(2)}) %collective-permute-start.5) | collective-permute-done | bytes 393248 | tf_op jit(solution)/shard_map/ppermute | solution.py:55
  27.4 3.6 %collective-permute-done.10.refs_3_.refs_6_ = bf16[192,1024]{1,0:T(8,128)(2,1)S(1)} collective-permute-done((bf16[192,1024]{1,0:T(8,128)(2,1)S(1)}, bf16[192,1024]{1,0:T(8,128)(2,1)S(1)}, u32[]{:S(2)}, u32[]{:S(2)}) %collective-permute-start.10) | collective-permute-done | bytes 393248 | tf_op jit(solution)/shard_map/ppermute | solution.py:55
  35.4 1.4 shard_map.90.refs_8_
  37.1 4.1 %shard_map.92 = (bf16[192,768]{1,0:T(8,128)(2,1)}, bf16[192,768]{1,0:T(8,128)(2,1)S(1)}, bf16[192,768]{1,0:T(8,128)(2,1)S(1)}, f32[192,768]{1,0:T(8,128)S(1)}) custom-call(bf16[1024,768]{1,0:T(8,128)(2,1)S(1)} %shard_map.86.own_ref, bf16[1024,768]{1,0:T(8,128)(2,1)S(1)} %collective-permute-done.2.other_ref, bf16[192,1024]{1,0:T(8,128)(2,1)S(1)} %copy-done.12, ...), custom_call_target="tpu_custom_call" | custom-call | flops 1024 | bytes 1024 | tf_op jit(solution)/shard_map/pallas_call | solution.py:149
  43.5 1.9 collective-permute-start.17
  46.1 2.9 %multiply_reduce_fusion = f32[1536]{0:T(1024)S(1)} fusion(f32[768,1536]{1,0:T(8,128)} %param.9), kind=kLoop, calls=%fused_computation | loop fusion | flops 2357760 | bytes 4724736 | tf_op jit(solution)/shard_map/reduce_sum | solution.py:408
  48.9 3.6 %collective-permute-done.17 = bf16[192,768]{1,0:T(8,128)(2,1)} collective-permute-done((bf16[192,768]{1,0:T(8,128)(2,1)}, bf16[192,768]{1,0:T(8,128)(2,1)}, u32[]{:S(2)}, u32[]{:S(2)}) %collective-permute-start.17) | collective-permute-done | bytes 294944 | tf_op jit(solution)/shard_map/ppermute | solution.py:55
  54.5 3.9 %collective-permute-start.19 = (f32[896]{0:T(1024)S(1)}, f32[896]{0:T(1024)S(1)}, u32[]{:S(2)}, u32[]{:S(2)}) collective-permute-start(f32[896]{0:T(1024)S(1)} %concatenate.10), channel_id=1, source_target_pairs={{0,1},{1,0},{2,3},{3,2},{4,5},{5,4},{6,7},{7,6},{8,9},{9,8},{10,11... | collective-permute-start | bytes 10760 | tf_op jit(solution)/shard_map/ppermute | solution.py:55
  59.8 1.8 collective-permute-done.18
  69.6 4.7 %shard_map.93 = (bf16[192,768]{1,0:T(8,128)(2,1)S(1)}, bf16[192,768]{1,0:T(8,128)(2,1)S(1)}, bf16[192,768]{1,0:T(8,128)(2,1)S(1)}, f32[192,768]{1,0:T(8,128)S(1)}) custom-call(bf16[1024,768]{1,0:T(8,128)(2,1)S(1)} %shard_map.86.own_ref, bf16[1024,768]{1,0:T(8,128)(2,1)S(1)} %collective-permute-done.2.other_ref, ...), custom_call_target="tpu_custom_call" | custom-call | flops 1024 | bytes 1024 | tf_op jit(solution)/shard_map/pallas_call | solution.py:149
  74.4 3.5 %collective-permute-done.24.refs_0_ = bf16[4,96,1024]{2,1,0:T(8,128)(2,1)S(1)} collective-permute-done((bf16[4,96,1024]{2,1,0:T(8,128)(2,1)S(1)}, bf16[4,96,1024]{2,1,0:T(8,128)(2,1)S(1)}, u32[]{:S(2)}, u32[]{:S(2)}) %collective-permute-start.24) | collective-permute-done | bytes 786464 | tf_op jit(solution)/shard_map/ppermute | solution.py:55
  79.6 2.7 %collective-permute-done.28 = bf16[192,768]{1,0:T(8,128)(2,1)S(1)} collective-permute-done((bf16[192,768]{1,0:T(8,128)(2,1)S(1)}, bf16[192,768]{1,0:T(8,128)(2,1)S(1)}, u32[]{:S(2)}, u32[]{:S(2)}) %collective-permute-start.28) | collective-permute-done | bytes 294944 | tf_op jit(solution)/shard_map/ppermute | solution.py:55
  82.5 5.4 %shard_map.94 = (bf16[480,768]{1,0:T(8,128)(2,1)S(1)}, bf16[480,768]{1,0:T(8,128)(2,1)S(1)}) custom-call(bf16[1024,768]{1,0:T(8,128)(2,1)S(1)} %shard_map.86.own_ref, bf16[1024,768]{1,0:T(8,128)(2,1)S(1)} %collective-permute-done.2.other_ref, bf16[4,96,1024]{2,1,0:T(8,128)(2,1)S(1)} %collective-permute-done.24.refs_0_, ...), custom_call_target="tpu_custom_call" | custom-call | flops 1024 | bytes 1024 | tf_op jit(solution)/shard_map/pallas_call | solution.py:149
  87.9 2.5 %collective-permute-done.29 = bf16[192,768]{1,0:T(8,128)(2,1)S(1)} collective-permute-done((bf16[192,768]{1,0:T(8,128)(2,1)S(1)}, bf16[192,768]{1,0:T(8,128)(2,1)S(1)}, u32[]{:S(2)}, u32[]{:S(2)}) %collective-permute-start.29) | collective-permute-done | bytes 294944 | tf_op jit(solution)/shard_map/ppermute | solution.py:55
  90.5 4.3 %collective-permute-done.22.refs_0_ = bf16[2,4,96,1024]{3,2,1,0:T(8,128)(2,1)S(1)} collective-permute-done((bf16[2,4,96,1024]{3,2,1,0:T(8,128)(2,1)S(1)}, bf16[2,4,96,1024]{3,2,1,0:T(8,128)(2,1)S(1)}, u32[]{:S(2)}, u32[]{:S(2)}) %collective-permute-start.22) | collective-permute-done | bytes 1572896 | tf_op jit(solution)/shard_map/ppermute | solution.py:55
  94.8 1.3 collective-permute-done.23.refs_3_.refs_1_
  99.6 2.3 %collective-permute-done.30.refs_4_.refs_2_ = bf16[2,4,96,1024]{3,2,1,0:T(8,128)(2,1)S(1)} collective-permute-done((bf16[2,4,96,1024]{3,2,1,0:T(8,128)(2,1)}, bf16[2,4,96,1024]{3,2,1,0:T(8,128)(2,1)S(1)}, u32[]{:S(2)}, u32[]{:S(2)}) %collective-permute-start.30) | collective-permute-done | bytes 1572896 | tf_op jit(solution)/shard_map/ppermute | solution.py:55
  103.1 1.5 collective-permute-start.35
  104.6 4.6 %collective-permute-done.34 = bf16[480,768]{1,0:T(8,128)(2,1)S(1)} collective-permute-done((bf16[480,768]{1,0:T(8,128)(2,1)S(1)}, bf16[480,768]{1,0:T(8,128)(2,1)S(1)}, u32[]{:S(2)}, u32[]{:S(2)}) %collective-permute-start.34) | collective-permute-done | bytes 737312 | tf_op jit(solution)/shard_map/ppermute | solution.py:55
  110.3 5.9 %shard_map.95 = (bf16[480,768]{1,0:T(8,128)(2,1)S(1)}, f32[480,768]{1,0:T(8,128)S(1)}) custom-call(bf16[1024,768]{1,0:T(8,128)(2,1)S(1)} %shard_map.86.own_ref, bf16[1024,768]{1,0:T(8,128)(2,1)S(1)} %collective-permute-done.2.other_ref, bf16[4,96,1024]{2,1,0:T(8,128)(2,1)S(1)} %collective-permute-done.24.refs_0_, ...), custom_call_target="tpu_custom_call" | custom-call | flops 1024 | bytes 1024 | tf_op jit(solution)/shard_map/pallas_call | solution.py:149
  120.3 3.7 %shard_map.98 = (bf16[192,768]{1,0:T(8,128)(2,1)S(1)}, bf16[192,768]{1,0:T(8,128)(2,1)S(1)}, bf16[192,768]{1,0:T(8,128)(2,1)S(1)}, f32[192,768]{1,0:T(8,128)S(1)}) custom-call(bf16[1024,768]{1,0:T(8,128)(2,1)S(1)} %copy-done.1, bf16[1024,768]{1,0:T(8,128)(2,1)S(1)} %copy-done.3, bf16[2,4,96,1024]{3,2,1,0:T(8,128)(2,1)S(1)} %copy-done.27, ...), custom_call_target="tpu_custom_call" | custom-call | flops 1024 | bytes 1024 | tf_op jit(solution)/shard_map/pallas_call | solution.py:149
  128.6 4.7 %shard_map.99 = (bf16[192,768]{1,0:T(8,128)(2,1)S(1)}, bf16[192,768]{1,0:T(8,128)(2,1)S(1)}, bf16[192,768]{1,0:T(8,128)(2,1)S(1)}, f32[192,768]{1,0:T(8,128)S(1)}) custom-call(bf16[1024,768]{1,0:T(8,128)(2,1)S(1)} %copy-done.1, bf16[1024,768]{1,0:T(8,128)(2,1)S(1)} %copy-done.3, bf16[4,96,1024]{2,1,0:T(8,128)(2,1)S(1)} %copy-done.47, ...), custom_call_target="tpu_custom_call" | custom-call | flops 1024 | bytes 1024 | tf_op jit(solution)/shard_map/pallas_call | solution.py:149
  133.3 8.2 %collective-permute-done.40 = bf16[192,768]{1,0:T(8,128)(2,1)S(1)} collective-permute-done((bf16[192,768]{1,0:T(8,128)(2,1)S(1)}, bf16[192,768]{1,0:T(8,128)(2,1)S(1)}, u32[]{:S(2)}, u32[]{:S(2)}) %collective-permute-start.40) | collective-permute-done | bytes 294944 | tf_op jit(solution)/shard_map/ppermute | solution.py:55
  141.9 2.0 collective-permute-start.43
  143.9 6.5 %shard_map.100 = (bf16[288,768]{1,0:T(8,128)(2,1)S(1)}, bf16[288,768]{1,0:T(8,128)(2,1)S(1)}, bf16[288,768]{1,0:T(8,128)(2,1)S(1)}, f32[288,768]{1,0:T(8,128)S(1)}) custom-call(bf16[1024,768]{1,0:T(8,128)(2,1)S(1)} %copy-done.1, bf16[1024,768]{1,0:T(8,128)(2,1)S(1)} %copy-done.3, bf16[2,4,96,1024]{3,2,1,0:T(8,128)(2,1)S(1)} %shard_map.89.refs_2_.refs_0_, ...), custom_call_target="tpu_custom_call" | custom-call | flops 1024 | bytes 1024 | tf_op jit(solution)/shard_map/pallas_call | solution.py:149
  150.5 2.7 %collective-permute-start.41 = (bf16[288,768]{1,0:T(8,128)(2,1)S(1)}, bf16[288,768]{1,0:T(8,128)(2,1)S(1)}, u32[]{:S(2)}, u32[]{:S(2)}) collective-permute-start(bf16[288,768]{1,0:T(8,128)(2,1)S(1)} %get-tuple-element.132), channel_id=1, source_target_pairs={{0,2},{1,7},{2,4},{3,1},{4,6},{5,3},{6,0},{7,5},{8,10},{9,15},{10,... | collective-permute-start | bytes 1327112 | tf_op jit(solution)/shard_map/ppermute | solution.py:55
  153.1 4.4 %collective-permute-done.47 = bf16[192,768]{1,0:T(8,128)(2,1)S(1)} collective-permute-done((bf16[192,768]{1,0:T(8,128)(2,1)S(1)}, bf16[192,768]{1,0:T(8,128)(2,1)S(1)}, u32[]{:S(2)}, u32[]{:S(2)}) %collective-permute-start.47) | collective-permute-done | bytes 294944 | tf_op jit(solution)/shard_map/ppermute | solution.py:55
  157.6 3.2 %collective-permute-done.43 = bf16[192,768]{1,0:T(8,128)(2,1)S(1)} collective-permute-done((bf16[192,768]{1,0:T(8,128)(2,1)S(1)}, bf16[192,768]{1,0:T(8,128)(2,1)S(1)}, u32[]{:S(2)}, u32[]{:S(2)}) %collective-permute-start.43) | collective-permute-done | bytes 294944 | tf_op jit(solution)/shard_map/ppermute | solution.py:55
  161.5 3.9 %collective-permute-done.41 = bf16[288,768]{1,0:T(8,128)(2,1)S(1)} collective-permute-done((bf16[288,768]{1,0:T(8,128)(2,1)S(1)}, bf16[288,768]{1,0:T(8,128)(2,1)S(1)}, u32[]{:S(2)}, u32[]{:S(2)}) %collective-permute-start.41) | collective-permute-done | bytes 442400 | tf_op jit(solution)/shard_map/ppermute | solution.py:55
  166.8 11.6 %collective-permute-done.48.got_ref = bf16[192,768]{1,0:T(8,128)(2,1)S(1)} collective-permute-done((bf16[192,768]{1,0:T(8,128)(2,1)S(1)}, bf16[192,768]{1,0:T(8,128)(2,1)S(1)}, u32[]{:S(2)}, u32[]{:S(2)}) %collective-permute-start.48) | collective-permute-done | bytes 294944 | tf_op jit(solution)/shard_map/ppermute | solution.py:55
  178.6 2.9 %collective-permute-done.46 = bf16[192,768]{1,0:T(8,128)(2,1)S(1)} collective-permute-done((bf16[192,768]{1,0:T(8,128)(2,1)S(1)}, bf16[192,768]{1,0:T(8,128)(2,1)S(1)}, u32[]{:S(2)}, u32[]{:S(2)}) %collective-permute-start.46) | collective-permute-done | bytes 294944 | tf_op jit(solution)/shard_map/ppermute | solution.py:55
  181.9 12.5 %collective-permute-done.49.got_ref = bf16[192,768]{1,0:T(8,128)(2,1)S(1)} collective-permute-done((bf16[192,768]{1,0:T(8,128)(2,1)S(1)}, bf16[192,768]{1,0:T(8,128)(2,1)S(1)}, u32[]{:S(2)}, u32[]{:S(2)}) %collective-permute-start.49) | collective-permute-done | bytes 294944 | tf_op jit(solution)/shard_map/ppermute | solution.py:55
  196.3 2.2 collective-permute-start.52
  198.5 1.6 collective-permute-done.50
  202.3 2.0 shard_map.105
  205.1 5.9 %all-to-all-start = ((f32[16,1,1024]{2,1,0:T(1,128)}), f32[16,1,1024]{2,1,0:T(1,128)S(1)}, u32[]{:S(2)}, u32[]{:S(2)}) async-start(f32[16,1,1024]{2,1,0:T(1,128)} %copy.19), calls=%async_computation | async-start | bytes 131072 | tf_op jit(solution)/shard_map/all_to_all | solution.py:483
  211.0 7.6 %all-to-all-done = f32[16,1,1024]{2,1,0:T(1,128)S(1)} async-done(((f32[16,1,1024]{2,1,0:T(1,128)}), f32[16,1,1024]{2,1,0:T(1,128)S(1)}, u32[]{:S(2)}, u32[]{:S(2)}) %all-to-all-start) | async-done | bytes 65568 | tf_op jit(solution)/shard_map/all_to_all | solution.py:483
  218.7 1.7 copy-done.9
  220.3 3.5 %shard_map.106 = (f32[768,1536]{1,0:T(8,128)}, f32[1,768]{1,0:T(1,128)S(1)}, f32[1,1536]{1,0:T(1,128)S(1)}) custom-call(f32[16,1024]{1,0:T(8,128)S(1)} %bitcast.12, f32[1,128]{1,0:T(1,128)S(1)} %slice.20.row_total_ref, f32[1,1536]{1,0:T(1,128)S(1)} %get-tuple-element.160.clip_ref, f32[1,1536]{1,0:T(1,128)S(1)} %get-tuple-element.161.sum_ref, ...), custom_call_target="tpu_custom_call" | custom-call | flops 1024 | bytes 1024 | tf_op jit(solution)/shard_map/pallas_call | solution.py:335
  (233 shorter events, 48.0 us)
Async XLA Ops:
  2.9 3.7 %collective-permute-start = (bf16[192,1024]{1,0:T(8,128)(2,1)}, bf16[192,1024]{1,0:T(8,128)(2,1)S(1)}, u32[]{:S(2)}, u32[]{:S(2)}) collective-permute-start(bf16[192,1024]{1,0:T(8,128)(2,1)} %get-tuple-element.84.refs_0_), channel_id=1, source_target_pairs={{0,1},{1,0},{2,3},{3,2},{4,5},{5,4},{6,7},{7,6},{8,9},{9,8},{10,11... | collective-permute-start | bytes 1179656 | tf_op jit(solution)/shard_map/ppermute | solution.py:55
  3.4 12.0 %collective-permute-start.3 = (bf16[192,1024]{1,0:T(8,128)(2,1)}, bf16[192,1024]{1,0:T(8,128)(2,1)S(1)}, u32[]{:S(2)}, u32[]{:S(2)}) collective-permute-start(bf16[192,1024]{1,0:T(8,128)(2,1)} %get-tuple-element.84.refs_0_), channel_id=1, source_target_pairs={{0,32},{1,97},{2,34},{3,99},{4,36},{5,101},{6,38},{7,103},{8,40},{... | collective-permute-start | bytes 1179656 | tf_op jit(solution)/shard_map/ppermute | solution.py:55
  5.1 10.4 %collective-permute-start.4 = (bf16[192,1024]{1,0:T(8,128)(2,1)}, bf16[192,1024]{1,0:T(8,128)(2,1)S(1)}, u32[]{:S(2)}, u32[]{:S(2)}) collective-permute-start(bf16[192,1024]{1,0:T(8,128)(2,1)} %get-tuple-element.85.refs_0_), channel_id=1, source_target_pairs={{0,8},{1,25},{2,10},{3,27},{4,12},{5,29},{6,14},{7,31},{8,16},{9,1... | collective-permute-start | bytes 1179656 | tf_op jit(solution)/shard_map/ppermute | solution.py:55
  15.5 4.9 %collective-permute-start.7 = (bf16[192,1024]{1,0:T(8,128)(2,1)S(1)}, bf16[192,1024]{1,0:T(8,128)(2,1)S(1)}, u32[]{:S(2)}, u32[]{:S(2)}) collective-permute-start(bf16[192,1024]{1,0:T(8,128)(2,1)S(1)} %collective-permute-done.3.refs_1_.refs_2_), channel_id=1, source_target_pairs={{0,1},{1,0},{2,3},{3,2},{4,5},{5,4},{6,7},{7,6},{8,9},{9,8},{10,11... | collective-permute-start | bytes 1179656 | tf_op jit(solution)/shard_map/ppermute | solution.py:55
  17.8 9.0 %collective-permute-start.5 = (bf16[192,1024]{1,0:T(8,128)(2,1)S(1)}, bf16[192,1024]{1,0:T(8,128)(2,1)S(1)}, u32[]{:S(2)}, u32[]{:S(2)}) collective-permute-start(bf16[192,1024]{1,0:T(8,128)(2,1)S(1)} %collective-permute-done.refs_0_.refs_4_.refs_1_), channel_id=1, source_target_pairs={{0,32},{1,97},{2,34},{3,99},{4,36},{5,101},{6,38},{7,103},{8,40},{... | collective-permute-start | bytes 1179656 | tf_op jit(solution)/shard_map/ppermute | solution.py:55
  17.8 9.0 %collective-permute-start.6 = (bf16[192,1024]{1,0:T(8,128)(2,1)S(1)}, bf16[192,1024]{1,0:T(8,128)(2,1)S(1)}, u32[]{:S(2)}, u32[]{:S(2)}) collective-permute-start(bf16[192,1024]{1,0:T(8,128)(2,1)S(1)} %collective-permute-done.1.refs_1_.refs_4_), channel_id=1, source_target_pairs={{0,8},{1,25},{2,10},{3,27},{4,12},{5,29},{6,14},{7,31},{8,16},{9,1... | collective-permute-start | bytes 1179656 | tf_op jit(solution)/shard_map/ppermute | solution.py:55
  19.2 17.9 %collective-permute-start.2 = (bf16[1024,768]{1,0:T(8,128)(2,1)S(1)}, bf16[1024,768]{1,0:T(8,128)(2,1)S(1)}, u32[]{:S(2)}, u32[]{:S(2)}) collective-permute-start(bf16[1024,768]{1,0:T(8,128)(2,1)S(1)} %shard_map.87), channel_id=1, source_target_pairs={{0,1},{1,0},{2,3},{3,2},{4,5},{5,4},{6,7},{7,6},{8,9},{9,8},{10,11... | collective-permute-start | bytes 4718600 | tf_op jit(solution)/shard_map/ppermute | solution.py:55
  20.4 10.7 %collective-permute-start.10 = (bf16[192,1024]{1,0:T(8,128)(2,1)S(1)}, bf16[192,1024]{1,0:T(8,128)(2,1)S(1)}, u32[]{:S(2)}, u32[]{:S(2)}) collective-permute-start(bf16[192,1024]{1,0:T(8,128)(2,1)S(1)} %collective-permute-done.3.refs_1_.refs_2_), channel_id=1, source_target_pairs={{0,32},{1,97},{2,34},{3,99},{4,36},{5,101},{6,38},{7,103},{8,40},{... | collective-permute-start | bytes 1179656 | tf_op jit(solution)/shard_map/ppermute | solution.py:55
  20.6 10.5 %collective-permute-start.11 = (bf16[192,1024]{1,0:T(8,128)(2,1)S(1)}, bf16[192,1024]{1,0:T(8,128)(2,1)S(1)}, u32[]{:S(2)}, u32[]{:S(2)}) collective-permute-start(bf16[192,1024]{1,0:T(8,128)(2,1)S(1)} %collective-permute-done.4.refs_1_), channel_id=1, source_target_pairs={{0,8},{1,25},{2,10},{3,27},{4,12},{5,29},{6,14},{7,31},{8,16},{9,1... | collective-permute-start | bytes 1179656 | tf_op jit(solution)/shard_map/ppermute | solution.py:55
  26.8 4.2 %collective-permute-start.9 = (bf16[192,1024]{1,0:T(8,128)(2,1)S(1)}, bf16[192,1024]{1,0:T(8,128)(2,1)S(1)}, u32[]{:S(2)}, u32[]{:S(2)}) collective-permute-start(bf16[192,1024]{1,0:T(8,128)(2,1)S(1)} %collective-permute-done.5.refs_5_.refs_3_), channel_id=1, source_target_pairs={{0,1},{1,0},{2,3},{3,2},{4,5},{5,4},{6,7},{7,6},{8,9},{9,8},{10,11... | collective-permute-start | bytes 1179656 | tf_op jit(solution)/shard_map/ppermute | solution.py:55
  26.9 4.1 %collective-permute-start.12 = (bf16[192,1024]{1,0:T(8,128)(2,1)S(1)}, bf16[192,1024]{1,0:T(8,128)(2,1)S(1)}, u32[]{:S(2)}, u32[]{:S(2)}) collective-permute-start(bf16[192,1024]{1,0:T(8,128)(2,1)S(1)} %collective-permute-done.6.refs_5_), channel_id=1, source_target_pairs={{0,1},{1,0},{2,3},{3,2},{4,5},{5,4},{6,7},{7,6},{8,9},{9,8},{10,11... | collective-permute-start | bytes 1179656 | tf_op jit(solution)/shard_map/ppermute | solution.py:55
  31.2 4.2 %collective-permute-start.13 = (bf16[192,1024]{1,0:T(8,128)(2,1)S(1)}, bf16[192,1024]{1,0:T(8,128)(2,1)S(1)}, u32[]{:S(2)}, u32[]{:S(2)}) collective-permute-start(bf16[192,1024]{1,0:T(8,128)(2,1)S(1)} %collective-permute-done.10.refs_3_.refs_6_), channel_id=1, source_target_pairs={{0,1},{1,0},{2,3},{3,2},{4,5},{5,4},{6,7},{7,6},{8,9},{9,8},{10,11... | collective-permute-start | bytes 1179656 | tf_op jit(solution)/shard_map/ppermute | solution.py:55
  34.2 27.4 %collective-permute-start.16 = (bf16[2,4,96,1024]{3,2,1,0:T(8,128)(2,1)}, bf16[2,4,96,1024]{3,2,1,0:T(8,128)(2,1)}, u32[]{:S(2)}, u32[]{:S(2)}) collective-permute-start(bf16[2,4,96,1024]{3,2,1,0:T(8,128)(2,1)} %shard_map.91.refs_9_.refs_2_), channel_id=1, source_target_pairs={{0,32},{1,97},{2,34},{3,99},{4,36},{5,101},{6,38},{7,103},{8,40},{... | collective-permute-start | bytes 4718600 | tf_op jit(solution)/shard_map/ppermute | solution.py:55
  36.8 24.9 %collective-permute-start.15 = (bf16[2,4,96,1024]{3,2,1,0:T(8,128)(2,1)}, bf16[2,4,96,1024]{3,2,1,0:T(8,128)(2,1)}, u32[]{:S(2)}, u32[]{:S(2)}) collective-permute-start(bf16[2,4,96,1024]{3,2,1,0:T(8,128)(2,1)} %shard_map.90.refs_8_), channel_id=1, source_target_pairs={{0,8},{1,25},{2,10},{3,27},{4,12},{5,29},{6,14},{7,31},{8,16},{9,1... | collective-permute-start | bytes 4718600 | tf_op jit(solution)/shard_map/ppermute | solution.py:55
  43.5 9.0 %collective-permute-start.17 = (bf16[192,768]{1,0:T(8,128)(2,1)}, bf16[192,768]{1,0:T(8,128)(2,1)}, u32[]{:S(2)}, u32[]{:S(2)}) collective-permute-start(bf16[192,768]{1,0:T(8,128)(2,1)} %get-tuple-element.94), channel_id=1, source_target_pairs={{0,2},{1,7},{2,4},{3,1},{4,6},{5,3},{6,0},{7,5},{8,10},{9,15},{10,... | collective-permute-start | bytes 884744 | tf_op jit(solution)/shard_map/ppermute | solution.py:55
  53.6 8.0 %collective-permute-start.18 = (bf16[192,768]{1,0:T(8,128)(2,1)S(1)}, bf16[192,768]{1,0:T(8,128)(2,1)S(1)}, u32[]{:S(2)}, u32[]{:S(2)}) collective-permute-start(bf16[192,768]{1,0:T(8,128)(2,1)S(1)} %add_convert_fusion.11), channel_id=1, source_target_pairs={{0,2},{1,7},{2,4},{3,1},{4,6},{5,3},{6,0},{7,5},{8,10},{9,15},{10,... | collective-permute-start | bytes 884744 | tf_op jit(solution)/shard_map/ppermute | solution.py:55
  54.5 4.7 %collective-permute-start.19 = (f32[896]{0:T(1024)S(1)}, f32[896]{0:T(1024)S(1)}, u32[]{:S(2)}, u32[]{:S(2)}) collective-permute-start(f32[896]{0:T(1024)S(1)} %concatenate.10), channel_id=1, source_target_pairs={{0,1},{1,0},{2,3},{3,2},{4,5},{5,4},{6,7},{7,6},{8,9},{9,8},{10,11... | collective-permute-start | bytes 10760 | tf_op jit(solution)/shard_map/ppermute | solution.py:55
  61.7 5.0 %collective-permute-start.20 = (bf16[2,4,96,1024]{3,2,1,0:T(8,128)(2,1)}, bf16[2,4,96,1024]{3,2,1,0:T(8,128)(2,1)S(1)}, u32[]{:S(2)}, u32[]{:S(2)}) collective-permute-start(bf16[2,4,96,1024]{3,2,1,0:T(8,128)(2,1)} %collective-permute-done.15.refs_0_), channel_id=1, source_target_pairs={{0,1},{1,0},{2,3},{3,2},{4,5},{5,4},{6,7},{7,6},{8,9},{9,8},{10,11... | collective-permute-start | bytes 4718600 | tf_op jit(solution)/shard_map/ppermute | solution.py:55
  61.8 5.9 %collective-permute-start.21 = (bf16[2,4,96,1024]{3,2,1,0:T(8,128)(2,1)}, bf16[2,4,96,1024]{3,2,1,0:T(8,128)(2,1)S(1)}, u32[]{:S(2)}, u32[]{:S(2)}) collective-permute-start(bf16[2,4,96,1024]{3,2,1,0:T(8,128)(2,1)} %collective-permute-done.16.refs_3_), channel_id=1, source_target_pairs={{0,1},{1,0},{2,3},{3,2},{4,5},{5,4},{6,7},{7,6},{8,9},{9,8},{10,11... | collective-permute-start | bytes 4718600 | tf_op jit(solution)/shard_map/ppermute | solution.py:55
  64.6 13.3 %collective-permute-start.24 = (bf16[4,96,1024]{2,1,0:T(8,128)(2,1)S(1)}, bf16[4,96,1024]{2,1,0:T(8,128)(2,1)S(1)}, u32[]{:S(2)}, u32[]{:S(2)}) collective-permute-start(bf16[4,96,1024]{2,1,0:T(8,128)(2,1)S(1)} %slice_bitcast_fusion.3), channel_id=1, source_target_pairs={{0,8},{1,25},{2,10},{3,27},{4,12},{5,29},{6,14},{7,31},{8,16},{9,1... | collective-permute-start | bytes 2359304 | tf_op jit(solution)/shard_map/ppermute | solution.py:55
  65.9 13.2 %collective-permute-start.25 = (bf16[4,96,1024]{2,1,0:T(8,128)(2,1)S(1)}, bf16[4,96,1024]{2,1,0:T(8,128)(2,1)S(1)}, u32[]{:S(2)}, u32[]{:S(2)}) collective-permute-start(bf16[4,96,1024]{2,1,0:T(8,128)(2,1)S(1)} %slice_bitcast_fusion.2), channel_id=1, source_target_pairs={{0,32},{1,97},{2,34},{3,99},{4,36},{5,101},{6,38},{7,103},{8,40},{... | collective-permute-start | bytes 2359304 | tf_op jit(solution)/shard_map/ppermute | solution.py:55
  67.6 27.1 %collective-permute-start.22 = (bf16[2,4,96,1024]{3,2,1,0:T(8,128)(2,1)S(1)}, bf16[2,4,96,1024]{3,2,1,0:T(8,128)(2,1)S(1)}, u32[]{:S(2)}, u32[]{:S(2)}) collective-permute-start(bf16[2,4,96,1024]{3,2,1,0:T(8,128)(2,1)S(1)} %shard_map.88), channel_id=1, source_target_pairs={{0,8},{1,25},{2,10},{3,27},{4,12},{5,29},{6,14},{7,31},{8,16},{9,1... | collective-permute-start | bytes 4718600 | tf_op jit(solution)/shard_map/ppermute | solution.py:55
  68.8 27.2 %collective-permute-start.23 = (bf16[2,4,96,1024]{3,2,1,0:T(8,128)(2,1)S(1)}, bf16[2,4,96,1024]{3,2,1,0:T(8,128)(2,1)}, u32[]{:S(2)}, u32[]{:S(2)}) collective-permute-start(bf16[2,4,96,1024]{3,2,1,0:T(8,128)(2,1)S(1)} %shard_map.89.refs_2_.refs_0_), channel_id=1, source_target_pairs={{0,32},{1,97},{2,34},{3,99},{4,36},{5,101},{6,38},{7,103},{8,40},{... | collective-permute-start | bytes 4718600 | tf_op jit(solution)/shard_map/ppermute | solution.py:55
  74.3 8.0 %collective-permute-start.28 = (bf16[192,768]{1,0:T(8,128)(2,1)S(1)}, bf16[192,768]{1,0:T(8,128)(2,1)S(1)}, u32[]{:S(2)}, u32[]{:S(2)}) collective-permute-start(bf16[192,768]{1,0:T(8,128)(2,1)S(1)} %get-tuple-element.100), channel_id=1, source_target_pairs={{0,2},{1,7},{2,4},{3,1},{4,6},{5,3},{6,0},{7,5},{8,10},{9,15},{10,... | collective-permute-start | bytes 884744 | tf_op jit(solution)/shard_map/ppermute | solution.py:55
  82.4 8.0 %collective-permute-start.29 = (bf16[192,768]{1,0:T(8,128)(2,1)S(1)}, bf16[192,768]{1,0:T(8,128)(2,1)S(1)}, u32[]{:S(2)}, u32[]{:S(2)}) collective-permute-start(bf16[192,768]{1,0:T(8,128)(2,1)S(1)} %add_convert_fusion.9.refs_7_), channel_id=1, source_target_pairs={{0,2},{1,7},{2,4},{3,1},{4,6},{5,3},{6,0},{7,5},{8,10},{9,15},{10,... | collective-permute-start | bytes 884744 | tf_op jit(solution)/shard_map/ppermute | solution.py:55
  96.1 5.8 %collective-permute-start.30 = (bf16[2,4,96,1024]{3,2,1,0:T(8,128)(2,1)}, bf16[2,4,96,1024]{3,2,1,0:T(8,128)(2,1)S(1)}, u32[]{:S(2)}, u32[]{:S(2)}) collective-permute-start(bf16[2,4,96,1024]{3,2,1,0:T(8,128)(2,1)} %collective-permute-done.23.refs_3_.refs_1_), channel_id=1, source_target_pairs={{0,1},{1,0},{2,3},{3,2},{4,5},{5,4},{6,7},{7,6},{8,9},{9,8},{10,11... | collective-permute-start | bytes 4718600 | tf_op jit(solution)/shard_map/ppermute | solution.py:55
  96.1 5.8 %collective-permute-start.33 = (bf16[2,4,96,1024]{3,2,1,0:T(8,128)(2,1)S(1)}, bf16[2,4,96,1024]{3,2,1,0:T(8,128)(2,1)S(1)}, u32[]{:S(2)}, u32[]{:S(2)}) collective-permute-start(bf16[2,4,96,1024]{3,2,1,0:T(8,128)(2,1)S(1)} %collective-permute-done.22.refs_0_), channel_id=1, source_target_pairs={{0,1},{1,0},{2,3},{3,2},{4,5},{5,4},{6,7},{7,6},{8,9},{9,8},{10,11... | collective-permute-start | bytes 4718600 | tf_op jit(solution)/shard_map/ppermute | solution.py:55
  96.6 12.7 %collective-permute-start.34 = (bf16[480,768]{1,0:T(8,128)(2,1)S(1)}, bf16[480,768]{1,0:T(8,128)(2,1)S(1)}, u32[]{:S(2)}, u32[]{:S(2)}) collective-permute-start(bf16[480,768]{1,0:T(8,128)(2,1)S(1)} %get-tuple-element.104), channel_id=1, source_target_pairs={{0,2},{1,7},{2,4},{3,1},{4,6},{5,3},{6,0},{7,5},{8,10},{9,15},{10,... | collective-permute-start | bytes 2211848 | tf_op jit(solution)/shard_map/ppermute | solution.py:55
  98.8 25.2 %collective-permute-start.31 = (bf16[4,96,1024]{2,1,0:T(8,128)(2,1)}, bf16[4,96,1024]{2,1,0:T(8,128)(2,1)S(1)}, u32[]{:S(2)}, u32[]{:S(2)}) collective-permute-start(bf16[4,96,1024]{2,1,0:T(8,128)(2,1)} %slice_bitcast_fusion.1), channel_id=1, source_target_pairs={{0,8},{1,25},{2,10},{3,27},{4,12},{5,29},{6,14},{7,31},{8,16},{9,1... | collective-permute-start | bytes 2359304 | tf_op jit(solution)/shard_map/ppermute | solution.py:55
  99.5 24.5 %collective-permute-start.32 = (bf16[4,96,1024]{2,1,0:T(8,128)(2,1)S(1)}, bf16[4,96,1024]{2,1,0:T(8,128)(2,1)}, u32[]{:S(2)}, u32[]{:S(2)}) collective-permute-start(bf16[4,96,1024]{2,1,0:T(8,128)(2,1)S(1)} %slice_bitcast_fusion), channel_id=1, source_target_pairs={{0,32},{1,97},{2,34},{3,99},{4,36},{5,101},{6,38},{7,103},{8,40},{... | collective-permute-start | bytes 2359304 | tf_op jit(solution)/shard_map/ppermute | solution.py:55
  103.1 14.2 %collective-permute-start.36 = (bf16[192,768]{1,0:T(8,128)(2,1)S(1)}, bf16[192,768]{1,0:T(8,128)(2,1)S(1)}, u32[]{:S(2)}, u32[]{:S(2)}) collective-permute-start(bf16[192,768]{1,0:T(8,128)(2,1)S(1)} %add_convert_fusion.10), channel_id=1, source_target_pairs={{0,2},{1,7},{2,4},{3,1},{4,6},{5,3},{6,0},{7,5},{8,10},{9,15},{10,... | collective-permute-start | bytes 884744 | tf_op jit(solution)/shard_map/ppermute | solution.py:55
  103.1 14.5 %collective-permute-start.35 = (bf16[192,768]{1,0:T(8,128)(2,1)S(1)}, bf16[192,768]{1,0:T(8,128)(2,1)S(1)}, u32[]{:S(2)}, u32[]{:S(2)}) collective-permute-start(bf16[192,768]{1,0:T(8,128)(2,1)S(1)} %add_convert_fusion.8), channel_id=1, source_target_pairs={{0,2},{1,7},{2,4},{3,1},{4,6},{5,3},{6,0},{7,5},{8,10},{9,15},{10,... | collective-permute-start | bytes 884744 | tf_op jit(solution)/shard_map/ppermute | solution.py:55
  125.4 16.0 %collective-permute-start.38 = (bf16[480,768]{1,0:T(8,128)(2,1)}, bf16[480,768]{1,0:T(8,128)(2,1)S(1)}, u32[]{:S(2)}, u32[]{:S(2)}) collective-permute-start(bf16[480,768]{1,0:T(8,128)(2,1)} %add_convert_fusion.1.refs_7_), channel_id=1, source_target_pairs={{0,2},{1,7},{2,4},{3,1},{4,6},{5,3},{6,0},{7,5},{8,10},{9,15},{10,... | collective-permute-start | bytes 2211848 | tf_op jit(solution)/shard_map/ppermute | solution.py:55
  125.4 16.0 %collective-permute-start.40 = (bf16[192,768]{1,0:T(8,128)(2,1)S(1)}, bf16[192,768]{1,0:T(8,128)(2,1)S(1)}, u32[]{:S(2)}, u32[]{:S(2)}) collective-permute-start(bf16[192,768]{1,0:T(8,128)(2,1)S(1)} %get-tuple-element.122), channel_id=1, source_target_pairs={{0,2},{1,7},{2,4},{3,1},{4,6},{5,3},{6,0},{7,5},{8,10},{9,15},{10,... | collective-permute-start | bytes 884744 | tf_op jit(solution)/shard_map/ppermute | solution.py:55
  141.7 19.2 %collective-permute-start.42 = (bf16[480,768]{1,0:T(8,128)(2,1)S(1)}, bf16[480,768]{1,0:T(8,128)(2,1)S(1)}, u32[]{:S(2)}, u32[]{:S(2)}) collective-permute-start(bf16[480,768]{1,0:T(8,128)(2,1)S(1)} %add_convert_fusion.refs_5_), channel_id=1, source_target_pairs={{0,2},{1,7},{2,4},{3,1},{4,6},{5,3},{6,0},{7,5},{8,10},{9,15},{10,... | collective-permute-start | bytes 2211848 | tf_op jit(solution)/shard_map/ppermute | solution.py:55
  141.8 15.7 %collective-permute-start.47 = (bf16[192,768]{1,0:T(8,128)(2,1)S(1)}, bf16[192,768]{1,0:T(8,128)(2,1)S(1)}, u32[]{:S(2)}, u32[]{:S(2)}) collective-permute-start(bf16[192,768]{1,0:T(8,128)(2,1)S(1)} %add_convert_fusion.7.refs_6_), channel_id=1, source_target_pairs={{0,2},{1,7},{2,4},{3,1},{4,6},{5,3},{6,0},{7,5},{8,10},{9,15},{10,... | collective-permute-start | bytes 884744 | tf_op jit(solution)/shard_map/ppermute | solution.py:55
  141.9 18.8 %collective-permute-start.43 = (bf16[192,768]{1,0:T(8,128)(2,1)S(1)}, bf16[192,768]{1,0:T(8,128)(2,1)S(1)}, u32[]{:S(2)}, u32[]{:S(2)}) collective-permute-start(bf16[192,768]{1,0:T(8,128)(2,1)S(1)} %get-tuple-element.125), channel_id=1, source_target_pairs={{0,2},{1,7},{2,4},{3,1},{4,6},{5,3},{6,0},{7,5},{8,10},{9,15},{10,... | collective-permute-start | bytes 884744 | tf_op jit(solution)/shard_map/ppermute | solution.py:55
  150.5 15.0 %collective-permute-start.41 = (bf16[288,768]{1,0:T(8,128)(2,1)S(1)}, bf16[288,768]{1,0:T(8,128)(2,1)S(1)}, u32[]{:S(2)}, u32[]{:S(2)}) collective-permute-start(bf16[288,768]{1,0:T(8,128)(2,1)S(1)} %get-tuple-element.132), channel_id=1, source_target_pairs={{0,2},{1,7},{2,4},{3,1},{4,6},{5,3},{6,0},{7,5},{8,10},{9,15},{10,... | collective-permute-start | bytes 1327112 | tf_op jit(solution)/shard_map/ppermute | solution.py:55
  165.6 15.9 %collective-permute-start.44 = (bf16[288,768]{1,0:T(8,128)(2,1)S(1)}, bf16[288,768]{1,0:T(8,128)(2,1)S(1)}, u32[]{:S(2)}, u32[]{:S(2)}) collective-permute-start(bf16[288,768]{1,0:T(8,128)(2,1)S(1)} %add_convert_fusion.3), channel_id=1, source_target_pairs={{0,2},{1,7},{2,4},{3,1},{4,6},{5,3},{6,0},{7,5},{8,10},{9,15},{10,... | collective-permute-start | bytes 1327112 | tf_op jit(solution)/shard_map/ppermute | solution.py:55
  165.8 12.6 %collective-permute-start.48 = (bf16[192,768]{1,0:T(8,128)(2,1)S(1)}, bf16[192,768]{1,0:T(8,128)(2,1)S(1)}, u32[]{:S(2)}, u32[]{:S(2)}) collective-permute-start(bf16[192,768]{1,0:T(8,128)(2,1)S(1)} %add_convert_fusion.5), channel_id=1, source_target_pairs={{0,2},{1,7},{2,4},{3,1},{4,6},{5,3},{6,0},{7,5},{8,10},{9,15},{10,... | collective-permute-start | bytes 884744 | tf_op jit(solution)/shard_map/ppermute | solution.py:55
  165.9 15.7 %collective-permute-start.46 = (bf16[192,768]{1,0:T(8,128)(2,1)S(1)}, bf16[192,768]{1,0:T(8,128)(2,1)S(1)}, u32[]{:S(2)}, u32[]{:S(2)}) collective-permute-start(bf16[192,768]{1,0:T(8,128)(2,1)S(1)} %add_convert_fusion.6), channel_id=1, source_target_pairs={{0,2},{1,7},{2,4},{3,1},{4,6},{5,3},{6,0},{7,5},{8,10},{9,15},{10,... | collective-permute-start | bytes 884744 | tf_op jit(solution)/shard_map/ppermute | solution.py:55
  181.6 13.0 %collective-permute-start.45 = (bf16[288,768]{1,0:T(8,128)(2,1)S(1)}, bf16[288,768]{1,0:T(8,128)(2,1)S(1)}, u32[]{:S(2)}, u32[]{:S(2)}) collective-permute-start(bf16[288,768]{1,0:T(8,128)(2,1)S(1)} %add_convert_fusion.2), channel_id=1, source_target_pairs={{0,2},{1,7},{2,4},{3,1},{4,6},{5,3},{6,0},{7,5},{8,10},{9,15},{10,... | collective-permute-start | bytes 1327112 | tf_op jit(solution)/shard_map/ppermute | solution.py:55
  181.8 12.6 %collective-permute-start.49 = (bf16[192,768]{1,0:T(8,128)(2,1)S(1)}, bf16[192,768]{1,0:T(8,128)(2,1)S(1)}, u32[]{:S(2)}, u32[]{:S(2)}) collective-permute-start(bf16[192,768]{1,0:T(8,128)(2,1)S(1)} %add_convert_fusion.4), channel_id=1, source_target_pairs={{0,2},{1,7},{2,4},{3,1},{4,6},{5,3},{6,0},{7,5},{8,10},{9,15},{10,... | collective-permute-start | bytes 884744 | tf_op jit(solution)/shard_map/ppermute | solution.py:55
  195.1 7.2 %collective-permute-start.54 = (f32[768,768]{1,0:T(8,128)S(1)}, f32[768,768]{1,0:T(8,128)S(1)}, u32[]{:S(2)}, u32[]{:S(2)}) collective-permute-start(f32[768,768]{1,0:T(8,128)S(1)} %get-tuple-element.158), channel_id=1, source_target_pairs={{0,1},{1,0},{2,3},{3,2},{4,5},{5,4},{6,7},{7,6},{8,9},{9,8},{10,11... | collective-permute-start | bytes 7077896 | tf_op jit(solution)/shard_map/ppermute | solution.py:55
  195.2 4.9 %collective-permute-start.50 = (f32[1,1664]{1,0:T(1,128)S(1)}, f32[1,1664]{1,0:T(1,128)S(1)}, u32[]{:S(2)}, u32[]{:S(2)}) collective-permute-start(f32[1,1664]{1,0:T(1,128)S(1)} %constant_dynamic-update-slice_fusion), channel_id=1, source_target_pairs={{0,2},{1,7},{2,4},{3,1},{4,6},{5,3},{6,0},{7,5},{8,10},{9,15},{10,... | collective-permute-start | bytes 19976 | tf_op jit(solution)/shard_map/ppermute | solution.py:55
  195.3 5.2 %collective-permute-start.51 = (f32[1,1664]{1,0:T(1,128)S(1)}, f32[1,1664]{1,0:T(1,128)S(1)}, u32[]{:S(2)}, u32[]{:S(2)}) collective-permute-start(f32[1,1664]{1,0:T(1,128)S(1)} %constant_dynamic-update-slice_fusion), channel_id=1, source_target_pairs={{0,4},{1,5},{2,6},{3,7},{4,0},{5,1},{6,2},{7,3},{8,12},{9,13},{10,... | collective-permute-start | bytes 19976 | tf_op jit(solution)/shard_map/ppermute | solution.py:55
  196.3 4.8 %collective-permute-start.52 = (f32[1,1664]{1,0:T(1,128)S(1)}, f32[1,1664]{1,0:T(1,128)S(1)}, u32[]{:S(2)}, u32[]{:S(2)}) collective-permute-start(f32[1,1664]{1,0:T(1,128)S(1)} %constant_dynamic-update-slice_fusion), channel_id=1, source_target_pairs={{0,6},{1,3},{2,0},{3,5},{4,2},{5,7},{6,4},{7,1},{8,14},{9,11},{10,... | collective-permute-start | bytes 19976 | tf_op jit(solution)/shard_map/ppermute | solution.py:55
  205.1 13.6 %all-to-all-start = ((f32[16,1,1024]{2,1,0:T(1,128)}), f32[16,1,1024]{2,1,0:T(1,128)S(1)}, u32[]{:S(2)}, u32[]{:S(2)}) async-start(f32[16,1,1024]{2,1,0:T(1,128)} %copy.19), calls=%async_computation | async-start | bytes 131072 | tf_op jit(solution)/shard_map/all_to_all | solution.py:483
  (66 other events, 607.6 us)

commit v3 on v2

--- a/solution.py
+++ b/solution.py
@@ -39,6 +39,8 @@
 ALONG_Z = moves(0, 0, 1, False)
 ALONG_Z2 = moves(0, 0, 2, False)
 ALONG_Z3 = moves(0, 0, 3, False)
+ROUND_X = [moves(k, 0, 0, False) for k in (1, 2, 3)]
+ROUND_Y = [moves(0, k, 0, False) for k in (1, 2, 3)]
 SWAP = moves(0, 0, 0, True)
 
 
@@ -252,8 +254,8 @@
     )(last, got, *before)
 
 
-def clip_rows(mine, yours, kept, got):
-    def kernel(mine_ref, yours_ref, kept_ref, got_ref, payload, clips, sums):
+def clip_rows(mine, yours, column_factor, kept, got):
+    def kernel(mine_ref, yours_ref, column_ref, kept_ref, got_ref, payload, clips, news):
         core = coordinates()[3]
         total = weights = None
         squares = None
@@ -275,56 +277,56 @@
             columns = pl.ds(at * HALF, HALF)
             here = core == at
             clips[:, columns] = jnp.where(here, both[0][0], both[1][0])
-            sums[:, columns] = jnp.where(here, both[0][1], both[1][1])
-        payload[:, :HALF] = lax.dot_general(
-            jnp.ones((16, HALF), jnp.float32),
+            sums = jnp.where(here, both[0][1], both[1][1])
+            news[:, columns] = second_decay * column_ref[:, columns] + (1.0 - second_decay) * (
+                sums / D + factor_eps
+            )
+        row_sums = lax.dot_general(
+            jnp.ones((8, HALF), jnp.float32),
             squares,
             (((1,), (1,)), ((), ())),
             precision=lax.Precision.HIGHEST,
             preferred_element_type=jnp.float32,
         )
-        payload[:, HALF : HALF + 128] = jnp.broadcast_to(total, (16, 128))
-        payload[:, HALF + 128 :] = jnp.broadcast_to(weights, (16, 128))
+        payload[:, :HALF] = row_sums[:1]
+        payload[:, HALF : HALF + 128] = jnp.broadcast_to(total, (1, 128))
+        payload[:, HALF + 128 :] = jnp.broadcast_to(weights, (1, 128))
 
     vmem = pl.BlockSpec(memory_space=pltpu.VMEM)
     columns = jax.ShapeDtypeStruct((1, 2 * HALF), jnp.float32)
     return pl.pallas_call(
         kernel,
-        out_shape=(jax.ShapeDtypeStruct((16, HALF + 256), jnp.float32), columns, columns),
-        in_specs=[vmem] * 4,
+        out_shape=(jax.ShapeDtypeStruct((1, HALF + 256), jnp.float32), columns, columns),
+        in_specs=[vmem] * 5,
         out_specs=(vmem,) * 3,
         compiler_params=pltpu.CompilerParams(vmem_limit_bytes=32 << 20),
         cost_estimate=CHEAP,
-    )(mine, yours, kept, got)
-
-
-def finish(gathered, row_total, clips, sums, row_factor, column_factor, kept, got):
+    )(mine, yours, column_factor, kept, got)
+
+
+def finish(summed, row_total, clips, new_column, row_factor, kept, got):
     step = 128
 
     def kernel(
-        gathered_ref, row_total_ref, clip_ref, sum_ref, row_ref, column_ref, kept_ref, got_ref,
-        update, new_row_ref, new_column_ref,
+        summed_ref, row_total_ref, clip_ref, column_ref, row_ref, kept_ref, got_ref,
+        update, new_row_ref,
     ):
         core = coordinates()[3]
         at = pl.ds(pl.multiple_of(pl.program_id(0) * step, step), step)
-        clipped_total = jnp.sum(gathered_ref[:, HALF : HALF + 1], axis=0, keepdims=True)
-        weight_total = jnp.sum(gathered_ref[:, HALF + 128 : HALF + 129], axis=0, keepdims=True)
+        clipped_total = summed_ref[:, HALF : HALF + 1]
+        weight_total = summed_ref[:, HALF + 128 : HALF + 129]
         row_mean = (
             second_decay * row_total_ref[:, :1]
             + (1.0 - second_decay) * (clipped_total / FF + D * factor_eps)
         ) / D
         weight_rms = jnp.sqrt(weight_total / (D * FF))
-        new_column = second_decay * column_ref[...] + (1.0 - second_decay) * (
-            sum_ref[...] / D + factor_eps
-        )
-        new_column_ref[...] = new_column
-        row_sums = jnp.sum(gathered_ref[:, at], axis=0, keepdims=True)
+        row_sums = summed_ref[:, at]
         new_row = second_decay * row_ref[:, at] + (1.0 - second_decay) * (
             row_sums / FF + factor_eps
         )
         new_row_ref[:, at] = new_row
         down = jnp.broadcast_to(lax.rsqrt(new_row), (step, step)).T[:, :1]
-        across = -weight_rms * clip_ref[...] * (jnp.sqrt(row_mean) * lax.rsqrt(new_column))
+        across = -weight_rms * clip_ref[...] * (jnp.sqrt(row_mean) * lax.rsqrt(column_ref[...]))
         first = jnp.where(core == 0, kept_ref[...], got_ref[...])
         second = jnp.where(core == 0, got_ref[...], kept_ref[...])
         update[:, :HALF] = first * across[:, :HALF] * down
@@ -338,16 +340,15 @@
         out_shape=(
             jax.ShapeDtypeStruct((HALF, 2 * HALF), jnp.float32),
             jax.ShapeDtypeStruct((1, HALF), jnp.float32),
-            jax.ShapeDtypeStruct((1, 2 * HALF), jnp.float32),
         ),
         in_specs=[
-            whole(16, HALF + 256), whole(1, 128), whole(1, 2 * HALF), whole(1, 2 * HALF),
-            whole(1, HALF), whole(1, 2 * HALF), rows(HALF), rows(HALF),
+            whole(1, HALF + 256), whole(1, 128), whole(1, 2 * HALF), whole(1, 2 * HALF),
+            whole(1, HALF), rows(HALF), rows(HALF),
         ],
-        out_specs=(rows(2 * HALF), whole(1, HALF), whole(1, 2 * HALF)),
+        out_specs=(rows(2 * HALF), whole(1, HALF)),
         compiler_params=pltpu.CompilerParams(vmem_limit_bytes=32 << 20),
         cost_estimate=CHEAP,
-    )(gathered, row_total, clips, sums, row_factor, column_factor, kept, got)
+    )(summed, row_total, clips, new_column, row_factor, kept, got)
 
 
 def per_device(inputs, preact, upstream, weight, row_factor, column_factor):
@@ -445,19 +446,19 @@
         (g, FEAT // 2 + chunk * size, (g + 1) * size, size) for g in range(4)
     ]
     placed = place_rows(own[3], after(own_got, far0[2]), [(0, 0, 0, FEAT // 2)], ())
-    placed = place_rows(near0[3], after(near0_got, far0[2]), near_pieces(0), placed)
     near1 = units(near_entries(x1, x1_swap), waits=(far0[2], placed[2], y1_swap))
     near1_got = hop(near1[0])
     x2, y2 = lax.optimization_barrier((x2, y2, near1[0]))[:2]
     x2_swap, y2_swap = send(x2, SWAP), send(y2, SWAP)
     far1_entries = far_entries(q_next, y1, y1_swap, x2, x2_swap, y2, y2_swap)
-    far1 = units(far1_entries[:2])
+    far0_3 = add_narrow(far0[2], far0_got)
+    far0_got = hop(far0_3)
+    far1 = units(far1_entries[:2], waits=(far0_3,))
     far1_got = hop(far1[0])
     near1_2 = add_narrow(near1[1], after(near1_got, far1[0]))
     near1_got = hop(near1_2)
-    far0_3 = add_narrow(far0[2], after(far0_got, far1[0]))
-    far0_got = hop(far0_3)
-    last1 = units(far1_entries[2:], waits=(far0_3, near1_2))
+    placed = place_rows(near0[3], after(near0_got, far1[0]), near_pieces(0), placed)
+    last1 = units(far1_entries[2:], waits=(near1_2, placed[2]))
     last1_got = hop(last1[0])
     near1_3 = add_narrow(near1[2], after(near1_got, last1[0]))
     far1_2 = add_narrow(far1[1], after(far1_got, last1[0]))
@@ -479,11 +480,13 @@
     for pairs in (ALONG_Z, ALONG_Z2, ALONG_Z3):
         column_stats = column_stats + send(local, pairs)
     yours_stats = send(column_stats, SWAP)
-    payload, clips, sums = clip_rows(column_stats, yours_stats, kept, got)
-    gathered = lax.all_to_all(payload[:, None, :], "gx", 0, 0, tiled=True)[:, 0]
-    update, new_row, new_column = finish(
-        gathered, column_stats[:, 2 * HALF :], clips, sums, row_factor[None, :],
-        column_factor[None, :], kept, got,
+    summed, clips, new_column = clip_rows(
+        column_stats, yours_stats, column_factor[None, :], kept, got
+    )
+    for along in (ROUND_X, ROUND_Y):
+        summed = sum((send(summed, pairs) for pairs in along), summed)
+    update, new_row = finish(
+        summed, column_stats[:, 2 * HALF :], clips, new_column, row_factor[None, :], kept, got
     )
     return (update, new_row[0], new_column[0])
 

time: 226 us -> 218 us (0.965)
  waiting for transfers between devices: 98.9 us -> 80 us
  starting transfers between devices: 42.8 us -> 47.6 us
  other arithmetic: 8.36 us -> 12.5 us
    ppermute x55 -> x61, waiting for transfers between devices: 91.3 us -> 80 us  [send(): return lax.ppermute(value, BOTH, pairs)]
    ppermute x55 -> x61, starting transfers between devices: 36.9 us -> 47.6 us  [send(): return lax.ppermute(value, BOTH, pairs)]
    all_to_all x1 -> x0, waiting for transfers between devices: 7.62 us -> none  [per_device(): gathered = lax.all_to_all(payload[:, None, :], 'gx', 0, 0, tiled=True)[:, 0]]
    all_to_all x1 -> x0, starting transfers between devices: 5.9 us -> none  [per_device(): gathered = lax.all_to_all(payload[:, None, :], 'gx', 0, 0, tiled=True)[:, 0]]
    convert_element_type x12, other arithmetic: 3 us -> 7.07 us  [add_narrow(): return (a.astype(jnp.float32) + b.astype(jnp.float32)).astype(jnp.bfloat16)]
    unnamed x118 -> x127, local copies, waits for them, and re-layouts: 14.5 us -> 13.9 us
  transfers between devices with their start and end apart: 56 -> 61, of which waited for: 29 -> 30; matrix products, arithmetic and copies ran while one was open for 5% -> 8% of each run, Pallas kernels for 20% -> 21%
where the time goes in v3:
time: 218 us; the launch traced here: 216 us
  waiting for transfers between devices  80 us (37%)
  Pallas kernels  54.5 us (25%)
  starting transfers between devices  47.6 us (22%)
  local copies, waits for them, and re-layouts  20.1 us (9%)
  other arithmetic  12.5 us (6%)
    ppermute x61, waiting for transfers between devices, send(): return lax.ppermute(value, BOTH, pairs)  80 us
    ppermute x61, starting transfers between devices, send(): return lax.ppermute(value, BOTH, pairs)  47.6 us
    pallas_call x7, Pallas kernels, unit_partials(): pl.pallas_call(kernel, out_shape=tuple((jax.ShapeDtypeStruct((rows, HALF)...  36.6 us
    unnamed x127, local copies, waits for them, and re-layouts  13.9 us
    convert_element_type x12, other arithmetic, add_narrow(): return (a.astype(jnp.float32) + b.astype(jnp.float32)).astype(jnp.bfloat16)  7.07 us
    squeeze x4, local copies, waits for them, and re-layouts, per_device(): x2, y2 = (send(x1[0], ALONG_X), send(y1[0], ALONG_Y))  5.41 us
    pallas_call x2, Pallas kernels, slope_half(): pl.pallas_call(kernel, out_shape=jax.ShapeDtypeStruct((TOK, HALF), jnp.bf...  5.05 us
  transfers between devices with their start and end apart: 61, of which 30 were waited for; matrix products, arithmetic and copies ran while one was open for 8% of the time, Pallas kernels for 21%

profile of v3, /device:TPU:0, one launch (start us, length us, event | category | flops | bytes accessed | tf_op | source)
XLA Modules:
  0.0 216.3 jit_solution(7297719974852599933)
XLA Ops:
  0.6 2.3 %shard_map.85 = (bf16[192,1024]{1,0:T(8,128)(2,1)}, bf16[192,1024]{1,0:T(8,128)(2,1)}) custom-call(bf16[1024,384]{1,0:T(8,128)(2,1)} %ref.1), custom_call_target="tpu_custom_call" | custom-call | flops 1024 | bytes 1024 | tf_op jit(solution)/shard_map/pallas_call | solution.py:186
  3.4 1.7 collective-permute-start.3
  5.1 1.5 collective-permute-start.4
  6.6 1.9 copy-done.9
  8.5 1.9 copy-done.10
  10.4 2.5 %shard_map.86.own_ref = bf16[1024,768]{1,0:T(8,128)(2,1)S(1)} custom-call(bf16[1024,1536]{1,0:T(8,128)(2,1)S(1)} %copy-done.9, bf16[1024,1536]{1,0:T(8,128)(2,1)S(1)} %copy-done.10, bf16[192,1024]{1,0:T(8,128)(2,1)S(1)} %collective-permute-done.refs_0_.refs_4_.refs_1_, bf16[192,1024]{1,0:T(8,128)(2,1)S(1)} %collective-permute-done.1.refs_1_.refs_4_), custom_call_target="tpu_custom_call" | custom-call | flops 1024 | bytes 1024 | tf_op jit(solution)/shard_map/pallas_call | solution.py:89
  12.9 2.5 %shard_map.87 = bf16[1024,768]{1,0:T(8,128)(2,1)S(1)} custom-call(bf16[1024,1536]{1,0:T(8,128)(2,1)S(1)} %copy-done.9, bf16[1024,1536]{1,0:T(8,128)(2,1)S(1)} %copy-done.10, bf16[192,1024]{1,0:T(8,128)(2,1)S(1)} %collective-permute-done.refs_0_.refs_4_.refs_1_, bf16[192,1024]{1,0:T(8,128)(2,1)S(1)} %collective-permute-done.1.refs_1_.refs_4_), custom_call_target="tpu_custom_call" | custom-call | flops 1024 | bytes 1024 | tf_op jit(solution)/shard_map/pallas_call | solution.py:89
  15.5 2.2 %collective-permute-start.7 = (bf16[192,1024]{1,0:T(8,128)(2,1)S(1)}, bf16[192,1024]{1,0:T(8,128)(2,1)S(1)}, u32[]{:S(2)}, u32[]{:S(2)}) collective-permute-start(bf16[192,1024]{1,0:T(8,128)(2,1)S(1)} %collective-permute-done.3.refs_1_.refs_2_), channel_id=1, source_target_pairs={{0,1},{1,0},{2,3},{3,2},{4,5},{5,4},{6,7},{7,6},{8,9},{9,8},{10,11... | collective-permute-start | bytes 1179656 | tf_op jit(solution)/shard_map/ppermute | solution.py:57
  21.7 5.1 %collective-permute-done.5.refs_5_.refs_3_ = bf16[192,1024]{1,0:T(8,128)(2,1)S(1)} collective-permute-done((bf16[192,1024]{1,0:T(8,128)(2,1)S(1)}, bf16[192,1024]{1,0:T(8,128)(2,1)S(1)}, u32[]{:S(2)}, u32[]{:S(2)}) %collective-permute-start.5) | collective-permute-done | bytes 393248 | tf_op jit(solution)/shard_map/ppermute | solution.py:57
  27.4 3.6 %collective-permute-done.10.refs_3_.refs_6_ = bf16[192,1024]{1,0:T(8,128)(2,1)S(1)} collective-permute-done((bf16[192,1024]{1,0:T(8,128)(2,1)S(1)}, bf16[192,1024]{1,0:T(8,128)(2,1)S(1)}, u32[]{:S(2)}, u32[]{:S(2)}) %collective-permute-start.10) | collective-permute-done | bytes 393248 | tf_op jit(solution)/shard_map/ppermute | solution.py:57
  37.1 4.1 %shard_map.92 = (bf16[192,768]{1,0:T(8,128)(2,1)}, bf16[192,768]{1,0:T(8,128)(2,1)S(1)}, bf16[192,768]{1,0:T(8,128)(2,1)S(1)}, f32[192,768]{1,0:T(8,128)S(1)}) custom-call(bf16[1024,768]{1,0:T(8,128)(2,1)S(1)} %shard_map.86.own_ref, bf16[1024,768]{1,0:T(8,128)(2,1)S(1)} %collective-permute-done.2.other_ref, bf16[192,1024]{1,0:T(8,128)(2,1)S(1)} %copy-done.17, ...), custom_call_target="tpu_custom_call" | custom-call | flops 1024 | bytes 1024 | tf_op jit(solution)/shard_map/pallas_call | solution.py:151
  43.5 1.9 collective-permute-start.17
  46.1 2.9 %multiply_reduce_fusion = f32[1536]{0:T(1024)S(1)} fusion(f32[768,1536]{1,0:T(8,128)} %param.9), kind=kLoop, calls=%fused_computation | loop fusion | flops 2357760 | bytes 4724736 | tf_op jit(solution)/shard_map/reduce_sum | solution.py:409
  48.9 3.6 %collective-permute-done.17 = bf16[192,768]{1,0:T(8,128)(2,1)} collective-permute-done((bf16[192,768]{1,0:T(8,128)(2,1)}, bf16[192,768]{1,0:T(8,128)(2,1)}, u32[]{:S(2)}, u32[]{:S(2)}) %collective-permute-start.17) | collective-permute-done | bytes 294944 | tf_op jit(solution)/shard_map/ppermute | solution.py:57
  54.5 3.8 %collective-permute-start.19 = (f32[896]{0:T(1024)S(1)}, f32[896]{0:T(1024)S(1)}, u32[]{:S(2)}, u32[]{:S(2)}) collective-permute-start(f32[896]{0:T(1024)S(1)} %concatenate.10), channel_id=1, source_target_pairs={{0,1},{1,0},{2,3},{3,2},{4,5},{5,4},{6,7},{7,6},{8,9},{9,8},{10,11... | collective-permute-start | bytes 10760 | tf_op jit(solution)/shard_map/ppermute | solution.py:57
  59.8 1.8 collective-permute-done.18
  69.6 4.7 %shard_map.93 = (bf16[192,768]{1,0:T(8,128)(2,1)S(1)}, bf16[192,768]{1,0:T(8,128)(2,1)S(1)}, bf16[192,768]{1,0:T(8,128)(2,1)S(1)}, f32[192,768]{1,0:T(8,128)S(1)}) custom-call(bf16[1024,768]{1,0:T(8,128)(2,1)S(1)} %shard_map.86.own_ref, bf16[1024,768]{1,0:T(8,128)(2,1)S(1)} %collective-permute-done.2.other_ref, ...), custom_call_target="tpu_custom_call" | custom-call | flops 1024 | bytes 1024 | tf_op jit(solution)/shard_map/pallas_call | solution.py:151
  74.4 3.5 %collective-permute-done.24.refs_0_ = bf16[4,96,1024]{2,1,0:T(8,128)(2,1)S(1)} collective-permute-done((bf16[4,96,1024]{2,1,0:T(8,128)(2,1)S(1)}, bf16[4,96,1024]{2,1,0:T(8,128)(2,1)S(1)}, u32[]{:S(2)}, u32[]{:S(2)}) %collective-permute-start.24) | collective-permute-done | bytes 786464 | tf_op jit(solution)/shard_map/ppermute | solution.py:57
  79.6 2.7 %collective-permute-done.28 = bf16[192,768]{1,0:T(8,128)(2,1)S(1)} collective-permute-done((bf16[192,768]{1,0:T(8,128)(2,1)S(1)}, bf16[192,768]{1,0:T(8,128)(2,1)S(1)}, u32[]{:S(2)}, u32[]{:S(2)}) %collective-permute-start.28) | collective-permute-done | bytes 294944 | tf_op jit(solution)/shard_map/ppermute | solution.py:57
  82.5 5.3 %shard_map.94 = (bf16[480,768]{1,0:T(8,128)(2,1)S(1)}, bf16[480,768]{1,0:T(8,128)(2,1)S(1)}) custom-call(bf16[1024,768]{1,0:T(8,128)(2,1)S(1)} %shard_map.86.own_ref, bf16[1024,768]{1,0:T(8,128)(2,1)S(1)} %collective-permute-done.2.other_ref, bf16[4,96,1024]{2,1,0:T(8,128)(2,1)S(1)} %collective-permute-done.24.refs_0_, ...), custom_call_target="tpu_custom_call" | custom-call | flops 1024 | bytes 1024 | tf_op jit(solution)/shard_map/pallas_call | solution.py:151
  87.9 2.5 %collective-permute-done.29 = bf16[192,768]{1,0:T(8,128)(2,1)S(1)} collective-permute-done((bf16[192,768]{1,0:T(8,128)(2,1)S(1)}, bf16[192,768]{1,0:T(8,128)(2,1)S(1)}, u32[]{:S(2)}, u32[]{:S(2)}) %collective-permute-start.29) | collective-permute-done | bytes 294944 | tf_op jit(solution)/shard_map/ppermute | solution.py:57
  91.2 3.7 %collective-permute-done.22.refs_0_ = bf16[2,4,96,1024]{3,2,1,0:T(8,128)(2,1)} collective-permute-done((bf16[2,4,96,1024]{3,2,1,0:T(8,128)(2,1)S(1)}, bf16[2,4,96,1024]{3,2,1,0:T(8,128)(2,1)}, u32[]{:S(2)}, u32[]{:S(2)}) %collective-permute-start.22) | collective-permute-done | bytes 1572896 | tf_op jit(solution)/shard_map/ppermute | solution.py:57
  96.5 2.1 slice_bitcast_fusion.1
  100.3 8.9 %collective-permute-done.34 = bf16[480,768]{1,0:T(8,128)(2,1)S(1)} collective-permute-done((bf16[480,768]{1,0:T(8,128)(2,1)S(1)}, bf16[480,768]{1,0:T(8,128)(2,1)S(1)}, u32[]{:S(2)}, u32[]{:S(2)}) %collective-permute-start.34) | collective-permute-done | bytes 737312 | tf_op jit(solution)/shard_map/ppermute | solution.py:57
  111.1 5.8 %shard_map.95 = (bf16[480,768]{1,0:T(8,128)(2,1)S(1)}, f32[480,768]{1,0:T(8,128)S(1)}) custom-call(bf16[1024,768]{1,0:T(8,128)(2,1)S(1)} %shard_map.86.own_ref, bf16[1024,768]{1,0:T(8,128)(2,1)S(1)} %collective-permute-done.2.other_ref, bf16[4,96,1024]{2,1,0:T(8,128)(2,1)S(1)} %collective-permute-done.24.refs_0_, ...), custom_call_target="tpu_custom_call" | custom-call | flops 1024 | bytes 1024 | tf_op jit(solution)/shard_map/pallas_call | solution.py:151
  117.5 1.4 copy-done.1
  118.9 1.4 copy-done.3
  120.3 5.3 %shard_map.97 = (bf16[192,768]{1,0:T(8,128)(2,1)}, bf16[192,768]{1,0:T(8,128)(2,1)S(1)}, bf16[192,768]{1,0:T(8,128)(2,1)S(1)}, f32[192,768]{1,0:T(8,128)S(1)}) custom-call(bf16[1024,768]{1,0:T(8,128)(2,1)S(1)} %copy-done.1, bf16[1024,768]{1,0:T(8,128)(2,1)S(1)} %copy-done.3, bf16[2,4,96,1024]{3,2,1,0:T(8,128)(2,1)} %collective-permute-done.22.refs_0_, ...), custom_call_target="tpu_custom_call" | custom-call | flops 1024 | bytes 1024 | tf_op jit(solution)/shard_map/pallas_call | solution.py:151
  127.6 1.5 collective-permute-start.37
  132.2 1.4 copy-done.7
  133.6 5.2 %shard_map.98 = (bf16[192,768]{1,0:T(8,128)(2,1)}, bf16[192,768]{1,0:T(8,128)(2,1)S(1)}, bf16[192,768]{1,0:T(8,128)(2,1)S(1)}, f32[192,768]{1,0:T(8,128)S(1)}) custom-call(bf16[1024,768]{1,0:T(8,128)(2,1)S(1)} %copy-done.1, bf16[1024,768]{1,0:T(8,128)(2,1)S(1)} %copy-done.4, bf16[4,96,1024]{2,1,0:T(8,128)(2,1)S(1)} %collective-permute-done.31.refs_0_, ...), custom_call_target="tpu_custom_call" | custom-call | flops 1024 | bytes 1024 | tf_op jit(solution)/shard_map/pallas_call | solution.py:151
  139.0 1.5 collective-permute-start.47
  140.5 1.5 collective-permute-start.43
  143.5 6.1 %shard_map.100 = (bf16[288,768]{1,0:T(8,128)(2,1)S(1)}, bf16[288,768]{1,0:T(8,128)(2,1)S(1)}, bf16[288,768]{1,0:T(8,128)(2,1)S(1)}, f32[288,768]{1,0:T(8,128)S(1)}) custom-call(bf16[1024,768]{1,0:T(8,128)(2,1)S(1)} %copy-done.1, bf16[1024,768]{1,0:T(8,128)(2,1)S(1)} %copy-done.4, bf16[2,4,96,1024]{3,2,1,0:T(8,128)(2,1)S(1)} %copy-done.7, ...), custom_call_target="tpu_custom_call" | custom-call | flops 1024 | bytes 1024 | tf_op jit(solution)/shard_map/pallas_call | solution.py:151
  150.6 2.6 %collective-permute-done.43 = bf16[192,768]{1,0:T(8,128)(2,1)} collective-permute-done((bf16[192,768]{1,0:T(8,128)(2,1)}, bf16[192,768]{1,0:T(8,128)(2,1)}, u32[]{:S(2)}, u32[]{:S(2)}) %collective-permute-start.43) | collective-permute-done | bytes 294944 | tf_op jit(solution)/shard_map/ppermute | solution.py:57
  155.0 4.2 %collective-permute-done.41 = bf16[288,768]{1,0:T(8,128)(2,1)S(1)} collective-permute-done((bf16[288,768]{1,0:T(8,128)(2,1)S(1)}, bf16[288,768]{1,0:T(8,128)(2,1)S(1)}, u32[]{:S(2)}, u32[]{:S(2)}) %collective-permute-start.41) | collective-permute-done | bytes 442400 | tf_op jit(solution)/shard_map/ppermute | solution.py:57
  160.9 1.5 collective-permute-start.46
  162.4 9.7 %collective-permute-done.48.got_ref = bf16[192,768]{1,0:T(8,128)(2,1)S(1)} collective-permute-done((bf16[192,768]{1,0:T(8,128)(2,1)S(1)}, bf16[192,768]{1,0:T(8,128)(2,1)S(1)}, u32[]{:S(2)}, u32[]{:S(2)}) %collective-permute-start.48) | collective-permute-done | bytes 294944 | tf_op jit(solution)/shard_map/ppermute | solution.py:57
  172.3 2.9 %collective-permute-done.46 = bf16[192,768]{1,0:T(8,128)(2,1)S(1)} collective-permute-done((bf16[192,768]{1,0:T(8,128)(2,1)S(1)}, bf16[192,768]{1,0:T(8,128)(2,1)S(1)}, u32[]{:S(2)}, u32[]{:S(2)}) %collective-permute-start.46) | collective-permute-done | bytes 294944 | tf_op jit(solution)/shard_map/ppermute | solution.py:57
  175.6 12.5 %collective-permute-done.49.got_ref = bf16[192,768]{1,0:T(8,128)(2,1)S(1)} collective-permute-done((bf16[192,768]{1,0:T(8,128)(2,1)S(1)}, bf16[192,768]{1,0:T(8,128)(2,1)S(1)}, u32[]{:S(2)}, u32[]{:S(2)}) %collective-permute-start.49) | collective-permute-done | bytes 294944 | tf_op jit(solution)/shard_map/ppermute | solution.py:57
  190.0 2.2 %collective-permute-start.52 = (f32[1,1664]{1,0:T(1,128)S(1)}, f32[1,1664]{1,0:T(1,128)S(1)}, u32[]{:S(2)}, u32[]{:S(2)}) collective-permute-start(f32[1,1664]{1,0:T(1,128)S(1)} %constant_dynamic-update-slice_fusion), channel_id=1, source_target_pairs={{0,6},{1,3},{2,0},{3,5},{4,2},{5,7},{6,4},{7,1},{8,14},{9,11},{10,... | collective-permute-start | bytes 19976 | tf_op jit(solution)/shard_map/ppermute | solution.py:57
  192.2 1.6 collective-permute-done.50
  196.0 2.0 shard_map.105
  198.2 2.9 %collective-permute-start.56 = (f32[1,1024]{1,0:T(1,128)S(1)}, f32[1,1024]{1,0:T(1,128)S(1)}, u32[]{:S(2)}, u32[]{:S(2)}) collective-permute-start(f32[1,1024]{1,0:T(1,128)S(1)} %get-tuple-element.156), channel_id=1, source_target_pairs={{0,16},{1,17},{2,18},{3,19},{4,20},{5,21},{6,22},{7,23},{8,24},{9,... | collective-permute-start | bytes 12296 | tf_op jit(solution)/shard_map/ppermute | solution.py:57
  203.3 1.4 collective-permute-done.57
  206.0 2.5 %collective-permute-start.60 = (f32[1,1024]{1,0:T(1,128)S(1)}, f32[1,1024]{1,0:T(1,128)S(1)}, u32[]{:S(2)}, u32[]{:S(2)}) collective-permute-start(f32[1,1024]{1,0:T(1,128)S(1)} %add_add_fusion.2), channel_id=1, source_target_pairs={{0,96},{1,33},{2,98},{3,35},{4,100},{5,37},{6,102},{7,39},{8,104},... | collective-permute-start | bytes 12296 | tf_op jit(solution)/shard_map/ppermute | solution.py:57
  210.5 1.7 copy-done.14
  212.1 3.5 %shard_map.106 = (f32[768,1536]{1,0:T(8,128)}, f32[1,768]{1,0:T(1,128)S(1)}) custom-call(f32[1,1024]{1,0:T(1,128)S(1)} %add_add_fusion.1.summed_ref, f32[1,128]{1,0:T(1,128)S(1)} %slice.20.row_total_ref, f32[1,1536]{1,0:T(1,128)S(1)} %get-tuple-element.157.clip_ref, f32[1,1536]{1,0:T(1,128)S(1)} %get-tuple-element.158.column_ref, ...), custom_call_target="tpu_custom_call" | custom-call | flops 1024 | bytes 1024 | tf_op jit(solution)/shard_map/pallas_call | solution.py:337
  (253 shorter events, 55.6 us)
Async XLA Ops:
  3.4 12.0 %collective-permute-start.3 = (bf16[192,1024]{1,0:T(8,128)(2,1)}, bf16[192,1024]{1,0:T(8,128)(2,1)S(1)}, u32[]{:S(2)}, u32[]{:S(2)}) collective-permute-start(bf16[192,1024]{1,0:T(8,128)(2,1)} %get-tuple-element.82.refs_0_), channel_id=1, source_target_pairs={{0,32},{1,97},{2,34},{3,99},{4,36},{5,101},{6,38},{7,103},{8,40},{... | collective-permute-start | bytes 1179656 | tf_op jit(solution)/shard_map/ppermute | solution.py:57
  5.1 10.4 %collective-permute-start.4 = (bf16[192,1024]{1,0:T(8,128)(2,1)}, bf16[192,1024]{1,0:T(8,128)(2,1)S(1)}, u32[]{:S(2)}, u32[]{:S(2)}) collective-permute-start(bf16[192,1024]{1,0:T(8,128)(2,1)} %get-tuple-element.83.refs_0_), channel_id=1, source_target_pairs={{0,8},{1,25},{2,10},{3,27},{4,12},{5,29},{6,14},{7,31},{8,16},{9,1... | collective-permute-start | bytes 1179656 | tf_op jit(solution)/shard_map/ppermute | solution.py:57
  15.5 4.9 %collective-permute-start.7 = (bf16[192,1024]{1,0:T(8,128)(2,1)S(1)}, bf16[192,1024]{1,0:T(8,128)(2,1)S(1)}, u32[]{:S(2)}, u32[]{:S(2)}) collective-permute-start(bf16[192,1024]{1,0:T(8,128)(2,1)S(1)} %collective-permute-done.3.refs_1_.refs_2_), channel_id=1, source_target_pairs={{0,1},{1,0},{2,3},{3,2},{4,5},{5,4},{6,7},{7,6},{8,9},{9,8},{10,11... | collective-permute-start | bytes 1179656 | tf_op jit(solution)/shard_map/ppermute | solution.py:57
  17.8 9.0 %collective-permute-start.5 = (bf16[192,1024]{1,0:T(8,128)(2,1)S(1)}, bf16[192,1024]{1,0:T(8,128)(2,1)S(1)}, u32[]{:S(2)}, u32[]{:S(2)}) collective-permute-start(bf16[192,1024]{1,0:T(8,128)(2,1)S(1)} %collective-permute-done.refs_0_.refs_4_.refs_1_), channel_id=1, source_target_pairs={{0,32},{1,97},{2,34},{3,99},{4,36},{5,101},{6,38},{7,103},{8,40},{... | collective-permute-start | bytes 1179656 | tf_op jit(solution)/shard_map/ppermute | solution.py:57
  17.8 9.0 %collective-permute-start.6 = (bf16[192,1024]{1,0:T(8,128)(2,1)S(1)}, bf16[192,1024]{1,0:T(8,128)(2,1)S(1)}, u32[]{:S(2)}, u32[]{:S(2)}) collective-permute-start(bf16[192,1024]{1,0:T(8,128)(2,1)S(1)} %collective-permute-done.1.refs_1_.refs_4_), channel_id=1, source_target_pairs={{0,8},{1,25},{2,10},{3,27},{4,12},{5,29},{6,14},{7,31},{8,16},{9,1... | collective-permute-start | bytes 1179656 | tf_op jit(solution)/shard_map/ppermute | solution.py:57
  19.2 17.9 %collective-permute-start.2 = (bf16[1024,768]{1,0:T(8,128)(2,1)S(1)}, bf16[1024,768]{1,0:T(8,128)(2,1)S(1)}, u32[]{:S(2)}, u32[]{:S(2)}) collective-permute-start(bf16[1024,768]{1,0:T(8,128)(2,1)S(1)} %shard_map.87), channel_id=1, source_target_pairs={{0,1},{1,0},{2,3},{3,2},{4,5},{5,4},{6,7},{7,6},{8,9},{9,8},{10,11... | collective-permute-start | bytes 4718600 | tf_op jit(solution)/shard_map/ppermute | solution.py:57
  20.3 10.7 %collective-permute-start.10 = (bf16[192,1024]{1,0:T(8,128)(2,1)S(1)}, bf16[192,1024]{1,0:T(8,128)(2,1)S(1)}, u32[]{:S(2)}, u32[]{:S(2)}) collective-permute-start(bf16[192,1024]{1,0:T(8,128)(2,1)S(1)} %collective-permute-done.3.refs_1_.refs_2_), channel_id=1, source_target_pairs={{0,32},{1,97},{2,34},{3,99},{4,36},{5,101},{6,38},{7,103},{8,40},{... | collective-permute-start | bytes 1179656 | tf_op jit(solution)/shard_map/ppermute | solution.py:57
  20.5 10.5 %collective-permute-start.11 = (bf16[192,1024]{1,0:T(8,128)(2,1)S(1)}, bf16[192,1024]{1,0:T(8,128)(2,1)S(1)}, u32[]{:S(2)}, u32[]{:S(2)}) collective-permute-start(bf16[192,1024]{1,0:T(8,128)(2,1)S(1)} %collective-permute-done.4.refs_1_), channel_id=1, source_target_pairs={{0,8},{1,25},{2,10},{3,27},{4,12},{5,29},{6,14},{7,31},{8,16},{9,1... | collective-permute-start | bytes 1179656 | tf_op jit(solution)/shard_map/ppermute | solution.py:57
  34.2 27.4 %collective-permute-start.16 = (bf16[2,4,96,1024]{3,2,1,0:T(8,128)(2,1)}, bf16[2,4,96,1024]{3,2,1,0:T(8,128)(2,1)}, u32[]{:S(2)}, u32[]{:S(2)}) collective-permute-start(bf16[2,4,96,1024]{3,2,1,0:T(8,128)(2,1)} %shard_map.91.refs_9_.refs_2_), channel_id=1, source_target_pairs={{0,32},{1,97},{2,34},{3,99},{4,36},{5,101},{6,38},{7,103},{8,40},{... | collective-permute-start | bytes 4718600 | tf_op jit(solution)/shard_map/ppermute | solution.py:57
  36.8 24.9 %collective-permute-start.15 = (bf16[2,4,96,1024]{3,2,1,0:T(8,128)(2,1)}, bf16[2,4,96,1024]{3,2,1,0:T(8,128)(2,1)}, u32[]{:S(2)}, u32[]{:S(2)}) collective-permute-start(bf16[2,4,96,1024]{3,2,1,0:T(8,128)(2,1)} %shard_map.90.refs_8_), channel_id=1, source_target_pairs={{0,8},{1,25},{2,10},{3,27},{4,12},{5,29},{6,14},{7,31},{8,16},{9,1... | collective-permute-start | bytes 4718600 | tf_op jit(solution)/shard_map/ppermute | solution.py:57
  43.5 9.1 %collective-permute-start.17 = (bf16[192,768]{1,0:T(8,128)(2,1)}, bf16[192,768]{1,0:T(8,128)(2,1)}, u32[]{:S(2)}, u32[]{:S(2)}) collective-permute-start(bf16[192,768]{1,0:T(8,128)(2,1)} %get-tuple-element.92), channel_id=1, source_target_pairs={{0,2},{1,7},{2,4},{3,1},{4,6},{5,3},{6,0},{7,5},{8,10},{9,15},{10,... | collective-permute-start | bytes 884744 | tf_op jit(solution)/shard_map/ppermute | solution.py:57
  53.6 8.0 %collective-permute-start.18 = (bf16[192,768]{1,0:T(8,128)(2,1)S(1)}, bf16[192,768]{1,0:T(8,128)(2,1)S(1)}, u32[]{:S(2)}, u32[]{:S(2)}) collective-permute-start(bf16[192,768]{1,0:T(8,128)(2,1)S(1)} %add_convert_fusion.11), channel_id=1, source_target_pairs={{0,2},{1,7},{2,4},{3,1},{4,6},{5,3},{6,0},{7,5},{8,10},{9,15},{10,... | collective-permute-start | bytes 884744 | tf_op jit(solution)/shard_map/ppermute | solution.py:57
  61.7 5.0 %collective-permute-start.20 = (bf16[2,4,96,1024]{3,2,1,0:T(8,128)(2,1)}, bf16[2,4,96,1024]{3,2,1,0:T(8,128)(2,1)S(1)}, u32[]{:S(2)}, u32[]{:S(2)}) collective-permute-start(bf16[2,4,96,1024]{3,2,1,0:T(8,128)(2,1)} %collective-permute-done.15.refs_0_), channel_id=1, source_target_pairs={{0,1},{1,0},{2,3},{3,2},{4,5},{5,4},{6,7},{7,6},{8,9},{9,8},{10,11... | collective-permute-start | bytes 4718600 | tf_op jit(solution)/shard_map/ppermute | solution.py:57
  61.8 5.9 %collective-permute-start.21 = (bf16[2,4,96,1024]{3,2,1,0:T(8,128)(2,1)}, bf16[2,4,96,1024]{3,2,1,0:T(8,128)(2,1)S(1)}, u32[]{:S(2)}, u32[]{:S(2)}) collective-permute-start(bf16[2,4,96,1024]{3,2,1,0:T(8,128)(2,1)} %collective-permute-done.16.refs_3_), channel_id=1, source_target_pairs={{0,1},{1,0},{2,3},{3,2},{4,5},{5,4},{6,7},{7,6},{8,9},{9,8},{10,11... | collective-permute-start | bytes 4718600 | tf_op jit(solution)/shard_map/ppermute | solution.py:57
  64.7 13.3 %collective-permute-start.24 = (bf16[4,96,1024]{2,1,0:T(8,128)(2,1)S(1)}, bf16[4,96,1024]{2,1,0:T(8,128)(2,1)S(1)}, u32[]{:S(2)}, u32[]{:S(2)}) collective-permute-start(bf16[4,96,1024]{2,1,0:T(8,128)(2,1)S(1)} %slice_bitcast_fusion.3), channel_id=1, source_target_pairs={{0,8},{1,25},{2,10},{3,27},{4,12},{5,29},{6,14},{7,31},{8,16},{9,1... | collective-permute-start | bytes 2359304 | tf_op jit(solution)/shard_map/ppermute | solution.py:57
  65.9 13.2 %collective-permute-start.25 = (bf16[4,96,1024]{2,1,0:T(8,128)(2,1)S(1)}, bf16[4,96,1024]{2,1,0:T(8,128)(2,1)S(1)}, u32[]{:S(2)}, u32[]{:S(2)}) collective-permute-start(bf16[4,96,1024]{2,1,0:T(8,128)(2,1)S(1)} %slice_bitcast_fusion.2), channel_id=1, source_target_pairs={{0,32},{1,97},{2,34},{3,99},{4,36},{5,101},{6,38},{7,103},{8,40},{... | collective-permute-start | bytes 2359304 | tf_op jit(solution)/shard_map/ppermute | solution.py:57
  67.6 27.2 %collective-permute-start.22 = (bf16[2,4,96,1024]{3,2,1,0:T(8,128)(2,1)S(1)}, bf16[2,4,96,1024]{3,2,1,0:T(8,128)(2,1)}, u32[]{:S(2)}, u32[]{:S(2)}) collective-permute-start(bf16[2,4,96,1024]{3,2,1,0:T(8,128)(2,1)S(1)} %shard_map.88), channel_id=1, source_target_pairs={{0,8},{1,25},{2,10},{3,27},{4,12},{5,29},{6,14},{7,31},{8,16},{9,1... | collective-permute-start | bytes 4718600 | tf_op jit(solution)/shard_map/ppermute | solution.py:57
  68.8 27.1 %collective-permute-start.23 = (bf16[2,4,96,1024]{3,2,1,0:T(8,128)(2,1)S(1)}, bf16[2,4,96,1024]{3,2,1,0:T(8,128)(2,1)S(1)}, u32[]{:S(2)}, u32[]{:S(2)}) collective-permute-start(bf16[2,4,96,1024]{3,2,1,0:T(8,128)(2,1)S(1)} %shard_map.89.refs_2_.refs_0_), channel_id=1, source_target_pairs={{0,32},{1,97},{2,34},{3,99},{4,36},{5,101},{6,38},{7,103},{8,40},{... | collective-permute-start | bytes 4718600 | tf_op jit(solution)/shard_map/ppermute | solution.py:57
  74.3 8.0 %collective-permute-start.28 = (bf16[192,768]{1,0:T(8,128)(2,1)S(1)}, bf16[192,768]{1,0:T(8,128)(2,1)S(1)}, u32[]{:S(2)}, u32[]{:S(2)}) collective-permute-start(bf16[192,768]{1,0:T(8,128)(2,1)S(1)} %get-tuple-element.98), channel_id=1, source_target_pairs={{0,2},{1,7},{2,4},{3,1},{4,6},{5,3},{6,0},{7,5},{8,10},{9,15},{10,... | collective-permute-start | bytes 884744 | tf_op jit(solution)/shard_map/ppermute | solution.py:57
  82.4 8.0 %collective-permute-start.29 = (bf16[192,768]{1,0:T(8,128)(2,1)S(1)}, bf16[192,768]{1,0:T(8,128)(2,1)S(1)}, u32[]{:S(2)}, u32[]{:S(2)}) collective-permute-start(bf16[192,768]{1,0:T(8,128)(2,1)S(1)} %add_convert_fusion.9.refs_7_), channel_id=1, source_target_pairs={{0,2},{1,7},{2,4},{3,1},{4,6},{5,3},{6,0},{7,5},{8,10},{9,15},{10,... | collective-permute-start | bytes 884744 | tf_op jit(solution)/shard_map/ppermute | solution.py:57
  96.0 13.2 %collective-permute-start.33 = (bf16[2,4,96,1024]{3,2,1,0:T(8,128)(2,1)}, bf16[2,4,96,1024]{3,2,1,0:T(8,128)(2,1)S(1)}, u32[]{:S(2)}, u32[]{:S(2)}) collective-permute-start(bf16[2,4,96,1024]{3,2,1,0:T(8,128)(2,1)} %collective-permute-done.22.refs_0_), channel_id=1, source_target_pairs={{0,1},{1,0},{2,3},{3,2},{4,5},{5,4},{6,7},{7,6},{8,9},{9,8},{10,11... | collective-permute-start | bytes 4718600 | tf_op jit(solution)/shard_map/ppermute | solution.py:57
  96.0 13.2 %collective-permute-start.30 = (bf16[2,4,96,1024]{3,2,1,0:T(8,128)(2,1)S(1)}, bf16[2,4,96,1024]{3,2,1,0:T(8,128)(2,1)S(1)}, u32[]{:S(2)}, u32[]{:S(2)}) collective-permute-start(bf16[2,4,96,1024]{3,2,1,0:T(8,128)(2,1)S(1)} %collective-permute-done.23.refs_3_.refs_1_), channel_id=1, source_target_pairs={{0,1},{1,0},{2,3},{3,2},{4,5},{5,4},{6,7},{7,6},{8,9},{9,8},{10,11... | collective-permute-start | bytes 4718600 | tf_op jit(solution)/shard_map/ppermute | solution.py:57
  96.5 12.7 %collective-permute-start.34 = (bf16[480,768]{1,0:T(8,128)(2,1)S(1)}, bf16[480,768]{1,0:T(8,128)(2,1)S(1)}, u32[]{:S(2)}, u32[]{:S(2)}) collective-permute-start(bf16[480,768]{1,0:T(8,128)(2,1)S(1)} %get-tuple-element.102), channel_id=1, source_target_pairs={{0,2},{1,7},{2,4},{3,1},{4,6},{5,3},{6,0},{7,5},{8,10},{9,15},{10,... | collective-permute-start | bytes 2211848 | tf_op jit(solution)/shard_map/ppermute | solution.py:57
  99.5 26.7 %collective-permute-start.31 = (bf16[4,96,1024]{2,1,0:T(8,128)(2,1)}, bf16[4,96,1024]{2,1,0:T(8,128)(2,1)S(1)}, u32[]{:S(2)}, u32[]{:S(2)}) collective-permute-start(bf16[4,96,1024]{2,1,0:T(8,128)(2,1)} %slice_bitcast_fusion.1), channel_id=1, source_target_pairs={{0,8},{1,25},{2,10},{3,27},{4,12},{5,29},{6,14},{7,31},{8,16},{9,1... | collective-permute-start | bytes 2359304 | tf_op jit(solution)/shard_map/ppermute | solution.py:57
  100.2 26.0 %collective-permute-start.32 = (bf16[4,96,1024]{2,1,0:T(8,128)(2,1)}, bf16[4,96,1024]{2,1,0:T(8,128)(2,1)S(1)}, u32[]{:S(2)}, u32[]{:S(2)}) collective-permute-start(bf16[4,96,1024]{2,1,0:T(8,128)(2,1)} %slice_bitcast_fusion), channel_id=1, source_target_pairs={{0,32},{1,97},{2,34},{3,99},{4,36},{5,101},{6,38},{7,103},{8,40},{... | collective-permute-start | bytes 2359304 | tf_op jit(solution)/shard_map/ppermute | solution.py:57
  109.2 8.0 %collective-permute-start.35 = (bf16[192,768]{1,0:T(8,128)(2,1)S(1)}, bf16[192,768]{1,0:T(8,128)(2,1)S(1)}, u32[]{:S(2)}, u32[]{:S(2)}) collective-permute-start(bf16[192,768]{1,0:T(8,128)(2,1)S(1)} %add_convert_fusion.10), channel_id=1, source_target_pairs={{0,2},{1,7},{2,4},{3,1},{4,6},{5,3},{6,0},{7,5},{8,10},{9,15},{10,... | collective-permute-start | bytes 884744 | tf_op jit(solution)/shard_map/ppermute | solution.py:57
  110.5 19.5 %collective-permute-start.39 = (bf16[480,768]{1,0:T(8,128)(2,1)}, bf16[480,768]{1,0:T(8,128)(2,1)}, u32[]{:S(2)}, u32[]{:S(2)}) collective-permute-start(bf16[480,768]{1,0:T(8,128)(2,1)} %add_convert_fusion.1.refs_7_), channel_id=1, source_target_pairs={{0,2},{1,7},{2,4},{3,1},{4,6},{5,3},{6,0},{7,5},{8,10},{9,15},{10,... | collective-permute-start | bytes 2211848 | tf_op jit(solution)/shard_map/ppermute | solution.py:57
  126.3 5.9 %collective-permute-start.36 = (bf16[4,96,1024]{2,1,0:T(8,128)(2,1)S(1)}, bf16[4,96,1024]{2,1,0:T(8,128)(2,1)S(1)}, u32[]{:S(2)}, u32[]{:S(2)}) collective-permute-start(bf16[4,96,1024]{2,1,0:T(8,128)(2,1)S(1)} %collective-permute-done.32.refs_5_.refs_3_), channel_id=1, source_target_pairs={{0,1},{1,0},{2,3},{3,2},{4,5},{5,4},{6,7},{7,6},{8,9},{9,8},{10,11... | collective-permute-start | bytes 2359304 | tf_op jit(solution)/shard_map/ppermute | solution.py:57
  127.5 4.7 %collective-permute-start.38 = (bf16[4,96,1024]{2,1,0:T(8,128)(2,1)S(1)}, bf16[4,96,1024]{2,1,0:T(8,128)(2,1)S(1)}, u32[]{:S(2)}, u32[]{:S(2)}) collective-permute-start(bf16[4,96,1024]{2,1,0:T(8,128)(2,1)S(1)} %collective-permute-done.31.refs_0_), channel_id=1, source_target_pairs={{0,1},{1,0},{2,3},{3,2},{4,5},{5,4},{6,7},{7,6},{8,9},{9,8},{10,11... | collective-permute-start | bytes 2359304 | tf_op jit(solution)/shard_map/ppermute | solution.py:57
  127.6 11.3 %collective-permute-start.37 = (bf16[192,768]{1,0:T(8,128)(2,1)}, bf16[192,768]{1,0:T(8,128)(2,1)S(1)}, u32[]{:S(2)}, u32[]{:S(2)}) collective-permute-start(bf16[192,768]{1,0:T(8,128)(2,1)} %get-tuple-element.114), channel_id=1, source_target_pairs={{0,2},{1,7},{2,4},{3,1},{4,6},{5,3},{6,0},{7,5},{8,10},{9,15},{10,... | collective-permute-start | bytes 884744 | tf_op jit(solution)/shard_map/ppermute | solution.py:57
  129.1 12.9 %collective-permute-start.40 = (bf16[192,768]{1,0:T(8,128)(2,1)}, bf16[192,768]{1,0:T(8,128)(2,1)S(1)}, u32[]{:S(2)}, u32[]{:S(2)}) collective-permute-start(bf16[192,768]{1,0:T(8,128)(2,1)} %add_convert_fusion.8), channel_id=1, source_target_pairs={{0,2},{1,7},{2,4},{3,1},{4,6},{5,3},{6,0},{7,5},{8,10},{9,15},{10,... | collective-permute-start | bytes 884744 | tf_op jit(solution)/shard_map/ppermute | solution.py:57
  131.4 22.8 %collective-permute-start.42 = (bf16[480,768]{1,0:T(8,128)(2,1)S(1)}, bf16[480,768]{1,0:T(8,128)(2,1)S(1)}, u32[]{:S(2)}, u32[]{:S(2)}) collective-permute-start(bf16[480,768]{1,0:T(8,128)(2,1)S(1)} %add_convert_fusion.refs_7_), channel_id=1, source_target_pairs={{0,2},{1,7},{2,4},{3,1},{4,6},{5,3},{6,0},{7,5},{8,10},{9,15},{10,... | collective-permute-start | bytes 2211848 | tf_op jit(solution)/shard_map/ppermute | solution.py:57
  139.0 11.6 %collective-permute-start.47 = (bf16[192,768]{1,0:T(8,128)(2,1)S(1)}, bf16[192,768]{1,0:T(8,128)(2,1)}, u32[]{:S(2)}, u32[]{:S(2)}) collective-permute-start(bf16[192,768]{1,0:T(8,128)(2,1)S(1)} %add_convert_fusion.7.refs_5_), channel_id=1, source_target_pairs={{0,2},{1,7},{2,4},{3,1},{4,6},{5,3},{6,0},{7,5},{8,10},{9,15},{10,... | collective-permute-start | bytes 884744 | tf_op jit(solution)/shard_map/ppermute | solution.py:57
  140.5 12.7 %collective-permute-start.43 = (bf16[192,768]{1,0:T(8,128)(2,1)}, bf16[192,768]{1,0:T(8,128)(2,1)}, u32[]{:S(2)}, u32[]{:S(2)}) collective-permute-start(bf16[192,768]{1,0:T(8,128)(2,1)} %get-tuple-element.118), channel_id=1, source_target_pairs={{0,2},{1,7},{2,4},{3,1},{4,6},{5,3},{6,0},{7,5},{8,10},{9,15},{10,... | collective-permute-start | bytes 884744 | tf_op jit(solution)/shard_map/ppermute | solution.py:57
  149.6 9.6 %collective-permute-start.41 = (bf16[288,768]{1,0:T(8,128)(2,1)S(1)}, bf16[288,768]{1,0:T(8,128)(2,1)S(1)}, u32[]{:S(2)}, u32[]{:S(2)}) collective-permute-start(bf16[288,768]{1,0:T(8,128)(2,1)S(1)} %get-tuple-element.129), channel_id=1, source_target_pairs={{0,2},{1,7},{2,4},{3,1},{4,6},{5,3},{6,0},{7,5},{8,10},{9,15},{10,... | collective-permute-start | bytes 1327112 | tf_op jit(solution)/shard_map/ppermute | solution.py:57
  159.3 15.9 %collective-permute-start.44 = (bf16[288,768]{1,0:T(8,128)(2,1)S(1)}, bf16[288,768]{1,0:T(8,128)(2,1)S(1)}, u32[]{:S(2)}, u32[]{:S(2)}) collective-permute-start(bf16[288,768]{1,0:T(8,128)(2,1)S(1)} %add_convert_fusion.3), channel_id=1, source_target_pairs={{0,2},{1,7},{2,4},{3,1},{4,6},{5,3},{6,0},{7,5},{8,10},{9,15},{10,... | collective-permute-start | bytes 1327112 | tf_op jit(solution)/shard_map/ppermute | solution.py:57
  160.4 11.6 %collective-permute-start.48 = (bf16[192,768]{1,0:T(8,128)(2,1)S(1)}, bf16[192,768]{1,0:T(8,128)(2,1)S(1)}, u32[]{:S(2)}, u32[]{:S(2)}) collective-permute-start(bf16[192,768]{1,0:T(8,128)(2,1)S(1)} %add_convert_fusion.5), channel_id=1, source_target_pairs={{0,2},{1,7},{2,4},{3,1},{4,6},{5,3},{6,0},{7,5},{8,10},{9,15},{10,... | collective-permute-start | bytes 884744 | tf_op jit(solution)/shard_map/ppermute | solution.py:57
  160.9 14.3 %collective-permute-start.46 = (bf16[192,768]{1,0:T(8,128)(2,1)S(1)}, bf16[192,768]{1,0:T(8,128)(2,1)S(1)}, u32[]{:S(2)}, u32[]{:S(2)}) collective-permute-start(bf16[192,768]{1,0:T(8,128)(2,1)S(1)} %add_convert_fusion.6), channel_id=1, source_target_pairs={{0,2},{1,7},{2,4},{3,1},{4,6},{5,3},{6,0},{7,5},{8,10},{9,15},{10,... | collective-permute-start | bytes 884744 | tf_op jit(solution)/shard_map/ppermute | solution.py:57
  175.3 13.0 %collective-permute-start.45 = (bf16[288,768]{1,0:T(8,128)(2,1)S(1)}, bf16[288,768]{1,0:T(8,128)(2,1)S(1)}, u32[]{:S(2)}, u32[]{:S(2)}) collective-permute-start(bf16[288,768]{1,0:T(8,128)(2,1)S(1)} %add_convert_fusion.2), channel_id=1, source_target_pairs={{0,2},{1,7},{2,4},{3,1},{4,6},{5,3},{6,0},{7,5},{8,10},{9,15},{10,... | collective-permute-start | bytes 1327112 | tf_op jit(solution)/shard_map/ppermute | solution.py:57
  175.5 12.6 %collective-permute-start.49 = (bf16[192,768]{1,0:T(8,128)(2,1)S(1)}, bf16[192,768]{1,0:T(8,128)(2,1)S(1)}, u32[]{:S(2)}, u32[]{:S(2)}) collective-permute-start(bf16[192,768]{1,0:T(8,128)(2,1)S(1)} %add_convert_fusion.4), channel_id=1, source_target_pairs={{0,2},{1,7},{2,4},{3,1},{4,6},{5,3},{6,0},{7,5},{8,10},{9,15},{10,... | collective-permute-start | bytes 884744 | tf_op jit(solution)/shard_map/ppermute | solution.py:57
  188.8 7.2 %collective-permute-start.54 = (f32[768,768]{1,0:T(8,128)S(1)}, f32[768,768]{1,0:T(8,128)S(1)}, u32[]{:S(2)}, u32[]{:S(2)}) collective-permute-start(f32[768,768]{1,0:T(8,128)S(1)} %get-tuple-element.155), channel_id=1, source_target_pairs={{0,1},{1,0},{2,3},{3,2},{4,5},{5,4},{6,7},{7,6},{8,9},{9,8},{10,11... | collective-permute-start | bytes 7077896 | tf_op jit(solution)/shard_map/ppermute | solution.py:57
  188.9 4.9 %collective-permute-start.50 = (f32[1,1664]{1,0:T(1,128)S(1)}, f32[1,1664]{1,0:T(1,128)S(1)}, u32[]{:S(2)}, u32[]{:S(2)}) collective-permute-start(f32[1,1664]{1,0:T(1,128)S(1)} %constant_dynamic-update-slice_fusion), channel_id=1, source_target_pairs={{0,2},{1,7},{2,4},{3,1},{4,6},{5,3},{6,0},{7,5},{8,10},{9,15},{10,... | collective-permute-start | bytes 19976 | tf_op jit(solution)/shard_map/ppermute | solution.py:57
  189.0 5.2 %collective-permute-start.51 = (f32[1,1664]{1,0:T(1,128)S(1)}, f32[1,1664]{1,0:T(1,128)S(1)}, u32[]{:S(2)}, u32[]{:S(2)}) collective-permute-start(f32[1,1664]{1,0:T(1,128)S(1)} %constant_dynamic-update-slice_fusion), channel_id=1, source_target_pairs={{0,4},{1,5},{2,6},{3,7},{4,0},{5,1},{6,2},{7,3},{8,12},{9,13},{10,... | collective-permute-start | bytes 19976 | tf_op jit(solution)/shard_map/ppermute | solution.py:57
  190.0 4.8 %collective-permute-start.52 = (f32[1,1664]{1,0:T(1,128)S(1)}, f32[1,1664]{1,0:T(1,128)S(1)}, u32[]{:S(2)}, u32[]{:S(2)}) collective-permute-start(f32[1,1664]{1,0:T(1,128)S(1)} %constant_dynamic-update-slice_fusion), channel_id=1, source_target_pairs={{0,6},{1,3},{2,0},{3,5},{4,2},{5,7},{6,4},{7,1},{8,14},{9,11},{10,... | collective-permute-start | bytes 19976 | tf_op jit(solution)/shard_map/ppermute | solution.py:57
  198.1 4.8 %collective-permute-start.55 = (f32[1,1024]{1,0:T(1,128)S(1)}, f32[1,1024]{1,0:T(1,128)S(1)}, u32[]{:S(2)}, u32[]{:S(2)}) collective-permute-start(f32[1,1024]{1,0:T(1,128)S(1)} %get-tuple-element.156), channel_id=1, source_target_pairs={{0,8},{1,25},{2,10},{3,27},{4,12},{5,29},{6,14},{7,31},{8,16},{9,1... | collective-permute-start | bytes 12296 | tf_op jit(solution)/shard_map/ppermute | solution.py:57
  198.2 5.1 %collective-permute-start.56 = (f32[1,1024]{1,0:T(1,128)S(1)}, f32[1,1024]{1,0:T(1,128)S(1)}, u32[]{:S(2)}, u32[]{:S(2)}) collective-permute-start(f32[1,1024]{1,0:T(1,128)S(1)} %get-tuple-element.156), channel_id=1, source_target_pairs={{0,16},{1,17},{2,18},{3,19},{4,20},{5,21},{6,22},{7,23},{8,24},{9,... | collective-permute-start | bytes 12296 | tf_op jit(solution)/shard_map/ppermute | solution.py:57
  204.7 4.9 %collective-permute-start.58 = (f32[1,1024]{1,0:T(1,128)S(1)}, f32[1,1024]{1,0:T(1,128)S(1)}, u32[]{:S(2)}, u32[]{:S(2)}) collective-permute-start(f32[1,1024]{1,0:T(1,128)S(1)} %add_add_fusion.2), channel_id=1, source_target_pairs={{0,32},{1,97},{2,34},{3,99},{4,36},{5,101},{6,38},{7,103},{8,40},{... | collective-permute-start | bytes 12296 | tf_op jit(solution)/shard_map/ppermute | solution.py:57
  204.8 5.2 %collective-permute-start.59 = (f32[1,1024]{1,0:T(1,128)S(1)}, f32[1,1024]{1,0:T(1,128)S(1)}, u32[]{:S(2)}, u32[]{:S(2)}) collective-permute-start(f32[1,1024]{1,0:T(1,128)S(1)} %add_add_fusion.2), channel_id=1, source_target_pairs={{0,64},{1,65},{2,66},{3,67},{4,68},{5,69},{6,70},{7,71},{8,72},{9,... | collective-permute-start | bytes 12296 | tf_op jit(solution)/shard_map/ppermute | solution.py:57
  (76 other events, 665.7 us)

commit v4 on v3

--- a/solution.py
+++ b/solution.py
@@ -363,7 +363,7 @@
     slope_yours = slope_half(preact, upstream, True, (p_swap, q_swap))
     slope_other = send(slope_yours, SWAP)
     slope_mine = slope_half(preact, upstream, False, (p_swap, q_swap))
-    ya, xa = lax.optimization_barrier((ya, xa, slope_yours, slope_mine))[:2]
+    ya, xa, yb, xb = lax.optimization_barrier((ya, xa, yb, xb, slope_yours, slope_mine))[:4]
     y2, x2 = send(ya, ALONG_Y), send(xa, ALONG_X)
     ya_swap, xa_swap = send(ya, SWAP), send(xa, SWAP)
     yb, xb = lax.optimization_barrier((yb, xb, ya_swap, xa_swap))[:2]
@@ -438,27 +438,27 @@
     x1_swap, y1_swap = send(x1, SWAP), send(y1, SWAP)
     near0_got = hop(after(near0_3, x1_swap, y1_swap))
     own_got = hop(after(own_3, x1_swap, y1_swap))
-    far0_2 = add_narrow(far0[1], after(far0_got, x1_swap))
-    far0_got = hop(far0_2)
-    far0 += units(far0_entries, 2, 4, waits=(far0_2,))
+    far0 += units(far0_entries, 2, 4)
     near_pieces = lambda chunk: [(1, chunk * size, 0, size), (2, chunk * size, size, size)]
     far_pieces = lambda chunk: [(3, chunk * size, 0, size)] + [
         (g, FEAT // 2 + chunk * size, (g + 1) * size, size) for g in range(4)
     ]
-    placed = place_rows(own[3], after(own_got, far0[2]), [(0, 0, 0, FEAT // 2)], ())
-    near1 = units(near_entries(x1, x1_swap), waits=(far0[2], placed[2], y1_swap))
+    near1 = units(near_entries(x1, x1_swap), waits=(far0[2], y1_swap))
     near1_got = hop(near1[0])
-    x2, y2 = lax.optimization_barrier((x2, y2, near1[0]))[:2]
+    far0_2 = add_narrow(far0[1], after(far0_got, near1[0]))
+    far0_got = hop(far0_2)
+    placed = place_rows(own[3], after(own_got, near1[0]), [(0, 0, 0, FEAT // 2)], ())
+    placed = place_rows(near0[3], after(near0_got, near1[0]), near_pieces(0), placed)
+    x2, y2 = lax.optimization_barrier((x2, y2, near1[0], far0_2, placed[2]))[:2]
     x2_swap, y2_swap = send(x2, SWAP), send(y2, SWAP)
     far1_entries = far_entries(q_next, y1, y1_swap, x2, x2_swap, y2, y2_swap)
-    far0_3 = add_narrow(far0[2], far0_got)
-    far0_got = hop(far0_3)
-    far1 = units(far1_entries[:2], waits=(far0_3,))
+    far1 = units(far1_entries[:2])
     far1_got = hop(far1[0])
     near1_2 = add_narrow(near1[1], after(near1_got, far1[0]))
     near1_got = hop(near1_2)
-    placed = place_rows(near0[3], after(near0_got, far1[0]), near_pieces(0), placed)
-    last1 = units(far1_entries[2:], waits=(near1_2, placed[2]))
+    far0_3 = add_narrow(far0[2], after(far0_got, far1[0]))
+    far0_got = hop(far0_3)
+    last1 = units(far1_entries[2:], waits=(near1_2, far0_3))
     last1_got = hop(last1[0])
     near1_3 = add_narrow(near1[2], after(near1_got, last1[0]))
     far1_2 = add_narrow(far1[1], after(far1_got, last1[0]))

time: 218 us -> 216 us (level)
  waiting for transfers between devices: 80 us -> 86.5 us
  local copies, waits for them, and re-layouts: 20.1 us -> 14.1 us
  other arithmetic: 12.5 us -> 8.72 us
  starting transfers between devices: 47.6 us -> 50.4 us
    ppermute x61, waiting for transfers between devices: 80 us -> 86.5 us  [send(): return lax.ppermute(value, BOTH, pairs)]
    unnamed x127 -> x105, local copies, waits for them, and re-layouts: 13.9 us -> 7.93 us
    convert_element_type x12, other arithmetic: 7.07 us -> 3.34 us  [add_narrow(): return (a.astype(jnp.float32) + b.astype(jnp.float32)).astype(jnp.bfloat16)]
    ppermute x61, starting transfers between devices: 47.6 us -> 50.4 us  [send(): return lax.ppermute(value, BOTH, pairs)]
  transfers between devices with their start and end apart: 61 -> 61, of which waited for: 30 -> 31; matrix products, arithmetic and copies ran while one was open for 8% -> 7% of each run, Pallas kernels for 21% -> 21%
where the time goes in v4:
time: 216 us; the launch traced here: 215 us
  waiting for transfers between devices  86.5 us (40%)
  Pallas kernels  53.5 us (25%)
  starting transfers between devices  50.4 us (23%)
  local copies, waits for them, and re-layouts  14.1 us (7%)
  other arithmetic  8.72 us (4%)
    ppermute x61, waiting for transfers between devices, send(): return lax.ppermute(value, BOTH, pairs)  86.5 us
    ppermute x61, starting transfers between devices, send(): return lax.ppermute(value, BOTH, pairs)  50.4 us
    pallas_call x7, Pallas kernels, unit_partials(): pl.pallas_call(kernel, out_shape=tuple((jax.ShapeDtypeStruct((rows, HALF)...  35.5 us
    unnamed x105, local copies, waits for them, and re-layouts  7.93 us
    squeeze x4, local copies, waits for them, and re-layouts, per_device(): x2, y2 = (send(x1[0], ALONG_X), send(y1[0], ALONG_Y))  5.45 us
    pallas_call x2, Pallas kernels, slope_half(): pl.pallas_call(kernel, out_shape=jax.ShapeDtypeStruct((TOK, HALF), jnp.bf...  5.05 us
  transfers between devices with their start and end apart: 61, of which 31 were waited for; matrix products, arithmetic and copies ran while one was open for 7% of the time, Pallas kernels for 21%

profile of v4, /device:TPU:0, one launch (start us, length us, event | category | flops | bytes accessed | tf_op | source)
XLA Modules:
  0.0 214.9 jit_solution(9558283866239689853)
XLA Ops:
  0.6 2.3 %shard_map.85 = (bf16[192,1024]{1,0:T(8,128)(2,1)}, bf16[192,1024]{1,0:T(8,128)(2,1)}) custom-call(bf16[1024,384]{1,0:T(8,128)(2,1)} %ref.1), custom_call_target="tpu_custom_call" | custom-call | flops 1024 | bytes 1024 | tf_op jit(solution)/shard_map/pallas_call | solution.py:186
  3.4 1.7 collective-permute-start.3
  6.6 1.6 collective-permute-start.5
  8.2 1.5 collective-permute-start.6
  9.7 1.9 copy-done.6
  11.6 1.9 copy-done.7
  13.4 2.5 %shard_map.86.own_ref = bf16[1024,768]{1,0:T(8,128)(2,1)S(1)} custom-call(bf16[1024,1536]{1,0:T(8,128)(2,1)S(1)} %copy-done.6, bf16[1024,1536]{1,0:T(8,128)(2,1)S(1)} %copy-done.7, bf16[192,1024]{1,0:T(8,128)(2,1)S(1)} %collective-permute-done.refs_0_.refs_4_.refs_1_, bf16[192,1024]{1,0:T(8,128)(2,1)S(1)} %collective-permute-done.1.refs_1_.refs_4_), custom_call_target="tpu_custom_call" | custom-call | flops 1024 | bytes 1024 | tf_op jit(solution)/shard_map/pallas_call | solution.py:89
  16.0 2.5 %shard_map.87 = bf16[1024,768]{1,0:T(8,128)(2,1)S(1)} custom-call(bf16[1024,1536]{1,0:T(8,128)(2,1)S(1)} %copy-done.6, bf16[1024,1536]{1,0:T(8,128)(2,1)S(1)} %copy-done.7, bf16[192,1024]{1,0:T(8,128)(2,1)S(1)} %collective-permute-done.refs_0_.refs_4_.refs_1_, bf16[192,1024]{1,0:T(8,128)(2,1)S(1)} %collective-permute-done.1.refs_1_.refs_4_), custom_call_target="tpu_custom_call" | custom-call | flops 1024 | bytes 1024 | tf_op jit(solution)/shard_map/pallas_call | solution.py:89
  22.8 6.1 %collective-permute-done.10.refs_3_.refs_6_ = bf16[192,1024]{1,0:T(8,128)(2,1)S(1)} collective-permute-done((bf16[192,1024]{1,0:T(8,128)(2,1)S(1)}, bf16[192,1024]{1,0:T(8,128)(2,1)S(1)}, u32[]{:S(2)}, u32[]{:S(2)}) %collective-permute-start.10) | collective-permute-done | bytes 393248 | tf_op jit(solution)/shard_map/ppermute | solution.py:57
  35.6 4.1 %shard_map.92 = (bf16[192,768]{1,0:T(8,128)(2,1)}, bf16[192,768]{1,0:T(8,128)(2,1)S(1)}, bf16[192,768]{1,0:T(8,128)(2,1)S(1)}, f32[192,768]{1,0:T(8,128)S(1)}) custom-call(bf16[1024,768]{1,0:T(8,128)(2,1)S(1)} %shard_map.86.own_ref, bf16[1024,768]{1,0:T(8,128)(2,1)S(1)} %collective-permute-done.2.other_ref, bf16[192,1024]{1,0:T(8,128)(2,1)S(1)} %copy-done.12, ...), custom_call_target="tpu_custom_call" | custom-call | flops 1024 | bytes 1024 | tf_op jit(solution)/shard_map/pallas_call | solution.py:151
  42.0 1.9 collective-permute-start.17
  44.6 2.9 %multiply_reduce_fusion = f32[1536]{0:T(1024)S(1)} fusion(f32[768,1536]{1,0:T(8,128)} %param.9), kind=kLoop, calls=%fused_computation | loop fusion | flops 2357760 | bytes 4724736 | tf_op jit(solution)/shard_map/reduce_sum | solution.py:409
  47.5 3.6 %collective-permute-done.17 = bf16[192,768]{1,0:T(8,128)(2,1)} collective-permute-done((bf16[192,768]{1,0:T(8,128)(2,1)}, bf16[192,768]{1,0:T(8,128)(2,1)}, u32[]{:S(2)}, u32[]{:S(2)}) %collective-permute-start.17) | collective-permute-done | bytes 294944 | tf_op jit(solution)/shard_map/ppermute | solution.py:57
  53.0 3.6 %collective-permute-start.19 = (f32[896]{0:T(1024)S(1)}, f32[896]{0:T(1024)S(1)}, u32[]{:S(2)}, u32[]{:S(2)}) collective-permute-start(f32[896]{0:T(1024)S(1)} %concatenate.10), channel_id=1, source_target_pairs={{0,1},{1,0},{2,3},{3,2},{4,5},{5,4},{6,7},{7,6},{8,9},{9,8},{10,11... | collective-permute-start | bytes 10760 | tf_op jit(solution)/shard_map/ppermute | solution.py:57
  58.1 2.0 collective-permute-done.18
  64.2 1.9 collective-permute-done.21.refs_2_.refs_4_
  68.1 4.7 %shard_map.93 = (bf16[192,768]{1,0:T(8,128)(2,1)S(1)}, bf16[192,768]{1,0:T(8,128)(2,1)S(1)}, bf16[192,768]{1,0:T(8,128)(2,1)S(1)}, f32[192,768]{1,0:T(8,128)S(1)}) custom-call(bf16[1024,768]{1,0:T(8,128)(2,1)S(1)} %shard_map.86.own_ref, bf16[1024,768]{1,0:T(8,128)(2,1)S(1)} %collective-permute-done.2.other_ref, ...), custom_call_target="tpu_custom_call" | custom-call | flops 1024 | bytes 1024 | tf_op jit(solution)/shard_map/pallas_call | solution.py:151
  72.9 3.5 %collective-permute-done.24.refs_0_ = bf16[4,96,1024]{2,1,0:T(8,128)(2,1)S(1)} collective-permute-done((bf16[4,96,1024]{2,1,0:T(8,128)(2,1)S(1)}, bf16[4,96,1024]{2,1,0:T(8,128)(2,1)S(1)}, u32[]{:S(2)}, u32[]{:S(2)}) %collective-permute-start.24) | collective-permute-done | bytes 786464 | tf_op jit(solution)/shard_map/ppermute | solution.py:57
  77.5 3.3 %collective-permute-done.28 = bf16[192,768]{1,0:T(8,128)(2,1)S(1)} collective-permute-done((bf16[192,768]{1,0:T(8,128)(2,1)S(1)}, bf16[192,768]{1,0:T(8,128)(2,1)S(1)}, u32[]{:S(2)}, u32[]{:S(2)}) %collective-permute-start.28) | collective-permute-done | bytes 294944 | tf_op jit(solution)/shard_map/ppermute | solution.py:57
  81.0 6.1 %shard_map.94 = (bf16[480,768]{1,0:T(8,128)(2,1)}, bf16[480,768]{1,0:T(8,128)(2,1)S(1)}) custom-call(bf16[1024,768]{1,0:T(8,128)(2,1)S(1)} %shard_map.86.own_ref, bf16[1024,768]{1,0:T(8,128)(2,1)S(1)} %collective-permute-done.2.other_ref, bf16[4,96,1024]{2,1,0:T(8,128)(2,1)S(1)} %collective-permute-done.24.refs_0_, ...), custom_call_target="tpu_custom_call" | custom-call | flops 1024 | bytes 1024 | tf_op jit(solution)/shard_map/pallas_call | solution.py:151
  87.1 1.8 collective-permute-done.29
  89.0 4.3 %collective-permute-done.22.refs_0_ = bf16[2,4,96,1024]{3,2,1,0:T(8,128)(2,1)S(1)} collective-permute-done((bf16[2,4,96,1024]{3,2,1,0:T(8,128)(2,1)S(1)}, bf16[2,4,96,1024]{3,2,1,0:T(8,128)(2,1)S(1)}, u32[]{:S(2)}, u32[]{:S(2)}) %collective-permute-start.22) | collective-permute-done | bytes 1572896 | tf_op jit(solution)/shard_map/ppermute | solution.py:57
  95.5 2.1 slice_bitcast_fusion
  99.6 2.6 %collective-permute-start.35 = (bf16[192,768]{1,0:T(8,128)(2,1)S(1)}, bf16[192,768]{1,0:T(8,128)(2,1)S(1)}, u32[]{:S(2)}, u32[]{:S(2)}) collective-permute-start(bf16[192,768]{1,0:T(8,128)(2,1)S(1)} %add_convert_fusion.8), channel_id=1, source_target_pairs={{0,2},{1,7},{2,4},{3,1},{4,6},{5,3},{6,0},{7,5},{8,10},{9,15},{10,... | collective-permute-start | bytes 884744 | tf_op jit(solution)/shard_map/ppermute | solution.py:57
  102.2 5.8 %shard_map.95 = (bf16[480,768]{1,0:T(8,128)(2,1)S(1)}, f32[480,768]{1,0:T(8,128)S(1)}) custom-call(bf16[1024,768]{1,0:T(8,128)(2,1)S(1)} %shard_map.86.own_ref, bf16[1024,768]{1,0:T(8,128)(2,1)S(1)} %collective-permute-done.2.other_ref, bf16[4,96,1024]{2,1,0:T(8,128)(2,1)S(1)} %collective-permute-done.24.refs_0_, ...), custom_call_target="tpu_custom_call" | custom-call | flops 1024 | bytes 1024 | tf_op jit(solution)/shard_map/pallas_call | solution.py:151
  108.1 3.7 %shard_map.96 = (bf16[192,768]{1,0:T(8,128)(2,1)S(1)}, bf16[192,768]{1,0:T(8,128)(2,1)S(1)}, bf16[192,768]{1,0:T(8,128)(2,1)S(1)}, f32[192,768]{1,0:T(8,128)S(1)}) custom-call(bf16[1024,768]{1,0:T(8,128)(2,1)S(1)} %shard_map.86.own_ref, bf16[1024,768]{1,0:T(8,128)(2,1)S(1)} %collective-permute-done.2.other_ref, ...), custom_call_target="tpu_custom_call" | custom-call | flops 1024 | bytes 1024 | tf_op jit(solution)/shard_map/pallas_call | solution.py:151
  114.6 1.7 collective-permute-start.40
  117.7 4.7 %shard_map.99 = (bf16[192,768]{1,0:T(8,128)(2,1)S(1)}, bf16[192,768]{1,0:T(8,128)(2,1)S(1)}, bf16[192,768]{1,0:T(8,128)(2,1)S(1)}, f32[192,768]{1,0:T(8,128)S(1)}) custom-call(bf16[1024,768]{1,0:T(8,128)(2,1)S(1)} %copy-done.1, bf16[1024,768]{1,0:T(8,128)(2,1)S(1)} %copy-done.3, bf16[4,96,1024]{2,1,0:T(8,128)(2,1)} %collective-permute-done.31.refs_0_, ...), custom_call_target="tpu_custom_call" | custom-call | flops 1024 | bytes 1024 | tf_op jit(solution)/shard_map/pallas_call | solution.py:151
  122.5 4.8 %collective-permute-done.40 = bf16[480,768]{1,0:T(8,128)(2,1)S(1)} collective-permute-done((bf16[480,768]{1,0:T(8,128)(2,1)S(1)}, bf16[480,768]{1,0:T(8,128)(2,1)S(1)}, u32[]{:S(2)}, u32[]{:S(2)}) %collective-permute-start.40) | collective-permute-done | bytes 737312 | tf_op jit(solution)/shard_map/ppermute | solution.py:57
  127.4 3.0 %collective-permute-done.38 = bf16[192,768]{1,0:T(8,128)(2,1)S(1)} collective-permute-done((bf16[192,768]{1,0:T(8,128)(2,1)S(1)}, bf16[192,768]{1,0:T(8,128)(2,1)S(1)}, u32[]{:S(2)}, u32[]{:S(2)}) %collective-permute-start.38) | collective-permute-done | bytes 294944 | tf_op jit(solution)/shard_map/ppermute | solution.py:57
  132.6 6.3 %shard_map.100 = (bf16[288,768]{1,0:T(8,128)(2,1)S(1)}, bf16[288,768]{1,0:T(8,128)(2,1)S(1)}, bf16[288,768]{1,0:T(8,128)(2,1)S(1)}, f32[288,768]{1,0:T(8,128)S(1)}) custom-call(bf16[1024,768]{1,0:T(8,128)(2,1)S(1)} %copy-done.1, bf16[1024,768]{1,0:T(8,128)(2,1)S(1)} %copy-done.3, bf16[2,4,96,1024]{3,2,1,0:T(8,128)(2,1)S(1)} %shard_map.89.refs_2_.refs_0_, ...), custom_call_target="tpu_custom_call" | custom-call | flops 1024 | bytes 1024 | tf_op jit(solution)/shard_map/pallas_call | solution.py:151
  138.9 2.7 %collective-permute-start.41 = (bf16[288,768]{1,0:T(8,128)(2,1)S(1)}, bf16[288,768]{1,0:T(8,128)(2,1)S(1)}, u32[]{:S(2)}, u32[]{:S(2)}) collective-permute-start(bf16[288,768]{1,0:T(8,128)(2,1)S(1)} %get-tuple-element.135), channel_id=1, source_target_pairs={{0,2},{1,7},{2,4},{3,1},{4,6},{5,3},{6,0},{7,5},{8,10},{9,15},{10,... | collective-permute-start | bytes 1327112 | tf_op jit(solution)/shard_map/ppermute | solution.py:57
  141.6 4.6 %collective-permute-done.47 = bf16[192,768]{1,0:T(8,128)(2,1)S(1)} collective-permute-done((bf16[192,768]{1,0:T(8,128)(2,1)S(1)}, bf16[192,768]{1,0:T(8,128)(2,1)S(1)}, u32[]{:S(2)}, u32[]{:S(2)}) %collective-permute-start.47) | collective-permute-done | bytes 294944 | tf_op jit(solution)/shard_map/ppermute | solution.py:57
  146.3 3.2 %collective-permute-done.43 = bf16[192,768]{1,0:T(8,128)(2,1)S(1)} collective-permute-done((bf16[192,768]{1,0:T(8,128)(2,1)S(1)}, bf16[192,768]{1,0:T(8,128)(2,1)S(1)}, u32[]{:S(2)}, u32[]{:S(2)}) %collective-permute-start.43) | collective-permute-done | bytes 294944 | tf_op jit(solution)/shard_map/ppermute | solution.py:57
  150.2 3.9 %collective-permute-done.41 = bf16[288,768]{1,0:T(8,128)(2,1)S(1)} collective-permute-done((bf16[288,768]{1,0:T(8,128)(2,1)S(1)}, bf16[288,768]{1,0:T(8,128)(2,1)S(1)}, u32[]{:S(2)}, u32[]{:S(2)}) %collective-permute-start.41) | collective-permute-done | bytes 442400 | tf_op jit(solution)/shard_map/ppermute | solution.py:57
  155.4 11.6 %collective-permute-done.48.got_ref = bf16[192,768]{1,0:T(8,128)(2,1)S(1)} collective-permute-done((bf16[192,768]{1,0:T(8,128)(2,1)S(1)}, bf16[192,768]{1,0:T(8,128)(2,1)S(1)}, u32[]{:S(2)}, u32[]{:S(2)}) %collective-permute-start.48) | collective-permute-done | bytes 294944 | tf_op jit(solution)/shard_map/ppermute | solution.py:57
  167.3 2.9 %collective-permute-done.46 = bf16[192,768]{1,0:T(8,128)(2,1)S(1)} collective-permute-done((bf16[192,768]{1,0:T(8,128)(2,1)S(1)}, bf16[192,768]{1,0:T(8,128)(2,1)S(1)}, u32[]{:S(2)}, u32[]{:S(2)}) %collective-permute-start.46) | collective-permute-done | bytes 294944 | tf_op jit(solution)/shard_map/ppermute | solution.py:57
  170.5 12.5 %collective-permute-done.49.got_ref = bf16[192,768]{1,0:T(8,128)(2,1)S(1)} collective-permute-done((bf16[192,768]{1,0:T(8,128)(2,1)S(1)}, bf16[192,768]{1,0:T(8,128)(2,1)S(1)}, u32[]{:S(2)}, u32[]{:S(2)}) %collective-permute-start.49) | collective-permute-done | bytes 294944 | tf_op jit(solution)/shard_map/ppermute | solution.py:57
  185.0 2.2 %collective-permute-start.52 = (f32[1,1664]{1,0:T(1,128)S(1)}, f32[1,1664]{1,0:T(1,128)S(1)}, u32[]{:S(2)}, u32[]{:S(2)}) collective-permute-start(f32[1,1664]{1,0:T(1,128)S(1)} %constant_dynamic-update-slice_fusion), channel_id=1, source_target_pairs={{0,6},{1,3},{2,0},{3,5},{4,2},{5,7},{6,4},{7,1},{8,14},{9,11},{10,... | collective-permute-start | bytes 19976 | tf_op jit(solution)/shard_map/ppermute | solution.py:57
  187.2 1.6 collective-permute-done.50
  191.0 2.1 shard_map.105
  193.1 1.6 collective-permute-start.55
  194.7 2.8 %collective-permute-start.56 = (f32[1,1024]{1,0:T(1,128)S(1)}, f32[1,1024]{1,0:T(1,128)S(1)}, u32[]{:S(2)}, u32[]{:S(2)}) collective-permute-start(f32[1,1024]{1,0:T(1,128)S(1)} %get-tuple-element.162), channel_id=1, source_target_pairs={{0,16},{1,17},{2,18},{3,19},{4,20},{5,21},{6,22},{7,23},{8,24},{9,... | collective-permute-start | bytes 12296 | tf_op jit(solution)/shard_map/ppermute | solution.py:57
  197.6 2.3 %collective-permute-start.57 = (f32[1,1024]{1,0:T(1,128)S(1)}, f32[1,1024]{1,0:T(1,128)S(1)}, u32[]{:S(2)}, u32[]{:S(2)}) collective-permute-start(f32[1,1024]{1,0:T(1,128)S(1)} %get-tuple-element.162), channel_id=1, source_target_pairs={{0,24},{1,9},{2,26},{3,11},{4,28},{5,13},{6,30},{7,15},{8,0},{9,17... | collective-permute-start | bytes 12296 | tf_op jit(solution)/shard_map/ppermute | solution.py:57
  201.4 4.0 %collective-permute-start.59 = (f32[1,1024]{1,0:T(1,128)S(1)}, f32[1,1024]{1,0:T(1,128)S(1)}, u32[]{:S(2)}, u32[]{:S(2)}) collective-permute-start(f32[1,1024]{1,0:T(1,128)S(1)} %add_add_fusion.2), channel_id=1, source_target_pairs={{0,64},{1,65},{2,66},{3,67},{4,68},{5,69},{6,70},{7,71},{8,72},{9,... | collective-permute-start | bytes 12296 | tf_op jit(solution)/shard_map/ppermute | solution.py:57
  207.1 2.0 collective-permute-done.60
  209.1 1.7 copy-done.9
  210.8 3.5 %shard_map.106 = (f32[768,1536]{1,0:T(8,128)}, f32[1,768]{1,0:T(1,128)S(1)}) custom-call(f32[1,1024]{1,0:T(1,128)S(1)} %add_add_fusion.1.summed_ref, f32[1,128]{1,0:T(1,128)S(1)} %slice.20.row_total_ref, f32[1,1536]{1,0:T(1,128)S(1)} %get-tuple-element.163.clip_ref, f32[1,1536]{1,0:T(1,128)S(1)} %get-tuple-element.164.column_ref, ...), custom_call_target="tpu_custom_call" | custom-call | flops 1024 | bytes 1024 | tf_op jit(solution)/shard_map/pallas_call | solution.py:337
  (231 shorter events, 47.6 us)
Async XLA Ops:
  2.9 5.2 %collective-permute-start.1 = (bf16[192,1024]{1,0:T(8,128)(2,1)}, bf16[192,1024]{1,0:T(8,128)(2,1)S(1)}, u32[]{:S(2)}, u32[]{:S(2)}) collective-permute-start(bf16[192,1024]{1,0:T(8,128)(2,1)} %get-tuple-element.86.refs_0_), channel_id=1, source_target_pairs={{0,1},{1,0},{2,3},{3,2},{4,5},{5,4},{6,7},{7,6},{8,9},{9,8},{10,11... | collective-permute-start | bytes 1179656 | tf_op jit(solution)/shard_map/ppermute | solution.py:57
  3.4 15.1 %collective-permute-start.3 = (bf16[192,1024]{1,0:T(8,128)(2,1)}, bf16[192,1024]{1,0:T(8,128)(2,1)S(1)}, u32[]{:S(2)}, u32[]{:S(2)}) collective-permute-start(bf16[192,1024]{1,0:T(8,128)(2,1)} %get-tuple-element.85.refs_0_), channel_id=1, source_target_pairs={{0,32},{1,97},{2,34},{3,99},{4,36},{5,101},{6,38},{7,103},{8,40},{... | collective-permute-start | bytes 1179656 | tf_op jit(solution)/shard_map/ppermute | solution.py:57
  5.1 13.5 %collective-permute-start.4 = (bf16[192,1024]{1,0:T(8,128)(2,1)}, bf16[192,1024]{1,0:T(8,128)(2,1)S(1)}, u32[]{:S(2)}, u32[]{:S(2)}) collective-permute-start(bf16[192,1024]{1,0:T(8,128)(2,1)} %get-tuple-element.86.refs_0_), channel_id=1, source_target_pairs={{0,8},{1,25},{2,10},{3,27},{4,12},{5,29},{6,14},{7,31},{8,16},{9,1... | collective-permute-start | bytes 1179656 | tf_op jit(solution)/shard_map/ppermute | solution.py:57
  6.6 12.0 %collective-permute-start.5 = (bf16[192,1024]{1,0:T(8,128)(2,1)S(1)}, bf16[192,1024]{1,0:T(8,128)(2,1)S(1)}, u32[]{:S(2)}, u32[]{:S(2)}) collective-permute-start(bf16[192,1024]{1,0:T(8,128)(2,1)S(1)} %collective-permute-done.refs_0_.refs_4_.refs_1_), channel_id=1, source_target_pairs={{0,32},{1,97},{2,34},{3,99},{4,36},{5,101},{6,38},{7,103},{8,40},{... | collective-permute-start | bytes 1179656 | tf_op jit(solution)/shard_map/ppermute | solution.py:57
  8.2 10.4 %collective-permute-start.6 = (bf16[192,1024]{1,0:T(8,128)(2,1)S(1)}, bf16[192,1024]{1,0:T(8,128)(2,1)S(1)}, u32[]{:S(2)}, u32[]{:S(2)}) collective-permute-start(bf16[192,1024]{1,0:T(8,128)(2,1)S(1)} %collective-permute-done.1.refs_1_.refs_4_), channel_id=1, source_target_pairs={{0,8},{1,25},{2,10},{3,27},{4,12},{5,29},{6,14},{7,31},{8,16},{9,1... | collective-permute-start | bytes 1179656 | tf_op jit(solution)/shard_map/ppermute | solution.py:57
  19.4 16.1 %collective-permute-start.2 = (bf16[1024,768]{1,0:T(8,128)(2,1)S(1)}, bf16[1024,768]{1,0:T(8,128)(2,1)S(1)}, u32[]{:S(2)}, u32[]{:S(2)}) collective-permute-start(bf16[1024,768]{1,0:T(8,128)(2,1)S(1)} %shard_map.87), channel_id=1, source_target_pairs={{0,1},{1,0},{2,3},{3,2},{4,5},{5,4},{6,7},{7,6},{8,9},{9,8},{10,11... | collective-permute-start | bytes 4718600 | tf_op jit(solution)/shard_map/ppermute | solution.py:57
  19.8 9.0 %collective-permute-start.10 = (bf16[192,1024]{1,0:T(8,128)(2,1)S(1)}, bf16[192,1024]{1,0:T(8,128)(2,1)S(1)}, u32[]{:S(2)}, u32[]{:S(2)}) collective-permute-start(bf16[192,1024]{1,0:T(8,128)(2,1)S(1)} %collective-permute-done.3.refs_1_.refs_2_), channel_id=1, source_target_pairs={{0,32},{1,97},{2,34},{3,99},{4,36},{5,101},{6,38},{7,103},{8,40},{... | collective-permute-start | bytes 1179656 | tf_op jit(solution)/shard_map/ppermute | solution.py:57
  20.6 9.0 %collective-permute-start.11 = (bf16[192,1024]{1,0:T(8,128)(2,1)S(1)}, bf16[192,1024]{1,0:T(8,128)(2,1)S(1)}, u32[]{:S(2)}, u32[]{:S(2)}) collective-permute-start(bf16[192,1024]{1,0:T(8,128)(2,1)S(1)} %collective-permute-done.4.refs_1_), channel_id=1, source_target_pairs={{0,8},{1,25},{2,10},{3,27},{4,12},{5,29},{6,14},{7,31},{8,16},{9,1... | collective-permute-start | bytes 1179656 | tf_op jit(solution)/shard_map/ppermute | solution.py:57
  21.8 7.8 %collective-permute-start.9 = (bf16[192,1024]{1,0:T(8,128)(2,1)S(1)}, bf16[192,1024]{1,0:T(8,128)(2,1)S(1)}, u32[]{:S(2)}, u32[]{:S(2)}) collective-permute-start(bf16[192,1024]{1,0:T(8,128)(2,1)S(1)} %collective-permute-done.5.refs_5_.refs_3_), channel_id=1, source_target_pairs={{0,1},{1,0},{2,3},{3,2},{4,5},{5,4},{6,7},{7,6},{8,9},{9,8},{10,11... | collective-permute-start | bytes 1179656 | tf_op jit(solution)/shard_map/ppermute | solution.py:57
  22.7 6.9 %collective-permute-start.12 = (bf16[192,1024]{1,0:T(8,128)(2,1)S(1)}, bf16[192,1024]{1,0:T(8,128)(2,1)S(1)}, u32[]{:S(2)}, u32[]{:S(2)}) collective-permute-start(bf16[192,1024]{1,0:T(8,128)(2,1)S(1)} %collective-permute-done.6.refs_5_), channel_id=1, source_target_pairs={{0,1},{1,0},{2,3},{3,2},{4,5},{5,4},{6,7},{7,6},{8,9},{9,8},{10,11... | collective-permute-start | bytes 1179656 | tf_op jit(solution)/shard_map/ppermute | solution.py:57
  32.8 27.4 %collective-permute-start.16 = (bf16[2,4,96,1024]{3,2,1,0:T(8,128)(2,1)}, bf16[2,4,96,1024]{3,2,1,0:T(8,128)(2,1)}, u32[]{:S(2)}, u32[]{:S(2)}) collective-permute-start(bf16[2,4,96,1024]{3,2,1,0:T(8,128)(2,1)} %shard_map.91.refs_9_.refs_2_), channel_id=1, source_target_pairs={{0,32},{1,97},{2,34},{3,99},{4,36},{5,101},{6,38},{7,103},{8,40},{... | collective-permute-start | bytes 4718600 | tf_op jit(solution)/shard_map/ppermute | solution.py:57
  35.5 24.7 %collective-permute-start.15 = (bf16[2,4,96,1024]{3,2,1,0:T(8,128)(2,1)}, bf16[2,4,96,1024]{3,2,1,0:T(8,128)(2,1)}, u32[]{:S(2)}, u32[]{:S(2)}) collective-permute-start(bf16[2,4,96,1024]{3,2,1,0:T(8,128)(2,1)} %shard_map.90.refs_8_), channel_id=1, source_target_pairs={{0,8},{1,25},{2,10},{3,27},{4,12},{5,29},{6,14},{7,31},{8,16},{9,1... | collective-permute-start | bytes 4718600 | tf_op jit(solution)/shard_map/ppermute | solution.py:57
  42.0 9.1 %collective-permute-start.17 = (bf16[192,768]{1,0:T(8,128)(2,1)}, bf16[192,768]{1,0:T(8,128)(2,1)}, u32[]{:S(2)}, u32[]{:S(2)}) collective-permute-start(bf16[192,768]{1,0:T(8,128)(2,1)} %get-tuple-element.97), channel_id=1, source_target_pairs={{0,2},{1,7},{2,4},{3,1},{4,6},{5,3},{6,0},{7,5},{8,10},{9,15},{10,... | collective-permute-start | bytes 884744 | tf_op jit(solution)/shard_map/ppermute | solution.py:57
  52.1 8.0 %collective-permute-start.18 = (bf16[192,768]{1,0:T(8,128)(2,1)S(1)}, bf16[192,768]{1,0:T(8,128)(2,1)S(1)}, u32[]{:S(2)}, u32[]{:S(2)}) collective-permute-start(bf16[192,768]{1,0:T(8,128)(2,1)S(1)} %add_convert_fusion.11), channel_id=1, source_target_pairs={{0,2},{1,7},{2,4},{3,1},{4,6},{5,3},{6,0},{7,5},{8,10},{9,15},{10,... | collective-permute-start | bytes 884744 | tf_op jit(solution)/shard_map/ppermute | solution.py:57
  53.0 4.5 %collective-permute-start.19 = (f32[896]{0:T(1024)S(1)}, f32[896]{0:T(1024)S(1)}, u32[]{:S(2)}, u32[]{:S(2)}) collective-permute-start(f32[896]{0:T(1024)S(1)} %concatenate.10), channel_id=1, source_target_pairs={{0,1},{1,0},{2,3},{3,2},{4,5},{5,4},{6,7},{7,6},{8,9},{9,8},{10,11... | collective-permute-start | bytes 10760 | tf_op jit(solution)/shard_map/ppermute | solution.py:57
  60.3 5.9 %collective-permute-start.21 = (bf16[2,4,96,1024]{3,2,1,0:T(8,128)(2,1)}, bf16[2,4,96,1024]{3,2,1,0:T(8,128)(2,1)S(1)}, u32[]{:S(2)}, u32[]{:S(2)}) collective-permute-start(bf16[2,4,96,1024]{3,2,1,0:T(8,128)(2,1)} %collective-permute-done.16.refs_3_), channel_id=1, source_target_pairs={{0,1},{1,0},{2,3},{3,2},{4,5},{5,4},{6,7},{7,6},{8,9},{9,8},{10,11... | collective-permute-start | bytes 4718600 | tf_op jit(solution)/shard_map/ppermute | solution.py:57
  63.2 13.3 %collective-permute-start.24 = (bf16[4,96,1024]{2,1,0:T(8,128)(2,1)S(1)}, bf16[4,96,1024]{2,1,0:T(8,128)(2,1)S(1)}, u32[]{:S(2)}, u32[]{:S(2)}) collective-permute-start(bf16[4,96,1024]{2,1,0:T(8,128)(2,1)S(1)} %slice_bitcast_fusion.3), channel_id=1, source_target_pairs={{0,8},{1,25},{2,10},{3,27},{4,12},{5,29},{6,14},{7,31},{8,16},{9,1... | collective-permute-start | bytes 2359304 | tf_op jit(solution)/shard_map/ppermute | solution.py:57
  63.8 13.2 %collective-permute-start.25 = (bf16[4,96,1024]{2,1,0:T(8,128)(2,1)S(1)}, bf16[4,96,1024]{2,1,0:T(8,128)(2,1)S(1)}, u32[]{:S(2)}, u32[]{:S(2)}) collective-permute-start(bf16[4,96,1024]{2,1,0:T(8,128)(2,1)S(1)} %slice_bitcast_fusion.2), channel_id=1, source_target_pairs={{0,32},{1,97},{2,34},{3,99},{4,36},{5,101},{6,38},{7,103},{8,40},{... | collective-permute-start | bytes 2359304 | tf_op jit(solution)/shard_map/ppermute | solution.py:57
  66.2 27.1 %collective-permute-start.22 = (bf16[2,4,96,1024]{3,2,1,0:T(8,128)(2,1)S(1)}, bf16[2,4,96,1024]{3,2,1,0:T(8,128)(2,1)S(1)}, u32[]{:S(2)}, u32[]{:S(2)}) collective-permute-start(bf16[2,4,96,1024]{3,2,1,0:T(8,128)(2,1)S(1)} %shard_map.88), channel_id=1, source_target_pairs={{0,8},{1,25},{2,10},{3,27},{4,12},{5,29},{6,14},{7,31},{8,16},{9,1... | collective-permute-start | bytes 4718600 | tf_op jit(solution)/shard_map/ppermute | solution.py:57
  66.7 27.2 %collective-permute-start.23 = (bf16[2,4,96,1024]{3,2,1,0:T(8,128)(2,1)S(1)}, bf16[2,4,96,1024]{3,2,1,0:T(8,128)(2,1)}, u32[]{:S(2)}, u32[]{:S(2)}) collective-permute-start(bf16[2,4,96,1024]{3,2,1,0:T(8,128)(2,1)S(1)} %shard_map.89.refs_2_.refs_0_), channel_id=1, source_target_pairs={{0,32},{1,97},{2,34},{3,99},{4,36},{5,101},{6,38},{7,103},{8,40},{... | collective-permute-start | bytes 4718600 | tf_op jit(solution)/shard_map/ppermute | solution.py:57
  72.8 8.0 %collective-permute-start.28 = (bf16[192,768]{1,0:T(8,128)(2,1)S(1)}, bf16[192,768]{1,0:T(8,128)(2,1)S(1)}, u32[]{:S(2)}, u32[]{:S(2)}) collective-permute-start(bf16[192,768]{1,0:T(8,128)(2,1)S(1)} %get-tuple-element.103), channel_id=1, source_target_pairs={{0,2},{1,7},{2,4},{3,1},{4,6},{5,3},{6,0},{7,5},{8,10},{9,15},{10,... | collective-permute-start | bytes 884744 | tf_op jit(solution)/shard_map/ppermute | solution.py:57
  80.9 8.0 %collective-permute-start.29 = (bf16[192,768]{1,0:T(8,128)(2,1)S(1)}, bf16[192,768]{1,0:T(8,128)(2,1)S(1)}, u32[]{:S(2)}, u32[]{:S(2)}) collective-permute-start(bf16[192,768]{1,0:T(8,128)(2,1)S(1)} %add_convert_fusion.9.refs_7_), channel_id=1, source_target_pairs={{0,2},{1,7},{2,4},{3,1},{4,6},{5,3},{6,0},{7,5},{8,10},{9,15},{10,... | collective-permute-start | bytes 884744 | tf_op jit(solution)/shard_map/ppermute | solution.py:57
  93.9 4.8 %collective-permute-start.30 = (bf16[2,4,96,1024]{3,2,1,0:T(8,128)(2,1)}, bf16[2,4,96,1024]{3,2,1,0:T(8,128)(2,1)S(1)}, u32[]{:S(2)}, u32[]{:S(2)}) collective-permute-start(bf16[2,4,96,1024]{3,2,1,0:T(8,128)(2,1)} %collective-permute-done.23.refs_3_.refs_1_), channel_id=1, source_target_pairs={{0,1},{1,0},{2,3},{3,2},{4,5},{5,4},{6,7},{7,6},{8,9},{9,8},{10,11... | collective-permute-start | bytes 4718600 | tf_op jit(solution)/shard_map/ppermute | solution.py:57
  94.1 5.5 %collective-permute-start.33 = (bf16[2,4,96,1024]{3,2,1,0:T(8,128)(2,1)S(1)}, bf16[2,4,96,1024]{3,2,1,0:T(8,128)(2,1)S(1)}, u32[]{:S(2)}, u32[]{:S(2)}) collective-permute-start(bf16[2,4,96,1024]{3,2,1,0:T(8,128)(2,1)S(1)} %collective-permute-done.22.refs_0_), channel_id=1, source_target_pairs={{0,1},{1,0},{2,3},{3,2},{4,5},{5,4},{6,7},{7,6},{8,9},{9,8},{10,11... | collective-permute-start | bytes 4718600 | tf_op jit(solution)/shard_map/ppermute | solution.py:57
  94.5 17.3 %collective-permute-start.34 = (bf16[480,768]{1,0:T(8,128)(2,1)}, bf16[480,768]{1,0:T(8,128)(2,1)}, u32[]{:S(2)}, u32[]{:S(2)}) collective-permute-start(bf16[480,768]{1,0:T(8,128)(2,1)} %get-tuple-element.107), channel_id=1, source_target_pairs={{0,2},{1,7},{2,4},{3,1},{4,6},{5,3},{6,0},{7,5},{8,10},{9,15},{10,... | collective-permute-start | bytes 2211848 | tf_op jit(solution)/shard_map/ppermute | solution.py:57
  97.5 16.4 %collective-permute-start.31 = (bf16[4,96,1024]{2,1,0:T(8,128)(2,1)}, bf16[4,96,1024]{2,1,0:T(8,128)(2,1)}, u32[]{:S(2)}, u32[]{:S(2)}) collective-permute-start(bf16[4,96,1024]{2,1,0:T(8,128)(2,1)} %slice_bitcast_fusion.1), channel_id=1, source_target_pairs={{0,8},{1,25},{2,10},{3,27},{4,12},{5,29},{6,14},{7,31},{8,16},{9,1... | collective-permute-start | bytes 2359304 | tf_op jit(solution)/shard_map/ppermute | solution.py:57
  98.7 15.2 %collective-permute-start.32 = (bf16[4,96,1024]{2,1,0:T(8,128)(2,1)}, bf16[4,96,1024]{2,1,0:T(8,128)(2,1)S(1)}, u32[]{:S(2)}, u32[]{:S(2)}) collective-permute-start(bf16[4,96,1024]{2,1,0:T(8,128)(2,1)} %slice_bitcast_fusion), channel_id=1, source_target_pairs={{0,32},{1,97},{2,34},{3,99},{4,36},{5,101},{6,38},{7,103},{8,40},{... | collective-permute-start | bytes 2359304 | tf_op jit(solution)/shard_map/ppermute | solution.py:57
  99.6 13.6 %collective-permute-start.36 = (bf16[192,768]{1,0:T(8,128)(2,1)S(1)}, bf16[192,768]{1,0:T(8,128)(2,1)S(1)}, u32[]{:S(2)}, u32[]{:S(2)}) collective-permute-start(bf16[192,768]{1,0:T(8,128)(2,1)S(1)} %add_convert_fusion.10), channel_id=1, source_target_pairs={{0,2},{1,7},{2,4},{3,1},{4,6},{5,3},{6,0},{7,5},{8,10},{9,15},{10,... | collective-permute-start | bytes 884744 | tf_op jit(solution)/shard_map/ppermute | solution.py:57
  99.6 14.1 %collective-permute-start.35 = (bf16[192,768]{1,0:T(8,128)(2,1)S(1)}, bf16[192,768]{1,0:T(8,128)(2,1)S(1)}, u32[]{:S(2)}, u32[]{:S(2)}) collective-permute-start(bf16[192,768]{1,0:T(8,128)(2,1)S(1)} %add_convert_fusion.8), channel_id=1, source_target_pairs={{0,2},{1,7},{2,4},{3,1},{4,6},{5,3},{6,0},{7,5},{8,10},{9,15},{10,... | collective-permute-start | bytes 884744 | tf_op jit(solution)/shard_map/ppermute | solution.py:57
  114.6 12.7 %collective-permute-start.40 = (bf16[480,768]{1,0:T(8,128)(2,1)S(1)}, bf16[480,768]{1,0:T(8,128)(2,1)S(1)}, u32[]{:S(2)}, u32[]{:S(2)}) collective-permute-start(bf16[480,768]{1,0:T(8,128)(2,1)S(1)} %add_convert_fusion.1), channel_id=1, source_target_pairs={{0,2},{1,7},{2,4},{3,1},{4,6},{5,3},{6,0},{7,5},{8,10},{9,15},{10,... | collective-permute-start | bytes 2211848 | tf_op jit(solution)/shard_map/ppermute | solution.py:57
  116.3 14.2 %collective-permute-start.38 = (bf16[192,768]{1,0:T(8,128)(2,1)S(1)}, bf16[192,768]{1,0:T(8,128)(2,1)S(1)}, u32[]{:S(2)}, u32[]{:S(2)}) collective-permute-start(bf16[192,768]{1,0:T(8,128)(2,1)S(1)} %get-tuple-element.113), channel_id=1, source_target_pairs={{0,2},{1,7},{2,4},{3,1},{4,6},{5,3},{6,0},{7,5},{8,10},{9,15},{10,... | collective-permute-start | bytes 884744 | tf_op jit(solution)/shard_map/ppermute | solution.py:57
  130.4 19.1 %collective-permute-start.42 = (bf16[480,768]{1,0:T(8,128)(2,1)S(1)}, bf16[480,768]{1,0:T(8,128)(2,1)S(1)}, u32[]{:S(2)}, u32[]{:S(2)}) collective-permute-start(bf16[480,768]{1,0:T(8,128)(2,1)S(1)} %add_convert_fusion.refs_6_), channel_id=1, source_target_pairs={{0,2},{1,7},{2,4},{3,1},{4,6},{5,3},{6,0},{7,5},{8,10},{9,15},{10,... | collective-permute-start | bytes 2211848 | tf_op jit(solution)/shard_map/ppermute | solution.py:57
  131.0 15.3 %collective-permute-start.47 = (bf16[192,768]{1,0:T(8,128)(2,1)S(1)}, bf16[192,768]{1,0:T(8,128)(2,1)S(1)}, u32[]{:S(2)}, u32[]{:S(2)}) collective-permute-start(bf16[192,768]{1,0:T(8,128)(2,1)S(1)} %add_convert_fusion.7.refs_5_), channel_id=1, source_target_pairs={{0,2},{1,7},{2,4},{3,1},{4,6},{5,3},{6,0},{7,5},{8,10},{9,15},{10,... | collective-permute-start | bytes 884744 | tf_op jit(solution)/shard_map/ppermute | solution.py:57
  131.7 17.8 %collective-permute-start.43 = (bf16[192,768]{1,0:T(8,128)(2,1)S(1)}, bf16[192,768]{1,0:T(8,128)(2,1)S(1)}, u32[]{:S(2)}, u32[]{:S(2)}) collective-permute-start(bf16[192,768]{1,0:T(8,128)(2,1)S(1)} %get-tuple-element.129), channel_id=1, source_target_pairs={{0,2},{1,7},{2,4},{3,1},{4,6},{5,3},{6,0},{7,5},{8,10},{9,15},{10,... | collective-permute-start | bytes 884744 | tf_op jit(solution)/shard_map/ppermute | solution.py:57
  138.9 15.2 %collective-permute-start.41 = (bf16[288,768]{1,0:T(8,128)(2,1)S(1)}, bf16[288,768]{1,0:T(8,128)(2,1)S(1)}, u32[]{:S(2)}, u32[]{:S(2)}) collective-permute-start(bf16[288,768]{1,0:T(8,128)(2,1)S(1)} %get-tuple-element.135), channel_id=1, source_target_pairs={{0,2},{1,7},{2,4},{3,1},{4,6},{5,3},{6,0},{7,5},{8,10},{9,15},{10,... | collective-permute-start | bytes 1327112 | tf_op jit(solution)/shard_map/ppermute | solution.py:57
  154.3 15.9 %collective-permute-start.44 = (bf16[288,768]{1,0:T(8,128)(2,1)S(1)}, bf16[288,768]{1,0:T(8,128)(2,1)S(1)}, u32[]{:S(2)}, u32[]{:S(2)}) collective-permute-start(bf16[288,768]{1,0:T(8,128)(2,1)S(1)} %add_convert_fusion.3), channel_id=1, source_target_pairs={{0,2},{1,7},{2,4},{3,1},{4,6},{5,3},{6,0},{7,5},{8,10},{9,15},{10,... | collective-permute-start | bytes 1327112 | tf_op jit(solution)/shard_map/ppermute | solution.py:57
  154.4 12.6 %collective-permute-start.48 = (bf16[192,768]{1,0:T(8,128)(2,1)S(1)}, bf16[192,768]{1,0:T(8,128)(2,1)S(1)}, u32[]{:S(2)}, u32[]{:S(2)}) collective-permute-start(bf16[192,768]{1,0:T(8,128)(2,1)S(1)} %add_convert_fusion.5), channel_id=1, source_target_pairs={{0,2},{1,7},{2,4},{3,1},{4,6},{5,3},{6,0},{7,5},{8,10},{9,15},{10,... | collective-permute-start | bytes 884744 | tf_op jit(solution)/shard_map/ppermute | solution.py:57
  154.5 15.7 %collective-permute-start.46 = (bf16[192,768]{1,0:T(8,128)(2,1)S(1)}, bf16[192,768]{1,0:T(8,128)(2,1)S(1)}, u32[]{:S(2)}, u32[]{:S(2)}) collective-permute-start(bf16[192,768]{1,0:T(8,128)(2,1)S(1)} %add_convert_fusion.6), channel_id=1, source_target_pairs={{0,2},{1,7},{2,4},{3,1},{4,6},{5,3},{6,0},{7,5},{8,10},{9,15},{10,... | collective-permute-start | bytes 884744 | tf_op jit(solution)/shard_map/ppermute | solution.py:57
  170.3 13.0 %collective-permute-start.45 = (bf16[288,768]{1,0:T(8,128)(2,1)S(1)}, bf16[288,768]{1,0:T(8,128)(2,1)S(1)}, u32[]{:S(2)}, u32[]{:S(2)}) collective-permute-start(bf16[288,768]{1,0:T(8,128)(2,1)S(1)} %add_convert_fusion.2), channel_id=1, source_target_pairs={{0,2},{1,7},{2,4},{3,1},{4,6},{5,3},{6,0},{7,5},{8,10},{9,15},{10,... | collective-permute-start | bytes 1327112 | tf_op jit(solution)/shard_map/ppermute | solution.py:57
  170.5 12.6 %collective-permute-start.49 = (bf16[192,768]{1,0:T(8,128)(2,1)S(1)}, bf16[192,768]{1,0:T(8,128)(2,1)S(1)}, u32[]{:S(2)}, u32[]{:S(2)}) collective-permute-start(bf16[192,768]{1,0:T(8,128)(2,1)S(1)} %add_convert_fusion.4), channel_id=1, source_target_pairs={{0,2},{1,7},{2,4},{3,1},{4,6},{5,3},{6,0},{7,5},{8,10},{9,15},{10,... | collective-permute-start | bytes 884744 | tf_op jit(solution)/shard_map/ppermute | solution.py:57
  183.8 7.2 %collective-permute-start.54 = (f32[768,768]{1,0:T(8,128)S(1)}, f32[768,768]{1,0:T(8,128)S(1)}, u32[]{:S(2)}, u32[]{:S(2)}) collective-permute-start(f32[768,768]{1,0:T(8,128)S(1)} %get-tuple-element.161), channel_id=1, source_target_pairs={{0,1},{1,0},{2,3},{3,2},{4,5},{5,4},{6,7},{7,6},{8,9},{9,8},{10,11... | collective-permute-start | bytes 7077896 | tf_op jit(solution)/shard_map/ppermute | solution.py:57
  183.9 4.9 %collective-permute-start.50 = (f32[1,1664]{1,0:T(1,128)S(1)}, f32[1,1664]{1,0:T(1,128)S(1)}, u32[]{:S(2)}, u32[]{:S(2)}) collective-permute-start(f32[1,1664]{1,0:T(1,128)S(1)} %constant_dynamic-update-slice_fusion), channel_id=1, source_target_pairs={{0,2},{1,7},{2,4},{3,1},{4,6},{5,3},{6,0},{7,5},{8,10},{9,15},{10,... | collective-permute-start | bytes 19976 | tf_op jit(solution)/shard_map/ppermute | solution.py:57
  184.0 5.2 %collective-permute-start.51 = (f32[1,1664]{1,0:T(1,128)S(1)}, f32[1,1664]{1,0:T(1,128)S(1)}, u32[]{:S(2)}, u32[]{:S(2)}) collective-permute-start(f32[1,1664]{1,0:T(1,128)S(1)} %constant_dynamic-update-slice_fusion), channel_id=1, source_target_pairs={{0,4},{1,5},{2,6},{3,7},{4,0},{5,1},{6,2},{7,3},{8,12},{9,13},{10,... | collective-permute-start | bytes 19976 | tf_op jit(solution)/shard_map/ppermute | solution.py:57
  185.0 4.8 %collective-permute-start.52 = (f32[1,1664]{1,0:T(1,128)S(1)}, f32[1,1664]{1,0:T(1,128)S(1)}, u32[]{:S(2)}, u32[]{:S(2)}) collective-permute-start(f32[1,1664]{1,0:T(1,128)S(1)} %constant_dynamic-update-slice_fusion), channel_id=1, source_target_pairs={{0,6},{1,3},{2,0},{3,5},{4,2},{5,7},{6,4},{7,1},{8,14},{9,11},{10,... | collective-permute-start | bytes 19976 | tf_op jit(solution)/shard_map/ppermute | solution.py:57
  193.1 6.8 %collective-permute-start.55 = (f32[1,1024]{1,0:T(1,128)S(1)}, f32[1,1024]{1,0:T(1,128)S(1)}, u32[]{:S(2)}, u32[]{:S(2)}) collective-permute-start(f32[1,1024]{1,0:T(1,128)S(1)} %get-tuple-element.162), channel_id=1, source_target_pairs={{0,8},{1,25},{2,10},{3,27},{4,12},{5,29},{6,14},{7,31},{8,16},{9,1... | collective-permute-start | bytes 12296 | tf_op jit(solution)/shard_map/ppermute | solution.py:57
  194.7 5.1 %collective-permute-start.56 = (f32[1,1024]{1,0:T(1,128)S(1)}, f32[1,1024]{1,0:T(1,128)S(1)}, u32[]{:S(2)}, u32[]{:S(2)}) collective-permute-start(f32[1,1024]{1,0:T(1,128)S(1)} %get-tuple-element.162), channel_id=1, source_target_pairs={{0,16},{1,17},{2,18},{3,19},{4,20},{5,21},{6,22},{7,23},{8,24},{9,... | collective-permute-start | bytes 12296 | tf_op jit(solution)/shard_map/ppermute | solution.py:57
  201.2 4.9 %collective-permute-start.58 = (f32[1,1024]{1,0:T(1,128)S(1)}, f32[1,1024]{1,0:T(1,128)S(1)}, u32[]{:S(2)}, u32[]{:S(2)}) collective-permute-start(f32[1,1024]{1,0:T(1,128)S(1)} %add_add_fusion.2), channel_id=1, source_target_pairs={{0,32},{1,97},{2,34},{3,99},{4,36},{5,101},{6,38},{7,103},{8,40},{... | collective-permute-start | bytes 12296 | tf_op jit(solution)/shard_map/ppermute | solution.py:57
  201.4 5.7 %collective-permute-start.59 = (f32[1,1024]{1,0:T(1,128)S(1)}, f32[1,1024]{1,0:T(1,128)S(1)}, u32[]{:S(2)}, u32[]{:S(2)}) collective-permute-start(f32[1,1024]{1,0:T(1,128)S(1)} %add_add_fusion.2), channel_id=1, source_target_pairs={{0,64},{1,65},{2,66},{3,67},{4,68},{5,69},{6,70},{7,71},{8,72},{9,... | collective-permute-start | bytes 12296 | tf_op jit(solution)/shard_map/ppermute | solution.py:57
  (65 other events, 584.3 us)

commit v5 on v4

--- a/solution.py
+++ b/solution.py
@@ -434,7 +434,10 @@
     far0_got = hop(far0[0])
     near0_3 = add_narrow(near0[2], after(near0_got, far0[0]))
     x1, y1 = lax.optimization_barrier((x1_next, y1_next, far0[0], near0_3))[:2]
-    x2, y2 = send(x1[0], ALONG_X), send(y1[0], ALONG_Y)
+    far0_2 = add_narrow(far0[1], far0_got)
+    x2, y2 = lax.optimization_barrier((x1[0], y1[0], far0_2))[:2]
+    x2, y2 = send(x2, ALONG_X), send(y2, ALONG_Y)
+    far0_got = hop(far0_2)
     x1_swap, y1_swap = send(x1, SWAP), send(y1, SWAP)
     near0_got = hop(after(near0_3, x1_swap, y1_swap))
     own_got = hop(after(own_3, x1_swap, y1_swap))
@@ -445,20 +448,18 @@
     ]
     near1 = units(near_entries(x1, x1_swap), waits=(far0[2], y1_swap))
     near1_got = hop(near1[0])
-    far0_2 = add_narrow(far0[1], after(far0_got, near1[0]))
-    far0_got = hop(far0_2)
     placed = place_rows(own[3], after(own_got, near1[0]), [(0, 0, 0, FEAT // 2)], ())
     placed = place_rows(near0[3], after(near0_got, near1[0]), near_pieces(0), placed)
-    x2, y2 = lax.optimization_barrier((x2, y2, near1[0], far0_2, placed[2]))[:2]
+    x2, y2 = lax.optimization_barrier((x2, y2, near1[0], placed[2]))[:2]
     x2_swap, y2_swap = send(x2, SWAP), send(y2, SWAP)
     far1_entries = far_entries(q_next, y1, y1_swap, x2, x2_swap, y2, y2_swap)
-    far1 = units(far1_entries[:2])
+    far0_3 = add_narrow(far0[2], after(far0_got, near1[0]))
+    far0_got = hop(far0_3)
+    far1 = units(far1_entries[:2], waits=(far0_3,))
     far1_got = hop(far1[0])
     near1_2 = add_narrow(near1[1], after(near1_got, far1[0]))
     near1_got = hop(near1_2)
-    far0_3 = add_narrow(far0[2], after(far0_got, far1[0]))
-    far0_got = hop(far0_3)
-    last1 = units(far1_entries[2:], waits=(near1_2, far0_3))
+    last1 = units(far1_entries[2:], waits=(near1_2,))
     last1_got = hop(last1[0])
     near1_3 = add_narrow(near1[2], after(near1_got, last1[0]))
     far1_2 = add_narrow(far1[1], after(far1_got, last1[0]))

time: 216 us -> 212 us (0.981)
  waiting for transfers between devices: 86.5 us -> 72.6 us
  starting transfers between devices: 50.4 us -> 56.2 us
  other arithmetic: 8.72 us -> 11.9 us
    ppermute x61, waiting for transfers between devices: 86.5 us -> 72.6 us  [send(): return lax.ppermute(value, BOTH, pairs)]
    ppermute x61, starting transfers between devices: 50.4 us -> 56.2 us  [send(): return lax.ppermute(value, BOTH, pairs)]
    convert_element_type x12, other arithmetic: 3.34 us -> 6.51 us  [add_narrow(): return (a.astype(jnp.float32) + b.astype(jnp.float32)).astype(jnp.bfloat16)]
    squeeze x4 -> x2, local copies, waits for them, and re-layouts: 5.45 us -> 2.37 us  [per_device(): x2, y2 = (send(x1[0], ALONG_X), send(y1[0], ALONG_Y))]
    unnamed x105 -> x121, local copies, waits for them, and re-layouts: 7.93 us -> 9.86 us
  transfers between devices with their start and end apart: 61 -> 61, of which waited for: 31 -> 26; matrix products, arithmetic and copies ran while one was open for 7% -> 7% of each run, Pallas kernels for 21% -> 22%
where the time goes in v5:
time: 212 us; the launch traced here: 210 us
  waiting for transfers between devices  72.6 us (34%)
  starting transfers between devices  56.2 us (27%)
  Pallas kernels  53.5 us (25%)
  local copies, waits for them, and re-layouts  14.3 us (7%)
  other arithmetic  11.9 us (6%)
    ppermute x61, waiting for transfers between devices, send(): return lax.ppermute(value, BOTH, pairs)  72.6 us
    ppermute x61, starting transfers between devices, send(): return lax.ppermute(value, BOTH, pairs)  56.2 us
    pallas_call x7, Pallas kernels, unit_partials(): pl.pallas_call(kernel, out_shape=tuple((jax.ShapeDtypeStruct((rows, HALF)...  35.6 us
    unnamed x121, local copies, waits for them, and re-layouts  9.86 us
    convert_element_type x12, other arithmetic, add_narrow(): return (a.astype(jnp.float32) + b.astype(jnp.float32)).astype(jnp.bfloat16)  6.51 us
    pallas_call x2, Pallas kernels, slope_half(): pl.pallas_call(kernel, out_shape=jax.ShapeDtypeStruct((TOK, HALF), jnp.bf...  5.05 us
  transfers between devices with their start and end apart: 61, of which 26 were waited for; matrix products, arithmetic and copies ran while one was open for 7% of the time, Pallas kernels for 22%

profile of v5, /device:TPU:0, one launch (start us, length us, event | category | flops | bytes accessed | tf_op | source)
XLA Modules:
  0.0 210.2 jit_solution(11940299668494634699)
XLA Ops:
  0.6 2.3 %shard_map.85 = (bf16[192,1024]{1,0:T(8,128)(2,1)}, bf16[192,1024]{1,0:T(8,128)(2,1)}) custom-call(bf16[1024,384]{1,0:T(8,128)(2,1)} %ref.1), custom_call_target="tpu_custom_call" | custom-call | flops 1024 | bytes 1024 | tf_op jit(solution)/shard_map/pallas_call | solution.py:186
  3.4 1.7 collective-permute-start.3
  5.1 1.5 collective-permute-start.4
  6.6 1.6 collective-permute-start.5
  8.1 1.5 collective-permute-start.6
  9.6 1.9 copy-done.8
  11.5 1.9 copy-done.9
  13.4 2.5 %shard_map.86.own_ref = bf16[1024,768]{1,0:T(8,128)(2,1)S(1)} custom-call(bf16[1024,1536]{1,0:T(8,128)(2,1)S(1)} %copy-done.8, bf16[1024,1536]{1,0:T(8,128)(2,1)S(1)} %copy-done.9, bf16[192,1024]{1,0:T(8,128)(2,1)S(1)} %collective-permute-done.refs_0_.refs_4_.refs_1_, bf16[192,1024]{1,0:T(8,128)(2,1)S(1)} %collective-permute-done.1.refs_1_.refs_4_), custom_call_target="tpu_custom_call" | custom-call | flops 1024 | bytes 1024 | tf_op jit(solution)/shard_map/pallas_call | solution.py:89
  16.0 2.5 %shard_map.87 = bf16[1024,768]{1,0:T(8,128)(2,1)S(1)} custom-call(bf16[1024,1536]{1,0:T(8,128)(2,1)S(1)} %copy-done.8, bf16[1024,1536]{1,0:T(8,128)(2,1)S(1)} %copy-done.9, bf16[192,1024]{1,0:T(8,128)(2,1)S(1)} %collective-permute-done.refs_0_.refs_4_.refs_1_, bf16[192,1024]{1,0:T(8,128)(2,1)S(1)} %collective-permute-done.1.refs_1_.refs_4_), custom_call_target="tpu_custom_call" | custom-call | flops 1024 | bytes 1024 | tf_op jit(solution)/shard_map/pallas_call | solution.py:89
  22.7 6.1 %collective-permute-done.10.refs_3_.refs_6_ = bf16[192,1024]{1,0:T(8,128)(2,1)S(1)} collective-permute-done((bf16[192,1024]{1,0:T(8,128)(2,1)S(1)}, bf16[192,1024]{1,0:T(8,128)(2,1)S(1)}, u32[]{:S(2)}, u32[]{:S(2)}) %collective-permute-start.10) | collective-permute-done | bytes 393248 | tf_op jit(solution)/shard_map/ppermute | solution.py:57
  35.5 4.1 %shard_map.92 = (bf16[192,768]{1,0:T(8,128)(2,1)}, bf16[192,768]{1,0:T(8,128)(2,1)S(1)}, bf16[192,768]{1,0:T(8,128)(2,1)S(1)}, f32[192,768]{1,0:T(8,128)S(1)}) custom-call(bf16[1024,768]{1,0:T(8,128)(2,1)S(1)} %shard_map.86.own_ref, bf16[1024,768]{1,0:T(8,128)(2,1)S(1)} %collective-permute-done.2.other_ref, bf16[192,1024]{1,0:T(8,128)(2,1)S(1)} %copy-done.16, ...), custom_call_target="tpu_custom_call" | custom-call | flops 1024 | bytes 1024 | tf_op jit(solution)/shard_map/pallas_call | solution.py:151
  41.8 1.9 collective-permute-start.17
  44.4 2.9 %multiply_reduce_fusion = f32[1536]{0:T(1024)S(1)} fusion(f32[768,1536]{1,0:T(8,128)} %param.9), kind=kLoop, calls=%fused_computation | loop fusion | flops 2357760 | bytes 4724736 | tf_op jit(solution)/shard_map/reduce_sum | solution.py:409
  47.3 3.6 %collective-permute-done.17 = bf16[192,768]{1,0:T(8,128)(2,1)} collective-permute-done((bf16[192,768]{1,0:T(8,128)(2,1)}, bf16[192,768]{1,0:T(8,128)(2,1)}, u32[]{:S(2)}, u32[]{:S(2)}) %collective-permute-start.17) | collective-permute-done | bytes 294944 | tf_op jit(solution)/shard_map/ppermute | solution.py:57
  52.9 3.6 %collective-permute-start.19 = (f32[896]{0:T(1024)S(1)}, f32[896]{0:T(1024)S(1)}, u32[]{:S(2)}, u32[]{:S(2)}) collective-permute-start(f32[896]{0:T(1024)S(1)} %concatenate.10), channel_id=1, source_target_pairs={{0,1},{1,0},{2,3},{3,2},{4,5},{5,4},{6,7},{7,6},{8,9},{9,8},{10,11... | collective-permute-start | bytes 10760 | tf_op jit(solution)/shard_map/ppermute | solution.py:57
  58.0 2.0 collective-permute-done.18
  64.7 2.0 collective-permute-done.21.refs_2_.refs_4_
  68.6 4.7 %shard_map.93 = (bf16[192,768]{1,0:T(8,128)(2,1)S(1)}, bf16[192,768]{1,0:T(8,128)(2,1)S(1)}, bf16[192,768]{1,0:T(8,128)(2,1)S(1)}, f32[192,768]{1,0:T(8,128)S(1)}) custom-call(bf16[1024,768]{1,0:T(8,128)(2,1)S(1)} %shard_map.86.own_ref, bf16[1024,768]{1,0:T(8,128)(2,1)S(1)} %collective-permute-done.2.other_ref, ...), custom_call_target="tpu_custom_call" | custom-call | flops 1024 | bytes 1024 | tf_op jit(solution)/shard_map/pallas_call | solution.py:151
  73.4 3.6 %collective-permute-done.24.refs_0_ = bf16[4,96,1024]{2,1,0:T(8,128)(2,1)S(1)} collective-permute-done((bf16[4,96,1024]{2,1,0:T(8,128)(2,1)S(1)}, bf16[4,96,1024]{2,1,0:T(8,128)(2,1)S(1)}, u32[]{:S(2)}, u32[]{:S(2)}) %collective-permute-start.24) | collective-permute-done | bytes 786464 | tf_op jit(solution)/shard_map/ppermute | solution.py:57
  78.0 3.3 %collective-permute-done.28 = bf16[192,768]{1,0:T(8,128)(2,1)S(1)} collective-permute-done((bf16[192,768]{1,0:T(8,128)(2,1)S(1)}, bf16[192,768]{1,0:T(8,128)(2,1)S(1)}, u32[]{:S(2)}, u32[]{:S(2)}) %collective-permute-start.28) | collective-permute-done | bytes 294944 | tf_op jit(solution)/shard_map/ppermute | solution.py:57
  81.5 5.3 %shard_map.94 = (bf16[480,768]{1,0:T(8,128)(2,1)S(1)}, bf16[480,768]{1,0:T(8,128)(2,1)S(1)}) custom-call(bf16[1024,768]{1,0:T(8,128)(2,1)S(1)} %shard_map.86.own_ref, bf16[1024,768]{1,0:T(8,128)(2,1)S(1)} %collective-permute-done.2.other_ref, bf16[4,96,1024]{2,1,0:T(8,128)(2,1)S(1)} %collective-permute-done.24.refs_0_, ...), custom_call_target="tpu_custom_call" | custom-call | flops 1024 | bytes 1024 | tf_op jit(solution)/shard_map/pallas_call | solution.py:151
  87.0 2.4 %collective-permute-done.29 = bf16[192,768]{1,0:T(8,128)(2,1)S(1)} collective-permute-done((bf16[192,768]{1,0:T(8,128)(2,1)S(1)}, bf16[192,768]{1,0:T(8,128)(2,1)S(1)}, u32[]{:S(2)}, u32[]{:S(2)}) %collective-permute-start.29) | collective-permute-done | bytes 294944 | tf_op jit(solution)/shard_map/ppermute | solution.py:57
  90.2 3.6 %collective-permute-done.22.refs_0_ = bf16[2,4,96,1024]{3,2,1,0:T(8,128)(2,1)S(1)} collective-permute-done((bf16[2,4,96,1024]{3,2,1,0:T(8,128)(2,1)S(1)}, bf16[2,4,96,1024]{3,2,1,0:T(8,128)(2,1)S(1)}, u32[]{:S(2)}, u32[]{:S(2)}) %collective-permute-start.22) | collective-permute-done | bytes 1572896 | tf_op jit(solution)/shard_map/ppermute | solution.py:57
  94.8 4.8 %collective-permute-done.31 = bf16[480,768]{1,0:T(8,128)(2,1)S(1)} collective-permute-done((bf16[480,768]{1,0:T(8,128)(2,1)S(1)}, bf16[480,768]{1,0:T(8,128)(2,1)S(1)}, u32[]{:S(2)}, u32[]{:S(2)}) %collective-permute-start.31) | collective-permute-done | bytes 737312 | tf_op jit(solution)/shard_map/ppermute | solution.py:57
  102.0 2.5 %collective-permute-start.32 = (bf16[4,96,1024]{2,1,0:T(8,128)(2,1)}, bf16[4,96,1024]{2,1,0:T(8,128)(2,1)S(1)}, u32[]{:S(2)}, u32[]{:S(2)}) collective-permute-start(bf16[4,96,1024]{2,1,0:T(8,128)(2,1)} %get-tuple-element.114), channel_id=1, source_target_pairs={{0,8},{1,25},{2,10},{3,27},{4,12},{5,29},{6,14},{7,31},{8,16},{9,1... | collective-permute-start | bytes 2359304 | tf_op jit(solution)/shard_map/ppermute | solution.py:57
  106.7 2.5 %collective-permute-start.40 = (bf16[480,768]{1,0:T(8,128)(2,1)}, bf16[480,768]{1,0:T(8,128)(2,1)}, u32[]{:S(2)}, u32[]{:S(2)}) collective-permute-start(bf16[480,768]{1,0:T(8,128)(2,1)} %add_convert_fusion.1), channel_id=1, source_target_pairs={{0,2},{1,7},{2,4},{3,1},{4,6},{5,3},{6,0},{7,5},{8,10},{9,15},{10,... | collective-permute-start | bytes 2211848 | tf_op jit(solution)/shard_map/ppermute | solution.py:57
  109.2 5.8 %shard_map.95 = (bf16[480,768]{1,0:T(8,128)(2,1)S(1)}, f32[480,768]{1,0:T(8,128)S(1)}) custom-call(bf16[1024,768]{1,0:T(8,128)(2,1)S(1)} %shard_map.86.own_ref, bf16[1024,768]{1,0:T(8,128)(2,1)S(1)} %collective-permute-done.2.other_ref, bf16[4,96,1024]{2,1,0:T(8,128)(2,1)S(1)} %collective-permute-done.24.refs_0_, ...), custom_call_target="tpu_custom_call" | custom-call | flops 1024 | bytes 1024 | tf_op jit(solution)/shard_map/pallas_call | solution.py:151
  115.1 4.3 %shard_map.96 = (bf16[192,768]{1,0:T(8,128)(2,1)}, bf16[192,768]{1,0:T(8,128)(2,1)S(1)}, bf16[192,768]{1,0:T(8,128)(2,1)S(1)}, f32[192,768]{1,0:T(8,128)S(1)}) custom-call(bf16[1024,768]{1,0:T(8,128)(2,1)S(1)} %shard_map.86.own_ref, bf16[1024,768]{1,0:T(8,128)(2,1)S(1)} %collective-permute-done.2.other_ref, ...), custom_call_target="tpu_custom_call" | custom-call | flops 1024 | bytes 1024 | tf_op jit(solution)/shard_map/pallas_call | solution.py:151
  122.2 2.9 %collective-permute-done.40 = bf16[480,768]{1,0:T(8,128)(2,1)} collective-permute-done((bf16[480,768]{1,0:T(8,128)(2,1)}, bf16[480,768]{1,0:T(8,128)(2,1)}, u32[]{:S(2)}, u32[]{:S(2)}) %collective-permute-start.40) | collective-permute-done | bytes 737312 | tf_op jit(solution)/shard_map/ppermute | solution.py:57
  127.6 5.2 %shard_map.99 = (bf16[192,768]{1,0:T(8,128)(2,1)}, bf16[192,768]{1,0:T(8,128)(2,1)S(1)}, bf16[192,768]{1,0:T(8,128)(2,1)S(1)}, f32[192,768]{1,0:T(8,128)S(1)}) custom-call(bf16[1024,768]{1,0:T(8,128)(2,1)S(1)} %copy-done.1, bf16[1024,768]{1,0:T(8,128)(2,1)S(1)} %copy-done.3, bf16[4,96,1024]{2,1,0:T(8,128)(2,1)S(1)} %copy-done.49, ...), custom_call_target="tpu_custom_call" | custom-call | flops 1024 | bytes 1024 | tf_op jit(solution)/shard_map/pallas_call | solution.py:151
  133.3 6.1 %shard_map.100 = (bf16[288,768]{1,0:T(8,128)(2,1)S(1)}, bf16[288,768]{1,0:T(8,128)(2,1)S(1)}, bf16[288,768]{1,0:T(8,128)(2,1)S(1)}, f32[288,768]{1,0:T(8,128)S(1)}) custom-call(bf16[1024,768]{1,0:T(8,128)(2,1)S(1)} %copy-done.1, bf16[1024,768]{1,0:T(8,128)(2,1)S(1)} %copy-done.3, bf16[2,4,96,1024]{3,2,1,0:T(8,128)(2,1)S(1)} %copy-done.6, ...), custom_call_target="tpu_custom_call" | custom-call | flops 1024 | bytes 1024 | tf_op jit(solution)/shard_map/pallas_call | solution.py:151
  139.4 2.2 %collective-permute-start.41 = (bf16[288,768]{1,0:T(8,128)(2,1)S(1)}, bf16[288,768]{1,0:T(8,128)(2,1)S(1)}, u32[]{:S(2)}, u32[]{:S(2)}) collective-permute-start(bf16[288,768]{1,0:T(8,128)(2,1)S(1)} %get-tuple-element.137), channel_id=1, source_target_pairs={{0,2},{1,7},{2,4},{3,1},{4,6},{5,3},{6,0},{7,5},{8,10},{9,15},{10,... | collective-permute-start | bytes 1327112 | tf_op jit(solution)/shard_map/ppermute | solution.py:57
  141.7 2.4 %collective-permute-start.47 = (bf16[192,768]{1,0:T(8,128)(2,1)S(1)}, bf16[192,768]{1,0:T(8,128)(2,1)S(1)}, u32[]{:S(2)}, u32[]{:S(2)}) collective-permute-start(bf16[192,768]{1,0:T(8,128)(2,1)S(1)} %add_convert_fusion.7.refs_5_), channel_id=1, source_target_pairs={{0,2},{1,7},{2,4},{3,1},{4,6},{5,3},{6,0},{7,5},{8,10},{9,15},{10,... | collective-permute-start | bytes 884744 | tf_op jit(solution)/shard_map/ppermute | solution.py:57
  145.8 6.3 %collective-permute-done.47 = bf16[192,768]{1,0:T(8,128)(2,1)S(1)} collective-permute-done((bf16[192,768]{1,0:T(8,128)(2,1)S(1)}, bf16[192,768]{1,0:T(8,128)(2,1)S(1)}, u32[]{:S(2)}, u32[]{:S(2)}) %collective-permute-start.47) | collective-permute-done | bytes 294944 | tf_op jit(solution)/shard_map/ppermute | solution.py:57
  153.4 2.5 %collective-permute-start.48 = (bf16[192,768]{1,0:T(8,128)(2,1)S(1)}, bf16[192,768]{1,0:T(8,128)(2,1)S(1)}, u32[]{:S(2)}, u32[]{:S(2)}) collective-permute-start(bf16[192,768]{1,0:T(8,128)(2,1)S(1)} %add_convert_fusion.5), channel_id=1, source_target_pairs={{0,2},{1,7},{2,4},{3,1},{4,6},{5,3},{6,0},{7,5},{8,10},{9,15},{10,... | collective-permute-start | bytes 884744 | tf_op jit(solution)/shard_map/ppermute | solution.py:57
  155.9 9.1 %collective-permute-done.48.got_ref = bf16[192,768]{1,0:T(8,128)(2,1)S(1)} collective-permute-done((bf16[192,768]{1,0:T(8,128)(2,1)S(1)}, bf16[192,768]{1,0:T(8,128)(2,1)S(1)}, u32[]{:S(2)}, u32[]{:S(2)}) %collective-permute-start.48) | collective-permute-done | bytes 294944 | tf_op jit(solution)/shard_map/ppermute | solution.py:57
  165.3 2.9 %collective-permute-done.46 = bf16[192,768]{1,0:T(8,128)(2,1)S(1)} collective-permute-done((bf16[192,768]{1,0:T(8,128)(2,1)S(1)}, bf16[192,768]{1,0:T(8,128)(2,1)S(1)}, u32[]{:S(2)}, u32[]{:S(2)}) %collective-permute-start.46) | collective-permute-done | bytes 294944 | tf_op jit(solution)/shard_map/ppermute | solution.py:57
  168.5 2.2 %collective-permute-start.49 = (bf16[192,768]{1,0:T(8,128)(2,1)S(1)}, bf16[192,768]{1,0:T(8,128)(2,1)S(1)}, u32[]{:S(2)}, u32[]{:S(2)}) collective-permute-start(bf16[192,768]{1,0:T(8,128)(2,1)S(1)} %add_convert_fusion.4), channel_id=1, source_target_pairs={{0,2},{1,7},{2,4},{3,1},{4,6},{5,3},{6,0},{7,5},{8,10},{9,15},{10,... | collective-permute-start | bytes 884744 | tf_op jit(solution)/shard_map/ppermute | solution.py:57
  170.7 10.4 %collective-permute-done.49.got_ref = bf16[192,768]{1,0:T(8,128)(2,1)S(1)} collective-permute-done((bf16[192,768]{1,0:T(8,128)(2,1)S(1)}, bf16[192,768]{1,0:T(8,128)(2,1)S(1)}, u32[]{:S(2)}, u32[]{:S(2)}) %collective-permute-start.49) | collective-permute-done | bytes 294944 | tf_op jit(solution)/shard_map/ppermute | solution.py:57
  183.0 2.5 %collective-permute-start.52 = (f32[1,1664]{1,0:T(1,128)S(1)}, f32[1,1664]{1,0:T(1,128)S(1)}, u32[]{:S(2)}, u32[]{:S(2)}) collective-permute-start(f32[1,1664]{1,0:T(1,128)S(1)} %constant_dynamic-update-slice_fusion), channel_id=1, source_target_pairs={{0,6},{1,3},{2,0},{3,5},{4,2},{5,7},{6,4},{7,1},{8,14},{9,11},{10,... | collective-permute-start | bytes 19976 | tf_op jit(solution)/shard_map/ppermute | solution.py:57
  189.0 2.0 shard_map.105
  191.0 2.1 collective-permute-start.55
  193.7 2.3 %collective-permute-start.57 = (f32[1,1024]{1,0:T(1,128)S(1)}, f32[1,1024]{1,0:T(1,128)S(1)}, u32[]{:S(2)}, u32[]{:S(2)}) collective-permute-start(f32[1,1024]{1,0:T(1,128)S(1)} %get-tuple-element.164), channel_id=1, source_target_pairs={{0,24},{1,9},{2,26},{3,11},{4,28},{5,13},{6,30},{7,15},{8,0},{9,17... | collective-permute-start | bytes 12296 | tf_op jit(solution)/shard_map/ppermute | solution.py:57
  196.1 2.2 %collective-permute-done.56 = f32[1,1024]{1,0:T(1,128)S(1)} collective-permute-done((f32[1,1024]{1,0:T(1,128)S(1)}, f32[1,1024]{1,0:T(1,128)S(1)}, u32[]{:S(2)}, u32[]{:S(2)}) %collective-permute-start.56) | collective-permute-done | bytes 4128 | tf_op jit(solution)/shard_map/ppermute | solution.py:57
  199.1 1.7 collective-permute-start.59
  200.8 2.3 %collective-permute-start.60 = (f32[1,1024]{1,0:T(1,128)S(1)}, f32[1,1024]{1,0:T(1,128)S(1)}, u32[]{:S(2)}, u32[]{:S(2)}) collective-permute-start(f32[1,1024]{1,0:T(1,128)S(1)} %add_add_fusion.2), channel_id=1, source_target_pairs={{0,96},{1,33},{2,98},{3,35},{4,100},{5,37},{6,102},{7,39},{8,104},... | collective-permute-start | bytes 12296 | tf_op jit(solution)/shard_map/ppermute | solution.py:57
  204.4 1.7 copy-done.13
  206.1 3.5 %shard_map.106 = (f32[768,1536]{1,0:T(8,128)}, f32[1,768]{1,0:T(1,128)S(1)}) custom-call(f32[1,1024]{1,0:T(1,128)S(1)} %add_add_fusion.1.summed_ref, f32[1,128]{1,0:T(1,128)S(1)} %slice.20.row_total_ref, f32[1,1536]{1,0:T(1,128)S(1)} %get-tuple-element.165.clip_ref, f32[1,1536]{1,0:T(1,128)S(1)} %get-tuple-element.166.column_ref, ...), custom_call_target="tpu_custom_call" | custom-call | flops 1024 | bytes 1024 | tf_op jit(solution)/shard_map/pallas_call | solution.py:337
  (246 shorter events, 49.7 us)
Async XLA Ops:
  2.9 5.2 %collective-permute-start.1 = (bf16[192,1024]{1,0:T(8,128)(2,1)}, bf16[192,1024]{1,0:T(8,128)(2,1)S(1)}, u32[]{:S(2)}, u32[]{:S(2)}) collective-permute-start(bf16[192,1024]{1,0:T(8,128)(2,1)} %get-tuple-element.87.refs_0_), channel_id=1, source_target_pairs={{0,1},{1,0},{2,3},{3,2},{4,5},{5,4},{6,7},{7,6},{8,9},{9,8},{10,11... | collective-permute-start | bytes 1179656 | tf_op jit(solution)/shard_map/ppermute | solution.py:57
  3.4 15.1 %collective-permute-start.3 = (bf16[192,1024]{1,0:T(8,128)(2,1)}, bf16[192,1024]{1,0:T(8,128)(2,1)S(1)}, u32[]{:S(2)}, u32[]{:S(2)}) collective-permute-start(bf16[192,1024]{1,0:T(8,128)(2,1)} %get-tuple-element.86.refs_0_), channel_id=1, source_target_pairs={{0,32},{1,97},{2,34},{3,99},{4,36},{5,101},{6,38},{7,103},{8,40},{... | collective-permute-start | bytes 1179656 | tf_op jit(solution)/shard_map/ppermute | solution.py:57
  5.1 13.5 %collective-permute-start.4 = (bf16[192,1024]{1,0:T(8,128)(2,1)}, bf16[192,1024]{1,0:T(8,128)(2,1)S(1)}, u32[]{:S(2)}, u32[]{:S(2)}) collective-permute-start(bf16[192,1024]{1,0:T(8,128)(2,1)} %get-tuple-element.87.refs_0_), channel_id=1, source_target_pairs={{0,8},{1,25},{2,10},{3,27},{4,12},{5,29},{6,14},{7,31},{8,16},{9,1... | collective-permute-start | bytes 1179656 | tf_op jit(solution)/shard_map/ppermute | solution.py:57
  6.6 12.0 %collective-permute-start.5 = (bf16[192,1024]{1,0:T(8,128)(2,1)S(1)}, bf16[192,1024]{1,0:T(8,128)(2,1)S(1)}, u32[]{:S(2)}, u32[]{:S(2)}) collective-permute-start(bf16[192,1024]{1,0:T(8,128)(2,1)S(1)} %collective-permute-done.refs_0_.refs_4_.refs_1_), channel_id=1, source_target_pairs={{0,32},{1,97},{2,34},{3,99},{4,36},{5,101},{6,38},{7,103},{8,40},{... | collective-permute-start | bytes 1179656 | tf_op jit(solution)/shard_map/ppermute | solution.py:57
  8.1 10.4 %collective-permute-start.6 = (bf16[192,1024]{1,0:T(8,128)(2,1)S(1)}, bf16[192,1024]{1,0:T(8,128)(2,1)S(1)}, u32[]{:S(2)}, u32[]{:S(2)}) collective-permute-start(bf16[192,1024]{1,0:T(8,128)(2,1)S(1)} %collective-permute-done.1.refs_1_.refs_4_), channel_id=1, source_target_pairs={{0,8},{1,25},{2,10},{3,27},{4,12},{5,29},{6,14},{7,31},{8,16},{9,1... | collective-permute-start | bytes 1179656 | tf_op jit(solution)/shard_map/ppermute | solution.py:57
  19.4 16.0 %collective-permute-start.2 = (bf16[1024,768]{1,0:T(8,128)(2,1)S(1)}, bf16[1024,768]{1,0:T(8,128)(2,1)S(1)}, u32[]{:S(2)}, u32[]{:S(2)}) collective-permute-start(bf16[1024,768]{1,0:T(8,128)(2,1)S(1)} %shard_map.87), channel_id=1, source_target_pairs={{0,1},{1,0},{2,3},{3,2},{4,5},{5,4},{6,7},{7,6},{8,9},{9,8},{10,11... | collective-permute-start | bytes 4718600 | tf_op jit(solution)/shard_map/ppermute | solution.py:57
  19.8 9.0 %collective-permute-start.10 = (bf16[192,1024]{1,0:T(8,128)(2,1)S(1)}, bf16[192,1024]{1,0:T(8,128)(2,1)S(1)}, u32[]{:S(2)}, u32[]{:S(2)}) collective-permute-start(bf16[192,1024]{1,0:T(8,128)(2,1)S(1)} %collective-permute-done.3.refs_1_.refs_2_), channel_id=1, source_target_pairs={{0,32},{1,97},{2,34},{3,99},{4,36},{5,101},{6,38},{7,103},{8,40},{... | collective-permute-start | bytes 1179656 | tf_op jit(solution)/shard_map/ppermute | solution.py:57
  20.6 9.0 %collective-permute-start.11 = (bf16[192,1024]{1,0:T(8,128)(2,1)S(1)}, bf16[192,1024]{1,0:T(8,128)(2,1)S(1)}, u32[]{:S(2)}, u32[]{:S(2)}) collective-permute-start(bf16[192,1024]{1,0:T(8,128)(2,1)S(1)} %collective-permute-done.4.refs_1_), channel_id=1, source_target_pairs={{0,8},{1,25},{2,10},{3,27},{4,12},{5,29},{6,14},{7,31},{8,16},{9,1... | collective-permute-start | bytes 1179656 | tf_op jit(solution)/shard_map/ppermute | solution.py:57
  21.8 7.8 %collective-permute-start.9 = (bf16[192,1024]{1,0:T(8,128)(2,1)S(1)}, bf16[192,1024]{1,0:T(8,128)(2,1)S(1)}, u32[]{:S(2)}, u32[]{:S(2)}) collective-permute-start(bf16[192,1024]{1,0:T(8,128)(2,1)S(1)} %collective-permute-done.5.refs_5_.refs_3_), channel_id=1, source_target_pairs={{0,1},{1,0},{2,3},{3,2},{4,5},{5,4},{6,7},{7,6},{8,9},{9,8},{10,11... | collective-permute-start | bytes 1179656 | tf_op jit(solution)/shard_map/ppermute | solution.py:57
  22.6 6.9 %collective-permute-start.12 = (bf16[192,1024]{1,0:T(8,128)(2,1)S(1)}, bf16[192,1024]{1,0:T(8,128)(2,1)S(1)}, u32[]{:S(2)}, u32[]{:S(2)}) collective-permute-start(bf16[192,1024]{1,0:T(8,128)(2,1)S(1)} %collective-permute-done.6.refs_5_), channel_id=1, source_target_pairs={{0,1},{1,0},{2,3},{3,2},{4,5},{5,4},{6,7},{7,6},{8,9},{9,8},{10,11... | collective-permute-start | bytes 1179656 | tf_op jit(solution)/shard_map/ppermute | solution.py:57
  32.8 28.0 %collective-permute-start.16 = (bf16[2,4,96,1024]{3,2,1,0:T(8,128)(2,1)}, bf16[2,4,96,1024]{3,2,1,0:T(8,128)(2,1)}, u32[]{:S(2)}, u32[]{:S(2)}) collective-permute-start(bf16[2,4,96,1024]{3,2,1,0:T(8,128)(2,1)} %shard_map.91.refs_9_.refs_2_), channel_id=1, source_target_pairs={{0,32},{1,97},{2,34},{3,99},{4,36},{5,101},{6,38},{7,103},{8,40},{... | collective-permute-start | bytes 4718600 | tf_op jit(solution)/shard_map/ppermute | solution.py:57
  35.4 25.4 %collective-permute-start.15 = (bf16[2,4,96,1024]{3,2,1,0:T(8,128)(2,1)}, bf16[2,4,96,1024]{3,2,1,0:T(8,128)(2,1)}, u32[]{:S(2)}, u32[]{:S(2)}) collective-permute-start(bf16[2,4,96,1024]{3,2,1,0:T(8,128)(2,1)} %shard_map.90.refs_8_), channel_id=1, source_target_pairs={{0,8},{1,25},{2,10},{3,27},{4,12},{5,29},{6,14},{7,31},{8,16},{9,1... | collective-permute-start | bytes 4718600 | tf_op jit(solution)/shard_map/ppermute | solution.py:57
  41.8 9.1 %collective-permute-start.17 = (bf16[192,768]{1,0:T(8,128)(2,1)}, bf16[192,768]{1,0:T(8,128)(2,1)}, u32[]{:S(2)}, u32[]{:S(2)}) collective-permute-start(bf16[192,768]{1,0:T(8,128)(2,1)} %get-tuple-element.98), channel_id=1, source_target_pairs={{0,2},{1,7},{2,4},{3,1},{4,6},{5,3},{6,0},{7,5},{8,10},{9,15},{10,... | collective-permute-start | bytes 884744 | tf_op jit(solution)/shard_map/ppermute | solution.py:57
  52.0 8.0 %collective-permute-start.18 = (bf16[192,768]{1,0:T(8,128)(2,1)S(1)}, bf16[192,768]{1,0:T(8,128)(2,1)S(1)}, u32[]{:S(2)}, u32[]{:S(2)}) collective-permute-start(bf16[192,768]{1,0:T(8,128)(2,1)S(1)} %add_convert_fusion.11), channel_id=1, source_target_pairs={{0,2},{1,7},{2,4},{3,1},{4,6},{5,3},{6,0},{7,5},{8,10},{9,15},{10,... | collective-permute-start | bytes 884744 | tf_op jit(solution)/shard_map/ppermute | solution.py:57
  60.8 5.9 %collective-permute-start.21 = (bf16[2,4,96,1024]{3,2,1,0:T(8,128)(2,1)}, bf16[2,4,96,1024]{3,2,1,0:T(8,128)(2,1)S(1)}, u32[]{:S(2)}, u32[]{:S(2)}) collective-permute-start(bf16[2,4,96,1024]{3,2,1,0:T(8,128)(2,1)} %collective-permute-done.16.refs_3_), channel_id=1, source_target_pairs={{0,1},{1,0},{2,3},{3,2},{4,5},{5,4},{6,7},{7,6},{8,9},{9,8},{10,11... | collective-permute-start | bytes 4718600 | tf_op jit(solution)/shard_map/ppermute | solution.py:57
  63.7 13.3 %collective-permute-start.24 = (bf16[4,96,1024]{2,1,0:T(8,128)(2,1)S(1)}, bf16[4,96,1024]{2,1,0:T(8,128)(2,1)S(1)}, u32[]{:S(2)}, u32[]{:S(2)}) collective-permute-start(bf16[4,96,1024]{2,1,0:T(8,128)(2,1)S(1)} %slice_bitcast_fusion.3), channel_id=1, source_target_pairs={{0,8},{1,25},{2,10},{3,27},{4,12},{5,29},{6,14},{7,31},{8,16},{9,1... | collective-permute-start | bytes 2359304 | tf_op jit(solution)/shard_map/ppermute | solution.py:57
  64.3 13.2 %collective-permute-start.25 = (bf16[4,96,1024]{2,1,0:T(8,128)(2,1)S(1)}, bf16[4,96,1024]{2,1,0:T(8,128)(2,1)S(1)}, u32[]{:S(2)}, u32[]{:S(2)}) collective-permute-start(bf16[4,96,1024]{2,1,0:T(8,128)(2,1)S(1)} %slice_bitcast_fusion.2), channel_id=1, source_target_pairs={{0,32},{1,97},{2,34},{3,99},{4,36},{5,101},{6,38},{7,103},{8,40},{... | collective-permute-start | bytes 2359304 | tf_op jit(solution)/shard_map/ppermute | solution.py:57
  66.6 27.1 %collective-permute-start.22 = (bf16[2,4,96,1024]{3,2,1,0:T(8,128)(2,1)S(1)}, bf16[2,4,96,1024]{3,2,1,0:T(8,128)(2,1)S(1)}, u32[]{:S(2)}, u32[]{:S(2)}) collective-permute-start(bf16[2,4,96,1024]{3,2,1,0:T(8,128)(2,1)S(1)} %shard_map.88), channel_id=1, source_target_pairs={{0,8},{1,25},{2,10},{3,27},{4,12},{5,29},{6,14},{7,31},{8,16},{9,1... | collective-permute-start | bytes 4718600 | tf_op jit(solution)/shard_map/ppermute | solution.py:57
  67.2 27.1 %collective-permute-start.23 = (bf16[2,4,96,1024]{3,2,1,0:T(8,128)(2,1)S(1)}, bf16[2,4,96,1024]{3,2,1,0:T(8,128)(2,1)S(1)}, u32[]{:S(2)}, u32[]{:S(2)}) collective-permute-start(bf16[2,4,96,1024]{3,2,1,0:T(8,128)(2,1)S(1)} %shard_map.89.refs_2_.refs_0_), channel_id=1, source_target_pairs={{0,32},{1,97},{2,34},{3,99},{4,36},{5,101},{6,38},{7,103},{8,40},{... | collective-permute-start | bytes 4718600 | tf_op jit(solution)/shard_map/ppermute | solution.py:57
  73.3 8.0 %collective-permute-start.28 = (bf16[192,768]{1,0:T(8,128)(2,1)S(1)}, bf16[192,768]{1,0:T(8,128)(2,1)S(1)}, u32[]{:S(2)}, u32[]{:S(2)}) collective-permute-start(bf16[192,768]{1,0:T(8,128)(2,1)S(1)} %get-tuple-element.104), channel_id=1, source_target_pairs={{0,2},{1,7},{2,4},{3,1},{4,6},{5,3},{6,0},{7,5},{8,10},{9,15},{10,... | collective-permute-start | bytes 884744 | tf_op jit(solution)/shard_map/ppermute | solution.py:57
  81.4 8.0 %collective-permute-start.29 = (bf16[192,768]{1,0:T(8,128)(2,1)S(1)}, bf16[192,768]{1,0:T(8,128)(2,1)S(1)}, u32[]{:S(2)}, u32[]{:S(2)}) collective-permute-start(bf16[192,768]{1,0:T(8,128)(2,1)S(1)} %add_convert_fusion.9.refs_7_), channel_id=1, source_target_pairs={{0,2},{1,7},{2,4},{3,1},{4,6},{5,3},{6,0},{7,5},{8,10},{9,15},{10,... | collective-permute-start | bytes 884744 | tf_op jit(solution)/shard_map/ppermute | solution.py:57
  86.8 12.7 %collective-permute-start.31 = (bf16[480,768]{1,0:T(8,128)(2,1)S(1)}, bf16[480,768]{1,0:T(8,128)(2,1)S(1)}, u32[]{:S(2)}, u32[]{:S(2)}) collective-permute-start(bf16[480,768]{1,0:T(8,128)(2,1)S(1)} %get-tuple-element.108), channel_id=1, source_target_pairs={{0,2},{1,7},{2,4},{3,1},{4,6},{5,3},{6,0},{7,5},{8,10},{9,15},{10,... | collective-permute-start | bytes 2211848 | tf_op jit(solution)/shard_map/ppermute | solution.py:57
  94.3 11.4 %collective-permute-start.30 = (bf16[2,4,96,1024]{3,2,1,0:T(8,128)(2,1)S(1)}, bf16[2,4,96,1024]{3,2,1,0:T(8,128)(2,1)S(1)}, u32[]{:S(2)}, u32[]{:S(2)}) collective-permute-start(bf16[2,4,96,1024]{3,2,1,0:T(8,128)(2,1)S(1)} %collective-permute-done.23.refs_3_.refs_1_), channel_id=1, source_target_pairs={{0,1},{1,0},{2,3},{3,2},{4,5},{5,4},{6,7},{7,6},{8,9},{9,8},{10,11... | collective-permute-start | bytes 4718600 | tf_op jit(solution)/shard_map/ppermute | solution.py:57
  94.7 10.9 %collective-permute-start.34 = (bf16[2,4,96,1024]{3,2,1,0:T(8,128)(2,1)S(1)}, bf16[2,4,96,1024]{3,2,1,0:T(8,128)(2,1)S(1)}, u32[]{:S(2)}, u32[]{:S(2)}) collective-permute-start(bf16[2,4,96,1024]{3,2,1,0:T(8,128)(2,1)S(1)} %collective-permute-done.22.refs_0_), channel_id=1, source_target_pairs={{0,1},{1,0},{2,3},{3,2},{4,5},{5,4},{6,7},{7,6},{8,9},{9,8},{10,11... | collective-permute-start | bytes 4718600 | tf_op jit(solution)/shard_map/ppermute | solution.py:57
  102.0 18.9 %collective-permute-start.32 = (bf16[4,96,1024]{2,1,0:T(8,128)(2,1)}, bf16[4,96,1024]{2,1,0:T(8,128)(2,1)S(1)}, u32[]{:S(2)}, u32[]{:S(2)}) collective-permute-start(bf16[4,96,1024]{2,1,0:T(8,128)(2,1)} %get-tuple-element.114), channel_id=1, source_target_pairs={{0,8},{1,25},{2,10},{3,27},{4,12},{5,29},{6,14},{7,31},{8,16},{9,1... | collective-permute-start | bytes 2359304 | tf_op jit(solution)/shard_map/ppermute | solution.py:57
  104.5 16.4 %collective-permute-start.33 = (bf16[4,96,1024]{2,1,0:T(8,128)(2,1)}, bf16[4,96,1024]{2,1,0:T(8,128)(2,1)S(1)}, u32[]{:S(2)}, u32[]{:S(2)}) collective-permute-start(bf16[4,96,1024]{2,1,0:T(8,128)(2,1)} %get-tuple-element.115), channel_id=1, source_target_pairs={{0,32},{1,97},{2,34},{3,99},{4,36},{5,101},{6,38},{7,103},{8,40},{... | collective-permute-start | bytes 2359304 | tf_op jit(solution)/shard_map/ppermute | solution.py:57
  105.7 14.5 %collective-permute-start.36 = (bf16[192,768]{1,0:T(8,128)(2,1)}, bf16[192,768]{1,0:T(8,128)(2,1)S(1)}, u32[]{:S(2)}, u32[]{:S(2)}) collective-permute-start(bf16[192,768]{1,0:T(8,128)(2,1)} %add_convert_fusion.10), channel_id=1, source_target_pairs={{0,2},{1,7},{2,4},{3,1},{4,6},{5,3},{6,0},{7,5},{8,10},{9,15},{10,... | collective-permute-start | bytes 884744 | tf_op jit(solution)/shard_map/ppermute | solution.py:57
  105.8 14.7 %collective-permute-start.35 = (bf16[192,768]{1,0:T(8,128)(2,1)}, bf16[192,768]{1,0:T(8,128)(2,1)S(1)}, u32[]{:S(2)}, u32[]{:S(2)}) collective-permute-start(bf16[192,768]{1,0:T(8,128)(2,1)} %add_convert_fusion.8), channel_id=1, source_target_pairs={{0,2},{1,7},{2,4},{3,1},{4,6},{5,3},{6,0},{7,5},{8,10},{9,15},{10,... | collective-permute-start | bytes 884744 | tf_op jit(solution)/shard_map/ppermute | solution.py:57
  106.7 18.3 %collective-permute-start.40 = (bf16[480,768]{1,0:T(8,128)(2,1)}, bf16[480,768]{1,0:T(8,128)(2,1)}, u32[]{:S(2)}, u32[]{:S(2)}) collective-permute-start(bf16[480,768]{1,0:T(8,128)(2,1)} %add_convert_fusion.1), channel_id=1, source_target_pairs={{0,2},{1,7},{2,4},{3,1},{4,6},{5,3},{6,0},{7,5},{8,10},{9,15},{10,... | collective-permute-start | bytes 2211848 | tf_op jit(solution)/shard_map/ppermute | solution.py:57
  120.8 5.6 %collective-permute-start.37 = (bf16[4,96,1024]{2,1,0:T(8,128)(2,1)S(1)}, bf16[4,96,1024]{2,1,0:T(8,128)(2,1)S(1)}, u32[]{:S(2)}, u32[]{:S(2)}) collective-permute-start(bf16[4,96,1024]{2,1,0:T(8,128)(2,1)S(1)} %collective-permute-done.33.refs_5_.refs_3_), channel_id=1, source_target_pairs={{0,1},{1,0},{2,3},{3,2},{4,5},{5,4},{6,7},{7,6},{8,9},{9,8},{10,11... | collective-permute-start | bytes 2359304 | tf_op jit(solution)/shard_map/ppermute | solution.py:57
  120.9 5.5 %collective-permute-start.39 = (bf16[4,96,1024]{2,1,0:T(8,128)(2,1)S(1)}, bf16[4,96,1024]{2,1,0:T(8,128)(2,1)S(1)}, u32[]{:S(2)}, u32[]{:S(2)}) collective-permute-start(bf16[4,96,1024]{2,1,0:T(8,128)(2,1)S(1)} %collective-permute-done.32.refs_0_), channel_id=1, source_target_pairs={{0,1},{1,0},{2,3},{3,2},{4,5},{5,4},{6,7},{7,6},{8,9},{9,8},{10,11... | collective-permute-start | bytes 2359304 | tf_op jit(solution)/shard_map/ppermute | solution.py:57
  121.4 11.8 %collective-permute-start.38 = (bf16[192,768]{1,0:T(8,128)(2,1)}, bf16[192,768]{1,0:T(8,128)(2,1)S(1)}, u32[]{:S(2)}, u32[]{:S(2)}) collective-permute-start(bf16[192,768]{1,0:T(8,128)(2,1)} %get-tuple-element.117), channel_id=1, source_target_pairs={{0,2},{1,7},{2,4},{3,1},{4,6},{5,3},{6,0},{7,5},{8,10},{9,15},{10,... | collective-permute-start | bytes 884744 | tf_op jit(solution)/shard_map/ppermute | solution.py:57
  126.4 18.8 %collective-permute-start.42 = (bf16[480,768]{1,0:T(8,128)(2,1)S(1)}, bf16[480,768]{1,0:T(8,128)(2,1)S(1)}, u32[]{:S(2)}, u32[]{:S(2)}) collective-permute-start(bf16[480,768]{1,0:T(8,128)(2,1)S(1)} %add_convert_fusion.refs_7_), channel_id=1, source_target_pairs={{0,2},{1,7},{2,4},{3,1},{4,6},{5,3},{6,0},{7,5},{8,10},{9,15},{10,... | collective-permute-start | bytes 2211848 | tf_op jit(solution)/shard_map/ppermute | solution.py:57
  132.9 11.2 %collective-permute-start.43 = (bf16[192,768]{1,0:T(8,128)(2,1)}, bf16[192,768]{1,0:T(8,128)(2,1)}, u32[]{:S(2)}, u32[]{:S(2)}) collective-permute-start(bf16[192,768]{1,0:T(8,128)(2,1)} %get-tuple-element.132), channel_id=1, source_target_pairs={{0,2},{1,7},{2,4},{3,1},{4,6},{5,3},{6,0},{7,5},{8,10},{9,15},{10,... | collective-permute-start | bytes 884744 | tf_op jit(solution)/shard_map/ppermute | solution.py:57
  139.4 12.7 %collective-permute-start.41 = (bf16[288,768]{1,0:T(8,128)(2,1)S(1)}, bf16[288,768]{1,0:T(8,128)(2,1)S(1)}, u32[]{:S(2)}, u32[]{:S(2)}) collective-permute-start(bf16[288,768]{1,0:T(8,128)(2,1)S(1)} %get-tuple-element.137), channel_id=1, source_target_pairs={{0,2},{1,7},{2,4},{3,1},{4,6},{5,3},{6,0},{7,5},{8,10},{9,15},{10,... | collective-permute-start | bytes 1327112 | tf_op jit(solution)/shard_map/ppermute | solution.py:57
  141.7 10.5 %collective-permute-start.47 = (bf16[192,768]{1,0:T(8,128)(2,1)S(1)}, bf16[192,768]{1,0:T(8,128)(2,1)S(1)}, u32[]{:S(2)}, u32[]{:S(2)}) collective-permute-start(bf16[192,768]{1,0:T(8,128)(2,1)S(1)} %add_convert_fusion.7.refs_5_), channel_id=1, source_target_pairs={{0,2},{1,7},{2,4},{3,1},{4,6},{5,3},{6,0},{7,5},{8,10},{9,15},{10,... | collective-permute-start | bytes 884744 | tf_op jit(solution)/shard_map/ppermute | solution.py:57
  152.3 15.9 %collective-permute-start.44 = (bf16[288,768]{1,0:T(8,128)(2,1)S(1)}, bf16[288,768]{1,0:T(8,128)(2,1)S(1)}, u32[]{:S(2)}, u32[]{:S(2)}) collective-permute-start(bf16[288,768]{1,0:T(8,128)(2,1)S(1)} %add_convert_fusion.3), channel_id=1, source_target_pairs={{0,2},{1,7},{2,4},{3,1},{4,6},{5,3},{6,0},{7,5},{8,10},{9,15},{10,... | collective-permute-start | bytes 1327112 | tf_op jit(solution)/shard_map/ppermute | solution.py:57
  153.4 11.7 %collective-permute-start.48 = (bf16[192,768]{1,0:T(8,128)(2,1)S(1)}, bf16[192,768]{1,0:T(8,128)(2,1)S(1)}, u32[]{:S(2)}, u32[]{:S(2)}) collective-permute-start(bf16[192,768]{1,0:T(8,128)(2,1)S(1)} %add_convert_fusion.5), channel_id=1, source_target_pairs={{0,2},{1,7},{2,4},{3,1},{4,6},{5,3},{6,0},{7,5},{8,10},{9,15},{10,... | collective-permute-start | bytes 884744 | tf_op jit(solution)/shard_map/ppermute | solution.py:57
  155.9 12.3 %collective-permute-start.46 = (bf16[192,768]{1,0:T(8,128)(2,1)S(1)}, bf16[192,768]{1,0:T(8,128)(2,1)S(1)}, u32[]{:S(2)}, u32[]{:S(2)}) collective-permute-start(bf16[192,768]{1,0:T(8,128)(2,1)S(1)} %add_convert_fusion.6), channel_id=1, source_target_pairs={{0,2},{1,7},{2,4},{3,1},{4,6},{5,3},{6,0},{7,5},{8,10},{9,15},{10,... | collective-permute-start | bytes 884744 | tf_op jit(solution)/shard_map/ppermute | solution.py:57
  168.3 13.0 %collective-permute-start.45 = (bf16[288,768]{1,0:T(8,128)(2,1)S(1)}, bf16[288,768]{1,0:T(8,128)(2,1)S(1)}, u32[]{:S(2)}, u32[]{:S(2)}) collective-permute-start(bf16[288,768]{1,0:T(8,128)(2,1)S(1)} %add_convert_fusion.2), channel_id=1, source_target_pairs={{0,2},{1,7},{2,4},{3,1},{4,6},{5,3},{6,0},{7,5},{8,10},{9,15},{10,... | collective-permute-start | bytes 1327112 | tf_op jit(solution)/shard_map/ppermute | solution.py:57
  168.5 12.6 %collective-permute-start.49 = (bf16[192,768]{1,0:T(8,128)(2,1)S(1)}, bf16[192,768]{1,0:T(8,128)(2,1)S(1)}, u32[]{:S(2)}, u32[]{:S(2)}) collective-permute-start(bf16[192,768]{1,0:T(8,128)(2,1)S(1)} %add_convert_fusion.4), channel_id=1, source_target_pairs={{0,2},{1,7},{2,4},{3,1},{4,6},{5,3},{6,0},{7,5},{8,10},{9,15},{10,... | collective-permute-start | bytes 884744 | tf_op jit(solution)/shard_map/ppermute | solution.py:57
  181.8 7.2 %collective-permute-start.54 = (f32[768,768]{1,0:T(8,128)S(1)}, f32[768,768]{1,0:T(8,128)S(1)}, u32[]{:S(2)}, u32[]{:S(2)}) collective-permute-start(f32[768,768]{1,0:T(8,128)S(1)} %get-tuple-element.163), channel_id=1, source_target_pairs={{0,1},{1,0},{2,3},{3,2},{4,5},{5,4},{6,7},{7,6},{8,9},{9,8},{10,11... | collective-permute-start | bytes 7077896 | tf_op jit(solution)/shard_map/ppermute | solution.py:57
  181.9 4.9 %collective-permute-start.50 = (f32[1,1664]{1,0:T(1,128)S(1)}, f32[1,1664]{1,0:T(1,128)S(1)}, u32[]{:S(2)}, u32[]{:S(2)}) collective-permute-start(f32[1,1664]{1,0:T(1,128)S(1)} %constant_dynamic-update-slice_fusion), channel_id=1, source_target_pairs={{0,2},{1,7},{2,4},{3,1},{4,6},{5,3},{6,0},{7,5},{8,10},{9,15},{10,... | collective-permute-start | bytes 19976 | tf_op jit(solution)/shard_map/ppermute | solution.py:57
  182.0 5.2 %collective-permute-start.51 = (f32[1,1664]{1,0:T(1,128)S(1)}, f32[1,1664]{1,0:T(1,128)S(1)}, u32[]{:S(2)}, u32[]{:S(2)}) collective-permute-start(f32[1,1664]{1,0:T(1,128)S(1)} %constant_dynamic-update-slice_fusion), channel_id=1, source_target_pairs={{0,4},{1,5},{2,6},{3,7},{4,0},{5,1},{6,2},{7,3},{8,12},{9,13},{10,... | collective-permute-start | bytes 19976 | tf_op jit(solution)/shard_map/ppermute | solution.py:57
  191.0 5.0 %collective-permute-start.55 = (f32[1,1024]{1,0:T(1,128)S(1)}, f32[1,1024]{1,0:T(1,128)S(1)}, u32[]{:S(2)}, u32[]{:S(2)}) collective-permute-start(f32[1,1024]{1,0:T(1,128)S(1)} %get-tuple-element.164), channel_id=1, source_target_pairs={{0,8},{1,25},{2,10},{3,27},{4,12},{5,29},{6,14},{7,31},{8,16},{9,1... | collective-permute-start | bytes 12296 | tf_op jit(solution)/shard_map/ppermute | solution.py:57
  193.1 5.1 %collective-permute-start.56 = (f32[1,1024]{1,0:T(1,128)S(1)}, f32[1,1024]{1,0:T(1,128)S(1)}, u32[]{:S(2)}, u32[]{:S(2)}) collective-permute-start(f32[1,1024]{1,0:T(1,128)S(1)} %get-tuple-element.164), channel_id=1, source_target_pairs={{0,16},{1,17},{2,18},{3,19},{4,20},{5,21},{6,22},{7,23},{8,24},{9,... | collective-permute-start | bytes 12296 | tf_op jit(solution)/shard_map/ppermute | solution.py:57
  198.2 5.5 %collective-permute-start.58 = (f32[1,1024]{1,0:T(1,128)S(1)}, f32[1,1024]{1,0:T(1,128)S(1)}, u32[]{:S(2)}, u32[]{:S(2)}) collective-permute-start(f32[1,1024]{1,0:T(1,128)S(1)} %add_add_fusion.2), channel_id=1, source_target_pairs={{0,32},{1,97},{2,34},{3,99},{4,36},{5,101},{6,38},{7,103},{8,40},{... | collective-permute-start | bytes 12296 | tf_op jit(solution)/shard_map/ppermute | solution.py:57
  199.1 5.1 %collective-permute-start.59 = (f32[1,1024]{1,0:T(1,128)S(1)}, f32[1,1024]{1,0:T(1,128)S(1)}, u32[]{:S(2)}, u32[]{:S(2)}) collective-permute-start(f32[1,1024]{1,0:T(1,128)S(1)} %add_add_fusion.2), channel_id=1, source_target_pairs={{0,64},{1,65},{2,66},{3,67},{4,68},{5,69},{6,70},{7,71},{8,72},{9,... | collective-permute-start | bytes 12296 | tf_op jit(solution)/shard_map/ppermute | solution.py:57
  (73 other events, 668.9 us)

commit v6 on v5

--- a/solution.py
+++ b/solution.py
@@ -455,21 +455,21 @@
     far1_entries = far_entries(q_next, y1, y1_swap, x2, x2_swap, y2, y2_swap)
     far0_3 = add_narrow(far0[2], after(far0_got, near1[0]))
     far0_got = hop(far0_3)
-    far1 = units(far1_entries[:2], waits=(far0_3,))
+    near1_2 = add_narrow(near1[1], near1_got)
+    near1_got = hop(near1_2)
+    far1 = units(far1_entries[:2], waits=(far0_3, near1_2))
     far1_got = hop(far1[0])
-    near1_2 = add_narrow(near1[1], after(near1_got, far1[0]))
-    near1_got = hop(near1_2)
-    last1 = units(far1_entries[2:], waits=(near1_2,))
+    last1 = units(far1_entries[2:], waits=(far1[0],))
     last1_got = hop(last1[0])
     near1_3 = add_narrow(near1[2], after(near1_got, last1[0]))
-    far1_2 = add_narrow(far1[1], after(far1_got, last1[0]))
+    near1_got = hop(near1_3)
+    placed = place_rows(far0[3], after(far0_got, near1_3), far_pieces(0), placed)
+    far1_2 = add_narrow(far1[1], after(far1_got, near1_3))
+    last1_2 = add_narrow(last1[1], after(last1_got, placed[2], far1_2))
+    last1_got = hop(last1_2)
     far1_got = hop(far1_2)
-    near1_got = hop(near1_3)
-    placed = place_rows(far0[3], after(far0_got, far1_2), far_pieces(0), placed)
-    last1_2 = add_narrow(last1[1], after(last1_got, placed[2]))
-    last1_got = hop(last1_2)
     placed = place_rows(near1[3], after(near1_got, last1_2), near_pieces(1), placed)
-    far1_got = hop(add_narrow(far1[2], after(far1_got, placed[2])))
+    far1_got = hop(after(add_narrow(far1[2], far1_got), placed[2]))
     last1_got = hop(add_narrow(last1[2], last1_got))
     placed = place_rows(far1[3], far1_got, far_pieces(1)[:2], placed)
     last_pieces = [(g, low, start - 2 * size, count) for g, low, start, count in far_pieces(1)[2:]]

time: 212 us -> 209 us (0.986)
  starting transfers between devices: 56.2 us -> 50.1 us
  waiting for transfers between devices: 72.6 us -> 77.5 us
    ppermute x61, starting transfers between devices: 56.2 us -> 50.1 us  [send(): return lax.ppermute(value, BOTH, pairs)]
    ppermute x61, waiting for transfers between devices: 72.6 us -> 77.5 us  [send(): return lax.ppermute(value, BOTH, pairs)]
    unnamed x121 -> x125, local copies, waits for them, and re-layouts: 9.86 us -> 11.3 us
  transfers between devices with their start and end apart: 61 -> 61, of which waited for: 26 -> 31; matrix products, arithmetic and copies ran while one was open for 7% -> 7% of each run, Pallas kernels for 22% -> 21%
where the time goes in v6:
time: 209 us; the launch traced here: 208 us
  waiting for transfers between devices  77.5 us (37%)
  Pallas kernels  52.4 us (25%)
  starting transfers between devices  50.1 us (24%)
  local copies, waits for them, and re-layouts  15.5 us (7%)
  other arithmetic  10.6 us (5%)
    ppermute x61, waiting for transfers between devices, send(): return lax.ppermute(value, BOTH, pairs)  77.5 us
    ppermute x61, starting transfers between devices, send(): return lax.ppermute(value, BOTH, pairs)  50.1 us
    pallas_call x7, Pallas kernels, unit_partials(): pl.pallas_call(kernel, out_shape=tuple((jax.ShapeDtypeStruct((rows, HALF)...  34.4 us
    unnamed x125, local copies, waits for them, and re-layouts  11.3 us
    convert_element_type x12, other arithmetic, add_narrow(): return (a.astype(jnp.float32) + b.astype(jnp.float32)).astype(jnp.bfloat16)  5.23 us
    pallas_call x2, Pallas kernels, slope_half(): pl.pallas_call(kernel, out_shape=jax.ShapeDtypeStruct((TOK, HALF), jnp.bf...  5.05 us
  transfers between devices with their start and end apart: 61, of which 31 were waited for; matrix products, arithmetic and copies ran while one was open for 7% of the time, Pallas kernels for 21%

profile of v6, /device:TPU:0, one launch (start us, length us, event | category | flops | bytes accessed | tf_op | source)
XLA Modules:
  0.0 207.9 jit_solution(10380743230290990950)
XLA Ops:
  0.6 2.3 %shard_map.85 = (bf16[192,1024]{1,0:T(8,128)(2,1)}, bf16[192,1024]{1,0:T(8,128)(2,1)}) custom-call(bf16[1024,384]{1,0:T(8,128)(2,1)} %ref.1), custom_call_target="tpu_custom_call" | custom-call | flops 1024 | bytes 1024 | tf_op jit(solution)/shard_map/pallas_call | solution.py:186
  3.4 1.7 collective-permute-start.3
  5.1 1.5 collective-permute-start.4
  6.6 1.6 collective-permute-start.5
  8.2 1.5 collective-permute-start.6
  9.6 1.9 copy-done.8
  11.5 1.9 copy-done.9
  13.4 2.5 %shard_map.86.own_ref = bf16[1024,768]{1,0:T(8,128)(2,1)S(1)} custom-call(bf16[1024,1536]{1,0:T(8,128)(2,1)S(1)} %copy-done.8, bf16[1024,1536]{1,0:T(8,128)(2,1)S(1)} %copy-done.9, bf16[192,1024]{1,0:T(8,128)(2,1)S(1)} %collective-permute-done.refs_0_.refs_4_.refs_1_, bf16[192,1024]{1,0:T(8,128)(2,1)S(1)} %collective-permute-done.1.refs_1_.refs_4_), custom_call_target="tpu_custom_call" | custom-call | flops 1024 | bytes 1024 | tf_op jit(solution)/shard_map/pallas_call | solution.py:89
  16.0 2.5 %shard_map.87 = bf16[1024,768]{1,0:T(8,128)(2,1)S(1)} custom-call(bf16[1024,1536]{1,0:T(8,128)(2,1)S(1)} %copy-done.8, bf16[1024,1536]{1,0:T(8,128)(2,1)S(1)} %copy-done.9, bf16[192,1024]{1,0:T(8,128)(2,1)S(1)} %collective-permute-done.refs_0_.refs_4_.refs_1_, bf16[192,1024]{1,0:T(8,128)(2,1)S(1)} %collective-permute-done.1.refs_1_.refs_4_), custom_call_target="tpu_custom_call" | custom-call | flops 1024 | bytes 1024 | tf_op jit(solution)/shard_map/pallas_call | solution.py:89
  22.7 6.1 %collective-permute-done.10.refs_3_.refs_6_ = bf16[192,1024]{1,0:T(8,128)(2,1)S(1)} collective-permute-done((bf16[192,1024]{1,0:T(8,128)(2,1)S(1)}, bf16[192,1024]{1,0:T(8,128)(2,1)S(1)}, u32[]{:S(2)}, u32[]{:S(2)}) %collective-permute-start.10) | collective-permute-done | bytes 393248 | tf_op jit(solution)/shard_map/ppermute | solution.py:57
  35.6 4.1 %shard_map.92 = (bf16[192,768]{1,0:T(8,128)(2,1)}, bf16[192,768]{1,0:T(8,128)(2,1)S(1)}, bf16[192,768]{1,0:T(8,128)(2,1)S(1)}, f32[192,768]{1,0:T(8,128)S(1)}) custom-call(bf16[1024,768]{1,0:T(8,128)(2,1)S(1)} %shard_map.86.own_ref, bf16[1024,768]{1,0:T(8,128)(2,1)S(1)} %collective-permute-done.2.other_ref, bf16[192,1024]{1,0:T(8,128)(2,1)S(1)} %copy-done.16, ...), custom_call_target="tpu_custom_call" | custom-call | flops 1024 | bytes 1024 | tf_op jit(solution)/shard_map/pallas_call | solution.py:151
  41.9 1.9 collective-permute-start.17
  44.5 2.9 %multiply_reduce_fusion = f32[1536]{0:T(1024)S(1)} fusion(f32[768,1536]{1,0:T(8,128)} %param.9), kind=kLoop, calls=%fused_computation | loop fusion | flops 2357760 | bytes 4724736 | tf_op jit(solution)/shard_map/reduce_sum | solution.py:409
  47.4 3.6 %collective-permute-done.17 = bf16[192,768]{1,0:T(8,128)(2,1)} collective-permute-done((bf16[192,768]{1,0:T(8,128)(2,1)}, bf16[192,768]{1,0:T(8,128)(2,1)}, u32[]{:S(2)}, u32[]{:S(2)}) %collective-permute-start.17) | collective-permute-done | bytes 294944 | tf_op jit(solution)/shard_map/ppermute | solution.py:57
  52.9 3.6 %collective-permute-start.19 = (f32[896]{0:T(1024)S(1)}, f32[896]{0:T(1024)S(1)}, u32[]{:S(2)}, u32[]{:S(2)}) collective-permute-start(f32[896]{0:T(1024)S(1)} %concatenate.10), channel_id=1, source_target_pairs={{0,1},{1,0},{2,3},{3,2},{4,5},{5,4},{6,7},{7,6},{8,9},{9,8},{10,11... | collective-permute-start | bytes 10760 | tf_op jit(solution)/shard_map/ppermute | solution.py:57
  58.1 2.0 collective-permute-done.18
  66.9 2.3 %collective-permute-start.23 = (bf16[2,4,96,1024]{3,2,1,0:T(8,128)(2,1)S(1)}, bf16[2,4,96,1024]{3,2,1,0:T(8,128)(2,1)S(1)}, u32[]{:S(2)}, u32[]{:S(2)}) collective-permute-start(bf16[2,4,96,1024]{3,2,1,0:T(8,128)(2,1)S(1)} %shard_map.89.refs_2_.refs_0_), channel_id=1, source_target_pairs={{0,32},{1,97},{2,34},{3,99},{4,36},{5,101},{6,38},{7,103},{8,40},{... | collective-permute-start | bytes 4718600 | tf_op jit(solution)/shard_map/ppermute | solution.py:57
  69.1 1.4 copy-done.45
  70.5 4.7 %shard_map.93 = (bf16[192,768]{1,0:T(8,128)(2,1)S(1)}, bf16[192,768]{1,0:T(8,128)(2,1)S(1)}, bf16[192,768]{1,0:T(8,128)(2,1)S(1)}, f32[192,768]{1,0:T(8,128)S(1)}) custom-call(bf16[1024,768]{1,0:T(8,128)(2,1)S(1)} %shard_map.86.own_ref, bf16[1024,768]{1,0:T(8,128)(2,1)S(1)} %collective-permute-done.2.other_ref, ...), custom_call_target="tpu_custom_call" | custom-call | flops 1024 | bytes 1024 | tf_op jit(solution)/shard_map/pallas_call | solution.py:151
  77.6 5.6 %collective-permute-done.28 = bf16[192,768]{1,0:T(8,128)(2,1)S(1)} collective-permute-done((bf16[192,768]{1,0:T(8,128)(2,1)S(1)}, bf16[192,768]{1,0:T(8,128)(2,1)S(1)}, u32[]{:S(2)}, u32[]{:S(2)}) %collective-permute-start.28) | collective-permute-done | bytes 294944 | tf_op jit(solution)/shard_map/ppermute | solution.py:57
  83.5 5.3 %shard_map.94 = (bf16[480,768]{1,0:T(8,128)(2,1)S(1)}, bf16[480,768]{1,0:T(8,128)(2,1)S(1)}) custom-call(bf16[1024,768]{1,0:T(8,128)(2,1)S(1)} %shard_map.86.own_ref, bf16[1024,768]{1,0:T(8,128)(2,1)S(1)} %collective-permute-done.2.other_ref, bf16[4,96,1024]{2,1,0:T(8,128)(2,1)S(1)} %collective-permute-done.24.refs_0_, ...), custom_call_target="tpu_custom_call" | custom-call | flops 1024 | bytes 1024 | tf_op jit(solution)/shard_map/pallas_call | solution.py:151
  88.9 2.4 %collective-permute-done.29 = bf16[192,768]{1,0:T(8,128)(2,1)S(1)} collective-permute-done((bf16[192,768]{1,0:T(8,128)(2,1)S(1)}, bf16[192,768]{1,0:T(8,128)(2,1)S(1)}, u32[]{:S(2)}, u32[]{:S(2)}) %collective-permute-start.29) | collective-permute-done | bytes 294944 | tf_op jit(solution)/shard_map/ppermute | solution.py:57
  94.2 7.3 %collective-permute-done.31 = bf16[480,768]{1,0:T(8,128)(2,1)S(1)} collective-permute-done((bf16[480,768]{1,0:T(8,128)(2,1)S(1)}, bf16[480,768]{1,0:T(8,128)(2,1)S(1)}, u32[]{:S(2)}, u32[]{:S(2)}) %collective-permute-start.31) | collective-permute-done | bytes 737312 | tf_op jit(solution)/shard_map/ppermute | solution.py:57
  103.6 2.5 %collective-permute-start.32 = (bf16[4,96,1024]{2,1,0:T(8,128)(2,1)}, bf16[4,96,1024]{2,1,0:T(8,128)(2,1)S(1)}, u32[]{:S(2)}, u32[]{:S(2)}) collective-permute-start(bf16[4,96,1024]{2,1,0:T(8,128)(2,1)} %get-tuple-element.113), channel_id=1, source_target_pairs={{0,8},{1,25},{2,10},{3,27},{4,12},{5,29},{6,14},{7,31},{8,16},{9,1... | collective-permute-start | bytes 2359304 | tf_op jit(solution)/shard_map/ppermute | solution.py:57
  108.4 2.5 %collective-permute-start.35 = (bf16[192,768]{1,0:T(8,128)(2,1)}, bf16[192,768]{1,0:T(8,128)(2,1)S(1)}, u32[]{:S(2)}, u32[]{:S(2)}) collective-permute-start(bf16[192,768]{1,0:T(8,128)(2,1)} %add_convert_fusion.8), channel_id=1, source_target_pairs={{0,2},{1,7},{2,4},{3,1},{4,6},{5,3},{6,0},{7,5},{8,10},{9,15},{10,... | collective-permute-start | bytes 884744 | tf_op jit(solution)/shard_map/ppermute | solution.py:57
  110.9 5.8 %shard_map.95 = (bf16[480,768]{1,0:T(8,128)(2,1)S(1)}, f32[480,768]{1,0:T(8,128)S(1)}) custom-call(bf16[1024,768]{1,0:T(8,128)(2,1)S(1)} %shard_map.86.own_ref, bf16[1024,768]{1,0:T(8,128)(2,1)S(1)} %collective-permute-done.2.other_ref, bf16[4,96,1024]{2,1,0:T(8,128)(2,1)S(1)} %collective-permute-done.24.refs_0_, ...), custom_call_target="tpu_custom_call" | custom-call | flops 1024 | bytes 1024 | tf_op jit(solution)/shard_map/pallas_call | solution.py:151
  116.8 3.7 %shard_map.96 = (bf16[192,768]{1,0:T(8,128)(2,1)S(1)}, bf16[192,768]{1,0:T(8,128)(2,1)S(1)}, bf16[192,768]{1,0:T(8,128)(2,1)S(1)}, f32[192,768]{1,0:T(8,128)S(1)}) custom-call(bf16[1024,768]{1,0:T(8,128)(2,1)S(1)} %shard_map.86.own_ref, bf16[1024,768]{1,0:T(8,128)(2,1)S(1)} %collective-permute-done.2.other_ref, ...), custom_call_target="tpu_custom_call" | custom-call | flops 1024 | bytes 1024 | tf_op jit(solution)/shard_map/pallas_call | solution.py:151
  121.3 2.1 %collective-permute-done.36.got_ref = bf16[192,768]{1,0:T(8,128)(2,1)S(1)} collective-permute-done((bf16[192,768]{1,0:T(8,128)(2,1)S(1)}, bf16[192,768]{1,0:T(8,128)(2,1)S(1)}, u32[]{:S(2)}, u32[]{:S(2)}) %collective-permute-start.36) | collective-permute-done | bytes 294944 | tf_op jit(solution)/shard_map/ppermute | solution.py:57
  123.7 2.9 %collective-permute-done.35.got_ref = bf16[192,768]{1,0:T(8,128)(2,1)S(1)} collective-permute-done((bf16[192,768]{1,0:T(8,128)(2,1)}, bf16[192,768]{1,0:T(8,128)(2,1)S(1)}, u32[]{:S(2)}, u32[]{:S(2)}) %collective-permute-start.35) | collective-permute-done | bytes 294944 | tf_op jit(solution)/shard_map/ppermute | solution.py:57
  127.5 1.7 add_convert_fusion.refs_7_
  129.3 2.0 collective-permute-done.40
  131.8 4.6 %shard_map.99 = (bf16[192,768]{1,0:T(8,128)(2,1)S(1)}, bf16[192,768]{1,0:T(8,128)(2,1)S(1)}, bf16[192,768]{1,0:T(8,128)(2,1)S(1)}, f32[192,768]{1,0:T(8,128)S(1)}) custom-call(bf16[1024,768]{1,0:T(8,128)(2,1)S(1)} %copy-done.1, bf16[1024,768]{1,0:T(8,128)(2,1)S(1)} %copy-done.3, bf16[4,96,1024]{2,1,0:T(8,128)(2,1)S(1)} %collective-permute-done.32.refs_0_, ...), custom_call_target="tpu_custom_call" | custom-call | flops 1024 | bytes 1024 | tf_op jit(solution)/shard_map/pallas_call | solution.py:151
  136.7 6.1 %shard_map.100 = (bf16[288,768]{1,0:T(8,128)(2,1)S(1)}, bf16[288,768]{1,0:T(8,128)(2,1)S(1)}, bf16[288,768]{1,0:T(8,128)(2,1)S(1)}, f32[288,768]{1,0:T(8,128)S(1)}) custom-call(bf16[1024,768]{1,0:T(8,128)(2,1)S(1)} %copy-done.1, bf16[1024,768]{1,0:T(8,128)(2,1)S(1)} %copy-done.3, bf16[2,4,96,1024]{3,2,1,0:T(8,128)(2,1)S(1)} %copy-done.6, ...), custom_call_target="tpu_custom_call" | custom-call | flops 1024 | bytes 1024 | tf_op jit(solution)/shard_map/pallas_call | solution.py:151
  142.8 2.5 %collective-permute-start.41 = (bf16[288,768]{1,0:T(8,128)(2,1)S(1)}, bf16[288,768]{1,0:T(8,128)(2,1)S(1)}, u32[]{:S(2)}, u32[]{:S(2)}) collective-permute-start(bf16[288,768]{1,0:T(8,128)(2,1)S(1)} %get-tuple-element.135), channel_id=1, source_target_pairs={{0,2},{1,7},{2,4},{3,1},{4,6},{5,3},{6,0},{7,5},{8,10},{9,15},{10,... | collective-permute-start | bytes 1327112 | tf_op jit(solution)/shard_map/ppermute | solution.py:57
  146.1 2.2 %collective-permute-done.44 = bf16[192,768]{1,0:T(8,128)(2,1)S(1)} collective-permute-done((bf16[192,768]{1,0:T(8,128)(2,1)S(1)}, bf16[192,768]{1,0:T(8,128)(2,1)S(1)}, u32[]{:S(2)}, u32[]{:S(2)}) %collective-permute-start.44) | collective-permute-done | bytes 294944 | tf_op jit(solution)/shard_map/ppermute | solution.py:57
  148.4 4.7 %collective-permute-done.41 = bf16[288,768]{1,0:T(8,128)(2,1)S(1)} collective-permute-done((bf16[288,768]{1,0:T(8,128)(2,1)S(1)}, bf16[288,768]{1,0:T(8,128)(2,1)S(1)}, u32[]{:S(2)}, u32[]{:S(2)}) %collective-permute-start.41) | collective-permute-done | bytes 442400 | tf_op jit(solution)/shard_map/ppermute | solution.py:57
  153.8 2.1 collective-permute-start.48
  155.9 10.0 %collective-permute-done.48.got_ref = bf16[192,768]{1,0:T(8,128)(2,1)S(1)} collective-permute-done((bf16[192,768]{1,0:T(8,128)(2,1)S(1)}, bf16[192,768]{1,0:T(8,128)(2,1)S(1)}, u32[]{:S(2)}, u32[]{:S(2)}) %collective-permute-start.48) | collective-permute-done | bytes 294944 | tf_op jit(solution)/shard_map/ppermute | solution.py:57
  166.4 2.7 %collective-permute-done.47 = bf16[192,768]{1,0:T(8,128)(2,1)S(1)} collective-permute-done((bf16[192,768]{1,0:T(8,128)(2,1)S(1)}, bf16[192,768]{1,0:T(8,128)(2,1)S(1)}, u32[]{:S(2)}, u32[]{:S(2)}) %collective-permute-start.47) | collective-permute-done | bytes 294944 | tf_op jit(solution)/shard_map/ppermute | solution.py:57
  169.2 9.8 %collective-permute-done.49.got_ref = bf16[192,768]{1,0:T(8,128)(2,1)S(1)} collective-permute-done((bf16[192,768]{1,0:T(8,128)(2,1)S(1)}, bf16[192,768]{1,0:T(8,128)(2,1)S(1)}, u32[]{:S(2)}, u32[]{:S(2)}) %collective-permute-start.49) | collective-permute-done | bytes 294944 | tf_op jit(solution)/shard_map/ppermute | solution.py:57
  181.0 2.2 %collective-permute-start.52 = (f32[1,1664]{1,0:T(1,128)S(1)}, f32[1,1664]{1,0:T(1,128)S(1)}, u32[]{:S(2)}, u32[]{:S(2)}) collective-permute-start(f32[1,1664]{1,0:T(1,128)S(1)} %constant_dynamic-update-slice_fusion), channel_id=1, source_target_pairs={{0,6},{1,3},{2,0},{3,5},{4,2},{5,7},{6,4},{7,1},{8,14},{9,11},{10,... | collective-permute-start | bytes 19976 | tf_op jit(solution)/shard_map/ppermute | solution.py:57
  183.2 1.6 collective-permute-done.50
  187.0 2.1 %shard_map.105 = (f32[1,1024]{1,0:T(1,128)S(1)}, f32[1,1536]{1,0:T(1,128)S(1)}, f32[1,1536]{1,0:T(1,128)S(1)}) custom-call(f32[1,1664]{1,0:T(1,128)S(1)} %add_add_fusion.mine_ref, f32[1,1664]{1,0:T(1,128)S(1)} %collective-permute-done.53.yours_ref, f32[1,1536]{1,0:T(1,128)S(1)} %broadcast_in_dim.14.column_ref, f32[768,768]{1,0:T(8,128)S(1)} %get-tuple-element.160.kept_ref, ...), custom_call_target="tpu_custom_call" | custom-call | flops 1024 | bytes 1024 | tf_op jit(solution)/shard_map/pallas_call | solution.py:297
  190.0 1.7 collective-permute-start.56
  196.2 2.3 %collective-permute-start.59 = (f32[1,1024]{1,0:T(1,128)S(1)}, f32[1,1024]{1,0:T(1,128)S(1)}, u32[]{:S(2)}, u32[]{:S(2)}) collective-permute-start(f32[1,1024]{1,0:T(1,128)S(1)} %add_add_fusion.2), channel_id=1, source_target_pairs={{0,64},{1,65},{2,66},{3,67},{4,68},{5,69},{6,70},{7,71},{8,72},{9,... | collective-permute-start | bytes 12296 | tf_op jit(solution)/shard_map/ppermute | solution.py:57
  198.5 1.5 collective-permute-start.60
  202.1 1.7 copy-done.13
  203.8 3.5 %shard_map.106 = (f32[768,1536]{1,0:T(8,128)}, f32[1,768]{1,0:T(1,128)S(1)}) custom-call(f32[1,1024]{1,0:T(1,128)S(1)} %add_add_fusion.1.summed_ref, f32[1,128]{1,0:T(1,128)S(1)} %slice.20.row_total_ref, f32[1,1536]{1,0:T(1,128)S(1)} %get-tuple-element.163.clip_ref, f32[1,1536]{1,0:T(1,128)S(1)} %get-tuple-element.164.column_ref, ...), custom_call_target="tpu_custom_call" | custom-call | flops 1024 | bytes 1024 | tf_op jit(solution)/shard_map/pallas_call | solution.py:337
  (250 shorter events, 51.1 us)
Async XLA Ops:
  2.9 5.2 %collective-permute-start.1 = (bf16[192,1024]{1,0:T(8,128)(2,1)}, bf16[192,1024]{1,0:T(8,128)(2,1)S(1)}, u32[]{:S(2)}, u32[]{:S(2)}) collective-permute-start(bf16[192,1024]{1,0:T(8,128)(2,1)} %get-tuple-element.86.refs_0_), channel_id=1, source_target_pairs={{0,1},{1,0},{2,3},{3,2},{4,5},{5,4},{6,7},{7,6},{8,9},{9,8},{10,11... | collective-permute-start | bytes 1179656 | tf_op jit(solution)/shard_map/ppermute | solution.py:57
  3.4 15.1 %collective-permute-start.3 = (bf16[192,1024]{1,0:T(8,128)(2,1)}, bf16[192,1024]{1,0:T(8,128)(2,1)S(1)}, u32[]{:S(2)}, u32[]{:S(2)}) collective-permute-start(bf16[192,1024]{1,0:T(8,128)(2,1)} %get-tuple-element.85.refs_0_), channel_id=1, source_target_pairs={{0,32},{1,97},{2,34},{3,99},{4,36},{5,101},{6,38},{7,103},{8,40},{... | collective-permute-start | bytes 1179656 | tf_op jit(solution)/shard_map/ppermute | solution.py:57
  5.1 13.5 %collective-permute-start.4 = (bf16[192,1024]{1,0:T(8,128)(2,1)}, bf16[192,1024]{1,0:T(8,128)(2,1)S(1)}, u32[]{:S(2)}, u32[]{:S(2)}) collective-permute-start(bf16[192,1024]{1,0:T(8,128)(2,1)} %get-tuple-element.86.refs_0_), channel_id=1, source_target_pairs={{0,8},{1,25},{2,10},{3,27},{4,12},{5,29},{6,14},{7,31},{8,16},{9,1... | collective-permute-start | bytes 1179656 | tf_op jit(solution)/shard_map/ppermute | solution.py:57
  6.6 12.0 %collective-permute-start.5 = (bf16[192,1024]{1,0:T(8,128)(2,1)S(1)}, bf16[192,1024]{1,0:T(8,128)(2,1)S(1)}, u32[]{:S(2)}, u32[]{:S(2)}) collective-permute-start(bf16[192,1024]{1,0:T(8,128)(2,1)S(1)} %collective-permute-done.refs_0_.refs_4_.refs_1_), channel_id=1, source_target_pairs={{0,32},{1,97},{2,34},{3,99},{4,36},{5,101},{6,38},{7,103},{8,40},{... | collective-permute-start | bytes 1179656 | tf_op jit(solution)/shard_map/ppermute | solution.py:57
  8.2 10.4 %collective-permute-start.6 = (bf16[192,1024]{1,0:T(8,128)(2,1)S(1)}, bf16[192,1024]{1,0:T(8,128)(2,1)S(1)}, u32[]{:S(2)}, u32[]{:S(2)}) collective-permute-start(bf16[192,1024]{1,0:T(8,128)(2,1)S(1)} %collective-permute-done.1.refs_1_.refs_4_), channel_id=1, source_target_pairs={{0,8},{1,25},{2,10},{3,27},{4,12},{5,29},{6,14},{7,31},{8,16},{9,1... | collective-permute-start | bytes 1179656 | tf_op jit(solution)/shard_map/ppermute | solution.py:57
  19.4 16.1 %collective-permute-start.2 = (bf16[1024,768]{1,0:T(8,128)(2,1)S(1)}, bf16[1024,768]{1,0:T(8,128)(2,1)S(1)}, u32[]{:S(2)}, u32[]{:S(2)}) collective-permute-start(bf16[1024,768]{1,0:T(8,128)(2,1)S(1)} %shard_map.87), channel_id=1, source_target_pairs={{0,1},{1,0},{2,3},{3,2},{4,5},{5,4},{6,7},{7,6},{8,9},{9,8},{10,11... | collective-permute-start | bytes 4718600 | tf_op jit(solution)/shard_map/ppermute | solution.py:57
  19.8 9.0 %collective-permute-start.10 = (bf16[192,1024]{1,0:T(8,128)(2,1)S(1)}, bf16[192,1024]{1,0:T(8,128)(2,1)S(1)}, u32[]{:S(2)}, u32[]{:S(2)}) collective-permute-start(bf16[192,1024]{1,0:T(8,128)(2,1)S(1)} %collective-permute-done.3.refs_1_.refs_2_), channel_id=1, source_target_pairs={{0,32},{1,97},{2,34},{3,99},{4,36},{5,101},{6,38},{7,103},{8,40},{... | collective-permute-start | bytes 1179656 | tf_op jit(solution)/shard_map/ppermute | solution.py:57
  20.6 9.0 %collective-permute-start.11 = (bf16[192,1024]{1,0:T(8,128)(2,1)S(1)}, bf16[192,1024]{1,0:T(8,128)(2,1)S(1)}, u32[]{:S(2)}, u32[]{:S(2)}) collective-permute-start(bf16[192,1024]{1,0:T(8,128)(2,1)S(1)} %collective-permute-done.4.refs_1_), channel_id=1, source_target_pairs={{0,8},{1,25},{2,10},{3,27},{4,12},{5,29},{6,14},{7,31},{8,16},{9,1... | collective-permute-start | bytes 1179656 | tf_op jit(solution)/shard_map/ppermute | solution.py:57
  21.8 7.8 %collective-permute-start.9 = (bf16[192,1024]{1,0:T(8,128)(2,1)S(1)}, bf16[192,1024]{1,0:T(8,128)(2,1)S(1)}, u32[]{:S(2)}, u32[]{:S(2)}) collective-permute-start(bf16[192,1024]{1,0:T(8,128)(2,1)S(1)} %collective-permute-done.5.refs_5_.refs_3_), channel_id=1, source_target_pairs={{0,1},{1,0},{2,3},{3,2},{4,5},{5,4},{6,7},{7,6},{8,9},{9,8},{10,11... | collective-permute-start | bytes 1179656 | tf_op jit(solution)/shard_map/ppermute | solution.py:57
  22.7 6.9 %collective-permute-start.12 = (bf16[192,1024]{1,0:T(8,128)(2,1)S(1)}, bf16[192,1024]{1,0:T(8,128)(2,1)S(1)}, u32[]{:S(2)}, u32[]{:S(2)}) collective-permute-start(bf16[192,1024]{1,0:T(8,128)(2,1)S(1)} %collective-permute-done.6.refs_5_), channel_id=1, source_target_pairs={{0,1},{1,0},{2,3},{3,2},{4,5},{5,4},{6,7},{7,6},{8,9},{9,8},{10,11... | collective-permute-start | bytes 1179656 | tf_op jit(solution)/shard_map/ppermute | solution.py:57
  32.8 27.3 %collective-permute-start.16 = (bf16[2,4,96,1024]{3,2,1,0:T(8,128)(2,1)}, bf16[2,4,96,1024]{3,2,1,0:T(8,128)(2,1)}, u32[]{:S(2)}, u32[]{:S(2)}) collective-permute-start(bf16[2,4,96,1024]{3,2,1,0:T(8,128)(2,1)} %shard_map.91.refs_9_.refs_2_), channel_id=1, source_target_pairs={{0,32},{1,97},{2,34},{3,99},{4,36},{5,101},{6,38},{7,103},{8,40},{... | collective-permute-start | bytes 4718600 | tf_op jit(solution)/shard_map/ppermute | solution.py:57
  35.5 24.6 %collective-permute-start.15 = (bf16[2,4,96,1024]{3,2,1,0:T(8,128)(2,1)}, bf16[2,4,96,1024]{3,2,1,0:T(8,128)(2,1)}, u32[]{:S(2)}, u32[]{:S(2)}) collective-permute-start(bf16[2,4,96,1024]{3,2,1,0:T(8,128)(2,1)} %shard_map.90.refs_8_), channel_id=1, source_target_pairs={{0,8},{1,25},{2,10},{3,27},{4,12},{5,29},{6,14},{7,31},{8,16},{9,1... | collective-permute-start | bytes 4718600 | tf_op jit(solution)/shard_map/ppermute | solution.py:57
  41.9 9.1 %collective-permute-start.17 = (bf16[192,768]{1,0:T(8,128)(2,1)}, bf16[192,768]{1,0:T(8,128)(2,1)}, u32[]{:S(2)}, u32[]{:S(2)}) collective-permute-start(bf16[192,768]{1,0:T(8,128)(2,1)} %get-tuple-element.97), channel_id=1, source_target_pairs={{0,2},{1,7},{2,4},{3,1},{4,6},{5,3},{6,0},{7,5},{8,10},{9,15},{10,... | collective-permute-start | bytes 884744 | tf_op jit(solution)/shard_map/ppermute | solution.py:57
  52.0 8.0 %collective-permute-start.18 = (bf16[192,768]{1,0:T(8,128)(2,1)S(1)}, bf16[192,768]{1,0:T(8,128)(2,1)S(1)}, u32[]{:S(2)}, u32[]{:S(2)}) collective-permute-start(bf16[192,768]{1,0:T(8,128)(2,1)S(1)} %add_convert_fusion.11), channel_id=1, source_target_pairs={{0,2},{1,7},{2,4},{3,1},{4,6},{5,3},{6,0},{7,5},{8,10},{9,15},{10,... | collective-permute-start | bytes 884744 | tf_op jit(solution)/shard_map/ppermute | solution.py:57
  60.2 5.9 %collective-permute-start.21 = (bf16[2,4,96,1024]{3,2,1,0:T(8,128)(2,1)}, bf16[2,4,96,1024]{3,2,1,0:T(8,128)(2,1)S(1)}, u32[]{:S(2)}, u32[]{:S(2)}) collective-permute-start(bf16[2,4,96,1024]{3,2,1,0:T(8,128)(2,1)} %collective-permute-done.16.refs_3_), channel_id=1, source_target_pairs={{0,1},{1,0},{2,3},{3,2},{4,5},{5,4},{6,7},{7,6},{8,9},{9,8},{10,11... | collective-permute-start | bytes 4718600 | tf_op jit(solution)/shard_map/ppermute | solution.py:57
  63.1 13.3 %collective-permute-start.24 = (bf16[4,96,1024]{2,1,0:T(8,128)(2,1)S(1)}, bf16[4,96,1024]{2,1,0:T(8,128)(2,1)S(1)}, u32[]{:S(2)}, u32[]{:S(2)}) collective-permute-start(bf16[4,96,1024]{2,1,0:T(8,128)(2,1)S(1)} %slice_bitcast_fusion.3), channel_id=1, source_target_pairs={{0,8},{1,25},{2,10},{3,27},{4,12},{5,29},{6,14},{7,31},{8,16},{9,1... | collective-permute-start | bytes 2359304 | tf_op jit(solution)/shard_map/ppermute | solution.py:57
  63.7 13.2 %collective-permute-start.25 = (bf16[4,96,1024]{2,1,0:T(8,128)(2,1)S(1)}, bf16[4,96,1024]{2,1,0:T(8,128)(2,1)S(1)}, u32[]{:S(2)}, u32[]{:S(2)}) collective-permute-start(bf16[4,96,1024]{2,1,0:T(8,128)(2,1)S(1)} %slice_bitcast_fusion.2), channel_id=1, source_target_pairs={{0,32},{1,97},{2,34},{3,99},{4,36},{5,101},{6,38},{7,103},{8,40},{... | collective-permute-start | bytes 2359304 | tf_op jit(solution)/shard_map/ppermute | solution.py:57
  66.1 27.1 %collective-permute-start.22 = (bf16[2,4,96,1024]{3,2,1,0:T(8,128)(2,1)S(1)}, bf16[2,4,96,1024]{3,2,1,0:T(8,128)(2,1)S(1)}, u32[]{:S(2)}, u32[]{:S(2)}) collective-permute-start(bf16[2,4,96,1024]{3,2,1,0:T(8,128)(2,1)S(1)} %shard_map.88), channel_id=1, source_target_pairs={{0,8},{1,25},{2,10},{3,27},{4,12},{5,29},{6,14},{7,31},{8,16},{9,1... | collective-permute-start | bytes 4718600 | tf_op jit(solution)/shard_map/ppermute | solution.py:57
  66.9 26.9 %collective-permute-start.23 = (bf16[2,4,96,1024]{3,2,1,0:T(8,128)(2,1)S(1)}, bf16[2,4,96,1024]{3,2,1,0:T(8,128)(2,1)S(1)}, u32[]{:S(2)}, u32[]{:S(2)}) collective-permute-start(bf16[2,4,96,1024]{3,2,1,0:T(8,128)(2,1)S(1)} %shard_map.89.refs_2_.refs_0_), channel_id=1, source_target_pairs={{0,32},{1,97},{2,34},{3,99},{4,36},{5,101},{6,38},{7,103},{8,40},{... | collective-permute-start | bytes 4718600 | tf_op jit(solution)/shard_map/ppermute | solution.py:57
  75.3 8.0 %collective-permute-start.28 = (bf16[192,768]{1,0:T(8,128)(2,1)S(1)}, bf16[192,768]{1,0:T(8,128)(2,1)S(1)}, u32[]{:S(2)}, u32[]{:S(2)}) collective-permute-start(bf16[192,768]{1,0:T(8,128)(2,1)S(1)} %get-tuple-element.103), channel_id=1, source_target_pairs={{0,2},{1,7},{2,4},{3,1},{4,6},{5,3},{6,0},{7,5},{8,10},{9,15},{10,... | collective-permute-start | bytes 884744 | tf_op jit(solution)/shard_map/ppermute | solution.py:57
  76.9 6.6 %collective-permute-start.26 = (bf16[4,96,1024]{2,1,0:T(8,128)(2,1)S(1)}, bf16[4,96,1024]{2,1,0:T(8,128)(2,1)S(1)}, u32[]{:S(2)}, u32[]{:S(2)}) collective-permute-start(bf16[4,96,1024]{2,1,0:T(8,128)(2,1)S(1)} %collective-permute-done.24.refs_0_), channel_id=1, source_target_pairs={{0,1},{1,0},{2,3},{3,2},{4,5},{5,4},{6,7},{7,6},{8,9},{9,8},{10,11... | collective-permute-start | bytes 2359304 | tf_op jit(solution)/shard_map/ppermute | solution.py:57
  77.6 5.9 %collective-permute-start.27 = (bf16[4,96,1024]{2,1,0:T(8,128)(2,1)S(1)}, bf16[4,96,1024]{2,1,0:T(8,128)(2,1)S(1)}, u32[]{:S(2)}, u32[]{:S(2)}) collective-permute-start(bf16[4,96,1024]{2,1,0:T(8,128)(2,1)S(1)} %collective-permute-done.25.refs_5_), channel_id=1, source_target_pairs={{0,1},{1,0},{2,3},{3,2},{4,5},{5,4},{6,7},{7,6},{8,9},{9,8},{10,11... | collective-permute-start | bytes 2359304 | tf_op jit(solution)/shard_map/ppermute | solution.py:57
  83.3 8.0 %collective-permute-start.29 = (bf16[192,768]{1,0:T(8,128)(2,1)S(1)}, bf16[192,768]{1,0:T(8,128)(2,1)S(1)}, u32[]{:S(2)}, u32[]{:S(2)}) collective-permute-start(bf16[192,768]{1,0:T(8,128)(2,1)S(1)} %add_convert_fusion.9.refs_7_), channel_id=1, source_target_pairs={{0,2},{1,7},{2,4},{3,1},{4,6},{5,3},{6,0},{7,5},{8,10},{9,15},{10,... | collective-permute-start | bytes 884744 | tf_op jit(solution)/shard_map/ppermute | solution.py:57
  88.8 12.7 %collective-permute-start.31 = (bf16[480,768]{1,0:T(8,128)(2,1)S(1)}, bf16[480,768]{1,0:T(8,128)(2,1)S(1)}, u32[]{:S(2)}, u32[]{:S(2)}) collective-permute-start(bf16[480,768]{1,0:T(8,128)(2,1)S(1)} %get-tuple-element.107), channel_id=1, source_target_pairs={{0,2},{1,7},{2,4},{3,1},{4,6},{5,3},{6,0},{7,5},{8,10},{9,15},{10,... | collective-permute-start | bytes 2211848 | tf_op jit(solution)/shard_map/ppermute | solution.py:57
  93.7 13.6 %collective-permute-start.30 = (bf16[2,4,96,1024]{3,2,1,0:T(8,128)(2,1)S(1)}, bf16[2,4,96,1024]{3,2,1,0:T(8,128)(2,1)S(1)}, u32[]{:S(2)}, u32[]{:S(2)}) collective-permute-start(bf16[2,4,96,1024]{3,2,1,0:T(8,128)(2,1)S(1)} %collective-permute-done.23.refs_3_.refs_1_), channel_id=1, source_target_pairs={{0,1},{1,0},{2,3},{3,2},{4,5},{5,4},{6,7},{7,6},{8,9},{9,8},{10,11... | collective-permute-start | bytes 4718600 | tf_op jit(solution)/shard_map/ppermute | solution.py:57
  94.2 13.2 %collective-permute-start.34 = (bf16[2,4,96,1024]{3,2,1,0:T(8,128)(2,1)S(1)}, bf16[2,4,96,1024]{3,2,1,0:T(8,128)(2,1)S(1)}, u32[]{:S(2)}, u32[]{:S(2)}) collective-permute-start(bf16[2,4,96,1024]{3,2,1,0:T(8,128)(2,1)S(1)} %collective-permute-done.22.refs_0_), channel_id=1, source_target_pairs={{0,1},{1,0},{2,3},{3,2},{4,5},{5,4},{6,7},{7,6},{8,9},{9,8},{10,11... | collective-permute-start | bytes 4718600 | tf_op jit(solution)/shard_map/ppermute | solution.py:57
  103.6 23.2 %collective-permute-start.32 = (bf16[4,96,1024]{2,1,0:T(8,128)(2,1)}, bf16[4,96,1024]{2,1,0:T(8,128)(2,1)S(1)}, u32[]{:S(2)}, u32[]{:S(2)}) collective-permute-start(bf16[4,96,1024]{2,1,0:T(8,128)(2,1)} %get-tuple-element.113), channel_id=1, source_target_pairs={{0,8},{1,25},{2,10},{3,27},{4,12},{5,29},{6,14},{7,31},{8,16},{9,1... | collective-permute-start | bytes 2359304 | tf_op jit(solution)/shard_map/ppermute | solution.py:57
  106.2 20.7 %collective-permute-start.33 = (bf16[4,96,1024]{2,1,0:T(8,128)(2,1)S(1)}, bf16[4,96,1024]{2,1,0:T(8,128)(2,1)S(1)}, u32[]{:S(2)}, u32[]{:S(2)}) collective-permute-start(bf16[4,96,1024]{2,1,0:T(8,128)(2,1)S(1)} %get-tuple-element.114), channel_id=1, source_target_pairs={{0,32},{1,97},{2,34},{3,99},{4,36},{5,101},{6,38},{7,103},{8,40},{... | collective-permute-start | bytes 2359304 | tf_op jit(solution)/shard_map/ppermute | solution.py:57
  107.4 20.1 %collective-permute-start.39 = (bf16[480,768]{1,0:T(8,128)(2,1)}, bf16[480,768]{1,0:T(8,128)(2,1)}, u32[]{:S(2)}, u32[]{:S(2)}) collective-permute-start(bf16[480,768]{1,0:T(8,128)(2,1)} %add_convert_fusion.1), channel_id=1, source_target_pairs={{0,2},{1,7},{2,4},{3,1},{4,6},{5,3},{6,0},{7,5},{8,10},{9,15},{10,... | collective-permute-start | bytes 2211848 | tf_op jit(solution)/shard_map/ppermute | solution.py:57
  107.4 16.0 %collective-permute-start.36 = (bf16[192,768]{1,0:T(8,128)(2,1)S(1)}, bf16[192,768]{1,0:T(8,128)(2,1)S(1)}, u32[]{:S(2)}, u32[]{:S(2)}) collective-permute-start(bf16[192,768]{1,0:T(8,128)(2,1)S(1)} %add_convert_fusion.10), channel_id=1, source_target_pairs={{0,2},{1,7},{2,4},{3,1},{4,6},{5,3},{6,0},{7,5},{8,10},{9,15},{10,... | collective-permute-start | bytes 884744 | tf_op jit(solution)/shard_map/ppermute | solution.py:57
  108.4 18.2 %collective-permute-start.35 = (bf16[192,768]{1,0:T(8,128)(2,1)}, bf16[192,768]{1,0:T(8,128)(2,1)S(1)}, u32[]{:S(2)}, u32[]{:S(2)}) collective-permute-start(bf16[192,768]{1,0:T(8,128)(2,1)} %add_convert_fusion.8), channel_id=1, source_target_pairs={{0,2},{1,7},{2,4},{3,1},{4,6},{5,3},{6,0},{7,5},{8,10},{9,15},{10,... | collective-permute-start | bytes 884744 | tf_op jit(solution)/shard_map/ppermute | solution.py:57
  123.4 7.9 %collective-permute-start.40 = (bf16[192,768]{1,0:T(8,128)(2,1)S(1)}, bf16[192,768]{1,0:T(8,128)(2,1)S(1)}, u32[]{:S(2)}, u32[]{:S(2)}) collective-permute-start(bf16[192,768]{1,0:T(8,128)(2,1)S(1)} %get-tuple-element.116), channel_id=1, source_target_pairs={{0,2},{1,7},{2,4},{3,1},{4,6},{5,3},{6,0},{7,5},{8,10},{9,15},{10,... | collective-permute-start | bytes 884744 | tf_op jit(solution)/shard_map/ppermute | solution.py:57
  129.2 16.1 %collective-permute-start.42 = (bf16[480,768]{1,0:T(8,128)(2,1)S(1)}, bf16[480,768]{1,0:T(8,128)(2,1)S(1)}, u32[]{:S(2)}, u32[]{:S(2)}) collective-permute-start(bf16[480,768]{1,0:T(8,128)(2,1)S(1)} %add_convert_fusion.refs_7_), channel_id=1, source_target_pairs={{0,2},{1,7},{2,4},{3,1},{4,6},{5,3},{6,0},{7,5},{8,10},{9,15},{10,... | collective-permute-start | bytes 2211848 | tf_op jit(solution)/shard_map/ppermute | solution.py:57
  131.4 13.8 %collective-permute-start.43 = (bf16[192,768]{1,0:T(8,128)(2,1)S(1)}, bf16[192,768]{1,0:T(8,128)(2,1)S(1)}, u32[]{:S(2)}, u32[]{:S(2)}) collective-permute-start(bf16[192,768]{1,0:T(8,128)(2,1)S(1)} %add_convert_fusion.7.refs_8_), channel_id=1, source_target_pairs={{0,2},{1,7},{2,4},{3,1},{4,6},{5,3},{6,0},{7,5},{8,10},{9,15},{10,... | collective-permute-start | bytes 884744 | tf_op jit(solution)/shard_map/ppermute | solution.py:57
  136.4 11.9 %collective-permute-start.44 = (bf16[192,768]{1,0:T(8,128)(2,1)S(1)}, bf16[192,768]{1,0:T(8,128)(2,1)S(1)}, u32[]{:S(2)}, u32[]{:S(2)}) collective-permute-start(bf16[192,768]{1,0:T(8,128)(2,1)S(1)} %get-tuple-element.131.refs_5_), channel_id=1, source_target_pairs={{0,2},{1,7},{2,4},{3,1},{4,6},{5,3},{6,0},{7,5},{8,10},{9,15},{10,... | collective-permute-start | bytes 884744 | tf_op jit(solution)/shard_map/ppermute | solution.py:57
  142.8 10.3 %collective-permute-start.41 = (bf16[288,768]{1,0:T(8,128)(2,1)S(1)}, bf16[288,768]{1,0:T(8,128)(2,1)S(1)}, u32[]{:S(2)}, u32[]{:S(2)}) collective-permute-start(bf16[288,768]{1,0:T(8,128)(2,1)S(1)} %get-tuple-element.135), channel_id=1, source_target_pairs={{0,2},{1,7},{2,4},{3,1},{4,6},{5,3},{6,0},{7,5},{8,10},{9,15},{10,... | collective-permute-start | bytes 1327112 | tf_op jit(solution)/shard_map/ppermute | solution.py:57
  153.2 13.0 %collective-permute-start.45 = (bf16[288,768]{1,0:T(8,128)(2,1)S(1)}, bf16[288,768]{1,0:T(8,128)(2,1)S(1)}, u32[]{:S(2)}, u32[]{:S(2)}) collective-permute-start(bf16[288,768]{1,0:T(8,128)(2,1)S(1)} %add_convert_fusion.3), channel_id=1, source_target_pairs={{0,2},{1,7},{2,4},{3,1},{4,6},{5,3},{6,0},{7,5},{8,10},{9,15},{10,... | collective-permute-start | bytes 1327112 | tf_op jit(solution)/shard_map/ppermute | solution.py:57
  153.8 12.1 %collective-permute-start.48 = (bf16[192,768]{1,0:T(8,128)(2,1)S(1)}, bf16[192,768]{1,0:T(8,128)(2,1)S(1)}, u32[]{:S(2)}, u32[]{:S(2)}) collective-permute-start(bf16[192,768]{1,0:T(8,128)(2,1)S(1)} %add_convert_fusion.6), channel_id=1, source_target_pairs={{0,2},{1,7},{2,4},{3,1},{4,6},{5,3},{6,0},{7,5},{8,10},{9,15},{10,... | collective-permute-start | bytes 884744 | tf_op jit(solution)/shard_map/ppermute | solution.py:57
  155.8 13.2 %collective-permute-start.47 = (bf16[192,768]{1,0:T(8,128)(2,1)S(1)}, bf16[192,768]{1,0:T(8,128)(2,1)S(1)}, u32[]{:S(2)}, u32[]{:S(2)}) collective-permute-start(bf16[192,768]{1,0:T(8,128)(2,1)S(1)} %add_convert_fusion.5), channel_id=1, source_target_pairs={{0,2},{1,7},{2,4},{3,1},{4,6},{5,3},{6,0},{7,5},{8,10},{9,15},{10,... | collective-permute-start | bytes 884744 | tf_op jit(solution)/shard_map/ppermute | solution.py:57
  166.3 13.0 %collective-permute-start.46 = (bf16[288,768]{1,0:T(8,128)(2,1)S(1)}, bf16[288,768]{1,0:T(8,128)(2,1)S(1)}, u32[]{:S(2)}, u32[]{:S(2)}) collective-permute-start(bf16[288,768]{1,0:T(8,128)(2,1)S(1)} %add_convert_fusion.2), channel_id=1, source_target_pairs={{0,2},{1,7},{2,4},{3,1},{4,6},{5,3},{6,0},{7,5},{8,10},{9,15},{10,... | collective-permute-start | bytes 1327112 | tf_op jit(solution)/shard_map/ppermute | solution.py:57
  169.1 9.9 %collective-permute-start.49 = (bf16[192,768]{1,0:T(8,128)(2,1)S(1)}, bf16[192,768]{1,0:T(8,128)(2,1)S(1)}, u32[]{:S(2)}, u32[]{:S(2)}) collective-permute-start(bf16[192,768]{1,0:T(8,128)(2,1)S(1)} %add_convert_fusion.4), channel_id=1, source_target_pairs={{0,2},{1,7},{2,4},{3,1},{4,6},{5,3},{6,0},{7,5},{8,10},{9,15},{10,... | collective-permute-start | bytes 884744 | tf_op jit(solution)/shard_map/ppermute | solution.py:57
  179.8 7.2 %collective-permute-start.54 = (f32[768,768]{1,0:T(8,128)S(1)}, f32[768,768]{1,0:T(8,128)S(1)}, u32[]{:S(2)}, u32[]{:S(2)}) collective-permute-start(f32[768,768]{1,0:T(8,128)S(1)} %get-tuple-element.161), channel_id=1, source_target_pairs={{0,1},{1,0},{2,3},{3,2},{4,5},{5,4},{6,7},{7,6},{8,9},{9,8},{10,11... | collective-permute-start | bytes 7077896 | tf_op jit(solution)/shard_map/ppermute | solution.py:57
  179.9 4.9 %collective-permute-start.50 = (f32[1,1664]{1,0:T(1,128)S(1)}, f32[1,1664]{1,0:T(1,128)S(1)}, u32[]{:S(2)}, u32[]{:S(2)}) collective-permute-start(f32[1,1664]{1,0:T(1,128)S(1)} %constant_dynamic-update-slice_fusion), channel_id=1, source_target_pairs={{0,2},{1,7},{2,4},{3,1},{4,6},{5,3},{6,0},{7,5},{8,10},{9,15},{10,... | collective-permute-start | bytes 19976 | tf_op jit(solution)/shard_map/ppermute | solution.py:57
  180.0 5.2 %collective-permute-start.51 = (f32[1,1664]{1,0:T(1,128)S(1)}, f32[1,1664]{1,0:T(1,128)S(1)}, u32[]{:S(2)}, u32[]{:S(2)}) collective-permute-start(f32[1,1664]{1,0:T(1,128)S(1)} %constant_dynamic-update-slice_fusion), channel_id=1, source_target_pairs={{0,4},{1,5},{2,6},{3,7},{4,0},{5,1},{6,2},{7,3},{8,12},{9,13},{10,... | collective-permute-start | bytes 19976 | tf_op jit(solution)/shard_map/ppermute | solution.py:57
  189.1 4.8 %collective-permute-start.55 = (f32[1,1024]{1,0:T(1,128)S(1)}, f32[1,1024]{1,0:T(1,128)S(1)}, u32[]{:S(2)}, u32[]{:S(2)}) collective-permute-start(f32[1,1024]{1,0:T(1,128)S(1)} %get-tuple-element.162), channel_id=1, source_target_pairs={{0,8},{1,25},{2,10},{3,27},{4,12},{5,29},{6,14},{7,31},{8,16},{9,1... | collective-permute-start | bytes 12296 | tf_op jit(solution)/shard_map/ppermute | solution.py:57
  190.0 5.1 %collective-permute-start.56 = (f32[1,1024]{1,0:T(1,128)S(1)}, f32[1,1024]{1,0:T(1,128)S(1)}, u32[]{:S(2)}, u32[]{:S(2)}) collective-permute-start(f32[1,1024]{1,0:T(1,128)S(1)} %get-tuple-element.162), channel_id=1, source_target_pairs={{0,16},{1,17},{2,18},{3,19},{4,20},{5,21},{6,22},{7,23},{8,24},{9,... | collective-permute-start | bytes 12296 | tf_op jit(solution)/shard_map/ppermute | solution.py:57
  195.4 5.2 %collective-permute-start.58 = (f32[1,1024]{1,0:T(1,128)S(1)}, f32[1,1024]{1,0:T(1,128)S(1)}, u32[]{:S(2)}, u32[]{:S(2)}) collective-permute-start(f32[1,1024]{1,0:T(1,128)S(1)} %add_add_fusion.2), channel_id=1, source_target_pairs={{0,32},{1,97},{2,34},{3,99},{4,36},{5,101},{6,38},{7,103},{8,40},{... | collective-permute-start | bytes 12296 | tf_op jit(solution)/shard_map/ppermute | solution.py:57
  196.2 5.1 %collective-permute-start.59 = (f32[1,1024]{1,0:T(1,128)S(1)}, f32[1,1024]{1,0:T(1,128)S(1)}, u32[]{:S(2)}, u32[]{:S(2)}) collective-permute-start(f32[1,1024]{1,0:T(1,128)S(1)} %add_add_fusion.2), channel_id=1, source_target_pairs={{0,64},{1,65},{2,66},{3,67},{4,68},{5,69},{6,70},{7,71},{8,72},{9,... | collective-permute-start | bytes 12296 | tf_op jit(solution)/shard_map/ppermute | solution.py:57
  (75 other events, 683.8 us)

commit v7 on v6

--- a/solution.py
+++ b/solution.py
@@ -417,13 +417,13 @@
     own_2 = add_narrow(own[1], own_got)
     own_got = hop(own_2)
     own_3 = add_narrow(own[2], own_got)
-    x1, y1 = lax.optimization_barrier((x1, y1, own_3, p_next, q_next, early))[:2]
+    x1, y1 = lax.optimization_barrier((x1, y1, own_2, p_next, q_next, early))[:2]
     x2, y2 = send(x1[0], ALONG_X), send(y1[0], ALONG_Y)
     x1_swap, y1_swap = send(x1, SWAP), send(y1, SWAP)
 
     p_next, q_next = lax.optimization_barrier((p_next, q_next, x1_swap, y1_swap))[:2]
     x1_next, y1_next = send(p_next, ALONG_X), send(q_next, ALONG_Y)
-    near0 = units(near_entries(x1, x1_swap), waits=(y1_swap,))
+    near0 = units(near_entries(x1, x1_swap), waits=(y1_swap, own_3))
     near0_got = hop(near0[0])
     x2, y2 = lax.optimization_barrier((x2, y2, near0[0]))[:2]
     x2_swap, y2_swap = send(x2, SWAP), send(y2, SWAP)

time: 209 us -> 212 us (1.014)
  waiting for transfers between devices: 77.5 us -> 69 us
  starting transfers between devices: 50.1 us -> 55.9 us
  local copies, waits for them, and re-layouts: 15.5 us -> 20.8 us
    ppermute x61, waiting for transfers between devices: 77.5 us -> 69 us  [send(): return lax.ppermute(value, BOTH, pairs)]
    unnamed x125 -> x117, local copies, waits for them, and re-layouts: 11.3 us -> 17.6 us
    ppermute x61, starting transfers between devices: 50.1 us -> 55.9 us  [send(): return lax.ppermute(value, BOTH, pairs)]
  transfers between devices with their start and end apart: 61 -> 61, of which waited for: 31 -> 23; matrix products, arithmetic and copies ran while one was open for 7% -> 6% of each run, Pallas kernels for 21% -> 21%
where the time goes in v7:
time: 212 us; the launch traced here: 211 us
  waiting for transfers between devices  69 us (33%)
  starting transfers between devices  55.9 us (26%)
  Pallas kernels  52.9 us (25%)
  local copies, waits for them, and re-layouts  20.8 us (10%)
  other arithmetic  10.8 us (5%)
    ppermute x61, waiting for transfers between devices, send(): return lax.ppermute(value, BOTH, pairs)  69 us
    ppermute x61, starting transfers between devices, send(): return lax.ppermute(value, BOTH, pairs)  55.9 us
    pallas_call x7, Pallas kernels, unit_partials(): pl.pallas_call(kernel, out_shape=tuple((jax.ShapeDtypeStruct((rows, HALF)...  33.9 us
    unnamed x117, local copies, waits for them, and re-layouts  17.6 us
    pallas_call x2, Pallas kernels, slope_half(): pl.pallas_call(kernel, out_shape=jax.ShapeDtypeStruct((TOK, HALF), jnp.bf...  6.26 us
    convert_element_type x12, other arithmetic, add_narrow(): return (a.astype(jnp.float32) + b.astype(jnp.float32)).astype(jnp.bfloat16)  5.54 us
  transfers between devices with their start and end apart: 61, of which 23 were waited for; matrix products, arithmetic and copies ran while one was open for 6% of the time, Pallas kernels for 21%

profile of v7, /device:TPU:0, one launch (start us, length us, event | category | flops | bytes accessed | tf_op | source)
XLA Modules:
  0.0 210.9 jit_solution(11605026927711966958)
XLA Ops:
  0.6 2.3 %shard_map.85 = (bf16[192,1024]{1,0:T(8,128)(2,1)}, bf16[192,1024]{1,0:T(8,128)(2,1)}) custom-call(bf16[1024,384]{1,0:T(8,128)(2,1)} %ref.1), custom_call_target="tpu_custom_call" | custom-call | flops 1024 | bytes 1024 | tf_op jit(solution)/shard_map/pallas_call | solution.py:186
  3.4 1.7 collective-permute-start.3
  5.1 1.5 collective-permute-start.4
  6.6 1.6 collective-permute-start.5
  8.2 1.5 collective-permute-start.6
  9.7 1.9 copy-done.8
  11.6 1.9 copy-done.9
  13.5 2.5 %shard_map.86.own_ref = bf16[1024,768]{1,0:T(8,128)(2,1)S(1)} custom-call(bf16[1024,1536]{1,0:T(8,128)(2,1)S(1)} %copy-done.8, bf16[1024,1536]{1,0:T(8,128)(2,1)S(1)} %copy-done.9, bf16[192,1024]{1,0:T(8,128)(2,1)S(1)} %collective-permute-done.refs_0_.refs_4_.refs_1_, bf16[192,1024]{1,0:T(8,128)(2,1)S(1)} %collective-permute-done.1.refs_1_.refs_4_), custom_call_target="tpu_custom_call" | custom-call | flops 1024 | bytes 1024 | tf_op jit(solution)/shard_map/pallas_call | solution.py:89
  16.0 3.7 %shard_map.87 = bf16[1024,768]{1,0:T(8,128)(2,1)} custom-call(bf16[1024,1536]{1,0:T(8,128)(2,1)S(1)} %copy-done.8, bf16[1024,1536]{1,0:T(8,128)(2,1)S(1)} %copy-done.9, bf16[192,1024]{1,0:T(8,128)(2,1)S(1)} %collective-permute-done.refs_0_.refs_4_.refs_1_, bf16[192,1024]{1,0:T(8,128)(2,1)S(1)} %collective-permute-done.1.refs_1_.refs_4_), custom_call_target="tpu_custom_call" | custom-call | flops 1024 | bytes 1024 | tf_op jit(solution)/shard_map/pallas_call | solution.py:89
  24.0 6.1 %collective-permute-done.10.refs_3_.refs_6_ = bf16[192,1024]{1,0:T(8,128)(2,1)S(1)} collective-permute-done((bf16[192,1024]{1,0:T(8,128)(2,1)S(1)}, bf16[192,1024]{1,0:T(8,128)(2,1)S(1)}, u32[]{:S(2)}, u32[]{:S(2)}) %collective-permute-start.10) | collective-permute-done | bytes 393248 | tf_op jit(solution)/shard_map/ppermute | solution.py:57
  43.1 3.5 %shard_map.92 = (bf16[192,768]{1,0:T(8,128)(2,1)S(1)}, bf16[192,768]{1,0:T(8,128)(2,1)S(1)}, bf16[192,768]{1,0:T(8,128)(2,1)S(1)}, f32[192,768]{1,0:T(8,128)S(1)}) custom-call(bf16[1024,768]{1,0:T(8,128)(2,1)S(1)} %shard_map.86.own_ref, bf16[1024,768]{1,0:T(8,128)(2,1)S(1)} %collective-permute-done.2.other_ref, bf16[192,1024]{1,0:T(8,128)(2,1)S(1)} %copy-done.17, ...), custom_call_target="tpu_custom_call" | custom-call | flops 1024 | bytes 1024 | tf_op jit(solution)/shard_map/pallas_call | solution.py:151
  47.5 2.0 collective-permute-start.17
  49.5 2.7 %multiply_reduce_fusion = f32[1536]{0:T(1024)S(1)} fusion(f32[768,1536]{1,0:T(8,128)} %param.9), kind=kLoop, calls=%fused_computation | loop fusion | flops 2357760 | bytes 4724736 | tf_op jit(solution)/shard_map/reduce_sum | solution.py:409
  53.0 4.0 %collective-permute-start.18 = (f32[896]{0:T(1024)S(1)}, f32[896]{0:T(1024)S(1)}, u32[]{:S(2)}, u32[]{:S(2)}) collective-permute-start(f32[896]{0:T(1024)S(1)} %concatenate.10), channel_id=1, source_target_pairs={{0,1},{1,0},{2,3},{3,2},{4,5},{5,4},{6,7},{7,6},{8,9},{9,8},{10,11... | collective-permute-start | bytes 10760 | tf_op jit(solution)/shard_map/ppermute | solution.py:57
  61.6 1.8 collective-permute-start.23
  67.5 3.8 %collective-permute-done.25 = bf16[192,768]{1,0:T(8,128)(2,1)S(1)} collective-permute-done((bf16[192,768]{1,0:T(8,128)(2,1)S(1)}, bf16[192,768]{1,0:T(8,128)(2,1)S(1)}, u32[]{:S(2)}, u32[]{:S(2)}) %collective-permute-start.25) | collective-permute-done | bytes 294944 | tf_op jit(solution)/shard_map/ppermute | solution.py:57
  72.8 4.7 %shard_map.93 = (bf16[192,768]{1,0:T(8,128)(2,1)S(1)}, bf16[192,768]{1,0:T(8,128)(2,1)S(1)}, bf16[192,768]{1,0:T(8,128)(2,1)S(1)}, f32[192,768]{1,0:T(8,128)S(1)}) custom-call(bf16[1024,768]{1,0:T(8,128)(2,1)S(1)} %shard_map.86.own_ref, bf16[1024,768]{1,0:T(8,128)(2,1)S(1)} %collective-permute-done.2.other_ref, ...), custom_call_target="tpu_custom_call" | custom-call | flops 1024 | bytes 1024 | tf_op jit(solution)/shard_map/pallas_call | solution.py:151
  78.3 2.8 %collective-permute-start.26 = (bf16[4,96,1024]{2,1,0:T(8,128)(2,1)S(1)}, bf16[4,96,1024]{2,1,0:T(8,128)(2,1)S(1)}, u32[]{:S(2)}, u32[]{:S(2)}) collective-permute-start(bf16[4,96,1024]{2,1,0:T(8,128)(2,1)S(1)} %collective-permute-done.23.refs_0_), channel_id=1, source_target_pairs={{0,1},{1,0},{2,3},{3,2},{4,5},{5,4},{6,7},{7,6},{8,9},{9,8},{10,11... | collective-permute-start | bytes 2359304 | tf_op jit(solution)/shard_map/ppermute | solution.py:57
  81.2 5.0 %collective-permute-done.28 = bf16[192,768]{1,0:T(8,128)(2,1)S(1)} collective-permute-done((bf16[192,768]{1,0:T(8,128)(2,1)S(1)}, bf16[192,768]{1,0:T(8,128)(2,1)S(1)}, u32[]{:S(2)}, u32[]{:S(2)}) %collective-permute-start.28) | collective-permute-done | bytes 294944 | tf_op jit(solution)/shard_map/ppermute | solution.py:57
  86.5 5.4 %shard_map.94 = (bf16[480,768]{1,0:T(8,128)(2,1)S(1)}, bf16[480,768]{1,0:T(8,128)(2,1)S(1)}) custom-call(bf16[1024,768]{1,0:T(8,128)(2,1)S(1)} %shard_map.86.own_ref, bf16[1024,768]{1,0:T(8,128)(2,1)S(1)} %collective-permute-done.2.other_ref, bf16[4,96,1024]{2,1,0:T(8,128)(2,1)S(1)} %collective-permute-done.23.refs_0_, ...), custom_call_target="tpu_custom_call" | custom-call | flops 1024 | bytes 1024 | tf_op jit(solution)/shard_map/pallas_call | solution.py:151
  92.5 1.9 collective-permute-done.29
  95.0 9.5 %collective-permute-done.31 = bf16[480,768]{1,0:T(8,128)(2,1)S(1)} collective-permute-done((bf16[480,768]{1,0:T(8,128)(2,1)S(1)}, bf16[480,768]{1,0:T(8,128)(2,1)S(1)}, u32[]{:S(2)}, u32[]{:S(2)}) %collective-permute-start.31) | collective-permute-done | bytes 737312 | tf_op jit(solution)/shard_map/ppermute | solution.py:57
  106.0 2.0 collective-permute-start.33
  109.1 2.4 %collective-permute-start.35 = (bf16[192,768]{1,0:T(8,128)(2,1)S(1)}, bf16[192,768]{1,0:T(8,128)(2,1)S(1)}, u32[]{:S(2)}, u32[]{:S(2)}) collective-permute-start(bf16[192,768]{1,0:T(8,128)(2,1)S(1)} %add_convert_fusion.8), channel_id=1, source_target_pairs={{0,2},{1,7},{2,4},{3,1},{4,6},{5,3},{6,0},{7,5},{8,10},{9,15},{10,... | collective-permute-start | bytes 884744 | tf_op jit(solution)/shard_map/ppermute | solution.py:57
  111.6 5.8 %shard_map.95 = (bf16[480,768]{1,0:T(8,128)(2,1)S(1)}, f32[480,768]{1,0:T(8,128)S(1)}) custom-call(bf16[1024,768]{1,0:T(8,128)(2,1)S(1)} %shard_map.86.own_ref, bf16[1024,768]{1,0:T(8,128)(2,1)S(1)} %collective-permute-done.2.other_ref, bf16[4,96,1024]{2,1,0:T(8,128)(2,1)S(1)} %collective-permute-done.23.refs_0_, ...), custom_call_target="tpu_custom_call" | custom-call | flops 1024 | bytes 1024 | tf_op jit(solution)/shard_map/pallas_call | solution.py:151
  117.5 3.7 %shard_map.96 = (bf16[192,768]{1,0:T(8,128)(2,1)S(1)}, bf16[192,768]{1,0:T(8,128)(2,1)S(1)}, bf16[192,768]{1,0:T(8,128)(2,1)S(1)}, f32[192,768]{1,0:T(8,128)S(1)}) custom-call(bf16[1024,768]{1,0:T(8,128)(2,1)S(1)} %shard_map.86.own_ref, bf16[1024,768]{1,0:T(8,128)(2,1)S(1)} %collective-permute-done.2.other_ref, ...), custom_call_target="tpu_custom_call" | custom-call | flops 1024 | bytes 1024 | tf_op jit(solution)/shard_map/pallas_call | solution.py:151
  122.0 2.1 collective-permute-done.36.got_ref
  124.4 2.9 %collective-permute-done.35.got_ref = bf16[192,768]{1,0:T(8,128)(2,1)S(1)} collective-permute-done((bf16[192,768]{1,0:T(8,128)(2,1)S(1)}, bf16[192,768]{1,0:T(8,128)(2,1)S(1)}, u32[]{:S(2)}, u32[]{:S(2)}) %collective-permute-start.35) | collective-permute-done | bytes 294944 | tf_op jit(solution)/shard_map/ppermute | solution.py:57
  128.2 1.7 add_convert_fusion.refs_7_
  130.0 2.0 collective-permute-done.40
  132.5 4.6 %shard_map.99 = (bf16[192,768]{1,0:T(8,128)(2,1)S(1)}, bf16[192,768]{1,0:T(8,128)(2,1)S(1)}, bf16[192,768]{1,0:T(8,128)(2,1)S(1)}, f32[192,768]{1,0:T(8,128)S(1)}) custom-call(bf16[1024,768]{1,0:T(8,128)(2,1)S(1)} %copy-done.1, bf16[1024,768]{1,0:T(8,128)(2,1)S(1)} %copy-done.3, bf16[4,96,1024]{2,1,0:T(8,128)(2,1)S(1)} %collective-permute-done.32.refs_0_, ...), custom_call_target="tpu_custom_call" | custom-call | flops 1024 | bytes 1024 | tf_op jit(solution)/shard_map/pallas_call | solution.py:151
  137.3 6.1 %shard_map.100 = (bf16[288,768]{1,0:T(8,128)(2,1)S(1)}, bf16[288,768]{1,0:T(8,128)(2,1)S(1)}, bf16[288,768]{1,0:T(8,128)(2,1)S(1)}, f32[288,768]{1,0:T(8,128)S(1)}) custom-call(bf16[1024,768]{1,0:T(8,128)(2,1)S(1)} %copy-done.1, bf16[1024,768]{1,0:T(8,128)(2,1)S(1)} %copy-done.3, bf16[2,4,96,1024]{3,2,1,0:T(8,128)(2,1)S(1)} %copy-done.6, ...), custom_call_target="tpu_custom_call" | custom-call | flops 1024 | bytes 1024 | tf_op jit(solution)/shard_map/pallas_call | solution.py:151
  143.5 2.5 %collective-permute-start.41 = (bf16[288,768]{1,0:T(8,128)(2,1)S(1)}, bf16[288,768]{1,0:T(8,128)(2,1)S(1)}, u32[]{:S(2)}, u32[]{:S(2)}) collective-permute-start(bf16[288,768]{1,0:T(8,128)(2,1)S(1)} %get-tuple-element.135), channel_id=1, source_target_pairs={{0,2},{1,7},{2,4},{3,1},{4,6},{5,3},{6,0},{7,5},{8,10},{9,15},{10,... | collective-permute-start | bytes 1327112 | tf_op jit(solution)/shard_map/ppermute | solution.py:57
  150.1 3.6 %collective-permute-done.41 = bf16[288,768]{1,0:T(8,128)(2,1)S(1)} collective-permute-done((bf16[288,768]{1,0:T(8,128)(2,1)S(1)}, bf16[288,768]{1,0:T(8,128)(2,1)S(1)}, u32[]{:S(2)}, u32[]{:S(2)}) %collective-permute-start.41) | collective-permute-done | bytes 442400 | tf_op jit(solution)/shard_map/ppermute | solution.py:57
  154.5 2.0 collective-permute-start.48
  156.6 10.0 %collective-permute-done.48.got_ref = bf16[192,768]{1,0:T(8,128)(2,1)S(1)} collective-permute-done((bf16[192,768]{1,0:T(8,128)(2,1)S(1)}, bf16[192,768]{1,0:T(8,128)(2,1)S(1)}, u32[]{:S(2)}, u32[]{:S(2)}) %collective-permute-start.48) | collective-permute-done | bytes 294944 | tf_op jit(solution)/shard_map/ppermute | solution.py:57
  167.1 2.7 %collective-permute-done.47 = bf16[192,768]{1,0:T(8,128)(2,1)S(1)} collective-permute-done((bf16[192,768]{1,0:T(8,128)(2,1)S(1)}, bf16[192,768]{1,0:T(8,128)(2,1)S(1)}, u32[]{:S(2)}, u32[]{:S(2)}) %collective-permute-start.47) | collective-permute-done | bytes 294944 | tf_op jit(solution)/shard_map/ppermute | solution.py:57
  169.9 9.8 %collective-permute-done.49.got_ref = bf16[192,768]{1,0:T(8,128)(2,1)S(1)} collective-permute-done((bf16[192,768]{1,0:T(8,128)(2,1)S(1)}, bf16[192,768]{1,0:T(8,128)(2,1)S(1)}, u32[]{:S(2)}, u32[]{:S(2)}) %collective-permute-start.49) | collective-permute-done | bytes 294944 | tf_op jit(solution)/shard_map/ppermute | solution.py:57
  181.6 2.2 %collective-permute-start.52 = (f32[1,1664]{1,0:T(1,128)S(1)}, f32[1,1664]{1,0:T(1,128)S(1)}, u32[]{:S(2)}, u32[]{:S(2)}) collective-permute-start(f32[1,1664]{1,0:T(1,128)S(1)} %constant_dynamic-update-slice_fusion), channel_id=1, source_target_pairs={{0,6},{1,3},{2,0},{3,5},{4,2},{5,7},{6,4},{7,1},{8,14},{9,11},{10,... | collective-permute-start | bytes 19976 | tf_op jit(solution)/shard_map/ppermute | solution.py:57
  183.9 1.6 collective-permute-done.50
  187.7 2.0 shard_map.105
  189.7 2.7 %collective-permute-start.55 = (f32[1,1024]{1,0:T(1,128)S(1)}, f32[1,1024]{1,0:T(1,128)S(1)}, u32[]{:S(2)}, u32[]{:S(2)}) collective-permute-start(f32[1,1024]{1,0:T(1,128)S(1)} %get-tuple-element.162), channel_id=1, source_target_pairs={{0,8},{1,25},{2,10},{3,27},{4,12},{5,29},{6,14},{7,31},{8,16},{9,1... | collective-permute-start | bytes 12296 | tf_op jit(solution)/shard_map/ppermute | solution.py:57
  192.4 1.9 collective-permute-start.56
  194.4 2.5 %collective-permute-start.57 = (f32[1,1024]{1,0:T(1,128)S(1)}, f32[1,1024]{1,0:T(1,128)S(1)}, u32[]{:S(2)}, u32[]{:S(2)}) collective-permute-start(f32[1,1024]{1,0:T(1,128)S(1)} %get-tuple-element.162), channel_id=1, source_target_pairs={{0,24},{1,9},{2,26},{3,11},{4,28},{5,13},{6,30},{7,15},{8,0},{9,17... | collective-permute-start | bytes 12296 | tf_op jit(solution)/shard_map/ppermute | solution.py:57
  199.1 2.1 collective-permute-start.59
  201.2 2.5 %collective-permute-start.60 = (f32[1,1024]{1,0:T(1,128)S(1)}, f32[1,1024]{1,0:T(1,128)S(1)}, u32[]{:S(2)}, u32[]{:S(2)}) collective-permute-start(f32[1,1024]{1,0:T(1,128)S(1)} %add_add_fusion.2), channel_id=1, source_target_pairs={{0,96},{1,33},{2,98},{3,35},{4,100},{5,37},{6,102},{7,39},{8,104},... | collective-permute-start | bytes 12296 | tf_op jit(solution)/shard_map/ppermute | solution.py:57
  205.1 1.7 copy-done.13
  206.8 3.5 %shard_map.106 = (f32[768,1536]{1,0:T(8,128)}, f32[1,768]{1,0:T(1,128)S(1)}) custom-call(f32[1,1024]{1,0:T(1,128)S(1)} %add_add_fusion.1.summed_ref, f32[1,128]{1,0:T(1,128)S(1)} %slice.20.row_total_ref, f32[1,1536]{1,0:T(1,128)S(1)} %get-tuple-element.163.clip_ref, f32[1,1536]{1,0:T(1,128)S(1)} %get-tuple-element.164.column_ref, ...), custom_call_target="tpu_custom_call" | custom-call | flops 1024 | bytes 1024 | tf_op jit(solution)/shard_map/pallas_call | solution.py:337
  (242 shorter events, 50.6 us)
Async XLA Ops:
  2.9 5.2 %collective-permute-start.1 = (bf16[192,1024]{1,0:T(8,128)(2,1)}, bf16[192,1024]{1,0:T(8,128)(2,1)S(1)}, u32[]{:S(2)}, u32[]{:S(2)}) collective-permute-start(bf16[192,1024]{1,0:T(8,128)(2,1)} %get-tuple-element.86.refs_0_), channel_id=1, source_target_pairs={{0,1},{1,0},{2,3},{3,2},{4,5},{5,4},{6,7},{7,6},{8,9},{9,8},{10,11... | collective-permute-start | bytes 1179656 | tf_op jit(solution)/shard_map/ppermute | solution.py:57
  3.4 16.3 %collective-permute-start.3 = (bf16[192,1024]{1,0:T(8,128)(2,1)}, bf16[192,1024]{1,0:T(8,128)(2,1)S(1)}, u32[]{:S(2)}, u32[]{:S(2)}) collective-permute-start(bf16[192,1024]{1,0:T(8,128)(2,1)} %get-tuple-element.85.refs_0_), channel_id=1, source_target_pairs={{0,32},{1,97},{2,34},{3,99},{4,36},{5,101},{6,38},{7,103},{8,40},{... | collective-permute-start | bytes 1179656 | tf_op jit(solution)/shard_map/ppermute | solution.py:57
  5.1 14.7 %collective-permute-start.4 = (bf16[192,1024]{1,0:T(8,128)(2,1)}, bf16[192,1024]{1,0:T(8,128)(2,1)S(1)}, u32[]{:S(2)}, u32[]{:S(2)}) collective-permute-start(bf16[192,1024]{1,0:T(8,128)(2,1)} %get-tuple-element.86.refs_0_), channel_id=1, source_target_pairs={{0,8},{1,25},{2,10},{3,27},{4,12},{5,29},{6,14},{7,31},{8,16},{9,1... | collective-permute-start | bytes 1179656 | tf_op jit(solution)/shard_map/ppermute | solution.py:57
  6.6 13.2 %collective-permute-start.5 = (bf16[192,1024]{1,0:T(8,128)(2,1)S(1)}, bf16[192,1024]{1,0:T(8,128)(2,1)S(1)}, u32[]{:S(2)}, u32[]{:S(2)}) collective-permute-start(bf16[192,1024]{1,0:T(8,128)(2,1)S(1)} %collective-permute-done.refs_0_.refs_4_.refs_1_), channel_id=1, source_target_pairs={{0,32},{1,97},{2,34},{3,99},{4,36},{5,101},{6,38},{7,103},{8,40},{... | collective-permute-start | bytes 1179656 | tf_op jit(solution)/shard_map/ppermute | solution.py:57
  8.2 11.6 %collective-permute-start.6 = (bf16[192,1024]{1,0:T(8,128)(2,1)S(1)}, bf16[192,1024]{1,0:T(8,128)(2,1)S(1)}, u32[]{:S(2)}, u32[]{:S(2)}) collective-permute-start(bf16[192,1024]{1,0:T(8,128)(2,1)S(1)} %collective-permute-done.1.refs_1_.refs_4_), channel_id=1, source_target_pairs={{0,8},{1,25},{2,10},{3,27},{4,12},{5,29},{6,14},{7,31},{8,16},{9,1... | collective-permute-start | bytes 1179656 | tf_op jit(solution)/shard_map/ppermute | solution.py:57
  20.6 15.5 %collective-permute-start.2 = (bf16[1024,768]{1,0:T(8,128)(2,1)}, bf16[1024,768]{1,0:T(8,128)(2,1)S(1)}, u32[]{:S(2)}, u32[]{:S(2)}) collective-permute-start(bf16[1024,768]{1,0:T(8,128)(2,1)} %shard_map.87), channel_id=1, source_target_pairs={{0,1},{1,0},{2,3},{3,2},{4,5},{5,4},{6,7},{7,6},{8,9},{9,8},{10,11... | collective-permute-start | bytes 4718600 | tf_op jit(solution)/shard_map/ppermute | solution.py:57
  21.1 9.0 %collective-permute-start.10 = (bf16[192,1024]{1,0:T(8,128)(2,1)S(1)}, bf16[192,1024]{1,0:T(8,128)(2,1)S(1)}, u32[]{:S(2)}, u32[]{:S(2)}) collective-permute-start(bf16[192,1024]{1,0:T(8,128)(2,1)S(1)} %collective-permute-done.3.refs_1_.refs_2_), channel_id=1, source_target_pairs={{0,32},{1,97},{2,34},{3,99},{4,36},{5,101},{6,38},{7,103},{8,40},{... | collective-permute-start | bytes 1179656 | tf_op jit(solution)/shard_map/ppermute | solution.py:57
  21.8 9.0 %collective-permute-start.11 = (bf16[192,1024]{1,0:T(8,128)(2,1)S(1)}, bf16[192,1024]{1,0:T(8,128)(2,1)S(1)}, u32[]{:S(2)}, u32[]{:S(2)}) collective-permute-start(bf16[192,1024]{1,0:T(8,128)(2,1)S(1)} %collective-permute-done.4.refs_1_), channel_id=1, source_target_pairs={{0,8},{1,25},{2,10},{3,27},{4,12},{5,29},{6,14},{7,31},{8,16},{9,1... | collective-permute-start | bytes 1179656 | tf_op jit(solution)/shard_map/ppermute | solution.py:57
  23.0 7.8 %collective-permute-start.9 = (bf16[192,1024]{1,0:T(8,128)(2,1)S(1)}, bf16[192,1024]{1,0:T(8,128)(2,1)S(1)}, u32[]{:S(2)}, u32[]{:S(2)}) collective-permute-start(bf16[192,1024]{1,0:T(8,128)(2,1)S(1)} %collective-permute-done.5.refs_5_.refs_3_), channel_id=1, source_target_pairs={{0,1},{1,0},{2,3},{3,2},{4,5},{5,4},{6,7},{7,6},{8,9},{9,8},{10,11... | collective-permute-start | bytes 1179656 | tf_op jit(solution)/shard_map/ppermute | solution.py:57
  23.9 6.9 %collective-permute-start.12 = (bf16[192,1024]{1,0:T(8,128)(2,1)S(1)}, bf16[192,1024]{1,0:T(8,128)(2,1)S(1)}, u32[]{:S(2)}, u32[]{:S(2)}) collective-permute-start(bf16[192,1024]{1,0:T(8,128)(2,1)S(1)} %collective-permute-done.6.refs_5_), channel_id=1, source_target_pairs={{0,1},{1,0},{2,3},{3,2},{4,5},{5,4},{6,7},{7,6},{8,9},{9,8},{10,11... | collective-permute-start | bytes 1179656 | tf_op jit(solution)/shard_map/ppermute | solution.py:57
  33.9 24.6 %collective-permute-start.16 = (bf16[2,4,96,1024]{3,2,1,0:T(8,128)(2,1)}, bf16[2,4,96,1024]{3,2,1,0:T(8,128)(2,1)}, u32[]{:S(2)}, u32[]{:S(2)}) collective-permute-start(bf16[2,4,96,1024]{3,2,1,0:T(8,128)(2,1)} %shard_map.91.refs_9_.refs_2_), channel_id=1, source_target_pairs={{0,32},{1,97},{2,34},{3,99},{4,36},{5,101},{6,38},{7,103},{8,40},{... | collective-permute-start | bytes 4718600 | tf_op jit(solution)/shard_map/ppermute | solution.py:57
  35.6 23.0 %collective-permute-start.15 = (bf16[2,4,96,1024]{3,2,1,0:T(8,128)(2,1)}, bf16[2,4,96,1024]{3,2,1,0:T(8,128)(2,1)}, u32[]{:S(2)}, u32[]{:S(2)}) collective-permute-start(bf16[2,4,96,1024]{3,2,1,0:T(8,128)(2,1)} %shard_map.90.refs_8_), channel_id=1, source_target_pairs={{0,8},{1,25},{2,10},{3,27},{4,12},{5,29},{6,14},{7,31},{8,16},{9,1... | collective-permute-start | bytes 4718600 | tf_op jit(solution)/shard_map/ppermute | solution.py:57
  47.5 10.9 %collective-permute-start.17 = (bf16[192,768]{1,0:T(8,128)(2,1)S(1)}, bf16[192,768]{1,0:T(8,128)(2,1)S(1)}, u32[]{:S(2)}, u32[]{:S(2)}) collective-permute-start(bf16[192,768]{1,0:T(8,128)(2,1)S(1)} %get-tuple-element.96), channel_id=1, source_target_pairs={{0,2},{1,7},{2,4},{3,1},{4,6},{5,3},{6,0},{7,5},{8,10},{9,15},{10,... | collective-permute-start | bytes 884744 | tf_op jit(solution)/shard_map/ppermute | solution.py:57
  58.6 5.4 %collective-permute-start.19 = (bf16[2,4,96,1024]{3,2,1,0:T(8,128)(2,1)}, bf16[2,4,96,1024]{3,2,1,0:T(8,128)(2,1)S(1)}, u32[]{:S(2)}, u32[]{:S(2)}) collective-permute-start(bf16[2,4,96,1024]{3,2,1,0:T(8,128)(2,1)} %collective-permute-done.15.refs_0_), channel_id=1, source_target_pairs={{0,1},{1,0},{2,3},{3,2},{4,5},{5,4},{6,7},{7,6},{8,9},{9,8},{10,11... | collective-permute-start | bytes 4718600 | tf_op jit(solution)/shard_map/ppermute | solution.py:57
  59.0 6.1 %collective-permute-start.20 = (bf16[2,4,96,1024]{3,2,1,0:T(8,128)(2,1)}, bf16[2,4,96,1024]{3,2,1,0:T(8,128)(2,1)S(1)}, u32[]{:S(2)}, u32[]{:S(2)}) collective-permute-start(bf16[2,4,96,1024]{3,2,1,0:T(8,128)(2,1)} %collective-permute-done.16.refs_3_), channel_id=1, source_target_pairs={{0,1},{1,0},{2,3},{3,2},{4,5},{5,4},{6,7},{7,6},{8,9},{9,8},{10,11... | collective-permute-start | bytes 4718600 | tf_op jit(solution)/shard_map/ppermute | solution.py:57
  61.6 16.8 %collective-permute-start.23 = (bf16[4,96,1024]{2,1,0:T(8,128)(2,1)S(1)}, bf16[4,96,1024]{2,1,0:T(8,128)(2,1)S(1)}, u32[]{:S(2)}, u32[]{:S(2)}) collective-permute-start(bf16[4,96,1024]{2,1,0:T(8,128)(2,1)S(1)} %slice_bitcast_fusion.3), channel_id=1, source_target_pairs={{0,8},{1,25},{2,10},{3,27},{4,12},{5,29},{6,14},{7,31},{8,16},{9,1... | collective-permute-start | bytes 2359304 | tf_op jit(solution)/shard_map/ppermute | solution.py:57
  63.4 15.0 %collective-permute-start.24 = (bf16[4,96,1024]{2,1,0:T(8,128)(2,1)S(1)}, bf16[4,96,1024]{2,1,0:T(8,128)(2,1)S(1)}, u32[]{:S(2)}, u32[]{:S(2)}) collective-permute-start(bf16[4,96,1024]{2,1,0:T(8,128)(2,1)S(1)} %slice_bitcast_fusion.2), channel_id=1, source_target_pairs={{0,32},{1,97},{2,34},{3,99},{4,36},{5,101},{6,38},{7,103},{8,40},{... | collective-permute-start | bytes 2359304 | tf_op jit(solution)/shard_map/ppermute | solution.py:57
  63.4 7.9 %collective-permute-start.25 = (bf16[192,768]{1,0:T(8,128)(2,1)S(1)}, bf16[192,768]{1,0:T(8,128)(2,1)S(1)}, u32[]{:S(2)}, u32[]{:S(2)}) collective-permute-start(bf16[192,768]{1,0:T(8,128)(2,1)S(1)} %add_convert_fusion.11), channel_id=1, source_target_pairs={{0,2},{1,7},{2,4},{3,1},{4,6},{5,3},{6,0},{7,5},{8,10},{9,15},{10,... | collective-permute-start | bytes 884744 | tf_op jit(solution)/shard_map/ppermute | solution.py:57
  65.2 29.3 %collective-permute-start.21 = (bf16[2,4,96,1024]{3,2,1,0:T(8,128)(2,1)S(1)}, bf16[2,4,96,1024]{3,2,1,0:T(8,128)(2,1)S(1)}, u32[]{:S(2)}, u32[]{:S(2)}) collective-permute-start(bf16[2,4,96,1024]{3,2,1,0:T(8,128)(2,1)S(1)} %shard_map.88), channel_id=1, source_target_pairs={{0,8},{1,25},{2,10},{3,27},{4,12},{5,29},{6,14},{7,31},{8,16},{9,1... | collective-permute-start | bytes 4718600 | tf_op jit(solution)/shard_map/ppermute | solution.py:57
  66.3 28.2 %collective-permute-start.22 = (bf16[2,4,96,1024]{3,2,1,0:T(8,128)(2,1)S(1)}, bf16[2,4,96,1024]{3,2,1,0:T(8,128)(2,1)S(1)}, u32[]{:S(2)}, u32[]{:S(2)}) collective-permute-start(bf16[2,4,96,1024]{3,2,1,0:T(8,128)(2,1)S(1)} %shard_map.89.refs_2_.refs_0_), channel_id=1, source_target_pairs={{0,32},{1,97},{2,34},{3,99},{4,36},{5,101},{6,38},{7,103},{8,40},{... | collective-permute-start | bytes 4718600 | tf_op jit(solution)/shard_map/ppermute | solution.py:57
  78.3 7.9 %collective-permute-start.28 = (bf16[192,768]{1,0:T(8,128)(2,1)S(1)}, bf16[192,768]{1,0:T(8,128)(2,1)S(1)}, u32[]{:S(2)}, u32[]{:S(2)}) collective-permute-start(bf16[192,768]{1,0:T(8,128)(2,1)S(1)} %get-tuple-element.103), channel_id=1, source_target_pairs={{0,2},{1,7},{2,4},{3,1},{4,6},{5,3},{6,0},{7,5},{8,10},{9,15},{10,... | collective-permute-start | bytes 884744 | tf_op jit(solution)/shard_map/ppermute | solution.py:57
  78.3 8.1 %collective-permute-start.26 = (bf16[4,96,1024]{2,1,0:T(8,128)(2,1)S(1)}, bf16[4,96,1024]{2,1,0:T(8,128)(2,1)S(1)}, u32[]{:S(2)}, u32[]{:S(2)}) collective-permute-start(bf16[4,96,1024]{2,1,0:T(8,128)(2,1)S(1)} %collective-permute-done.23.refs_0_), channel_id=1, source_target_pairs={{0,1},{1,0},{2,3},{3,2},{4,5},{5,4},{6,7},{7,6},{8,9},{9,8},{10,11... | collective-permute-start | bytes 2359304 | tf_op jit(solution)/shard_map/ppermute | solution.py:57
  81.1 5.3 %collective-permute-start.27 = (bf16[4,96,1024]{2,1,0:T(8,128)(2,1)S(1)}, bf16[4,96,1024]{2,1,0:T(8,128)(2,1)S(1)}, u32[]{:S(2)}, u32[]{:S(2)}) collective-permute-start(bf16[4,96,1024]{2,1,0:T(8,128)(2,1)S(1)} %collective-permute-done.24.refs_5_), channel_id=1, source_target_pairs={{0,1},{1,0},{2,3},{3,2},{4,5},{5,4},{6,7},{7,6},{8,9},{9,8},{10,11... | collective-permute-start | bytes 2359304 | tf_op jit(solution)/shard_map/ppermute | solution.py:57
  86.3 8.0 %collective-permute-start.29 = (bf16[192,768]{1,0:T(8,128)(2,1)S(1)}, bf16[192,768]{1,0:T(8,128)(2,1)S(1)}, u32[]{:S(2)}, u32[]{:S(2)}) collective-permute-start(bf16[192,768]{1,0:T(8,128)(2,1)S(1)} %add_convert_fusion.9.refs_7_), channel_id=1, source_target_pairs={{0,2},{1,7},{2,4},{3,1},{4,6},{5,3},{6,0},{7,5},{8,10},{9,15},{10,... | collective-permute-start | bytes 884744 | tf_op jit(solution)/shard_map/ppermute | solution.py:57
  91.8 12.7 %collective-permute-start.31 = (bf16[480,768]{1,0:T(8,128)(2,1)S(1)}, bf16[480,768]{1,0:T(8,128)(2,1)S(1)}, u32[]{:S(2)}, u32[]{:S(2)}) collective-permute-start(bf16[480,768]{1,0:T(8,128)(2,1)S(1)} %get-tuple-element.107), channel_id=1, source_target_pairs={{0,2},{1,7},{2,4},{3,1},{4,6},{5,3},{6,0},{7,5},{8,10},{9,15},{10,... | collective-permute-start | bytes 2211848 | tf_op jit(solution)/shard_map/ppermute | solution.py:57
  94.5 13.6 %collective-permute-start.30 = (bf16[2,4,96,1024]{3,2,1,0:T(8,128)(2,1)S(1)}, bf16[2,4,96,1024]{3,2,1,0:T(8,128)(2,1)S(1)}, u32[]{:S(2)}, u32[]{:S(2)}) collective-permute-start(bf16[2,4,96,1024]{3,2,1,0:T(8,128)(2,1)S(1)} %collective-permute-done.22.refs_3_.refs_1_), channel_id=1, source_target_pairs={{0,1},{1,0},{2,3},{3,2},{4,5},{5,4},{6,7},{7,6},{8,9},{9,8},{10,11... | collective-permute-start | bytes 4718600 | tf_op jit(solution)/shard_map/ppermute | solution.py:57
  94.5 13.5 %collective-permute-start.34 = (bf16[2,4,96,1024]{3,2,1,0:T(8,128)(2,1)S(1)}, bf16[2,4,96,1024]{3,2,1,0:T(8,128)(2,1)S(1)}, u32[]{:S(2)}, u32[]{:S(2)}) collective-permute-start(bf16[2,4,96,1024]{3,2,1,0:T(8,128)(2,1)S(1)} %collective-permute-done.21.refs_0_), channel_id=1, source_target_pairs={{0,1},{1,0},{2,3},{3,2},{4,5},{5,4},{6,7},{7,6},{8,9},{9,8},{10,11... | collective-permute-start | bytes 4718600 | tf_op jit(solution)/shard_map/ppermute | solution.py:57
  105.8 21.8 %collective-permute-start.32 = (bf16[4,96,1024]{2,1,0:T(8,128)(2,1)S(1)}, bf16[4,96,1024]{2,1,0:T(8,128)(2,1)S(1)}, u32[]{:S(2)}, u32[]{:S(2)}) collective-permute-start(bf16[4,96,1024]{2,1,0:T(8,128)(2,1)S(1)} %get-tuple-element.113), channel_id=1, source_target_pairs={{0,8},{1,25},{2,10},{3,27},{4,12},{5,29},{6,14},{7,31},{8,16},{9,1... | collective-permute-start | bytes 2359304 | tf_op jit(solution)/shard_map/ppermute | solution.py:57
  106.0 21.6 %collective-permute-start.33 = (bf16[4,96,1024]{2,1,0:T(8,128)(2,1)S(1)}, bf16[4,96,1024]{2,1,0:T(8,128)(2,1)S(1)}, u32[]{:S(2)}, u32[]{:S(2)}) collective-permute-start(bf16[4,96,1024]{2,1,0:T(8,128)(2,1)S(1)} %get-tuple-element.114), channel_id=1, source_target_pairs={{0,32},{1,97},{2,34},{3,99},{4,36},{5,101},{6,38},{7,103},{8,40},{... | collective-permute-start | bytes 2359304 | tf_op jit(solution)/shard_map/ppermute | solution.py:57
  108.1 20.1 %collective-permute-start.39 = (bf16[480,768]{1,0:T(8,128)(2,1)}, bf16[480,768]{1,0:T(8,128)(2,1)}, u32[]{:S(2)}, u32[]{:S(2)}) collective-permute-start(bf16[480,768]{1,0:T(8,128)(2,1)} %add_convert_fusion.1), channel_id=1, source_target_pairs={{0,2},{1,7},{2,4},{3,1},{4,6},{5,3},{6,0},{7,5},{8,10},{9,15},{10,... | collective-permute-start | bytes 2211848 | tf_op jit(solution)/shard_map/ppermute | solution.py:57
  108.1 16.0 %collective-permute-start.36 = (bf16[192,768]{1,0:T(8,128)(2,1)S(1)}, bf16[192,768]{1,0:T(8,128)(2,1)S(1)}, u32[]{:S(2)}, u32[]{:S(2)}) collective-permute-start(bf16[192,768]{1,0:T(8,128)(2,1)S(1)} %add_convert_fusion.10.refs_3_), channel_id=1, source_target_pairs={{0,2},{1,7},{2,4},{3,1},{4,6},{5,3},{6,0},{7,5},{8,10},{9,15},{10,... | collective-permute-start | bytes 884744 | tf_op jit(solution)/shard_map/ppermute | solution.py:57
  109.1 18.1 %collective-permute-start.35 = (bf16[192,768]{1,0:T(8,128)(2,1)S(1)}, bf16[192,768]{1,0:T(8,128)(2,1)S(1)}, u32[]{:S(2)}, u32[]{:S(2)}) collective-permute-start(bf16[192,768]{1,0:T(8,128)(2,1)S(1)} %add_convert_fusion.8), channel_id=1, source_target_pairs={{0,2},{1,7},{2,4},{3,1},{4,6},{5,3},{6,0},{7,5},{8,10},{9,15},{10,... | collective-permute-start | bytes 884744 | tf_op jit(solution)/shard_map/ppermute | solution.py:57
  124.1 7.9 %collective-permute-start.40 = (bf16[192,768]{1,0:T(8,128)(2,1)S(1)}, bf16[192,768]{1,0:T(8,128)(2,1)S(1)}, u32[]{:S(2)}, u32[]{:S(2)}) collective-permute-start(bf16[192,768]{1,0:T(8,128)(2,1)S(1)} %get-tuple-element.116), channel_id=1, source_target_pairs={{0,2},{1,7},{2,4},{3,1},{4,6},{5,3},{6,0},{7,5},{8,10},{9,15},{10,... | collective-permute-start | bytes 884744 | tf_op jit(solution)/shard_map/ppermute | solution.py:57
  129.9 17.1 %collective-permute-start.42 = (bf16[480,768]{1,0:T(8,128)(2,1)S(1)}, bf16[480,768]{1,0:T(8,128)(2,1)S(1)}, u32[]{:S(2)}, u32[]{:S(2)}) collective-permute-start(bf16[480,768]{1,0:T(8,128)(2,1)S(1)} %add_convert_fusion.refs_7_), channel_id=1, source_target_pairs={{0,2},{1,7},{2,4},{3,1},{4,6},{5,3},{6,0},{7,5},{8,10},{9,15},{10,... | collective-permute-start | bytes 2211848 | tf_op jit(solution)/shard_map/ppermute | solution.py:57
  132.1 13.9 %collective-permute-start.43 = (bf16[192,768]{1,0:T(8,128)(2,1)S(1)}, bf16[192,768]{1,0:T(8,128)(2,1)}, u32[]{:S(2)}, u32[]{:S(2)}) collective-permute-start(bf16[192,768]{1,0:T(8,128)(2,1)S(1)} %add_convert_fusion.7.refs_8_), channel_id=1, source_target_pairs={{0,2},{1,7},{2,4},{3,1},{4,6},{5,3},{6,0},{7,5},{8,10},{9,15},{10,... | collective-permute-start | bytes 884744 | tf_op jit(solution)/shard_map/ppermute | solution.py:57
  137.1 12.0 %collective-permute-start.44 = (bf16[192,768]{1,0:T(8,128)(2,1)S(1)}, bf16[192,768]{1,0:T(8,128)(2,1)}, u32[]{:S(2)}, u32[]{:S(2)}) collective-permute-start(bf16[192,768]{1,0:T(8,128)(2,1)S(1)} %get-tuple-element.131.refs_5_), channel_id=1, source_target_pairs={{0,2},{1,7},{2,4},{3,1},{4,6},{5,3},{6,0},{7,5},{8,10},{9,15},{10,... | collective-permute-start | bytes 884744 | tf_op jit(solution)/shard_map/ppermute | solution.py:57
  143.5 10.3 %collective-permute-start.41 = (bf16[288,768]{1,0:T(8,128)(2,1)S(1)}, bf16[288,768]{1,0:T(8,128)(2,1)S(1)}, u32[]{:S(2)}, u32[]{:S(2)}) collective-permute-start(bf16[288,768]{1,0:T(8,128)(2,1)S(1)} %get-tuple-element.135), channel_id=1, source_target_pairs={{0,2},{1,7},{2,4},{3,1},{4,6},{5,3},{6,0},{7,5},{8,10},{9,15},{10,... | collective-permute-start | bytes 1327112 | tf_op jit(solution)/shard_map/ppermute | solution.py:57
  153.8 13.0 %collective-permute-start.45 = (bf16[288,768]{1,0:T(8,128)(2,1)S(1)}, bf16[288,768]{1,0:T(8,128)(2,1)S(1)}, u32[]{:S(2)}, u32[]{:S(2)}) collective-permute-start(bf16[288,768]{1,0:T(8,128)(2,1)S(1)} %add_convert_fusion.3), channel_id=1, source_target_pairs={{0,2},{1,7},{2,4},{3,1},{4,6},{5,3},{6,0},{7,5},{8,10},{9,15},{10,... | collective-permute-start | bytes 1327112 | tf_op jit(solution)/shard_map/ppermute | solution.py:57
  154.5 12.1 %collective-permute-start.48 = (bf16[192,768]{1,0:T(8,128)(2,1)S(1)}, bf16[192,768]{1,0:T(8,128)(2,1)S(1)}, u32[]{:S(2)}, u32[]{:S(2)}) collective-permute-start(bf16[192,768]{1,0:T(8,128)(2,1)S(1)} %add_convert_fusion.6), channel_id=1, source_target_pairs={{0,2},{1,7},{2,4},{3,1},{4,6},{5,3},{6,0},{7,5},{8,10},{9,15},{10,... | collective-permute-start | bytes 884744 | tf_op jit(solution)/shard_map/ppermute | solution.py:57
  156.5 13.2 %collective-permute-start.47 = (bf16[192,768]{1,0:T(8,128)(2,1)S(1)}, bf16[192,768]{1,0:T(8,128)(2,1)S(1)}, u32[]{:S(2)}, u32[]{:S(2)}) collective-permute-start(bf16[192,768]{1,0:T(8,128)(2,1)S(1)} %add_convert_fusion.5), channel_id=1, source_target_pairs={{0,2},{1,7},{2,4},{3,1},{4,6},{5,3},{6,0},{7,5},{8,10},{9,15},{10,... | collective-permute-start | bytes 884744 | tf_op jit(solution)/shard_map/ppermute | solution.py:57
  167.0 13.0 %collective-permute-start.46 = (bf16[288,768]{1,0:T(8,128)(2,1)S(1)}, bf16[288,768]{1,0:T(8,128)(2,1)S(1)}, u32[]{:S(2)}, u32[]{:S(2)}) collective-permute-start(bf16[288,768]{1,0:T(8,128)(2,1)S(1)} %add_convert_fusion.2), channel_id=1, source_target_pairs={{0,2},{1,7},{2,4},{3,1},{4,6},{5,3},{6,0},{7,5},{8,10},{9,15},{10,... | collective-permute-start | bytes 1327112 | tf_op jit(solution)/shard_map/ppermute | solution.py:57
  169.8 9.9 %collective-permute-start.49 = (bf16[192,768]{1,0:T(8,128)(2,1)S(1)}, bf16[192,768]{1,0:T(8,128)(2,1)S(1)}, u32[]{:S(2)}, u32[]{:S(2)}) collective-permute-start(bf16[192,768]{1,0:T(8,128)(2,1)S(1)} %add_convert_fusion.4), channel_id=1, source_target_pairs={{0,2},{1,7},{2,4},{3,1},{4,6},{5,3},{6,0},{7,5},{8,10},{9,15},{10,... | collective-permute-start | bytes 884744 | tf_op jit(solution)/shard_map/ppermute | solution.py:57
  180.5 7.2 %collective-permute-start.54 = (f32[768,768]{1,0:T(8,128)S(1)}, f32[768,768]{1,0:T(8,128)S(1)}, u32[]{:S(2)}, u32[]{:S(2)}) collective-permute-start(f32[768,768]{1,0:T(8,128)S(1)} %get-tuple-element.161), channel_id=1, source_target_pairs={{0,1},{1,0},{2,3},{3,2},{4,5},{5,4},{6,7},{7,6},{8,9},{9,8},{10,11... | collective-permute-start | bytes 7077896 | tf_op jit(solution)/shard_map/ppermute | solution.py:57
  180.7 5.2 %collective-permute-start.51 = (f32[1,1664]{1,0:T(1,128)S(1)}, f32[1,1664]{1,0:T(1,128)S(1)}, u32[]{:S(2)}, u32[]{:S(2)}) collective-permute-start(f32[1,1664]{1,0:T(1,128)S(1)} %constant_dynamic-update-slice_fusion), channel_id=1, source_target_pairs={{0,4},{1,5},{2,6},{3,7},{4,0},{5,1},{6,2},{7,3},{8,12},{9,13},{10,... | collective-permute-start | bytes 19976 | tf_op jit(solution)/shard_map/ppermute | solution.py:57
  189.7 7.2 %collective-permute-start.55 = (f32[1,1024]{1,0:T(1,128)S(1)}, f32[1,1024]{1,0:T(1,128)S(1)}, u32[]{:S(2)}, u32[]{:S(2)}) collective-permute-start(f32[1,1024]{1,0:T(1,128)S(1)} %get-tuple-element.162), channel_id=1, source_target_pairs={{0,8},{1,25},{2,10},{3,27},{4,12},{5,29},{6,14},{7,31},{8,16},{9,1... | collective-permute-start | bytes 12296 | tf_op jit(solution)/shard_map/ppermute | solution.py:57
  192.4 5.1 %collective-permute-start.56 = (f32[1,1024]{1,0:T(1,128)S(1)}, f32[1,1024]{1,0:T(1,128)S(1)}, u32[]{:S(2)}, u32[]{:S(2)}) collective-permute-start(f32[1,1024]{1,0:T(1,128)S(1)} %get-tuple-element.162), channel_id=1, source_target_pairs={{0,16},{1,17},{2,18},{3,19},{4,20},{5,21},{6,22},{7,23},{8,24},{9,... | collective-permute-start | bytes 12296 | tf_op jit(solution)/shard_map/ppermute | solution.py:57
  198.3 6.1 %collective-permute-start.58 = (f32[1,1024]{1,0:T(1,128)S(1)}, f32[1,1024]{1,0:T(1,128)S(1)}, u32[]{:S(2)}, u32[]{:S(2)}) collective-permute-start(f32[1,1024]{1,0:T(1,128)S(1)} %add_add_fusion.2), channel_id=1, source_target_pairs={{0,32},{1,97},{2,34},{3,99},{4,36},{5,101},{6,38},{7,103},{8,40},{... | collective-permute-start | bytes 12296 | tf_op jit(solution)/shard_map/ppermute | solution.py:57
  199.1 5.3 %collective-permute-start.59 = (f32[1,1024]{1,0:T(1,128)S(1)}, f32[1,1024]{1,0:T(1,128)S(1)}, u32[]{:S(2)}, u32[]{:S(2)}) collective-permute-start(f32[1,1024]{1,0:T(1,128)S(1)} %add_add_fusion.2), channel_id=1, source_target_pairs={{0,64},{1,65},{2,66},{3,67},{4,68},{5,69},{6,70},{7,71},{8,72},{9,... | collective-permute-start | bytes 12296 | tf_op jit(solution)/shard_map/ppermute | solution.py:57
  (71 other events, 603.8 us)
